TPU v7x, 512 devices: a whole 4x8x8 slice. The times are simulated.
512 devices in a mesh: wide: 32 (over y, x_hi, core), blk: 16 (over x_lo, z).
Axes of the slice: x: 4 (x_hi: 2, x_lo: 2; x = x_hi * 2 + x_lo), y: 8, z: 8, core: 2. Of those that a mesh axis runs over, the one named last changes fastest.
Arguments:
- audio: bfloat16 [65536, 1024], P(('wide', 'blk')), may hold values from -1 to 1
- video: bfloat16 [65536, 1024], P(('wide', 'blk')), may hold values from -1 to 1
- owner: int32 [65536, 1], P(('wide', 'blk')), may hold values from 0 to 31; in each aligned block of 128 rows (0 to 127, 128 to 255, ...) at most 8 rows name the same one
- clip_feats: bfloat16 [131072, 1024], P(('wide', 'blk')), may hold values from -48 to 48
- lengths: int32 [131072], P(('wide', 'blk')), may hold values from 1 to 16
- proj_weight: bfloat16 [1024, 1024], replicated, may hold values from -0.1875 to 0.1875
Outputs:
- audio_grad: bfloat16 [65536, 1024], P(('wide', 'blk'))
- feats_grad: bfloat16 [131072, 1024], P(('wide', 'blk'))
- weight_grad: float32 [1024, 1024], P('wide')
Inputs may be any that keep to these rules, and one draw needn't show every extreme that they name: Among the 128 rows of one device, no owner is named more than 8 times, a bound that some block reaches.
All inputs are finite; a program needn't handle non-finite values.
Results may differ from a plain program's by a relative error of at most 0.02.
Values may be sent and summed in bfloat16 or wider, within the bound.
No kernel may reach another device: no remote copies, remote signals or barrier semaphores. Data moves between devices by JAX's collectives and lax.ppermute only.
A program may use at most 64 MiB of HBM per device.

v0:
```python
from functools import partial

import jax
import jax.numpy as jnp
from jax import lax
from jax.sharding import Mesh
from jax.sharding import PartitionSpec as P

BLK = ("blk_0", "blk_1")
WIDE = ("wide_0", "wide_1", "wide_2")
WIDE_BLK = ("wide_0", "wide_1", "wide_2", "blk_0", "blk_1")


def joined_along(pieces, dim):
    lengths = list(pieces.shape[1:])
    lengths[dim] *= pieces.shape[0]
    return jnp.moveaxis(pieces, 0, dim).reshape(lengths)


def stacked_from(array, axes, turns):
    pieces = array[None]
    for k in turns:
        pieces = lax.all_gather(pieces, axes[k], axis=0, tiled=True)
    held = [lax.axis_size(axes[k]) for k in reversed(turns)]
    pieces = pieces.reshape(*held, *array.shape)
    turned = sorted(range(len(turns)), key=lambda place: turns[len(turns) - 1 - place])
    return pieces.transpose(*turned, *range(len(turns), pieces.ndim)).reshape(-1, *array.shape)


def whole_of(array, axes, turns, dim):
    return joined_along(stacked_from(array, axes, turns), dim)


def in_blocks(array, dim, peers):
    lengths = array.shape
    pieces = array.reshape(*lengths[:dim], peers, lengths[dim] // peers, *lengths[dim + 1 :])
    return jnp.moveaxis(pieces, dim, 0)


def sent_and_summed(array, axis, dim):
    peers = lax.axis_size(axis)
    pieces = lax.all_to_all(in_blocks(array, dim, peers), axis, 0, 0, tiled=True)
    return jnp.sum(pieces.astype(jnp.float32), axis=0)


def sum_in_two_steps(array, axes, dim):
    far, near = axes
    own = sent_and_summed(in_blocks(array, dim, lax.axis_size(far)), near, dim + 1)
    return jnp.sum(
        lax.all_to_all(own.astype(jnp.bfloat16), far, 0, 0, tiled=True).astype(jnp.float32), axis=0
    )


def rows_for(lines, peers):
    spare = -lines.shape[0] % peers
    if not spare:
        return lines
    return jnp.concatenate([lines, jnp.zeros((spare, *lines.shape[1:]), lines.dtype)])


def sent_to_all(array, axis):
    peers = lax.axis_size(axis)
    return lax.all_to_all(
        jnp.broadcast_to(array[None], (peers, *array.shape)), axis, 0, 0, tiled=True
    )


def collect(array, axis, dim):
    pieces = sent_to_all(array, axis)
    return joined_along(pieces, dim)


def total_of(array, axes):
    lines = array.reshape(-1, array.shape[-1])
    own = sent_and_summed(rows_for(lines, lax.axis_size(axes)), axes, 0)
    whole = collect(own.astype(jnp.bfloat16), axes, 0)
    return whole[: len(lines)].reshape(array.shape).astype(jnp.float32)


def rows_dot(matrix_a, matrix_b):
    return lax.dot_general(
        matrix_a, matrix_b, (((1,), (1,)), ((), ())), preferred_element_type=jnp.float32
    )


def cols_dot(matrix_a, matrix_b):
    return lax.dot_general(
        matrix_a, matrix_b, (((0,), (0,)), ((), ())), preferred_element_type=jnp.float32
    )


def pair_coeffs(scores, labels, factor):
    return (factor * (jax.nn.sigmoid(4.0 * scores - 2.0) - labels)).astype(jnp.bfloat16)


def shards(audio, video, owner, clip_feats, lengths, proj_weight):
    blocks = lax.axis_size(BLK)
    clip_count = audio.shape[0]
    feature_count = audio.shape[1]
    factor = 4.0 / blocks
    row_ids = jnp.arange(clip_count, dtype=jnp.int32)
    offset = lax.axis_index(BLK) * clip_count
    gathered = lax.all_gather(video, BLK, axis=0, tiled=True)
    other_ids = jnp.arange(gathered.shape[0], dtype=jnp.int32)
    labels = ((offset + row_ids)[:, None] == other_ids[None, :]).astype(jnp.float32)
    coeffs = pair_coeffs(rows_dot(audio, gathered), labels, factor)
    audio_total = jnp.dot(coeffs, gathered, preferred_element_type=jnp.float32)
    gathered = whole_of(audio, BLK, (0, 1), 0)
    other_ids = jnp.arange(gathered.shape[0], dtype=jnp.int32)
    labels = (other_ids[:, None] == (offset + row_ids)[None, :]).astype(jnp.float32)
    coeffs = pair_coeffs(rows_dot(gathered, video), labels, factor)
    video_sum = cols_dot(coeffs, gathered)
    audio_grad = audio_total.astype(jnp.bfloat16)
    video_grad = video_sum.astype(jnp.bfloat16)
    peer_count = lax.axis_size(WIDE)
    slot_count = clip_feats.shape[0]
    capacity = slot_count // peer_count
    owner_peer = owner[:, 0]
    onehot = (owner_peer[:, None] == jnp.arange(peer_count, dtype=jnp.int32)[None, :]).astype(
        jnp.int32
    )
    slot_rank = jnp.sum((jnp.cumsum(onehot, axis=0) - onehot) * onehot, axis=1)
    target = owner_peer * capacity + slot_rank
    placing = (jnp.arange(slot_count, dtype=jnp.int32)[:, None] == target[None, :]).astype(
        jnp.bfloat16
    )
    packed = jnp.dot(placing, video_grad, preferred_element_type=jnp.float32).astype(jnp.bfloat16)
    packed = packed.reshape(peer_count, capacity, feature_count)
    received = lax.all_to_all(packed, WIDE, split_axis=0, concat_axis=0, tiled=True).reshape(
        slot_count, feature_count
    )
    length_scale = lax.rsqrt(lengths.astype(jnp.float32))[:, None]
    pooled = (clip_feats.astype(jnp.float32) * length_scale).astype(jnp.bfloat16)
    preact = jnp.dot(pooled, proj_weight, preferred_element_type=jnp.float32)
    _, pullback = jax.vjp(partial(jax.nn.gelu, approximate=False), preact)
    pre_grad = pullback(received.astype(jnp.float32))[0].astype(jnp.bfloat16)
    feats_grad = (rows_dot(pre_grad, proj_weight) * length_scale).astype(jnp.bfloat16)
    partial_rows = sum_in_two_steps(
        cols_dot(pooled, pre_grad).astype(jnp.bfloat16), (("wide_0", "wide_1"), "wide_2"), 0
    )
    weight_grad = total_of(partial_rows.astype(jnp.bfloat16), BLK)
    return (audio_grad, feats_grad, weight_grad)


def solution(mesh):
    finer = Mesh(
        mesh.devices.reshape(8, 2, 2, 2, 8), ("wide_0", "wide_1", "wide_2", "blk_0", "blk_1")
    )
    return jax.shard_map(
        shards,
        mesh=finer,
        in_specs=(
            P(WIDE_BLK, None),
            P(WIDE_BLK, None),
            P(WIDE_BLK, None),
            P(WIDE_BLK, None),
            P(WIDE_BLK),
            P(),
        ),
        out_specs=(P(WIDE_BLK, None), P(WIDE_BLK, None), P(WIDE, None)),
        check_vma=False,
    )
```

profile of v0, /device:TPU:6, one launch (start us, length us, event | category | flops | bytes accessed | tf_op | source)
XLA Modules:
  0.0 207.4 jit_solution(776220707376634969)
XLA Ops:
  7.2 0.0 copy-start
  7.2 0.0 all-gather.6.cloned.1.call-start
  7.2 9.9 %all-gather = bf16[256,1024]{1,0:T(8,128)(2,1)} all-gather(bf16[128,1024]{1,0:T(8,128)(2,1)} %param.6), channel_id=2, replica_groups=mesh['wide_0'=8,'wide_1'=2,'wide_2'=2,'blk_0'=2,'blk_1'=8] {'blk_0'}, dimensions={0}, use_global_device_ids=true | all-gather | bytes 786432 | tf_op jit(solution)/shard_map/all_gather | solution.py:23
  17.1 0.0 all-gather.6.cloned.1.call-update
  17.2 0.0 all-gather.4.cloned.1.call-start
  17.2 0.7 all-gather.4.cloned.1.call-update
  17.9 0.7 fusion.45
  18.7 0.2 reduce_window_sum.11
  18.8 0.8 select_reduce_fusion
  19.7 0.7 multiply_add_fusion
  20.3 60.2 %all-gather.6.cloned.1.call-done = bf16[16,128,1024]{2,1,0:T(8,128)(2,1)} async-done(((bf16[2,128,1024]{2,1,0:T(8,128)(2,1)}), bf16[16,128,1024]{2,1,0:T(8,128)(2,1)}) %all-gather.6.cloned.1.call-update) | async-done | bytes 4194320 | tf_op jit(solution)/shard_map/all_gather | solution.py:23
  80.5 0.0 copy-start.5
  80.5 4.8 %copy.15 = bf16[2,8,128,1024]{3,2,1,0:T(8,128)(2,1)} copy(bf16[2,8,128,1024]{3,2,0,1:T(8,128)(2,1)} %bitcast.29) | data formatting | bytes 8388608 | tf_op jit(solution)/shard_map/transpose | solution.py:27
  85.3 0.0 copy-done.5
  85.3 0.0 copy-start.6
  85.3 0.0 copy-start.1
  85.3 6.1 %convolution_convert_fusion.2 = bf16[128,1024]{1,0:T(8,128)(2,1)S(1)} fusion(bf16[2048,1024]{1,0:T(8,128)(2,1)} %bitcast.30, bf16[128,1024]{1,0:T(8,128)(2,1)S(1)} %copy-done.5, s32[128]{0:T(128)S(1)} %iota_add_fusion), kind=kOutput, calls=%fused_computation.27 | convolution fusion | flops 1076494336 | bytes 4719104 | tf_op jit(solution)/shard_map/dot_general | solution.py:87
  91.4 1.1 fusion.17
  92.5 9.9 %all-to-all-start = ((bf16[32,8,1024]{2,1,0:T(8,128)(2,1)}), bf16[32,8,1024]{2,1,0:T(8,128)(2,1)S(1)}, u32[]{:S(2)}, u32[]{:S(2)}) async-start(bf16[32,8,1024]{2,1,0:T(8,128)(2,1)} %fusion.17), calls=%async_computation | async-start | bytes 1048576 | tf_op jit(solution)/shard_map/all_to_all | solution.py:129
  102.4 0.0 copy-done.6
  102.4 17.7 %all-to-all-done = bf16[32,8,1024]{2,1,0:T(8,128)(2,1)S(1)} async-done(((bf16[32,8,1024]{2,1,0:T(8,128)(2,1)}), bf16[32,8,1024]{2,1,0:T(8,128)(2,1)S(1)}, u32[]{:S(2)}, u32[]{:S(2)}) %all-to-all-start) | async-done | bytes 524320 | tf_op jit(solution)/shard_map/all_to_all | solution.py:129
  120.1 0.0 copy-done
  120.1 0.0 copy-done.1
  120.1 3.3 %fusion.23 = bf16[256,1024]{1,0:T(8,128)(2,1)S(1)} fusion(bf16[32,8,1024]{2,1,0:T(8,128)(2,1)S(1)} %all-to-all-done, bf16[1024,1024]{1,0:T(8,128)(2,1)S(1)} %copy-done, bf16[256,1024]{1,0:T(8,128)(2,1)S(1)} %copy-done.1, f32[256]{0:T(256)S(1)} %convert_rsqrt_fusion), kind=kOutput, calls=%fused_computation.34 | convolution fusion | flops 556793856 | bytes 3671040 | tf_op jit(solution)/shard_map/dot_general | solution.py:134
  123.4 0.0 copy-start.2
  123.4 0.8 convolution_convert_fusion
  124.2 0.0 copy-done.2
  124.2 0.3 copy.20
  124.5 6.3 %all_to_all.25 = bf16[2,16,32,1024]{3,2,1,0:T(8,128)(2,1)} all-to-all(bf16[2,16,32,1024]{3,2,1,0:T(8,128)(2,1)S(1)} %bitcast.27), channel_id=1, replica_groups=mesh['wide_0'=8,'wide_1'=2,'wide_2'=2,'blk_0'=2,'blk_1'=8] {'wide_2'}, dimensions={0} | all-to-all | bytes 4194304 | tf_op jit(solution)/shard_map/all_to_all | solution.py:42
  130.8 0.0 copy-start.4
  130.8 2.2 %reduce_sum.46 = bf16[16,32,1024]{2,1,0:T(8,128)(2,1)S(1)} reduce(bf16[2,16,32,1024]{3,2,1,0:T(8,128)(2,1)} %all_to_all.25, bf16[]{:T(256)} %constant.99.clone.1), dimensions={0}, to_apply=%region_2.3 | reduce | flops 524288 | bytes 3145730 | tf_op jit(solution)/shard_map/reduce_sum | solution.py:43
  133.0 35.6 %all_to_all.26 = bf16[16,32,1024]{2,1,0:T(8,128)(2,1)} all-to-all(bf16[16,32,1024]{2,1,0:T(8,128)(2,1)S(1)} %reduce_sum.46), channel_id=1, replica_groups=mesh['wide_0'=8,'wide_1'=2,'wide_2'=2,'blk_0'=2,'blk_1'=8] {'wide_0','wi..., dimensions={0} | all-to-all | bytes 2097152 | tf_op jit(solution)/shard_map/all_to_all | solution.py:50
  168.7 1.4 reduce_sum.47
  170.1 0.7 reshape.41
  170.7 6.6 %all-to-all-start.3 = ((bf16[16,2,1024]{2,1,0:T(2,128)(2,1)}), bf16[16,2,1024]{2,1,0:T(2,128)(2,1)S(1)}, u32[]{:S(2)}, u32[]{:S(2)}) async-start(bf16[16,2,1024]{2,1,0:T(2,128)(2,1)} %reshape.41), calls=%async_computation.3 | async-start | bytes 131072 | tf_op jit(solution)/shard_map/all_to_all | solution.py:42
  177.4 0.0 copy-start.3
  177.4 0.0 all-gather.4.cloned.1.call-done
  177.4 0.0 copy-done.4
  177.4 6.4 %convolution_convert_fusion.3 = bf16[128,1024]{1,0:T(8,128)(2,1)} fusion(bf16[2048,1024]{1,0:T(8,128)(2,1)} %all-gather.4.cloned.1.call-done, bf16[128,1024]{1,0:T(8,128)(2,1)S(1)} %copy-done.4, s32[128]{0:T(128)S(1)} %iota_add_fusion), kind=kOutput, calls=%fused_computation.28 | convolution fusion | flops 1076494336 | bytes 4719104 | tf_op jit(solution)/shard_map/dot_general | solution.py:107
  183.8 0.8 all-to-all-done.3
  184.6 0.1 reduce_sum.48
  184.7 0.7 broadcast_in_dim.5
  185.4 7.3 %all-to-all-start.4 = ((bf16[16,2,1024]{2,1,0:T(2,128)(2,1)}), bf16[16,2,1024]{2,1,0:T(2,128)(2,1)S(1)}, u32[]{:S(2)}, u32[]{:S(2)}) async-start(bf16[16,2,1024]{2,1,0:T(2,128)(2,1)} %broadcast_in_dim.5), calls=%async_computation.4 | async-start | bytes 131072 | tf_op jit(solution)/shard_map/all_to_all | solution.py:63
  192.7 0.0 copy-done.3
  192.7 1.5 fusion.16
  194.2 5.7 %all-to-all-done.4 = bf16[16,2,1024]{2,1,0:T(2,128)(2,1)S(1)} async-done(((bf16[16,2,1024]{2,1,0:T(2,128)(2,1)}), bf16[16,2,1024]{2,1,0:T(2,128)(2,1)S(1)}, u32[]{:S(2)}, u32[]{:S(2)}) %all-to-all-start.4) | async-done | bytes 65568 | tf_op jit(solution)/shard_map/all_to_all | solution.py:63
  199.9 0.7 reshape.43
  (2 shorter events, 0.0 us)
Async XLA Ops:
  7.2 112.9 %copy-start = (bf16[1024,1024]{1,0:T(8,128)(2,1)S(1)}, bf16[1024,1024]{1,0:T(8,128)(2,1)}, u32[]{:S(2)}) copy-start(bf16[1024,1024]{1,0:T(8,128)(2,1)} %param.11) | copy-start | bytes 6291460
  7.2 73.3 %all-gather.6.cloned.1.call-start = ((), (), s32[]{:S(2)}) async-start(), calls=%async_computation.6 | async-start | bytes 4718592 | tf_op jit(solution)/shard_map/all_gather | solution.py:23
  17.2 160.2 %all-gather.4.cloned.1.call-start = ((), (), s32[]{:S(2)}) async-start(), calls=%async_computation.5 | async-start | bytes 4456448 | tf_op jit(solution)/shard_map/all_gather | solution.py:103
  80.5 4.8 %copy-start.5 = (bf16[128,1024]{1,0:T(8,128)(2,1)S(1)}, bf16[128,1024]{1,0:T(8,128)(2,1)}, u32[]{:S(2)}) copy-start(bf16[128,1024]{1,0:T(8,128)(2,1)} %param.7) | copy-start | bytes 786436
  85.3 17.1 %copy-start.6 = (s32[256]{0:T(256)S(1)}, s32[256]{0:T(256)}, u32[]{:S(2)}) copy-start(s32[256]{0:T(256)} %param.10) | copy-start | bytes 3076
  85.3 34.8 %copy-start.1 = (bf16[256,1024]{1,0:T(8,128)(2,1)S(1)}, bf16[256,1024]{1,0:T(8,128)(2,1)}, u32[]{:S(2)}) copy-start(bf16[256,1024]{1,0:T(8,128)(2,1)} %param.9) | copy-start | bytes 1572868
  92.5 27.6 %all-to-all-start = ((bf16[32,8,1024]{2,1,0:T(8,128)(2,1)}), bf16[32,8,1024]{2,1,0:T(8,128)(2,1)S(1)}, u32[]{:S(2)}, u32[]{:S(2)}) async-start(bf16[32,8,1024]{2,1,0:T(8,128)(2,1)} %fusion.17), calls=%async_computation | async-start | bytes 1048576 | tf_op jit(solution)/shard_map/all_to_all | solution.py:129
  123.4 0.9 copy-start.2
  130.8 46.6 %copy-start.4 = (bf16[128,1024]{1,0:T(8,128)(2,1)S(1)}, bf16[128,1024]{1,0:T(8,128)(2,1)}, u32[]{:S(2)}) copy-start(bf16[128,1024]{1,0:T(8,128)(2,1)} %param.6) | copy-start | bytes 786436
  170.7 13.9 %all-to-all-start.3 = ((bf16[16,2,1024]{2,1,0:T(2,128)(2,1)}), bf16[16,2,1024]{2,1,0:T(2,128)(2,1)S(1)}, u32[]{:S(2)}, u32[]{:S(2)}) async-start(bf16[16,2,1024]{2,1,0:T(2,128)(2,1)} %reshape.41), calls=%async_computation.3 | async-start | bytes 131072 | tf_op jit(solution)/shard_map/all_to_all | solution.py:42
  177.4 15.3 %copy-start.3 = (bf16[256,1024]{1,0:T(8,128)(2,1)S(1)}, bf16[256,1024]{1,0:T(8,128)(2,1)}, u32[]{:S(2)}) copy-start(bf16[256,1024]{1,0:T(8,128)(2,1)} %copy-done.2) | copy-start | bytes 1572868
  185.4 14.5 %all-to-all-start.4 = ((bf16[16,2,1024]{2,1,0:T(2,128)(2,1)}), bf16[16,2,1024]{2,1,0:T(2,128)(2,1)S(1)}, u32[]{:S(2)}, u32[]{:S(2)}) async-start(bf16[16,2,1024]{2,1,0:T(2,128)(2,1)} %broadcast_in_dim.5), calls=%async_computation.4 | async-start | bytes 131072 | tf_op jit(solution)/shard_map/all_to_all | solution.py:63
Sparse Core Ops, SparseCore 0:
  17.3 63.1 all-gather.5
  82.6 82.0 all-gather.3
where the time goes:
time: 209 us; the launch traced here: 207 us
  waiting for transfers between devices  85.1 us (41%)
  blocking collectives  51.9 us (25%)
  starting transfers between devices  23.8 us (11%)
  matrix products  19.2 us (9%)
  between operations  14.2 us (7%)
  local copies, waits for them, and re-layouts  7.08 us (3%)
  other arithmetic  6.12 us (3%)
    all_gather x1, waiting for transfers between devices, stacked_from(): pieces = lax.all_gather(pieces, axes[k], axis=0, tiled=True)  60.2 us
    all_to_all x1, blocking collectives, sum_in_two_steps(): lax.all_to_all(own.astype(jnp.bfloat16), far, 0, 0, tiled=True)  35.6 us
    all_to_all x1, waiting for transfers between devices, shards(): lax.all_to_all(packed, WIDE, split_axis=0, concat_axis=0, tiled=True)  17.7 us
    all_gather x1, blocking collectives, stacked_from(): pieces = lax.all_gather(pieces, axes[k], axis=0, tiled=True)  9.91 us
    all_to_all x1, starting transfers between devices, shards(): lax.all_to_all(packed, WIDE, split_axis=0, concat_axis=0, tiled=True)  9.86 us
    all_to_all x1, starting transfers between devices, sent_to_all(): lax.all_to_all(jnp.broadcast_to(array[None], (peers, *array.shape)), axis...  7.29 us
    dot_general x2, matrix products, cols_dot(): lax.dot_general(matrix_a, matrix_b, (((0,), (0,)), ((), ())), preferred_e...  6.92 us
    all_to_all x1, starting transfers between devices, sent_and_summed(): lax.all_to_all(in_blocks(array, dim, peers), axis, 0, 0, tiled=True)  6.62 us
  transfers between devices with their start and end apart: 5, of which 4 were waited for; matrix products, arithmetic and copies ran while one was open for 15% of the time, Pallas kernels for 0%

commit v1 on v0

v1 whole, which is shorter than its diff:
```python
import jax
import jax.numpy as jnp
from jax import lax
from jax.sharding import Mesh
from jax.sharding import PartitionSpec as P

AXES = ("wide_y", "wide_x", "wide_c", "blk_x", "blk_z")
WIDE = ("wide_y", "wide_x", "wide_c")
BLK = ("blk_x", "blk_z")
BF16 = jnp.bfloat16
F32 = jnp.float32


def swapped(array, axis):
    return lax.ppermute(array, axis, [(0, 1), (1, 0)])


def rows_dot(matrix_a, matrix_b):
    return lax.dot_general(
        matrix_a, matrix_b, (((1,), (1,)), ((), ())), preferred_element_type=F32
    )


def cols_dot(matrix_a, matrix_b):
    return lax.dot_general(
        matrix_a, matrix_b, (((0,), (0,)), ((), ())), preferred_element_type=F32
    )


def plain_dot(matrix_a, matrix_b):
    return jnp.dot(matrix_a, matrix_b, preferred_element_type=F32)


def gelu_slope(v):
    cdf = 0.5 * (1.0 + lax.erf(v * 0.7071067811865476))
    return cdf + v * (0.3989422804014327 * jnp.exp(-0.5 * v * v))


def pair_coeffs(scores, labels, factor):
    return (factor * (jax.nn.sigmoid(4.0 * scores - 2.0) - labels)).astype(BF16)


def placing_of(owner, slot_count, capacity):
    count = owner.shape[0]
    ids = jnp.arange(count, dtype=jnp.int32)
    peer = owner[:, 0]
    before = (peer[:, None] == peer[None, :]) & (ids[:, None] < ids[None, :])
    target = peer * capacity + jnp.sum(before.astype(jnp.int32), axis=0)
    return (jnp.arange(slot_count, dtype=jnp.int32)[:, None] == target[None, :]).astype(BF16)


def picking_of(core, feature_count):
    half = feature_count // 2
    ny, nx = lax.axis_size("wide_y"), lax.axis_size("wide_x")
    bx, bz = lax.axis_size("blk_x"), lax.axis_size("blk_z")
    share = half // (ny * nx * bx)
    place = jnp.arange(half, dtype=jnp.int32)
    within, rest = place % share, place // share
    y, rest = rest % ny, rest // ny
    x_blk, x_wide = rest % bx, rest // bx
    feature = (((y * nx + x_wide) * 2 + core) * bx + x_blk) * share + within
    return (jnp.arange(feature_count, dtype=jnp.int32)[:, None] == feature[None, :]).astype(BF16)


def shards(audio, video, owner, clip_feats, lengths, proj_weight):
    clips, features = audio.shape
    blocks = lax.axis_size(BLK)
    factor = 4.0 / blocks
    z, core = lax.axis_index("blk_z"), lax.axis_index("wide_c")
    nz = lax.axis_size("blk_z")

    audio_line = lax.all_gather(audio, "blk_z", axis=0, tiled=True)
    video_line = lax.all_gather(video, "blk_z", axis=0, tiled=True)

    peers = lax.axis_size(WIDE)
    slots = clip_feats.shape[0]
    capacity = slots // peers
    length_scale = lax.rsqrt(lengths.astype(F32))[:, None]
    pooled = (clip_feats.astype(F32) * length_scale).astype(BF16)
    pooled_slots = lax.all_to_all(
        pooled.reshape(peers, capacity, features), WIDE, 0, 0, tiled=True
    ).reshape(slots, features)
    both = swapped(jnp.concatenate([video, audio]), "blk_x")
    video_pair = jnp.concatenate([video, both[:clips]])
    audio_pair = jnp.concatenate([audio, both[clips:]])
    slope_own = gelu_slope(plain_dot(pooled, proj_weight))

    placing = placing_of(owner, slots, capacity)
    clip_rows = cols_dot(placing, pooled_slots).astype(BF16)
    row_pair = jnp.concatenate([clip_rows, swapped(clip_rows, "blk_x")])
    slope_pair = gelu_slope(plain_dot(row_pair, proj_weight))
    picked = plain_dot(row_pair, picking_of(core, features)).astype(BF16)
    other = plain_dot(row_pair, picking_of(1 - core, features)).astype(BF16)
    picked = jnp.concatenate([picked, swapped(other, "wide_c")])

    row_ids = jnp.arange(nz * clips, dtype=jnp.int32)[:, None]
    col_ids = jnp.arange(2 * clips, dtype=jnp.int32)[None, :]
    labels = ((row_ids == z * clips + col_ids) & (col_ids < clips)).astype(F32)
    coeffs = pair_coeffs(rows_dot(audio_line, video_pair), labels, factor)
    video_part = cols_dot(coeffs, audio_line)

    pre_part = (video_part * slope_pair).astype(BF16)
    pre_both = jnp.concatenate([pre_part, swapped(pre_part, "wide_c")])
    weight_part = cols_dot(picked, pre_both).astype(BF16)
    nx = lax.axis_size(("wide_x", "blk_x"))
    ny = lax.axis_size("wide_y")
    pieces = lax.all_to_all(
        weight_part.reshape(nx, -1, features), ("wide_x", "blk_x"), 0, 0, tiled=True
    )
    summed = jnp.sum(pieces.astype(F32), axis=0).astype(BF16)
    rows, cols = summed.shape[0] // ny, features // nz
    summed = summed.reshape(ny, rows, nz, cols).transpose(0, 2, 1, 3).reshape(ny * nz, rows, cols)
    pieces = lax.all_to_all(summed, ("wide_y", "blk_z"), 0, 0, tiled=True)
    total = jnp.sum(pieces.astype(F32), axis=0).astype(BF16)
    gathered = lax.all_to_all(
        jnp.broadcast_to(total[None], (blocks, rows, cols)), BLK, 0, 0, tiled=True
    )
    weight_grad = (
        gathered.reshape(-1, nz, rows, cols).transpose(0, 2, 1, 3).reshape(-1, features).astype(F32)
    )

    arrived = swapped(video_part[clips:].astype(BF16), "blk_x")
    video_grad = (video_part[:clips] + arrived.astype(F32)).astype(BF16)
    packed = plain_dot(placing, video_grad).astype(BF16)
    received = lax.all_to_all(
        packed.reshape(peers, capacity, features), WIDE, 0, 0, tiled=True
    ).reshape(slots, features)
    pre_grad = (received.astype(F32) * slope_own).astype(BF16)
    feats_grad = (rows_dot(pre_grad, proj_weight) * length_scale).astype(BF16)

    coeffs = pair_coeffs(rows_dot(audio_pair, video_line), labels.T, factor)
    audio_part = plain_dot(coeffs, video_line)
    arrived = swapped(audio_part[clips:].astype(BF16), "blk_x")
    audio_grad = (audio_part[:clips] + arrived.astype(F32)).astype(BF16)
    return (audio_grad, feats_grad, weight_grad)


def solution(mesh):
    finer = Mesh(mesh.devices.reshape(8, 2, 2, 2, 8), AXES)
    rows = P(AXES, None)
    return jax.shard_map(
        shards,
        mesh=finer,
        in_specs=(rows, rows, rows, rows, P(AXES), P()),
        out_specs=(rows, rows, P(WIDE, None)),
        check_vma=False,
    )
```

time: 209 us -> 169 us (0.81)
  blocking collectives: 51.9 us -> 17.8 us
  waiting for transfers between devices: 85.1 us -> 51.3 us
  starting transfers between devices: 23.8 us -> 51 us
  matrix products: 19.2 us -> 21.4 us
    all_gather x2, waiting for transfers between devices: 60.2 us -> 10.6 us  [the longest x1 10.6 us: shards(): audio_line = lax.all_gather(audio, 'blk_z', axis=0, tiled=True)]
    ppermute x0 -> x6, waiting for transfers between devices: none -> 33.3 us  [swapped(): return lax.ppermute(array, axis, [(0, 1), (1, 0)])]
    all_to_all x2 -> x1, blocking collectives: 41.9 us -> 17.8 us  [shards(): lax.all_to_all(weight_part.reshape(nx, -1, features), ('wide_x', 'blk_x')...]
    all_to_all x3 -> x4, waiting for transfers between devices: 24.2 us -> 6.05 us  [the longest x1 3.8 us: shards(): lax.all_to_all(jnp.broadcast_to(total[None], (blocks, rows, cols)), BLK,...]
    ppermute x0 -> x6, starting transfers between devices: none -> 14.3 us  [swapped(): return lax.ppermute(array, axis, [(0, 1), (1, 0)])]
    all_to_all x3 -> x4, starting transfers between devices: 23.8 us -> 36.6 us  [the longest x1 10.5 us: shards(): pieces = lax.all_to_all(summed, ('wide_y', 'blk_z'), 0, 0, tiled=True)]
    all_gather x1 -> x0, blocking collectives: 9.91 us -> none  [stacked_from(): pieces = lax.all_gather(pieces, axes[k], axis=0, tiled=True)]
    reduce_sum x4 -> x3, other arithmetic: 4.54 us -> 0.37 us  [the longest x1 0.2 us: shards(): summed = jnp.sum(pieces.astype(F32), axis=0).astype(BF16)]
  transfers between devices with their start and end apart: 5 -> 12, of which waited for: 4 -> 6; matrix products, arithmetic and copies ran while one was open for 15% -> 19% of each run, Pallas kernels for 0% -> 0%
where the time goes in v1:
time: 169 us; the launch traced here: 168 us
  waiting for transfers between devices  51.3 us (30%)
  starting transfers between devices  51 us (30%)
  matrix products  21.4 us (13%)
  blocking collectives  17.8 us (11%)
  between operations  14.4 us (9%)
  local copies, waits for them, and re-layouts  6.22 us (4%)
  other arithmetic  5.79 us (3%)
    ppermute x6, waiting for transfers between devices, swapped(): return lax.ppermute(array, axis, [(0, 1), (1, 0)])  33.3 us
    all_to_all x1, blocking collectives, shards(): lax.all_to_all(weight_part.reshape(nx, -1, features), ('wide_x', 'blk_x')...  17.8 us
    ppermute x6, starting transfers between devices, swapped(): return lax.ppermute(array, axis, [(0, 1), (1, 0)])  14.3 us
    dot_general x5, matrix products, plain_dot(): return jnp.dot(matrix_a, matrix_b, preferred_element_type=F32)  12.5 us
    all_gather x1, waiting for transfers between devices, shards(): audio_line = lax.all_gather(audio, 'blk_z', axis=0, tiled=True)  10.6 us
    all_to_all x1, starting transfers between devices, shards(): pieces = lax.all_to_all(summed, ('wide_y', 'blk_z'), 0, 0, tiled=True)  10.5 us
    all_to_all x1, starting transfers between devices, shards(): lax.all_to_all(pooled.reshape(peers, capacity, features), WIDE, 0, 0, til...  10.2 us
    all_to_all x1, starting transfers between devices, shards(): lax.all_to_all(jnp.broadcast_to(total[None], (blocks, rows, cols)), BLK,...  8.14 us
  transfers between devices with their start and end apart: 12, of which 6 were waited for; matrix products, arithmetic and copies ran while one was open for 19% of the time, Pallas kernels for 0%

profile of v1, /device:TPU:6, one launch (start us, length us, event | category | flops | bytes accessed | tf_op | source)
XLA Modules:
  0.0 167.8 jit_solution(16764494256596705379)
XLA Ops:
  7.2 0.0 copy-start
  7.2 0.0 copy-start.2
  7.2 0.0 all-gather.5.cloned.1.call-start
  7.3 0.7 all-gather.5.cloned.1.call-update
  7.9 0.7 convert_rsqrt_fusion
  8.7 2.0 %fusion.78 = bf16[32,8,1024]{2,1,0:T(8,128)(2,1)} fusion(f32[256]{0:T(256)S(1)} %convert_rsqrt_fusion, bf16[256,1024]{1,0:T(8,128)(2,1)} %param.9), kind=kLoop, calls=%fused_computation.93 | loop fusion | flops 786432 | bytes 1049600 | tf_op jit(solution)/shard_map/reshape | solution.py:81
  10.7 10.2 %all-to-all-start.1 = ((bf16[32,8,1024]{2,1,0:T(8,128)(2,1)}), bf16[32,8,1024]{2,1,0:T(8,128)(2,1)S(1)}, u32[]{:S(2)}, u32[]{:S(2)}) async-start(bf16[32,8,1024]{2,1,0:T(8,128)(2,1)} %fusion.78), calls=%async_computation.1 | async-start | bytes 1048576 | tf_op jit(solution)/shard_map/all_to_all | solution.py:80
  20.9 0.0 all-gather.3.cloned.1.call-start
  20.9 0.7 all-gather.3.cloned.1.call-update
  21.7 0.8 pad_maximum_fusion.1
  22.5 2.7 %collective-permute-start = (bf16[256,1024]{1,0:T(8,128)(2,1)}, bf16[256,1024]{1,0:T(8,128)(2,1)}, u32[]{:S(2)}, u32[]{:S(2)}) collective-permute-start(bf16[256,1024]{1,0:T(8,128)(2,1)} %pad_maximum_fusion.1), channel_id=1, source_target_pairs={{0,8},{8,0},{1,9},{9,1},{2,10},{10,2},{3,11},{11,3},{4,12},{12,4},... | collective-permute-start | bytes 1572872 | tf_op jit(solution)/shard_map/ppermute | solution.py:15
  25.3 0.1 convert_reduce_fusion
  25.4 17.1 %collective-permute-done = bf16[256,1024]{1,0:T(8,128)(2,1)} collective-permute-done((bf16[256,1024]{1,0:T(8,128)(2,1)}, bf16[256,1024]{1,0:T(8,128)(2,1)}, u32[]{:S(2)}, u32[]{:S(2)}) %collective-permute-start) | collective-permute-done | bytes 524320 | tf_op jit(solution)/shard_map/ppermute | solution.py:15
  42.5 1.9 %fusion.120 = (bf16[128,1024]{1,0:T(8,128)(2,1)}, bf16[128,1024]{1,0:T(8,128)(2,1)}) fusion(bf16[256,1024]{1,0:T(8,128)(2,1)} %collective-permute-done), kind=kLoop, calls=%fused_computation.161 | loop fusion | bytes 1048576 | tf_op jit(solution)/shard_map/slice | solution.py:84
  44.3 1.0 convolution_convert_fusion.2
  45.3 3.0 %collective-permute-start.3 = (bf16[128,1024]{1,0:T(8,128)(2,1)}, bf16[128,1024]{1,0:T(8,128)(2,1)}, u32[]{:S(2)}, u32[]{:S(2)}) collective-permute-start(bf16[128,1024]{1,0:T(8,128)(2,1)} %convolution_convert_fusion.2), channel_id=1, source_target_pairs={{0,8},{8,0},{1,9},{9,1},{2,10},{10,2},{3,11},{11,3},{4,12},{12,4},... | collective-permute-start | bytes 786440 | tf_op jit(solution)/shard_map/ppermute | solution.py:15
  48.3 10.6 %all-gather.5.cloned.1.call-done = bf16[1024,1024]{1,0:T(8,128)(2,1)} async-done(((bf16[128,1024]{1,0:T(8,128)(2,1)}), bf16[1024,1024]{1,0:T(8,128)(2,1)}) %all-gather.5.cloned.1.call-update) | async-done | bytes 2097168 | tf_op jit(solution)/shard_map/all_gather | solution.py:72
  58.9 3.7 %fusion.43 = f32[256,1024]{1,0:T(8,128)S(1)} fusion(bf16[1024,1024]{1,0:T(8,128)(2,1)} %all-gather.5.cloned.1.call-done, bf16[128,1024]{1,0:T(8,128)(2,1)S(1)} %copy-done.1, bf16[128,1024]{1,0:T(8,128)(2,1)} %get-tuple-element.3, s32[256]{0:T(256)S(1)} %iota_add_fusion, pred[256]{0:T(512)(128)(4,1)S(1)} %iota_compare_fusion.14), kind=kOutput, calls=%fused_computation.56 | convolution fusion | flops 1077673984 | bytes 3671296 | tf_op jit(solution)/shard_map/dot_general | solution.py:25
  62.7 2.4 %fusion.34 = bf16[256,1024]{1,0:T(8,128)(2,1)S(1)} fusion(f32[256,1024]{1,0:T(8,128)S(1)} %fusion.43, bf16[1024,1024]{1,0:T(8,128)(2,1)S(1)} %copy-done, bf16[128,1024]{1,0:T(8,128)(2,1)} %collective-permute-done.3, bf16[128,1024]{1,0:T(8,128)(2,1)} %convolution_convert_fusion.2), kind=kOutput, calls=%fused_computation.44 | convolution fusion | flops 540540928 | bytes 4194304 | tf_op jit(solution)/shard_map/dot_general | solution.py:31
  65.1 1.9 %collective-permute-start.5 = (bf16[256,1024]{1,0:T(8,128)(2,1)S(1)}, bf16[256,1024]{1,0:T(8,128)(2,1)S(1)}, u32[]{:S(2)}, u32[]{:S(2)}) collective-permute-start(bf16[256,1024]{1,0:T(8,128)(2,1)S(1)} %fusion.34), channel_id=1, source_target_pairs={{0,16},{16,0},{1,17},{17,1},{2,18},{18,2},{3,19},{19,3},{4,20},{20... | collective-permute-start | bytes 1572872 | tf_op jit(solution)/shard_map/ppermute | solution.py:15
  67.0 1.6 fusion.21
  68.6 2.4 %collective-permute-start.4 = (bf16[256,512]{1,0:T(8,128)(2,1)S(1)}, bf16[256,512]{1,0:T(8,128)(2,1)S(1)}, u32[]{:S(2)}, u32[]{:S(2)}) collective-permute-start(bf16[256,512]{1,0:T(8,128)(2,1)S(1)} %fusion.21), channel_id=1, source_target_pairs={{0,16},{16,0},{1,17},{17,1},{2,18},{18,2},{3,19},{19,3},{4,20},{20... | collective-permute-start | bytes 786440 | tf_op jit(solution)/shard_map/ppermute | solution.py:15
  71.1 1.6 fusion.22
  72.7 0.7 convolution_convert_fusion
  73.4 17.8 %all_to_all.25 = bf16[4,128,1024]{2,1,0:T(8,128)(2,1)S(1)} all-to-all(bf16[4,128,1024]{2,1,0:T(8,128)(2,1)S(1)} %bitcast.51), channel_id=1, replica_groups=mesh['wide_y'=8,'wide_x'=2,'wide_c'=2,'blk_x'=2,'blk_z'=8] {'wide_x','bl..., dimensions={0} | all-to-all | bytes 2097152 | tf_op jit(solution)/shard_map/all_to_all | solution.py:107
  91.2 0.2 reduce_sum.34
  91.5 0.0 copy-start.3
  91.5 0.7 copy.11
  92.3 10.5 %all-to-all-start.3 = ((bf16[64,16,128]{2,1,0:T(8,128)(2,1)}), bf16[64,16,128]{2,1,0:T(8,128)(2,1)S(1)}, u32[]{:S(2)}, u32[]{:S(2)}) async-start(bf16[64,16,128]{2,1,0:T(8,128)(2,1)} %bitcast.8), calls=%async_computation.3 | async-start | bytes 524288 | tf_op jit(solution)/shard_map/all_to_all | solution.py:113
  102.8 1.1 slice.41
  103.9 2.1 %collective-permute-start.2 = (bf16[128,1024]{1,0:T(8,128)(2,1)S(1)}, bf16[128,1024]{1,0:T(8,128)(2,1)S(1)}, u32[]{:S(2)}, u32[]{:S(2)}) collective-permute-start(bf16[128,1024]{1,0:T(8,128)(2,1)S(1)} %slice.41), channel_id=1, source_target_pairs={{0,8},{8,0},{1,9},{9,1},{2,10},{10,2},{3,11},{11,3},{4,12},{12,4},... | collective-permute-start | bytes 786440 | tf_op jit(solution)/shard_map/ppermute | solution.py:15
  106.0 6.3 %collective-permute-done.2 = bf16[128,1024]{1,0:T(8,128)(2,1)S(1)} collective-permute-done((bf16[128,1024]{1,0:T(8,128)(2,1)S(1)}, bf16[128,1024]{1,0:T(8,128)(2,1)S(1)}, u32[]{:S(2)}, u32[]{:S(2)}) %collective-permute-start.2) | collective-permute-done | bytes 262176 | tf_op jit(solution)/shard_map/ppermute | solution.py:15
  112.3 2.1 %fusion.20 = bf16[32,8,1024]{2,1,0:T(8,128)(2,1)} fusion(f32[256,1024]{1,0:T(8,128)} %copy-done.4, bf16[128,1024]{1,0:T(8,128)(2,1)S(1)} %collective-permute-done.2, s32[128]{0:T(128)S(1)} %multiply_add_fusion.2), kind=kOutput, calls=%fused_computation.29 | convolution fusion | flops 67796992 | bytes 1311232 | tf_op jit(solution)/shard_map/dot_general | solution.py:31
  114.4 2.3 %all-to-all-done.3 = bf16[64,16,128]{2,1,0:T(8,128)(2,1)S(1)} async-done(((bf16[64,16,128]{2,1,0:T(8,128)(2,1)}), bf16[64,16,128]{2,1,0:T(8,128)(2,1)S(1)}, u32[]{:S(2)}, u32[]{:S(2)}) %all-to-all-start.3) | async-done | bytes 262176 | tf_op jit(solution)/shard_map/all_to_all | solution.py:113
  116.7 7.6 %all-to-all-start = ((bf16[32,8,1024]{2,1,0:T(8,128)(2,1)}), bf16[32,8,1024]{2,1,0:T(8,128)(2,1)}, u32[]{:S(2)}, u32[]{:S(2)}) async-start(bf16[32,8,1024]{2,1,0:T(8,128)(2,1)} %fusion.20), calls=%async_computation | async-start | bytes 1048576 | tf_op jit(solution)/shard_map/all_to_all | solution.py:125
  124.3 0.0 all-gather.3.cloned.1.call-done
  124.4 0.0 copy-start.5
  124.4 4.8 %fusion.41 = f32[256,1024]{1,0:T(8,128)} fusion(bf16[1024,1024]{1,0:T(8,128)(2,1)} %all-gather.3.cloned.1.call-done, bf16[128,1024]{1,0:T(8,128)(2,1)S(1)} %copy-done.6, bf16[128,1024]{1,0:T(8,128)(2,1)S(1)} %copy-done.3, s32[256]{0:T(256)S(1)} %iota_add_fusion, pred[256]{0:T(512)(128)(4,1)S(1)} %iota_compare_fusion.14), kind=kOutput, calls=%fused_computation.54 | convolution fusion | flops 1077673984 | bytes 3671296 | tf_op jit(solution)/shard_map/dot_general | solution.py:31
  129.2 1.1 slice.42
  130.2 2.1 %collective-permute-start.1 = (bf16[128,1024]{1,0:T(8,128)(2,1)S(1)}, bf16[128,1024]{1,0:T(8,128)(2,1)S(1)}, u32[]{:S(2)}, u32[]{:S(2)}) collective-permute-start(bf16[128,1024]{1,0:T(8,128)(2,1)S(1)} %slice.42), channel_id=1, source_target_pairs={{0,8},{8,0},{1,9},{9,1},{2,10},{10,2},{3,11},{11,3},{4,12},{12,4},... | collective-permute-start | bytes 786440 | tf_op jit(solution)/shard_map/ppermute | solution.py:15
  132.4 9.9 %collective-permute-done.1 = bf16[128,1024]{1,0:T(8,128)(2,1)S(1)} collective-permute-done((bf16[128,1024]{1,0:T(8,128)(2,1)S(1)}, bf16[128,1024]{1,0:T(8,128)(2,1)S(1)}, u32[]{:S(2)}, u32[]{:S(2)}) %collective-permute-start.1) | collective-permute-done | bytes 262176 | tf_op jit(solution)/shard_map/ppermute | solution.py:15
  142.3 1.8 %fusion.46 = bf16[128,1024]{1,0:T(8,128)(2,1)} fusion(f32[256,1024]{1,0:T(8,128)} %fusion.41, bf16[128,1024]{1,0:T(8,128)(2,1)S(1)} %collective-permute-done.1), kind=kLoop, calls=%fused_computation.64 | loop fusion | flops 393216 | bytes 1048576 | tf_op jit(solution)/shard_map/convert_element_type | solution.py:134
  144.1 0.1 reduce_sum.35
  144.2 0.6 broadcast_in_dim.2
  144.9 8.1 %all-to-all-start.4 = ((bf16[16,16,128]{2,1,0:T(8,128)(2,1)}), bf16[16,16,128]{2,1,0:T(8,128)(2,1)S(1)}, u32[]{:S(2)}, u32[]{:S(2)}) async-start(bf16[16,16,128]{2,1,0:T(8,128)(2,1)} %broadcast_in_dim.2), calls=%async_computation.4 | async-start | bytes 131072 | tf_op jit(solution)/shard_map/all_to_all | solution.py:115
  153.0 3.5 %fusion.19 = bf16[256,1024]{1,0:T(8,128)(2,1)} fusion(bf16[1024,1024]{1,0:T(8,128)(2,1)S(1)} %copy-done, bf16[32,8,1024]{2,1,0:T(8,128)(2,1)} %all-to-all-done, f32[256]{0:T(256)S(1)} %convert_rsqrt_fusion, bf16[256,1024]{1,0:T(8,128)(2,1)S(1)} %copy-done.5), kind=kOutput, calls=%fused_computation.27 | convolution fusion | flops 1077936128 | bytes 3671040 | tf_op jit(solution)/shard_map/dot_general | solution.py:19
  156.5 3.8 %all-to-all-done.4 = bf16[16,16,128]{2,1,0:T(8,128)(2,1)S(1)} async-done(((bf16[16,16,128]{2,1,0:T(8,128)(2,1)}), bf16[16,16,128]{2,1,0:T(8,128)(2,1)S(1)}, u32[]{:S(2)}, u32[]{:S(2)}) %all-to-all-start.4) | async-done | bytes 65568 | tf_op jit(solution)/shard_map/all_to_all | solution.py:115
  160.3 0.7 copy.16
  (26 shorter events, 0.2 us)
Async XLA Ops:
  7.2 55.5 %copy-start = (bf16[1024,1024]{1,0:T(8,128)(2,1)S(1)}, bf16[1024,1024]{1,0:T(8,128)(2,1)}, u32[]{:S(2)}) copy-start(bf16[1024,1024]{1,0:T(8,128)(2,1)} %param.11) | copy-start | bytes 6291460
  7.2 14.5 %copy-start.2 = (bf16[128,1024]{1,0:T(8,128)(2,1)S(1)}, bf16[128,1024]{1,0:T(8,128)(2,1)}, u32[]{:S(2)}) copy-start(bf16[128,1024]{1,0:T(8,128)(2,1)} %param.6) | copy-start | bytes 786436
  7.2 14.5 %copy-start.1 = (bf16[128,1024]{1,0:T(8,128)(2,1)S(1)}, bf16[128,1024]{1,0:T(8,128)(2,1)}, u32[]{:S(2)}) copy-start(bf16[128,1024]{1,0:T(8,128)(2,1)} %param.7) | copy-start | bytes 786436
  7.2 18.1 %copy-start.7 = (s32[128,1]{0,1:T(1,128)S(1)}, s32[128,1]{0,1:T(1,128)}, u32[]{:S(2)}) copy-start(s32[128,1]{0,1:T(1,128)} %param.8) | copy-start | bytes 1540
  7.2 51.7 %all-gather.5.cloned.1.call-start = ((), (), s32[]{:S(2)}) async-start(), calls=%async_computation.6 | async-start | bytes 2359296 | tf_op jit(solution)/shard_map/all_gather | solution.py:72
  10.7 33.7 %all-to-all-start.1 = ((bf16[32,8,1024]{2,1,0:T(8,128)(2,1)}), bf16[32,8,1024]{2,1,0:T(8,128)(2,1)S(1)}, u32[]{:S(2)}, u32[]{:S(2)}) async-start(bf16[32,8,1024]{2,1,0:T(8,128)(2,1)} %fusion.78), calls=%async_computation.1 | async-start | bytes 1048576 | tf_op jit(solution)/shard_map/all_to_all | solution.py:80
  20.9 103.5 %all-gather.3.cloned.1.call-start = ((), (), s32[]{:S(2)}) async-start(), calls=%async_computation.5 | async-start | bytes 2359296 | tf_op jit(solution)/shard_map/all_gather | solution.py:73
  22.5 20.0 %collective-permute-start = (bf16[256,1024]{1,0:T(8,128)(2,1)}, bf16[256,1024]{1,0:T(8,128)(2,1)}, u32[]{:S(2)}, u32[]{:S(2)}) collective-permute-start(bf16[256,1024]{1,0:T(8,128)(2,1)} %pad_maximum_fusion.1), channel_id=1, source_target_pairs={{0,8},{8,0},{1,9},{9,1},{2,10},{10,2},{3,11},{11,3},{4,12},{12,4},... | collective-permute-start | bytes 1572872 | tf_op jit(solution)/shard_map/ppermute | solution.py:15
  45.3 17.4 %collective-permute-start.3 = (bf16[128,1024]{1,0:T(8,128)(2,1)}, bf16[128,1024]{1,0:T(8,128)(2,1)}, u32[]{:S(2)}, u32[]{:S(2)}) collective-permute-start(bf16[128,1024]{1,0:T(8,128)(2,1)} %convolution_convert_fusion.2), channel_id=1, source_target_pairs={{0,8},{8,0},{1,9},{9,1},{2,10},{10,2},{3,11},{11,3},{4,12},{12,4},... | collective-permute-start | bytes 786440 | tf_op jit(solution)/shard_map/ppermute | solution.py:15
  62.7 2.5 %copy-start.4 = (f32[256,1024]{1,0:T(8,128)}, f32[256,1024]{1,0:T(8,128)S(1)}, u32[]{:S(2)}) copy-start(f32[256,1024]{1,0:T(8,128)S(1)} %fusion.43) | copy-start | bytes 3145732
  65.1 7.5 %collective-permute-start.5 = (bf16[256,1024]{1,0:T(8,128)(2,1)S(1)}, bf16[256,1024]{1,0:T(8,128)(2,1)S(1)}, u32[]{:S(2)}, u32[]{:S(2)}) collective-permute-start(bf16[256,1024]{1,0:T(8,128)(2,1)S(1)} %fusion.34), channel_id=1, source_target_pairs={{0,16},{16,0},{1,17},{17,1},{2,18},{18,2},{3,19},{19,3},{4,20},{20... | collective-permute-start | bytes 1572872 | tf_op jit(solution)/shard_map/ppermute | solution.py:15
  68.6 4.0 %collective-permute-start.4 = (bf16[256,512]{1,0:T(8,128)(2,1)S(1)}, bf16[256,512]{1,0:T(8,128)(2,1)S(1)}, u32[]{:S(2)}, u32[]{:S(2)}) collective-permute-start(bf16[256,512]{1,0:T(8,128)(2,1)S(1)} %fusion.21), channel_id=1, source_target_pairs={{0,16},{16,0},{1,17},{17,1},{2,18},{18,2},{3,19},{19,3},{4,20},{20... | collective-permute-start | bytes 786440 | tf_op jit(solution)/shard_map/ppermute | solution.py:15
  91.5 32.9 %copy-start.3 = (bf16[128,1024]{1,0:T(8,128)(2,1)S(1)}, bf16[128,1024]{1,0:T(8,128)(2,1)}, u32[]{:S(2)}) copy-start(bf16[128,1024]{1,0:T(8,128)(2,1)} %param.6) | copy-start | bytes 786436
  91.5 32.9 %copy-start.6 = (bf16[128,1024]{1,0:T(8,128)(2,1)S(1)}, bf16[128,1024]{1,0:T(8,128)(2,1)}, u32[]{:S(2)}) copy-start(bf16[128,1024]{1,0:T(8,128)(2,1)} %get-tuple-element.4) | copy-start | bytes 786436
  92.3 24.4 %all-to-all-start.3 = ((bf16[64,16,128]{2,1,0:T(8,128)(2,1)}), bf16[64,16,128]{2,1,0:T(8,128)(2,1)S(1)}, u32[]{:S(2)}, u32[]{:S(2)}) async-start(bf16[64,16,128]{2,1,0:T(8,128)(2,1)} %bitcast.8), calls=%async_computation.3 | async-start | bytes 524288 | tf_op jit(solution)/shard_map/all_to_all | solution.py:113
  103.9 8.4 %collective-permute-start.2 = (bf16[128,1024]{1,0:T(8,128)(2,1)S(1)}, bf16[128,1024]{1,0:T(8,128)(2,1)S(1)}, u32[]{:S(2)}, u32[]{:S(2)}) collective-permute-start(bf16[128,1024]{1,0:T(8,128)(2,1)S(1)} %slice.41), channel_id=1, source_target_pairs={{0,8},{8,0},{1,9},{9,1},{2,10},{10,2},{3,11},{11,3},{4,12},{12,4},... | collective-permute-start | bytes 786440 | tf_op jit(solution)/shard_map/ppermute | solution.py:15
  116.7 27.5 %all-to-all-start = ((bf16[32,8,1024]{2,1,0:T(8,128)(2,1)}), bf16[32,8,1024]{2,1,0:T(8,128)(2,1)}, u32[]{:S(2)}, u32[]{:S(2)}) async-start(bf16[32,8,1024]{2,1,0:T(8,128)(2,1)} %fusion.20), calls=%async_computation | async-start | bytes 1048576 | tf_op jit(solution)/shard_map/all_to_all | solution.py:125
  124.4 28.6 %copy-start.5 = (bf16[256,1024]{1,0:T(8,128)(2,1)S(1)}, bf16[256,1024]{1,0:T(8,128)(2,1)}, u32[]{:S(2)}) copy-start(bf16[256,1024]{1,0:T(8,128)(2,1)} %param.9) | copy-start | bytes 1572868
  130.2 12.1 %collective-permute-start.1 = (bf16[128,1024]{1,0:T(8,128)(2,1)S(1)}, bf16[128,1024]{1,0:T(8,128)(2,1)S(1)}, u32[]{:S(2)}, u32[]{:S(2)}) collective-permute-start(bf16[128,1024]{1,0:T(8,128)(2,1)S(1)} %slice.42), channel_id=1, source_target_pairs={{0,8},{8,0},{1,9},{9,1},{2,10},{10,2},{3,11},{11,3},{4,12},{12,4},... | collective-permute-start | bytes 786440 | tf_op jit(solution)/shard_map/ppermute | solution.py:15
  144.9 15.4 %all-to-all-start.4 = ((bf16[16,16,128]{2,1,0:T(8,128)(2,1)}), bf16[16,16,128]{2,1,0:T(8,128)(2,1)S(1)}, u32[]{:S(2)}, u32[]{:S(2)}) async-start(bf16[16,16,128]{2,1,0:T(8,128)(2,1)} %broadcast_in_dim.2), calls=%async_computation.4 | async-start | bytes 131072 | tf_op jit(solution)/shard_map/all_to_all | solution.py:115
Sparse Core Ops, SparseCore 0:
  10.1 48.7 all-gather.4
  61.0 43.2 all-gather.2

commit v2 on v1

--- a/solution.py
+++ b/solution.py
@@ -52,12 +52,13 @@
 def picking_of(core, feature_count):
     half = feature_count // 2
     ny, nx = lax.axis_size("wide_y"), lax.axis_size("wide_x")
-    bx, bz = lax.axis_size("blk_x"), lax.axis_size("blk_z")
+    bx = lax.axis_size("blk_x")
     share = half // (ny * nx * bx)
     place = jnp.arange(half, dtype=jnp.int32)
     within, rest = place % share, place // share
-    y, rest = rest % ny, rest // ny
-    x_blk, x_wide = rest % bx, rest // bx
+    y, apart = rest % ny, rest // ny
+    x_wide = (apart // bx) ^ lax.axis_index("wide_x")
+    x_blk = (apart % bx) ^ lax.axis_index("blk_x")
     feature = (((y * nx + x_wide) * 2 + core) * bx + x_blk) * share + within
     return (jnp.arange(feature_count, dtype=jnp.int32)[:, None] == feature[None, :]).astype(BF16)
 
@@ -93,6 +94,10 @@
     other = plain_dot(row_pair, picking_of(1 - core, features)).astype(BF16)
     picked = jnp.concatenate([picked, swapped(other, "wide_c")])
 
+    audio_line, slope_pair, picked, slope_own, placing = lax.optimization_barrier(
+        (audio_line, slope_pair, picked, slope_own, placing)
+    )
+
     row_ids = jnp.arange(nz * clips, dtype=jnp.int32)[:, None]
     col_ids = jnp.arange(2 * clips, dtype=jnp.int32)[None, :]
     labels = ((row_ids == z * clips + col_ids) & (col_ids < clips)).astype(F32)
@@ -100,38 +105,50 @@
     video_part = cols_dot(coeffs, audio_line)
 
     pre_part = (video_part * slope_pair).astype(BF16)
+    video_part, pre_part = lax.optimization_barrier((video_part, pre_part))
     pre_both = jnp.concatenate([pre_part, swapped(pre_part, "wide_c")])
-    weight_part = cols_dot(picked, pre_both).astype(BF16)
-    nx = lax.axis_size(("wide_x", "blk_x"))
     ny = lax.axis_size("wide_y")
-    pieces = lax.all_to_all(
-        weight_part.reshape(nx, -1, features), ("wide_x", "blk_x"), 0, 0, tiled=True
-    )
-    summed = jnp.sum(pieces.astype(F32), axis=0).astype(BF16)
-    rows, cols = summed.shape[0] // ny, features // nz
-    summed = summed.reshape(ny, rows, nz, cols).transpose(0, 2, 1, 3).reshape(ny * nz, rows, cols)
-    pieces = lax.all_to_all(summed, ("wide_y", "blk_z"), 0, 0, tiled=True)
-    total = jnp.sum(pieces.astype(F32), axis=0).astype(BF16)
-    gathered = lax.all_to_all(
-        jnp.broadcast_to(total[None], (blocks, rows, cols)), BLK, 0, 0, tiled=True
-    )
-    weight_grad = (
-        gathered.reshape(-1, nz, rows, cols).transpose(0, 2, 1, 3).reshape(-1, features).astype(F32)
-    )
+    share = features // 8
+    blocks_of = [
+        cols_dot(picked[:, d * share : (d + 1) * share], pre_both) for d in range(4)
+    ]
+    summed = blocks_of[0]
+    for d in (2, 1, 3):
+        pairs = [(place, place ^ d) for place in range(4)]
+        summed = summed + lax.ppermute(
+            blocks_of[d].astype(BF16), ("wide_x", "blk_x"), pairs
+        ).astype(F32)
+    summed = summed.astype(BF16)
 
     arrived = swapped(video_part[clips:].astype(BF16), "blk_x")
+    arrived, _ = lax.optimization_barrier((arrived, blocks_of))
     video_grad = (video_part[:clips] + arrived.astype(F32)).astype(BF16)
     packed = plain_dot(placing, video_grad).astype(BF16)
     received = lax.all_to_all(
         packed.reshape(peers, capacity, features), WIDE, 0, 0, tiled=True
     ).reshape(slots, features)
+    summed, received = lax.optimization_barrier((summed, received))
     pre_grad = (received.astype(F32) * slope_own).astype(BF16)
     feats_grad = (rows_dot(pre_grad, proj_weight) * length_scale).astype(BF16)
 
+    rows, cols = summed.shape[0] // ny, features // nz
+    summed = summed.reshape(ny, rows, nz, cols).transpose(0, 2, 1, 3).reshape(ny * nz, rows, cols)
+    pieces = lax.all_to_all(summed, ("wide_y", "blk_z"), 0, 0, tiled=True)
+    video_line, summed = lax.optimization_barrier((video_line, summed))
     coeffs = pair_coeffs(rows_dot(audio_pair, video_line), labels.T, factor)
     audio_part = plain_dot(coeffs, video_line)
+    audio_part, pieces = lax.optimization_barrier((audio_part, pieces))
     arrived = swapped(audio_part[clips:].astype(BF16), "blk_x")
+    total = jnp.sum(pieces.astype(F32), axis=0).astype(BF16)
+    gathered = lax.all_to_all(
+        jnp.broadcast_to(total[None], (blocks, rows, cols)), BLK, 0, 0, tiled=True
+    )
+
+    arrived, gathered = lax.optimization_barrier((arrived, gathered))
     audio_grad = (audio_part[:clips] + arrived.astype(F32)).astype(BF16)
+    weight_grad = (
+        gathered.reshape(-1, nz, rows, cols).transpose(0, 2, 1, 3).reshape(-1, features).astype(F32)
+    )
     return (audio_grad, feats_grad, weight_grad)
 
 

time: 169 us -> 164 us (0.970)
  blocking collectives: 17.8 us -> 0 us
  starting transfers between devices: 51 us -> 58.5 us
  other arithmetic: 5.79 us -> 9.03 us
  matrix products: 21.4 us -> 23.9 us
  local copies, waits for them, and re-layouts: 6.22 us -> 4.21 us
    ppermute x6, waiting for transfers between devices: 33.3 us -> 9.26 us  [swapped(): return lax.ppermute(array, axis, [(0, 1), (1, 0)])]
    all_to_all x1 -> x0, blocking collectives: 17.8 us -> none  [shards(): lax.all_to_all(weight_part.reshape(nx, -1, features), ('wide_x', 'blk_x')...]
    ppermute x0 -> x3, waiting for transfers between devices: none -> 11 us  [shards(): lax.ppermute(blocks_of[d].astype(BF16), ('wide_x', 'blk_x'), pairs)]
    all_to_all x1, waiting for transfers between devices: 0.01 us -> 10.7 us  [shards(): lax.all_to_all(pooled.reshape(peers, capacity, features), WIDE, 0, 0, til...]
    ppermute x0 -> x3, starting transfers between devices: none -> 9.82 us  [shards(): lax.ppermute(blocks_of[d].astype(BF16), ('wide_x', 'blk_x'), pairs)]
    all_to_all x1, waiting for transfers between devices: 2.25 us -> 10.4 us  [shards(): pieces = lax.all_to_all(summed, ('wide_y', 'blk_z'), 0, 0, tiled=True)]
    all_gather x1, waiting for transfers between devices: 10.6 us -> 5.33 us  [shards(): audio_line = lax.all_gather(audio, 'blk_z', axis=0, tiled=True)]
    dot_general x3 -> x6, matrix products: 5.45 us -> 9.29 us  [cols_dot(): lax.dot_general(matrix_a, matrix_b, (((0,), (0,)), ((), ())), preferred_e...]
  transfers between devices with their start and end apart: 12 -> 15, of which waited for: 6 -> 10; matrix products, arithmetic and copies ran while one was open for 19% -> 21% of each run, Pallas kernels for 0% -> 0%
where the time goes in v2:
time: 164 us; the launch traced here: 162 us
  starting transfers between devices  58.5 us (36%)
  waiting for transfers between devices  52.1 us (32%)
  matrix products  23.9 us (15%)
  between operations  14.4 us (9%)
  other arithmetic  9.03 us (6%)
  local copies, waits for them, and re-layouts  4.21 us (3%)
    ppermute x6, starting transfers between devices, swapped(): return lax.ppermute(array, axis, [(0, 1), (1, 0)])  14.8 us
    dot_general x6, matrix products, plain_dot(): return jnp.dot(matrix_a, matrix_b, preferred_element_type=F32)  11.9 us
    ppermute x3, waiting for transfers between devices, shards(): lax.ppermute(blocks_of[d].astype(BF16), ('wide_x', 'blk_x'), pairs)  11 us
    all_to_all x1, waiting for transfers between devices, shards(): lax.all_to_all(pooled.reshape(peers, capacity, features), WIDE, 0, 0, til...  10.7 us
    all_to_all x1, waiting for transfers between devices, shards(): pieces = lax.all_to_all(summed, ('wide_y', 'blk_z'), 0, 0, tiled=True)  10.4 us
    all_to_all x1, starting transfers between devices, shards(): lax.all_to_all(pooled.reshape(peers, capacity, features), WIDE, 0, 0, til...  10.2 us
    all_to_all x1, starting transfers between devices, shards(): lax.all_to_all(packed.reshape(peers, capacity, features), WIDE, 0, 0, til...  9.99 us
    ppermute x3, starting transfers between devices, shards(): lax.ppermute(blocks_of[d].astype(BF16), ('wide_x', 'blk_x'), pairs)  9.82 us
  transfers between devices with their start and end apart: 15, of which 10 were waited for; matrix products, arithmetic and copies ran while one was open for 21% of the time, Pallas kernels for 0%

profile of v2, /device:TPU:6, one launch (start us, length us, event | category | flops | bytes accessed | tf_op | source)
XLA Modules:
  0.0 162.2 jit_solution(10243242646058370700)
XLA Ops:
  7.3 0.7 all-gather.5.cloned.1.call-update
  7.9 0.7 convert_rsqrt_fusion
  8.7 2.0 %fusion.58 = bf16[32,8,1024]{2,1,0:T(8,128)(2,1)} fusion(f32[256]{0:T(256)S(1)} %convert_rsqrt_fusion, bf16[256,1024]{1,0:T(8,128)(2,1)} %param.9), kind=kLoop, calls=%fused_computation.77 | loop fusion | flops 786432 | bytes 1049600 | tf_op jit(solution)/shard_map/reshape | solution.py:82
  10.7 10.2 %all-to-all-start = ((bf16[32,8,1024]{2,1,0:T(8,128)(2,1)}), bf16[32,8,1024]{2,1,0:T(8,128)(2,1)S(1)}, u32[]{:S(2)}, u32[]{:S(2)}) async-start(bf16[32,8,1024]{2,1,0:T(8,128)(2,1)} %fusion.58), calls=%async_computation | async-start | bytes 1048576 | tf_op jit(solution)/shard_map/all_to_all | solution.py:81
  21.0 0.8 pad_maximum_fusion.1
  21.8 2.7 %collective-permute-start = (bf16[256,1024]{1,0:T(8,128)(2,1)}, bf16[256,1024]{1,0:T(8,128)(2,1)S(1)}, u32[]{:S(2)}, u32[]{:S(2)}) collective-permute-start(bf16[256,1024]{1,0:T(8,128)(2,1)} %pad_maximum_fusion.1), channel_id=1, source_target_pairs={{0,8},{8,0},{1,9},{9,1},{2,10},{10,2},{3,11},{11,3},{4,12},{12,4},... | collective-permute-start | bytes 1572872 | tf_op jit(solution)/shard_map/ppermute | solution.py:15
  24.7 3.1 %fusion.29 = f32[256,1024]{1,0:T(8,128)} fusion(bf16[1024,1024]{1,0:T(8,128)(2,1)S(1)} %copy-done, bf16[256,1024]{1,0:T(8,128)(2,1)} %param.9, f32[256]{0:T(256)S(1)} %convert_rsqrt_fusion), kind=kOutput, calls=%fused_computation.38 | convolution fusion | flops 539754496 | bytes 3671040 | tf_op jit(solution)/shard_map/dot_general | solution.py:31
  27.8 10.7 %all-to-all-done = bf16[32,8,1024]{2,1,0:T(8,128)(2,1)S(1)} async-done(((bf16[32,8,1024]{2,1,0:T(8,128)(2,1)}), bf16[32,8,1024]{2,1,0:T(8,128)(2,1)S(1)}, u32[]{:S(2)}, u32[]{:S(2)}) %all-to-all-start) | async-done | bytes 524320 | tf_op jit(solution)/shard_map/all_to_all | solution.py:81
  38.9 2.7 %collective-permute-start.1 = (bf16[128,1024]{1,0:T(8,128)(2,1)S(1)}, bf16[128,1024]{1,0:T(8,128)(2,1)S(1)}, u32[]{:S(2)}, u32[]{:S(2)}) collective-permute-start(bf16[128,1024]{1,0:T(8,128)(2,1)S(1)} %convolution_convert_fusion.1), channel_id=1, source_target_pairs={{0,8},{8,0},{1,9},{9,1},{2,10},{10,2},{3,11},{11,3},{4,12},{12,4},... | collective-permute-start | bytes 786440 | tf_op jit(solution)/shard_map/ppermute | solution.py:15
  41.6 0.6 collective-permute-done
  42.2 0.8 fusion.103
  43.1 5.2 %collective-permute-done.1 = bf16[128,1024]{1,0:T(8,128)(2,1)S(1)} collective-permute-done((bf16[128,1024]{1,0:T(8,128)(2,1)S(1)}, bf16[128,1024]{1,0:T(8,128)(2,1)S(1)}, u32[]{:S(2)}, u32[]{:S(2)}) %collective-permute-start.1) | collective-permute-done | bytes 262176 | tf_op jit(solution)/shard_map/ppermute | solution.py:15
  48.2 0.5 fusion.20
  48.8 1.9 %collective-permute-start.2 = (bf16[256,512]{1,0:T(8,128)(2,1)S(1)}, bf16[256,512]{1,0:T(8,128)(2,1)S(1)}, u32[]{:S(2)}, u32[]{:S(2)}) collective-permute-start(bf16[256,512]{1,0:T(8,128)(2,1)S(1)} %fusion.20), channel_id=1, source_target_pairs={{0,16},{16,0},{1,17},{17,1},{2,18},{18,2},{3,19},{19,3},{4,20},{20... | collective-permute-start | bytes 786440 | tf_op jit(solution)/shard_map/ppermute | solution.py:15
  50.7 2.0 %fusion.25 = f32[256,1024]{1,0:T(8,128)} fusion(bf16[1024,1024]{1,0:T(8,128)(2,1)S(1)} %copy-done, bf16[128,1024]{1,0:T(8,128)(2,1)S(1)} %collective-permute-done.1, bf16[128,1024]{1,0:T(8,128)(2,1)S(1)} %convolution_convert_fusion.1), kind=kOutput, calls=%fused_computation.34 | convolution fusion | flops 540016640 | bytes 3670016 | tf_op jit(solution)/shard_map/dot_general | solution.py:31
  52.7 0.5 fusion.21
  53.2 0.8 pad_maximum_fusion.5
  54.1 5.3 %all-gather.5.cloned.1.call-done = bf16[1024,1024]{1,0:T(8,128)(2,1)} async-done(((bf16[128,1024]{1,0:T(8,128)(2,1)}), bf16[1024,1024]{1,0:T(8,128)(2,1)}) %all-gather.5.cloned.1.call-update) | async-done | bytes 2097168 | tf_op jit(solution)/shard_map/all_gather | solution.py:73
  59.4 4.8 %fusion.33 = f32[256,1024]{1,0:T(8,128)S(1)} fusion(bf16[1024,1024]{1,0:T(8,128)(2,1)} %all-gather.5.cloned.1.call-done, bf16[128,1024]{1,0:T(8,128)(2,1)S(1)} %copy-done.3, bf16[128,1024]{1,0:T(8,128)(2,1)} %get-tuple-element.34, s32[256]{0:T(256)S(1)} %iota_add_fusion, pred[256]{0:T(512)(128)(4,1)S(1)} %iota_compare_fusion.13), kind=kOutput, calls=%fused_computation.47 | convolution fusion | flops 1077673984 | bytes 3671296 | tf_op jit(solution)/shard_map/dot_general | solution.py:25
  64.2 1.4 multiply_convert_fusion.1
  65.6 1.9 %collective-permute-start.3 = (bf16[256,1024]{1,0:T(8,128)(2,1)S(1)}, bf16[256,1024]{1,0:T(8,128)(2,1)S(1)}, u32[]{:S(2)}, u32[]{:S(2)}) collective-permute-start(bf16[256,1024]{1,0:T(8,128)(2,1)S(1)} %multiply_convert_fusion.1), channel_id=1, source_target_pairs={{0,16},{16,0},{1,17},{17,1},{2,18},{18,2},{3,19},{19,3},{4,20},{20... | collective-permute-start | bytes 1572872 | tf_op jit(solution)/shard_map/ppermute | solution.py:15
  67.6 2.8 %collective-permute-start.7 = (bf16[128,1024]{1,0:T(8,128)(2,1)S(1)}, bf16[128,1024]{1,0:T(8,128)(2,1)S(1)}, u32[]{:S(2)}, u32[]{:S(2)}) collective-permute-start(bf16[128,1024]{1,0:T(8,128)(2,1)S(1)} %slice.60), channel_id=1, source_target_pairs={{0,8},{8,0},{1,9},{9,1},{2,10},{10,2},{3,11},{11,3},{4,12},{12,4},... | collective-permute-start | bytes 786440 | tf_op jit(solution)/shard_map/ppermute | solution.py:15
  70.4 1.0 fusion.64
  71.5 1.1 fusion.66
  72.6 1.0 fusion.62
  73.7 1.0 fusion.60
  74.7 3.5 %collective-permute-done.7 = bf16[128,1024]{1,0:T(8,128)(2,1)S(1)} collective-permute-done((bf16[128,1024]{1,0:T(8,128)(2,1)S(1)}, bf16[128,1024]{1,0:T(8,128)(2,1)S(1)}, u32[]{:S(2)}, u32[]{:S(2)}) %collective-permute-start.7) | collective-permute-done | bytes 262176 | tf_op jit(solution)/shard_map/ppermute | solution.py:15
  78.2 1.1 fusion.19
  79.3 10.0 %all-to-all-start.1 = ((bf16[32,8,1024]{2,1,0:T(8,128)(2,1)}), bf16[32,8,1024]{2,1,0:T(8,128)(2,1)S(1)}, u32[]{:S(2)}, u32[]{:S(2)}) async-start(bf16[32,8,1024]{2,1,0:T(8,128)(2,1)} %fusion.19), calls=%async_computation.1 | async-start | bytes 1048576 | tf_op jit(solution)/shard_map/all_to_all | solution.py:127
  89.3 2.1 %collective-permute-start.4 = (bf16[128,1024]{1,0:T(8,128)(2,1)}, bf16[128,1024]{1,0:T(8,128)(2,1)S(1)}, u32[]{:S(2)}, u32[]{:S(2)}) collective-permute-start(bf16[128,1024]{1,0:T(8,128)(2,1)} %fusion.64), channel_id=1, source_target_pairs={{0,32},{8,40},{32,0},{40,8},{1,33},{9,41},{33,1},{41,9},{2,34},{10... | collective-permute-start | bytes 786440 | tf_op jit(solution)/shard_map/ppermute | solution.py:118
  91.4 2.8 %collective-permute-start.5 = (bf16[128,1024]{1,0:T(8,128)(2,1)}, bf16[128,1024]{1,0:T(8,128)(2,1)S(1)}, u32[]{:S(2)}, u32[]{:S(2)}) collective-permute-start(bf16[128,1024]{1,0:T(8,128)(2,1)} %fusion.62), channel_id=1, source_target_pairs={{0,8},{8,0},{32,40},{40,32},{1,9},{9,1},{33,41},{41,33},{2,10},{10... | collective-permute-start | bytes 786440 | tf_op jit(solution)/shard_map/ppermute | solution.py:118
  94.2 4.9 %collective-permute-start.6 = (bf16[128,1024]{1,0:T(8,128)(2,1)}, bf16[128,1024]{1,0:T(8,128)(2,1)S(1)}, u32[]{:S(2)}, u32[]{:S(2)}) collective-permute-start(bf16[128,1024]{1,0:T(8,128)(2,1)} %fusion.60), channel_id=1, source_target_pairs={{0,40},{8,32},{32,8},{40,0},{1,41},{9,33},{33,9},{41,1},{2,42},{10... | collective-permute-start | bytes 786440 | tf_op jit(solution)/shard_map/ppermute | solution.py:118
  99.1 6.0 %collective-permute-done.4 = bf16[128,1024]{1,0:T(8,128)(2,1)S(1)} collective-permute-done((bf16[128,1024]{1,0:T(8,128)(2,1)}, bf16[128,1024]{1,0:T(8,128)(2,1)S(1)}, u32[]{:S(2)}, u32[]{:S(2)}) %collective-permute-start.4) | collective-permute-done | bytes 262176 | tf_op jit(solution)/shard_map/ppermute | solution.py:118
  105.1 4.4 %collective-permute-done.5 = bf16[128,1024]{1,0:T(8,128)(2,1)S(1)} collective-permute-done((bf16[128,1024]{1,0:T(8,128)(2,1)}, bf16[128,1024]{1,0:T(8,128)(2,1)S(1)}, u32[]{:S(2)}, u32[]{:S(2)}) %collective-permute-start.5) | collective-permute-done | bytes 262176 | tf_op jit(solution)/shard_map/ppermute | solution.py:118
  109.5 0.6 collective-permute-done.6
  110.1 1.2 add_convert_fusion.2
  111.4 0.8 copy.12
  112.1 9.1 %all-to-all-start.2 = ((bf16[64,16,128]{2,1,0:T(8,128)(2,1)}), bf16[64,16,128]{2,1,0:T(8,128)(2,1)S(1)}, u32[]{:S(2)}, u32[]{:S(2)}) async-start(bf16[64,16,128]{2,1,0:T(8,128)(2,1)} %bitcast.6), calls=%async_computation.2 | async-start | bytes 524288 | tf_op jit(solution)/shard_map/all_to_all | solution.py:136
  121.3 4.7 %fusion.35 = f32[256,1024]{1,0:T(8,128)} fusion(bf16[1024,1024]{1,0:T(8,128)(2,1)} %all-gather.3.cloned.1.call-done, bf16[128,1024]{1,0:T(8,128)(2,1)S(1)} %copy-done.6, bf16[128,1024]{1,0:T(8,128)(2,1)S(1)} %copy-done.5, s32[256]{0:T(256)S(1)} %iota_add_fusion, pred[256]{0:T(512)(128)(4,1)S(1)} %iota_compare_fusion.13), kind=kOutput, calls=%fused_computation.49 | convolution fusion | flops 1077673984 | bytes 3671296 | tf_op jit(solution)/shard_map/dot_general | solution.py:31
  125.9 10.4 %all-to-all-done.2 = bf16[64,16,128]{2,1,0:T(8,128)(2,1)S(1)} async-done(((bf16[64,16,128]{2,1,0:T(8,128)(2,1)}), bf16[64,16,128]{2,1,0:T(8,128)(2,1)S(1)}, u32[]{:S(2)}, u32[]{:S(2)}) %all-to-all-start.2) | async-done | bytes 262176 | tf_op jit(solution)/shard_map/all_to_all | solution.py:136
  136.4 1.1 slice.59
  137.4 2.8 %collective-permute-start.8 = (bf16[128,1024]{1,0:T(8,128)(2,1)S(1)}, bf16[128,1024]{1,0:T(8,128)(2,1)S(1)}, u32[]{:S(2)}, u32[]{:S(2)}) collective-permute-start(bf16[128,1024]{1,0:T(8,128)(2,1)S(1)} %slice.59), channel_id=1, source_target_pairs={{0,8},{8,0},{1,9},{9,1},{2,10},{10,2},{3,11},{11,3},{4,12},{12,4},... | collective-permute-start | bytes 786440 | tf_op jit(solution)/shard_map/ppermute | solution.py:15
  140.3 0.6 broadcast_in_dim.2
  140.9 4.5 %all-to-all-start.3 = ((bf16[16,16,128]{2,1,0:T(8,128)(2,1)}), bf16[16,16,128]{2,1,0:T(8,128)(2,1)S(1)}, u32[]{:S(2)}, u32[]{:S(2)}) async-start(bf16[16,16,128]{2,1,0:T(8,128)(2,1)} %broadcast_in_dim.2), calls=%async_computation.3 | async-start | bytes 131072 | tf_op jit(solution)/shard_map/all_to_all | solution.py:143
  145.4 2.8 %fusion.18 = bf16[256,1024]{1,0:T(8,128)(2,1)} fusion(bf16[1024,1024]{1,0:T(8,128)(2,1)S(1)} %copy-done, f32[256,1024]{1,0:T(8,128)} %fusion.29, bf16[256,1024]{1,0:T(8,128)(2,1)S(1)} %bitcast.37, f32[256]{0:T(256)S(1)} %convert_rsqrt_fusion), kind=kOutput, calls=%fused_computation.25 | convolution fusion | flops 538181632 | bytes 4195328 | tf_op jit(solution)/shard_map/dot_general | solution.py:19
  148.2 4.6 %all-to-all-done.3 = bf16[16,16,128]{2,1,0:T(8,128)(2,1)S(1)} async-done(((bf16[16,16,128]{2,1,0:T(8,128)(2,1)}), bf16[16,16,128]{2,1,0:T(8,128)(2,1)S(1)}, u32[]{:S(2)}, u32[]{:S(2)}) %all-to-all-start.3) | async-done | bytes 65568 | tf_op jit(solution)/shard_map/all_to_all | solution.py:143
  152.9 0.7 copy.17
  153.6 1.8 %add_convert_fusion = bf16[128,1024]{1,0:T(8,128)(2,1)} fusion(bf16[128,1024]{1,0:T(8,128)(2,1)S(1)} %collective-permute-done.8, f32[256,1024]{1,0:T(8,128)} %fusion.35), kind=kLoop, calls=%fused_computation.61 | loop fusion | flops 393216 | bytes 1048576 | tf_op jit(solution)/shard_map/convert_element_type | solution.py:148
  (39 shorter events, 0.9 us)
Async XLA Ops:
  7.2 17.6 %copy-start = (bf16[1024,1024]{1,0:T(8,128)(2,1)S(1)}, bf16[1024,1024]{1,0:T(8,128)(2,1)}, u32[]{:S(2)}) copy-start(bf16[1024,1024]{1,0:T(8,128)(2,1)} %param.11) | copy-start | bytes 6291460
  7.2 13.8 %copy-start.4 = (bf16[128,1024]{1,0:T(8,128)(2,1)S(1)}, bf16[128,1024]{1,0:T(8,128)(2,1)}, u32[]{:S(2)}) copy-start(bf16[128,1024]{1,0:T(8,128)(2,1)} %param.6) | copy-start | bytes 786436
  7.2 13.8 %copy-start.2 = (bf16[128,1024]{1,0:T(8,128)(2,1)S(1)}, bf16[128,1024]{1,0:T(8,128)(2,1)}, u32[]{:S(2)}) copy-start(bf16[128,1024]{1,0:T(8,128)(2,1)} %param.7) | copy-start | bytes 786436
  7.2 17.4 %copy-start.7 = (s32[128,1]{0,1:T(1,128)S(1)}, s32[128,1]{0,1:T(1,128)}, u32[]{:S(2)}) copy-start(s32[128,1]{0,1:T(1,128)} %param.8) | copy-start | bytes 1540
  7.2 52.2 %all-gather.5.cloned.1.call-start = ((), (), s32[]{:S(2)}) async-start(), calls=%async_computation.5 | async-start | bytes 2359296 | tf_op jit(solution)/shard_map/all_gather | solution.py:73
  10.7 27.9 %all-to-all-start = ((bf16[32,8,1024]{2,1,0:T(8,128)(2,1)}), bf16[32,8,1024]{2,1,0:T(8,128)(2,1)S(1)}, u32[]{:S(2)}, u32[]{:S(2)}) async-start(bf16[32,8,1024]{2,1,0:T(8,128)(2,1)} %fusion.58), calls=%async_computation | async-start | bytes 1048576 | tf_op jit(solution)/shard_map/all_to_all | solution.py:81
  20.9 100.4 %all-gather.3.cloned.1.call-start = ((), (), s32[]{:S(2)}) async-start(), calls=%async_computation.4 | async-start | bytes 2359296 | tf_op jit(solution)/shard_map/all_gather | solution.py:74
  21.8 20.4 %collective-permute-start = (bf16[256,1024]{1,0:T(8,128)(2,1)}, bf16[256,1024]{1,0:T(8,128)(2,1)S(1)}, u32[]{:S(2)}, u32[]{:S(2)}) collective-permute-start(bf16[256,1024]{1,0:T(8,128)(2,1)} %pad_maximum_fusion.1), channel_id=1, source_target_pairs={{0,8},{8,0},{1,9},{9,1},{2,10},{10,2},{3,11},{11,3},{4,12},{12,4},... | collective-permute-start | bytes 1572872 | tf_op jit(solution)/shard_map/ppermute | solution.py:15
  38.9 9.4 %collective-permute-start.1 = (bf16[128,1024]{1,0:T(8,128)(2,1)S(1)}, bf16[128,1024]{1,0:T(8,128)(2,1)S(1)}, u32[]{:S(2)}, u32[]{:S(2)}) collective-permute-start(bf16[128,1024]{1,0:T(8,128)(2,1)S(1)} %convolution_convert_fusion.1), channel_id=1, source_target_pairs={{0,8},{8,0},{1,9},{9,1},{2,10},{10,2},{3,11},{11,3},{4,12},{12,4},... | collective-permute-start | bytes 786440 | tf_op jit(solution)/shard_map/ppermute | solution.py:15
  48.8 4.4 %collective-permute-start.2 = (bf16[256,512]{1,0:T(8,128)(2,1)S(1)}, bf16[256,512]{1,0:T(8,128)(2,1)S(1)}, u32[]{:S(2)}, u32[]{:S(2)}) collective-permute-start(bf16[256,512]{1,0:T(8,128)(2,1)S(1)} %fusion.20), channel_id=1, source_target_pairs={{0,16},{16,0},{1,17},{17,1},{2,18},{18,2},{3,19},{19,3},{4,20},{20... | collective-permute-start | bytes 786440 | tf_op jit(solution)/shard_map/ppermute | solution.py:15
  52.7 6.7 %copy-start.3 = (bf16[128,1024]{1,0:T(8,128)(2,1)S(1)}, bf16[128,1024]{1,0:T(8,128)(2,1)}, u32[]{:S(2)}) copy-start(bf16[128,1024]{1,0:T(8,128)(2,1)} %param.7) | copy-start | bytes 786436
  64.2 6.3 %copy-start.1 = (bf16[512,512]{1,0:T(8,128)(2,1)S(1)}, bf16[512,512]{1,0:T(8,128)(2,1)}, u32[]{:S(2)}) copy-start(bf16[512,512]{1,0:T(8,128)(2,1)} %pad_maximum_fusion.5) | copy-start | bytes 1572868
  65.6 4.8 %collective-permute-start.3 = (bf16[256,1024]{1,0:T(8,128)(2,1)S(1)}, bf16[256,1024]{1,0:T(8,128)(2,1)S(1)}, u32[]{:S(2)}, u32[]{:S(2)}) collective-permute-start(bf16[256,1024]{1,0:T(8,128)(2,1)S(1)} %multiply_convert_fusion.1), channel_id=1, source_target_pairs={{0,16},{16,0},{1,17},{17,1},{2,18},{18,2},{3,19},{19,3},{4,20},{20... | collective-permute-start | bytes 1572872 | tf_op jit(solution)/shard_map/ppermute | solution.py:15
  67.6 10.6 %collective-permute-start.7 = (bf16[128,1024]{1,0:T(8,128)(2,1)S(1)}, bf16[128,1024]{1,0:T(8,128)(2,1)S(1)}, u32[]{:S(2)}, u32[]{:S(2)}) collective-permute-start(bf16[128,1024]{1,0:T(8,128)(2,1)S(1)} %slice.60), channel_id=1, source_target_pairs={{0,8},{8,0},{1,9},{9,1},{2,10},{10,2},{3,11},{11,3},{4,12},{12,4},... | collective-permute-start | bytes 786440 | tf_op jit(solution)/shard_map/ppermute | solution.py:15
  79.3 42.0 %copy-start.5 = (bf16[128,1024]{1,0:T(8,128)(2,1)S(1)}, bf16[128,1024]{1,0:T(8,128)(2,1)}, u32[]{:S(2)}) copy-start(bf16[128,1024]{1,0:T(8,128)(2,1)} %param.6) | copy-start | bytes 786436
  79.3 42.0 %copy-start.6 = (bf16[128,1024]{1,0:T(8,128)(2,1)S(1)}, bf16[128,1024]{1,0:T(8,128)(2,1)}, u32[]{:S(2)}) copy-start(bf16[128,1024]{1,0:T(8,128)(2,1)} %get-tuple-element.33) | copy-start | bytes 786436
  79.3 32.1 %all-to-all-start.1 = ((bf16[32,8,1024]{2,1,0:T(8,128)(2,1)}), bf16[32,8,1024]{2,1,0:T(8,128)(2,1)S(1)}, u32[]{:S(2)}, u32[]{:S(2)}) async-start(bf16[32,8,1024]{2,1,0:T(8,128)(2,1)} %fusion.19), calls=%async_computation.1 | async-start | bytes 1048576 | tf_op jit(solution)/shard_map/all_to_all | solution.py:127
  89.3 15.9 %collective-permute-start.4 = (bf16[128,1024]{1,0:T(8,128)(2,1)}, bf16[128,1024]{1,0:T(8,128)(2,1)S(1)}, u32[]{:S(2)}, u32[]{:S(2)}) collective-permute-start(bf16[128,1024]{1,0:T(8,128)(2,1)} %fusion.64), channel_id=1, source_target_pairs={{0,32},{8,40},{32,0},{40,8},{1,33},{9,41},{33,1},{41,9},{2,34},{10... | collective-permute-start | bytes 786440 | tf_op jit(solution)/shard_map/ppermute | solution.py:118
  91.4 18.1 %collective-permute-start.5 = (bf16[128,1024]{1,0:T(8,128)(2,1)}, bf16[128,1024]{1,0:T(8,128)(2,1)S(1)}, u32[]{:S(2)}, u32[]{:S(2)}) collective-permute-start(bf16[128,1024]{1,0:T(8,128)(2,1)} %fusion.62), channel_id=1, source_target_pairs={{0,8},{8,0},{32,40},{40,32},{1,9},{9,1},{33,41},{41,33},{2,10},{10... | collective-permute-start | bytes 786440 | tf_op jit(solution)/shard_map/ppermute | solution.py:118
  94.2 15.9 %collective-permute-start.6 = (bf16[128,1024]{1,0:T(8,128)(2,1)}, bf16[128,1024]{1,0:T(8,128)(2,1)S(1)}, u32[]{:S(2)}, u32[]{:S(2)}) collective-permute-start(bf16[128,1024]{1,0:T(8,128)(2,1)} %fusion.60), channel_id=1, source_target_pairs={{0,40},{8,32},{32,8},{40,0},{1,41},{9,33},{33,9},{41,1},{2,42},{10... | collective-permute-start | bytes 786440 | tf_op jit(solution)/shard_map/ppermute | solution.py:118
  112.1 24.2 %all-to-all-start.2 = ((bf16[64,16,128]{2,1,0:T(8,128)(2,1)}), bf16[64,16,128]{2,1,0:T(8,128)(2,1)S(1)}, u32[]{:S(2)}, u32[]{:S(2)}) async-start(bf16[64,16,128]{2,1,0:T(8,128)(2,1)} %bitcast.6), calls=%async_computation.2 | async-start | bytes 524288 | tf_op jit(solution)/shard_map/all_to_all | solution.py:136
  137.4 15.4 %collective-permute-start.8 = (bf16[128,1024]{1,0:T(8,128)(2,1)S(1)}, bf16[128,1024]{1,0:T(8,128)(2,1)S(1)}, u32[]{:S(2)}, u32[]{:S(2)}) collective-permute-start(bf16[128,1024]{1,0:T(8,128)(2,1)S(1)} %slice.59), channel_id=1, source_target_pairs={{0,8},{8,0},{1,9},{9,1},{2,10},{10,2},{3,11},{11,3},{4,12},{12,4},... | collective-permute-start | bytes 786440 | tf_op jit(solution)/shard_map/ppermute | solution.py:15
  140.9 11.9 %all-to-all-start.3 = ((bf16[16,16,128]{2,1,0:T(8,128)(2,1)}), bf16[16,16,128]{2,1,0:T(8,128)(2,1)S(1)}, u32[]{:S(2)}, u32[]{:S(2)}) async-start(bf16[16,16,128]{2,1,0:T(8,128)(2,1)} %broadcast_in_dim.2), calls=%async_computation.3 | async-start | bytes 131072 | tf_op jit(solution)/shard_map/all_to_all | solution.py:143
Sparse Core Ops, SparseCore 0:
  10.1 49.2 all-gather.4
  61.5 42.7 all-gather.2

commit v3 on v1

v3 whole, which is shorter than its diff:
```python
import jax
import jax.numpy as jnp
from jax import lax
from jax.experimental import pallas as pl
from jax.experimental.pallas import tpu as pltpu
from jax.sharding import Mesh
from jax.sharding import PartitionSpec as P

AXES = ("wide_y", "wide_x", "wide_c", "blk_x", "blk_z")
WIDE = ("wide_y", "wide_x", "wide_c")
BLK = ("blk_x", "blk_z")
BF16 = jnp.bfloat16
F32 = jnp.float32
ROOM = pltpu.CompilerParams(vmem_limit_bytes=40 * 2**20)
SCALAR = pl.BlockSpec(memory_space=pltpu.SMEM)


def swapped(array, axis):
    return lax.ppermute(array, axis, [(0, 1), (1, 0)])


def dot_of(matrix_a, matrix_b, dim_a, dim_b):
    return lax.dot_general(
        matrix_a, matrix_b, (((dim_a,), (dim_b,)), ((), ())), preferred_element_type=F32
    )


def gelu_slope(v):
    cdf = 0.5 * (1.0 + lax.erf(v * 0.7071067811865476))
    return cdf + v * (0.3989422804014327 * jnp.exp(-0.5 * v * v))


def targets_of(owner, capacity):
    ids = jnp.arange(owner.shape[0], dtype=jnp.int32)
    peer = owner[:, 0]
    before = (peer[:, None] == peer[None, :]) & (ids[:, None] < ids[None, :])
    return peer * capacity + jnp.sum(before.astype(jnp.int32), axis=0)


def picking_of(core, feature_count):
    half = feature_count // 2
    ny, nx = lax.axis_size("wide_y"), lax.axis_size("wide_x")
    bx = lax.axis_size("blk_x")
    share = half // (ny * nx * bx)
    place = jnp.arange(half, dtype=jnp.int32)
    within, rest = place % share, place // share
    y, apart = rest % ny, rest // ny
    x_wide = (apart // bx) ^ lax.axis_index("wide_x")
    x_blk = (apart % bx) ^ lax.axis_index("blk_x")
    feature = (((y * nx + x_wide) * 2 + core) * bx + x_blk) * share + within
    return (jnp.arange(feature_count, dtype=jnp.int32)[:, None] == feature[None, :]).astype(BF16)


def pair_kernel(factor, place_ref, line_ref, own_ref, mate_ref, kept_ref, sent_ref, line_grad_ref, total):
    step = pl.program_id(0)
    rows, clips = line_ref.shape[0], own_ref.shape[0]
    line = line_ref[...]
    video = jnp.concatenate([own_ref[...], mate_ref[...]], axis=0)
    scores = dot_of(video, line, 1, 1)
    row = lax.broadcasted_iota(jnp.int32, scores.shape, 0)
    col = lax.broadcasted_iota(jnp.int32, scores.shape, 1) + step * rows
    labels = ((col == place_ref[0] * clips + row) & (row < clips)).astype(F32)
    coeffs = (factor * (jax.nn.sigmoid(4.0 * scores - 2.0) - labels)).astype(BF16)
    part = dot_of(coeffs, line, 1, 0)

    @pl.when(step == 0)
    def _():
        total[...] = part

    @pl.when(step > 0)
    def _():
        total[...] += part

    line_grad_ref[...] = dot_of(coeffs, video, 0, 0).astype(BF16)

    @pl.when(step == pl.num_programs(0) - 1)
    def _():
        kept_ref[...] = total[:clips]
        sent_ref[...] = total[clips:].astype(BF16)


def pair_grads(line, own, mate, place, factor, steps):
    rows, features = line.shape
    clips = own.shape[0]
    whole = pl.BlockSpec((clips, features), lambda i: (0, 0))
    part = pl.BlockSpec((rows // steps, features), lambda i: (i, 0))
    return pl.pallas_call(
        lambda *refs: pair_kernel(factor, *refs),
        grid=(steps,),
        in_specs=[SCALAR, part, whole, whole],
        out_specs=[whole, whole, part],
        out_shape=[
            jax.ShapeDtypeStruct((clips, features), F32),
            jax.ShapeDtypeStruct((clips, features), BF16),
            jax.ShapeDtypeStruct((rows, features), BF16),
        ],
        scratch_shapes=[pltpu.VMEM((2 * clips, features), F32)],
        compiler_params=ROOM,
        cost_estimate=pl.CostEstimate(
            flops=12 * rows * clips * features, bytes_accessed=5 * rows * features, transcendentals=0
        ),
    )(place, line, own, mate)


def clip_kernel(kept_ref, arrived_ref, slope_ref, target_ref, packed_ref, pre_ref):
    grad = (kept_ref[...] + arrived_ref[...].astype(F32)).astype(BF16)
    pre_ref[...] = (grad.astype(F32) * slope_ref[...]).astype(BF16)
    slots, clips = packed_ref.shape[0], grad.shape[0]
    slot = lax.broadcasted_iota(jnp.int32, (slots, clips), 0)
    placing = (slot == target_ref[...]).astype(BF16)
    packed_ref[...] = dot_of(placing, grad, 1, 0).astype(BF16)


def clip_grads(kept, arrived, slope, targets, slots):
    clips, features = kept.shape
    return pl.pallas_call(
        clip_kernel,
        out_shape=[
            jax.ShapeDtypeStruct((slots, features), BF16),
            jax.ShapeDtypeStruct((clips, features), BF16),
        ],
        compiler_params=ROOM,
    )(kept, arrived, slope, targets[None, :])


def weight_kernel(own_picked, mate_picked, own_pre, mate_pre, *out_refs):
    share = out_refs[0].shape[0]
    picked = jnp.concatenate([own_picked[...], mate_picked[...]], axis=0)
    pre = jnp.concatenate([own_pre[...], mate_pre[...]], axis=0)
    product = dot_of(picked, pre, 0, 0)
    for d, out_ref in enumerate(out_refs):
        out_ref[...] = product[d * share : (d + 1) * share].astype(out_ref.dtype)


def weight_parts(own_picked, mate_picked, own_pre, mate_pre, count):
    half, features = own_picked.shape[1], own_pre.shape[1]
    shape = (half // count, features)
    return pl.pallas_call(
        weight_kernel,
        out_shape=[jax.ShapeDtypeStruct(shape, F32 if d == 0 else BF16) for d in range(count)],
        compiler_params=ROOM,
    )(own_picked, mate_picked, own_pre, mate_pre)


def shards(audio, video, owner, clip_feats, lengths, proj_weight):
    clips, features = audio.shape
    blocks = lax.axis_size(BLK)
    core = lax.axis_index("wide_c")
    place = lax.axis_index("blk_z").astype(jnp.int32)[None]
    audio_line = lax.all_gather(audio, "blk_z", axis=0, tiled=True)

    peers = lax.axis_size(WIDE)
    slots = clip_feats.shape[0]
    capacity = slots // peers
    length_scale = lax.rsqrt(lengths.astype(F32))[:, None]
    pooled = (clip_feats.astype(F32) * length_scale).astype(BF16)
    pooled_slots = lax.all_to_all(
        pooled.reshape(peers, capacity, features), WIDE, 0, 0, tiled=True
    ).reshape(slots, features)
    video_mate = swapped(video, "blk_x")
    slope_own = gelu_slope(dot_of(pooled, proj_weight, 1, 0))

    targets = targets_of(owner, capacity)
    placing = (targets[:, None] == jnp.arange(slots, dtype=jnp.int32)[None, :]).astype(BF16)
    clip_rows = dot_of(placing, pooled_slots, 1, 0).astype(BF16)
    slope_rows = gelu_slope(dot_of(clip_rows, proj_weight, 1, 0))
    picked = dot_of(clip_rows, picking_of(core, features), 1, 0).astype(BF16)
    picked_mate = swapped(
        dot_of(clip_rows, picking_of(1 - core, features), 1, 0).astype(BF16), "wide_c"
    )
    audio_line, video_mate, slope_rows, picked, picked_mate, slope_own, targets = (
        lax.optimization_barrier(
            (audio_line, video_mate, slope_rows, picked, picked_mate, slope_own, targets)
        )
    )

    kept, sent, line_grads = pair_grads(audio_line, video, video_mate, place, 4.0 / blocks, 4)
    audio_grad = lax.psum_scatter(line_grads, "blk_z", scatter_dimension=0, tiled=True)
    arrived = swapped(sent, "blk_x")
    packed, pre_rows = clip_grads(kept, arrived, slope_rows, targets, slots)
    received = lax.all_to_all(
        packed.reshape(peers, capacity, features), WIDE, 0, 0, tiled=True
    ).reshape(slots, features)

    pre_mate = swapped(pre_rows, "wide_c")
    parts = weight_parts(picked, picked_mate, pre_rows, pre_mate, 4)
    summed = parts[0]
    for d in (2, 1, 3):
        pairs = [(at, at ^ d) for at in range(4)]
        summed = summed + lax.ppermute(parts[d], ("wide_x", "blk_x"), pairs).astype(F32)
    summed = summed.astype(BF16)
    summed, received = lax.optimization_barrier((summed, received))
    ny = lax.axis_size("wide_y")
    pieces = lax.all_to_all(summed.reshape(ny, -1, features), "wide_y", 0, 0, tiled=True)
    pre_grad = (received.astype(F32) * slope_own).astype(BF16)
    feats_grad = (dot_of(pre_grad, proj_weight, 1, 1) * length_scale).astype(BF16)
    pieces, feats_grad = lax.optimization_barrier((pieces, feats_grad))
    total = jnp.sum(pieces.astype(F32), axis=0).astype(BF16)
    gathered = lax.all_to_all(
        jnp.broadcast_to(total[None], (blocks, *total.shape)), BLK, 0, 0, tiled=True
    )
    gathered = gathered.reshape(lax.axis_size("blk_x"), -1, *total.shape)
    weight_grad = jnp.sum(gathered.astype(F32), axis=1).reshape(-1, features)
    return (audio_grad, feats_grad, weight_grad)


def solution(mesh):
    finer = Mesh(mesh.devices.reshape(8, 2, 2, 2, 8), AXES)
    rows = P(AXES, None)
    return jax.shard_map(
        shards,
        mesh=finer,
        in_specs=(rows, rows, rows, rows, P(AXES), P()),
        out_specs=(rows, rows, P(WIDE, None)),
        check_vma=False,
    )
```

time: 169 us -> 158 us (0.935)
  matrix products: 21.4 us -> 7.21 us
  starting transfers between devices: 51 us -> 44.9 us
  Pallas kernels: 0 us -> 5.65 us
  waiting for transfers between devices: 51.3 us -> 54.2 us
  local copies, waits for them, and re-layouts: 6.22 us -> 7.96 us
    ppermute x6 -> x4, waiting for transfers between devices: 33.3 us -> 6.92 us  [swapped(): return lax.ppermute(array, axis, [(0, 1), (1, 0)])]
    all_to_all x1, waiting for transfers between devices: 0.01 us -> 15.4 us  [shards(): lax.all_to_all(pooled.reshape(peers, capacity, features), WIDE, 0, 0, til...]
    dot_general x9 -> x6, matrix products: 21.4 us -> 7.21 us  [dot_of(): lax.dot_general(matrix_a, matrix_b, (((dim_a,), (dim_b,)), ((), ())), pre...]
    all_to_all x2 -> x1, starting transfers between devices: 18.7 us -> 5.54 us  [shards(): lax.all_to_all(summed.reshape(ny, -1, features), 'wide_y', 0, 0, tiled=True)]
    ppermute x0 -> x3, starting transfers between devices: none -> 9.82 us  [shards(): lax.ppermute(parts[d], ('wide_x', 'blk_x'), pairs).astype(F32)]
    ppermute x0 -> x3, waiting for transfers between devices: none -> 9.02 us  [shards(): lax.ppermute(parts[d], ('wide_x', 'blk_x'), pairs).astype(F32)]
    unnamed x18 -> x24, local copies, waits for them, and re-layouts: 0.77 us -> 7.91 us
    pallas_call x0 -> x3, Pallas kernels: none -> 5.65 us  [the longest x1 4.88 us: pair_grads(): pl.pallas_call(lambda *refs: pair_kernel(factor, *refs), grid=(steps,), i...]
  transfers between devices with their start and end apart: 12 -> 12, of which waited for: 6 -> 8; matrix products, arithmetic and copies ran while one was open for 19% -> 7% of each run, Pallas kernels for 0% -> 0%
where the time goes in v3:
time: 158 us; the launch traced here: 157 us
  waiting for transfers between devices  54.2 us (34%)
  starting transfers between devices  44.9 us (28%)
  blocking collectives  18.5 us (12%)
  between operations  14.3 us (9%)
  local copies, waits for them, and re-layouts  7.96 us (5%)
  matrix products  7.21 us (5%)
  Pallas kernels  5.65 us (4%)
  other arithmetic  4.44 us (3%)
    all_to_all x1, blocking collectives, shards(): lax.all_to_all(jnp.broadcast_to(total[None], (blocks, *total.shape)), BLK...  18.5 us
    all_to_all x1, waiting for transfers between devices, shards(): lax.all_to_all(pooled.reshape(peers, capacity, features), WIDE, 0, 0, til...  15.4 us
    all_gather x1, waiting for transfers between devices, shards(): audio_line = lax.all_gather(audio, 'blk_z', axis=0, tiled=True)  12.9 us
    all_to_all x1, starting transfers between devices, shards(): lax.all_to_all(pooled.reshape(peers, capacity, features), WIDE, 0, 0, til...  10.2 us
    ppermute x3, starting transfers between devices, shards(): lax.ppermute(parts[d], ('wide_x', 'blk_x'), pairs).astype(F32)  9.82 us
    all_to_all x1, starting transfers between devices, shards(): lax.all_to_all(packed.reshape(peers, capacity, features), WIDE, 0, 0, til...  9.72 us
    ppermute x4, starting transfers between devices, swapped(): return lax.ppermute(array, axis, [(0, 1), (1, 0)])  9.54 us
    all_to_all x1, waiting for transfers between devices, shards(): lax.all_to_all(summed.reshape(ny, -1, features), 'wide_y', 0, 0, tiled=True)  9.25 us
  transfers between devices with their start and end apart: 12, of which 8 were waited for; matrix products, arithmetic and copies ran while one was open for 7% of the time, Pallas kernels for 0%

profile of v3, /device:TPU:6, one launch (start us, length us, event | category | flops | bytes accessed | tf_op | source)
XLA Modules:
  0.0 157.2 jit_solution(7409759801201076626)
XLA Ops:
  7.2 0.0 copy-start
  7.2 0.0 copy-start.10
  7.2 0.0 all-gather.2.cloned.1.call-start
  7.2 0.7 all-gather.2.cloned.1.call-update
  7.9 2.9 %collective-permute-start = (bf16[128,1024]{1,0:T(8,128)(2,1)}, bf16[128,1024]{1,0:T(8,128)(2,1)S(1)}, u32[]{:S(2)}, u32[]{:S(2)}) collective-permute-start(bf16[128,1024]{1,0:T(8,128)(2,1)} %refs_2_.1), channel_id=1, source_target_pairs={{0,8},{8,0},{1,9},{9,1},{2,10},{10,2},{3,11},{11,3},{4,12},{12,4},... | collective-permute-start | bytes 786440 | tf_op jit(solution)/shard_map/ppermute | solution.py:19
  10.8 0.7 convert_rsqrt_fusion
  11.5 2.0 %fusion.17 = bf16[32,8,1024]{2,1,0:T(8,128)(2,1)} fusion(f32[256]{0:T(256)S(1)} %convert_rsqrt_fusion, bf16[256,1024]{1,0:T(8,128)(2,1)} %param.9), kind=kLoop, calls=%fused_computation.27 | loop fusion | flops 786432 | bytes 1049600 | tf_op jit(solution)/shard_map/reshape | solution.py:158
  13.5 10.2 %all-to-all-start = ((bf16[32,8,1024]{2,1,0:T(8,128)(2,1)}), bf16[32,8,1024]{2,1,0:T(8,128)(2,1)S(1)}, u32[]{:S(2)}, u32[]{:S(2)}) async-start(bf16[32,8,1024]{2,1,0:T(8,128)(2,1)} %fusion.17), calls=%async_computation | async-start | bytes 1048576 | tf_op jit(solution)/shard_map/all_to_all | solution.py:157
  23.7 0.0 reduce-scatter.2.cloned.1.call-start
  23.8 0.1 convert_reduce_fusion.1
  24.0 2.0 %fusion.8 = f32[256,1024]{1,0:T(8,128)} fusion(bf16[1024,1024]{1,0:T(8,128)(2,1)S(1)} %copy-done, bf16[256,1024]{1,0:T(8,128)(2,1)S(1)} %copy-done.10, f32[256]{0:T(256)S(1)} %convert_rsqrt_fusion), kind=kOutput, calls=%fused_computation.13 | convolution fusion | flops 539754496 | bytes 3671040 | tf_op jit(solution)/shard_map/dot_general | solution.py:23
  26.0 15.4 %all-to-all-done = bf16[32,8,1024]{2,1,0:T(8,128)(2,1)S(1)} async-done(((bf16[32,8,1024]{2,1,0:T(8,128)(2,1)}), bf16[32,8,1024]{2,1,0:T(8,128)(2,1)S(1)}, u32[]{:S(2)}, u32[]{:S(2)}) %all-to-all-start) | async-done | bytes 524320 | tf_op jit(solution)/shard_map/all_to_all | solution.py:157
  41.4 0.3 convolution_convert_fusion
  41.7 0.5 fusion.14.slope_ref
  42.2 0.5 fusion.3
  42.7 1.9 %collective-permute-start.1 = (bf16[128,512]{1,0:T(8,128)(2,1)S(1)}, bf16[128,512]{1,0:T(8,128)(2,1)S(1)}, u32[]{:S(2)}, u32[]{:S(2)}) collective-permute-start(bf16[128,512]{1,0:T(8,128)(2,1)S(1)} %fusion.3), channel_id=1, source_target_pairs={{0,16},{16,0},{1,17},{17,1},{2,18},{18,2},{3,19},{19,3},{4,20},{20... | collective-permute-start | bytes 393224 | tf_op jit(solution)/shard_map/ppermute | solution.py:19
  44.7 1.2 fusion.4.own_picked
  45.8 0.7 copy-done.6
  46.5 12.9 %all-gather.2.cloned.1.call-done.refs_1_ = bf16[1024,1024]{1,0:T(8,128)(2,1)} async-done(((bf16[128,1024]{1,0:T(8,128)(2,1)}), bf16[1024,1024]{1,0:T(8,128)(2,1)}) %all-gather.2.cloned.1.call-update) | async-done | bytes 2097168 | tf_op jit(solution)/shard_map/all_gather | solution.py:150
  59.4 1.6 %copy-done.4 = bf16[1024,1024]{1,0:T(8,128)(2,1)S(1)} copy-done((bf16[1024,1024]{1,0:T(8,128)(2,1)S(1)}, bf16[1024,1024]{1,0:T(8,128)(2,1)}, u32[]{:S(2)}) %copy-start.4) | copy-done | bytes 2097176
  61.0 0.9 copy-done.7
  62.0 4.9 %shard_map.85 = (f32[128,1024]{1,0:T(8,128)S(1)}, bf16[128,1024]{1,0:T(8,128)(2,1)S(1)}, bf16[1024,1024]{1,0:T(8,128)(2,1)S(1)}) custom-call(s32[1]{0:T(128)} %bitcast.refs_0_, bf16[1024,1024]{1,0:T(8,128)(2,1)S(1)} %copy-done.4, bf16[128,1024]{1,0:T(8,128)(2,1)S(1)} %copy-done.5, bf16[128,1024]{1,0:T(8,128)(2,1)S(1)} %copy-done.7), custom_call_target="tpu_custom_call" | custom-call | flops 1610612736 | bytes 5242880 | tf_op jit(solution)/shard_map/pallas_call | solution.py:87
  66.9 1.3 copy-done.1
  68.2 0.7 copy-done.8
  68.9 0.0 reduce-scatter.2.cloned.1.call-update
  68.9 0.9 copy-done.9
  69.8 2.7 %collective-permute-start.2 = (bf16[128,1024]{1,0:T(8,128)(2,1)S(1)}, bf16[128,1024]{1,0:T(8,128)(2,1)S(1)}, u32[]{:S(2)}, u32[]{:S(2)}) collective-permute-start(bf16[128,1024]{1,0:T(8,128)(2,1)S(1)} %copy-done.9), channel_id=1, source_target_pairs={{0,8},{8,0},{1,9},{9,1},{2,10},{10,2},{3,11},{11,3},{4,12},{12,4},... | collective-permute-start | bytes 786440 | tf_op jit(solution)/shard_map/ppermute | solution.py:19
  72.5 5.5 %collective-permute-done.2.arrived_ref = bf16[128,1024]{1,0:T(8,128)(2,1)S(1)} collective-permute-done((bf16[128,1024]{1,0:T(8,128)(2,1)S(1)}, bf16[128,1024]{1,0:T(8,128)(2,1)S(1)}, u32[]{:S(2)}, u32[]{:S(2)}) %collective-permute-start.2) | collective-permute-done | bytes 262176 | tf_op jit(solution)/shard_map/ppermute | solution.py:19
  78.1 0.3 shard_map.86
  78.4 0.8 copy-done.2
  79.2 9.7 %all-to-all-start.1 = ((bf16[32,8,1024]{2,1,0:T(8,128)(2,1)}), bf16[32,8,1024]{2,1,0:T(8,128)(2,1)S(1)}, u32[]{:S(2)}, u32[]{:S(2)}) async-start(bf16[32,8,1024]{2,1,0:T(8,128)(2,1)} %bitcast.28), calls=%async_computation.2 | async-start | bytes 1048576 | tf_op jit(solution)/shard_map/all_to_all | solution.py:181
  88.9 2.1 %collective-permute-start.3 = (bf16[128,1024]{1,0:T(8,128)(2,1)S(1)}, bf16[128,1024]{1,0:T(8,128)(2,1)S(1)}, u32[]{:S(2)}, u32[]{:S(2)}) collective-permute-start(bf16[128,1024]{1,0:T(8,128)(2,1)S(1)} %get-tuple-element.32.own_pre), channel_id=1, source_target_pairs={{0,16},{16,0},{1,17},{17,1},{2,18},{18,2},{3,19},{19,3},{4,20},{20... | collective-permute-start | bytes 786440 | tf_op jit(solution)/shard_map/ppermute | solution.py:19
  91.0 1.4 collective-permute-done.3.mate_pre
  92.4 0.9 copy-done.3
  93.3 0.5 shard_map.87
  93.7 2.1 %collective-permute-start.4 = (bf16[128,1024]{1,0:T(8,128)(2,1)S(1)}, bf16[128,1024]{1,0:T(8,128)(2,1)S(1)}, u32[]{:S(2)}, u32[]{:S(2)}) collective-permute-start(bf16[128,1024]{1,0:T(8,128)(2,1)S(1)} %get-tuple-element.34), channel_id=1, source_target_pairs={{0,32},{8,40},{32,0},{40,8},{1,33},{9,41},{33,1},{41,9},{2,34},{10... | collective-permute-start | bytes 786440 | tf_op jit(solution)/shard_map/ppermute | solution.py:190
  95.9 2.9 %collective-permute-start.5 = (bf16[128,1024]{1,0:T(8,128)(2,1)S(1)}, bf16[128,1024]{1,0:T(8,128)(2,1)S(1)}, u32[]{:S(2)}, u32[]{:S(2)}) collective-permute-start(bf16[128,1024]{1,0:T(8,128)(2,1)S(1)} %get-tuple-element.35), channel_id=1, source_target_pairs={{0,8},{8,0},{32,40},{40,32},{1,9},{9,1},{33,41},{41,33},{2,10},{10... | collective-permute-start | bytes 786440 | tf_op jit(solution)/shard_map/ppermute | solution.py:190
  98.8 4.8 %collective-permute-start.6 = (bf16[128,1024]{1,0:T(8,128)(2,1)S(1)}, bf16[128,1024]{1,0:T(8,128)(2,1)S(1)}, u32[]{:S(2)}, u32[]{:S(2)}) collective-permute-start(bf16[128,1024]{1,0:T(8,128)(2,1)S(1)} %get-tuple-element.36), channel_id=1, source_target_pairs={{0,40},{8,32},{32,8},{40,0},{1,41},{9,33},{33,9},{41,1},{2,42},{10... | collective-permute-start | bytes 786440 | tf_op jit(solution)/shard_map/ppermute | solution.py:190
  103.6 3.8 %collective-permute-done.4 = bf16[128,1024]{1,0:T(8,128)(2,1)S(1)} collective-permute-done((bf16[128,1024]{1,0:T(8,128)(2,1)S(1)}, bf16[128,1024]{1,0:T(8,128)(2,1)S(1)}, u32[]{:S(2)}, u32[]{:S(2)}) %collective-permute-start.4) | collective-permute-done | bytes 262176 | tf_op jit(solution)/shard_map/ppermute | solution.py:190
  107.4 4.4 %collective-permute-done.5 = bf16[128,1024]{1,0:T(8,128)(2,1)S(1)} collective-permute-done((bf16[128,1024]{1,0:T(8,128)(2,1)S(1)}, bf16[128,1024]{1,0:T(8,128)(2,1)S(1)}, u32[]{:S(2)}, u32[]{:S(2)}) %collective-permute-start.5) | collective-permute-done | bytes 262176 | tf_op jit(solution)/shard_map/ppermute | solution.py:190
  111.8 0.8 collective-permute-done.6
  112.6 0.8 add_convert_fusion
  113.4 5.5 %all-to-all-start.2 = ((bf16[8,16,1024]{2,1,0:T(8,128)(2,1)}), bf16[8,16,1024]{2,1,0:T(8,128)(2,1)S(1)}, u32[]{:S(2)}, u32[]{:S(2)}) async-start(bf16[8,16,1024]{2,1,0:T(8,128)(2,1)} %bitcast.9), calls=%async_computation.3 | async-start | bytes 524288 | tf_op jit(solution)/shard_map/all_to_all | solution.py:194
  119.0 2.8 %fusion.2 = bf16[256,1024]{1,0:T(8,128)(2,1)} fusion(bf16[1024,1024]{1,0:T(8,128)(2,1)S(1)} %copy-done, f32[256,1024]{1,0:T(8,128)} %fusion.8, bf16[256,1024]{1,0:T(8,128)(2,1)S(1)} %bitcast.30, f32[256]{0:T(256)S(1)} %convert_rsqrt_fusion), kind=kOutput, calls=%fused_computation.6 | convolution fusion | flops 538181632 | bytes 4195328 | tf_op jit(solution)/shard_map/dot_general | solution.py:23
  121.8 9.2 %all-to-all-done.2 = bf16[8,16,1024]{2,1,0:T(8,128)(2,1)S(1)} async-done(((bf16[8,16,1024]{2,1,0:T(8,128)(2,1)}), bf16[8,16,1024]{2,1,0:T(8,128)(2,1)S(1)}, u32[]{:S(2)}, u32[]{:S(2)}) %all-to-all-start.2) | async-done | bytes 262176 | tf_op jit(solution)/shard_map/all_to_all | solution.py:194
  131.1 0.1 broadcast_in_dim.8
  131.1 18.5 %all_to_all.20 = bf16[16,16,1024]{2,1,0:T(8,128)(2,1)S(1)} all-to-all(bf16[16,16,1024]{2,1,0:T(8,128)(2,1)S(1)} %broadcast_in_dim.8), channel_id=1, replica_groups=mesh['wide_y'=8,'wide_x'=2,'wide_c'=2,'blk_x'=2,'blk_z'=8] {'blk_x','blk..., dimensions={0} | all-to-all | bytes 1048576 | tf_op jit(solution)/shard_map/all_to_all | solution.py:199
  149.6 0.7 convert_reduce_fusion
  (23 shorter events, 0.1 us)
Async XLA Ops:
  7.2 16.8 %copy-start = (bf16[1024,1024]{1,0:T(8,128)(2,1)S(1)}, bf16[1024,1024]{1,0:T(8,128)(2,1)}, u32[]{:S(2)}) copy-start(bf16[1024,1024]{1,0:T(8,128)(2,1)} %param.11) | copy-start | bytes 6291460
  7.2 16.8 %copy-start.10 = (bf16[256,1024]{1,0:T(8,128)(2,1)S(1)}, bf16[256,1024]{1,0:T(8,128)(2,1)}, u32[]{:S(2)}) copy-start(bf16[256,1024]{1,0:T(8,128)(2,1)} %param.9) | copy-start | bytes 1572868
  7.2 16.6 %copy-start.11 = (s32[128,1]{0,1:T(1,128)S(1)}, s32[128,1]{0,1:T(1,128)}, u32[]{:S(2)}) copy-start(s32[128,1]{0,1:T(1,128)} %param.8) | copy-start | bytes 1540
  7.2 52.2 %all-gather.2.cloned.1.call-start = ((), (), s32[]{:S(2)}) async-start(), calls=%async_computation.5 | async-start | bytes 2359296 | tf_op jit(solution)/shard_map/all_gather | solution.py:150
  7.9 37.9 %collective-permute-start = (bf16[128,1024]{1,0:T(8,128)(2,1)}, bf16[128,1024]{1,0:T(8,128)(2,1)S(1)}, u32[]{:S(2)}, u32[]{:S(2)}) collective-permute-start(bf16[128,1024]{1,0:T(8,128)(2,1)} %refs_2_.1), channel_id=1, source_target_pairs={{0,8},{8,0},{1,9},{9,1},{2,10},{10,2},{3,11},{11,3},{4,12},{12,4},... | collective-permute-start | bytes 786440 | tf_op jit(solution)/shard_map/ppermute | solution.py:19
  13.5 27.9 %all-to-all-start = ((bf16[32,8,1024]{2,1,0:T(8,128)(2,1)}), bf16[32,8,1024]{2,1,0:T(8,128)(2,1)S(1)}, u32[]{:S(2)}, u32[]{:S(2)}) async-start(bf16[32,8,1024]{2,1,0:T(8,128)(2,1)} %fusion.17), calls=%async_computation | async-start | bytes 1048576 | tf_op jit(solution)/shard_map/all_to_all | solution.py:157
  23.7 126.6 %reduce-scatter.2.cloned.1.call-start = ((), (), s32[]{:S(2)}) async-start(), calls=%async_computation.6 | async-start | bytes 2359296 | tf_op jit(solution)/shard_map/reduce_scatter | solution.py:178
  41.7 17.7 %copy-start.5 = (bf16[128,1024]{1,0:T(8,128)(2,1)S(1)}, bf16[128,1024]{1,0:T(8,128)(2,1)}, u32[]{:S(2)}) copy-start(bf16[128,1024]{1,0:T(8,128)(2,1)} %refs_2_.1) | copy-start | bytes 786436
  42.7 3.8 %collective-permute-start.1 = (bf16[128,512]{1,0:T(8,128)(2,1)S(1)}, bf16[128,512]{1,0:T(8,128)(2,1)S(1)}, u32[]{:S(2)}, u32[]{:S(2)}) collective-permute-start(bf16[128,512]{1,0:T(8,128)(2,1)S(1)} %fusion.3), channel_id=1, source_target_pairs={{0,16},{16,0},{1,17},{17,1},{2,18},{18,2},{3,19},{19,3},{4,20},{20... | collective-permute-start | bytes 393224 | tf_op jit(solution)/shard_map/ppermute | solution.py:19
  45.8 0.7 copy-start.6
  59.4 1.6 %copy-start.4 = (bf16[1024,1024]{1,0:T(8,128)(2,1)S(1)}, bf16[1024,1024]{1,0:T(8,128)(2,1)}, u32[]{:S(2)}) copy-start(bf16[1024,1024]{1,0:T(8,128)(2,1)} %all-gather.2.cloned.1.call-done.refs_1_) | copy-start | bytes 6291460
  61.0 0.9 copy-start.7
  66.9 1.3 copy-start.1
  68.2 0.7 copy-start.8
  68.9 0.9 copy-start.9
  69.8 8.3 %collective-permute-start.2 = (bf16[128,1024]{1,0:T(8,128)(2,1)S(1)}, bf16[128,1024]{1,0:T(8,128)(2,1)S(1)}, u32[]{:S(2)}, u32[]{:S(2)}) collective-permute-start(bf16[128,1024]{1,0:T(8,128)(2,1)S(1)} %copy-done.9), channel_id=1, source_target_pairs={{0,8},{8,0},{1,9},{9,1},{2,10},{10,2},{3,11},{11,3},{4,12},{12,4},... | collective-permute-start | bytes 786440 | tf_op jit(solution)/shard_map/ppermute | solution.py:19
  78.4 0.8 copy-start.2
  79.2 34.2 %all-to-all-start.1 = ((bf16[32,8,1024]{2,1,0:T(8,128)(2,1)}), bf16[32,8,1024]{2,1,0:T(8,128)(2,1)S(1)}, u32[]{:S(2)}, u32[]{:S(2)}) async-start(bf16[32,8,1024]{2,1,0:T(8,128)(2,1)} %bitcast.28), calls=%async_computation.2 | async-start | bytes 1048576 | tf_op jit(solution)/shard_map/all_to_all | solution.py:181
  88.9 3.4 %collective-permute-start.3 = (bf16[128,1024]{1,0:T(8,128)(2,1)S(1)}, bf16[128,1024]{1,0:T(8,128)(2,1)S(1)}, u32[]{:S(2)}, u32[]{:S(2)}) collective-permute-start(bf16[128,1024]{1,0:T(8,128)(2,1)S(1)} %get-tuple-element.32.own_pre), channel_id=1, source_target_pairs={{0,16},{16,0},{1,17},{17,1},{2,18},{18,2},{3,19},{19,3},{4,20},{20... | collective-permute-start | bytes 786440 | tf_op jit(solution)/shard_map/ppermute | solution.py:19
  92.4 0.9 copy-start.3
  93.7 13.7 %collective-permute-start.4 = (bf16[128,1024]{1,0:T(8,128)(2,1)S(1)}, bf16[128,1024]{1,0:T(8,128)(2,1)S(1)}, u32[]{:S(2)}, u32[]{:S(2)}) collective-permute-start(bf16[128,1024]{1,0:T(8,128)(2,1)S(1)} %get-tuple-element.34), channel_id=1, source_target_pairs={{0,32},{8,40},{32,0},{40,8},{1,33},{9,41},{33,1},{41,9},{2,34},{10... | collective-permute-start | bytes 786440 | tf_op jit(solution)/shard_map/ppermute | solution.py:190
  95.9 15.9 %collective-permute-start.5 = (bf16[128,1024]{1,0:T(8,128)(2,1)S(1)}, bf16[128,1024]{1,0:T(8,128)(2,1)S(1)}, u32[]{:S(2)}, u32[]{:S(2)}) collective-permute-start(bf16[128,1024]{1,0:T(8,128)(2,1)S(1)} %get-tuple-element.35), channel_id=1, source_target_pairs={{0,8},{8,0},{32,40},{40,32},{1,9},{9,1},{33,41},{41,33},{2,10},{10... | collective-permute-start | bytes 786440 | tf_op jit(solution)/shard_map/ppermute | solution.py:190
  98.8 13.8 %collective-permute-start.6 = (bf16[128,1024]{1,0:T(8,128)(2,1)S(1)}, bf16[128,1024]{1,0:T(8,128)(2,1)S(1)}, u32[]{:S(2)}, u32[]{:S(2)}) collective-permute-start(bf16[128,1024]{1,0:T(8,128)(2,1)S(1)} %get-tuple-element.36), channel_id=1, source_target_pairs={{0,40},{8,32},{32,8},{40,0},{1,41},{9,33},{33,9},{41,1},{2,42},{10... | collective-permute-start | bytes 786440 | tf_op jit(solution)/shard_map/ppermute | solution.py:190
  113.4 17.6 %all-to-all-start.2 = ((bf16[8,16,1024]{2,1,0:T(8,128)(2,1)}), bf16[8,16,1024]{2,1,0:T(8,128)(2,1)S(1)}, u32[]{:S(2)}, u32[]{:S(2)}) async-start(bf16[8,16,1024]{2,1,0:T(8,128)(2,1)} %bitcast.9), calls=%async_computation.3 | async-start | bytes 524288 | tf_op jit(solution)/shard_map/all_to_all | solution.py:194
Sparse Core Ops, SparseCore 0:
  10.1 49.2 all-gather.1
  69.0 43.6 reduce-scatter.1

commit v4 on v3

v4 whole, which is shorter than its diff:
```python
import jax
import jax.numpy as jnp
from jax import lax
from jax.experimental import pallas as pl
from jax.experimental.pallas import tpu as pltpu
from jax.sharding import Mesh
from jax.sharding import PartitionSpec as P

AXES = ("wide_y", "wide_x", "wide_c", "blk_x", "blk_z")
WIDE = ("wide_y", "wide_x", "wide_c")
BLK = ("blk_x", "blk_z")
BF16 = jnp.bfloat16
F32 = jnp.float32
ROOM = pltpu.CompilerParams(vmem_limit_bytes=24 * 2**20)
ALL_ROOM = pltpu.CompilerParams(vmem_limit_bytes=56 * 2**20)
SCALAR = pl.BlockSpec(memory_space=pltpu.SMEM)


def swapped(array, axis):
    return lax.ppermute(array, axis, [(0, 1), (1, 0)])


def dot_of(matrix_a, matrix_b, dim_a, dim_b):
    return lax.dot_general(
        matrix_a, matrix_b, (((dim_a,), (dim_b,)), ((), ())), preferred_element_type=F32
    )


def gelu_slope(v):
    cdf = 0.5 * (1.0 + lax.erf(v * 0.7071067811865476))
    return cdf + v * (0.3989422804014327 * jnp.exp(-0.5 * v * v))


def targets_of(owner, capacity):
    ids = jnp.arange(owner.shape[0], dtype=jnp.int32)
    peer = owner[:, 0]
    before = (peer[:, None] == peer[None, :]) & (ids[:, None] < ids[None, :])
    return peer * capacity + jnp.sum(before.astype(jnp.int32), axis=0)


def picking_of(core, feature_count):
    half = feature_count // 2
    ny, nx = lax.axis_size("wide_y"), lax.axis_size("wide_x")
    bx = lax.axis_size("blk_x")
    share = half // (ny * nx * bx)
    place = jnp.arange(half, dtype=jnp.int32)
    within, rest = place % share, place // share
    y, apart = (rest + lax.axis_index("wide_y")) % ny, rest // ny
    x_wide = (apart // bx) ^ lax.axis_index("wide_x")
    x_blk = (apart % bx) ^ lax.axis_index("blk_x")
    feature = (((y * nx + x_wide) * 2 + core) * bx + x_blk) * share + within
    return (jnp.arange(feature_count, dtype=jnp.int32)[:, None] == feature[None, :]).astype(BF16)


def pair_kernel(factor, steps, place_ref, line_hbm, own_hbm, mate_hbm, slope_hbm,
                kept_ref, sent_ref, pre_ref, grads_hbm, line, video, slope, grads, total, came, gone):
    rows, clips = line.shape[0] // steps, own_hbm.shape[0]
    loads = [
        pltpu.make_async_copy(own_hbm, video.at[pl.ds(0, clips)], came.at[0]),
        pltpu.make_async_copy(mate_hbm, video.at[pl.ds(clips, clips)], came.at[1]),
    ]
    for step in range(steps):
        block = pl.ds(step * rows, rows)
        loads.append(pltpu.make_async_copy(line_hbm.at[block], line.at[block], came.at[2 + step]))
    loads.append(pltpu.make_async_copy(slope_hbm, slope, came.at[2 + steps]))
    for load in loads:
        load.start()
    loads[0].wait()
    loads[1].wait()
    stores = []
    for step in range(steps):
        block = pl.ds(step * rows, rows)
        loads[2 + step].wait()
        scores = dot_of(video[...], line[block], 1, 1)
        row = lax.broadcasted_iota(jnp.int32, scores.shape, 0)
        col = lax.broadcasted_iota(jnp.int32, scores.shape, 1) + step * rows
        labels = ((col == place_ref[0] * clips + row) & (row < clips)).astype(F32)
        coeffs = (factor * (jax.nn.sigmoid(4.0 * scores - 2.0) - labels)).astype(BF16)
        part = dot_of(coeffs, line[block], 1, 0)
        if step == 0:
            total[...] = part
        else:
            total[...] += part
        grads[block] = dot_of(coeffs, video[...], 0, 0).astype(BF16)
        stores.append(pltpu.make_async_copy(grads.at[block], grads_hbm.at[block], gone.at[step]))
        stores[-1].start()
    loads[-1].wait()
    kept_ref[...] = total[:clips]
    sent_ref[...] = total[clips:].astype(BF16)
    pre_ref[...] = (total[...] * slope[...]).astype(BF16)
    for store in stores:
        store.wait()


def pair_grads(line, own, mate, slope, place, factor, steps):
    rows, features = line.shape
    clips = own.shape[0]
    free = pl.BlockSpec(memory_space=pl.ANY)
    held = pl.BlockSpec(memory_space=pltpu.VMEM)
    return pl.pallas_call(
        lambda *refs: pair_kernel(factor, steps, *refs),
        in_specs=[SCALAR, free, free, free, free],
        out_specs=[held, held, held, free],
        out_shape=[
            jax.ShapeDtypeStruct((clips, features), F32),
            jax.ShapeDtypeStruct((clips, features), BF16),
            jax.ShapeDtypeStruct((2 * clips, features), BF16),
            jax.ShapeDtypeStruct((rows, features), BF16),
        ],
        scratch_shapes=[
            pltpu.VMEM((rows, features), BF16),
            pltpu.VMEM((2 * clips, features), BF16),
            pltpu.VMEM((2 * clips, features), F32),
            pltpu.VMEM((rows, features), BF16),
            pltpu.VMEM((2 * clips, features), F32),
            pltpu.SemaphoreType.DMA((3 + steps,)),
            pltpu.SemaphoreType.DMA((steps,)),
        ],
        compiler_params=ALL_ROOM,
        cost_estimate=pl.CostEstimate(
            flops=12 * rows * clips * features, bytes_accessed=5 * rows * features, transcendentals=0
        ),
    )(place, line, own, mate, slope)


def clip_kernel(kept_ref, arrived_ref, target_ref, packed_ref):
    grad = (kept_ref[...] + arrived_ref[...].astype(F32)).astype(BF16)
    slots, clips = packed_ref.shape[0], grad.shape[0]
    slot = lax.broadcasted_iota(jnp.int32, (slots, clips), 0)
    placing = (slot == target_ref[...]).astype(BF16)
    packed_ref[...] = dot_of(placing, grad, 1, 0).astype(BF16)


def clip_grads(kept, arrived, targets, slots):
    return pl.pallas_call(
        clip_kernel,
        out_shape=jax.ShapeDtypeStruct((slots, kept.shape[1]), BF16),
        compiler_params=ROOM,
        cost_estimate=pl.CostEstimate(flops=2 * 10**10, bytes_accessed=2**20, transcendentals=0),
    )(kept, arrived, targets[None, :])


def weight_kernel(own_picked, mate_picked, own_pre, mate_pre, *out_refs):
    share = out_refs[0].shape[0]
    for d, out_ref in enumerate(out_refs):
        block = pl.ds(d * share, share)
        product = dot_of(own_picked[block], own_pre[...], 1, 0)
        product += dot_of(mate_picked[block], mate_pre[...], 1, 0)
        out_ref[...] = product.astype(out_ref.dtype)


def weight_parts(own_picked, mate_picked, own_pre, mate_pre, count):
    half, features = own_picked.shape[0], own_pre.shape[1]
    shape = (half // count, features)
    return pl.pallas_call(
        weight_kernel,
        out_shape=[jax.ShapeDtypeStruct(shape, F32 if d == 0 else BF16) for d in range(count)],
        compiler_params=ROOM,
    )(own_picked, mate_picked, own_pre, mate_pre)


def sum_kernel(count, *refs):
    total = refs[0][...].astype(F32)
    for ref in refs[1:count]:
        total += ref[...].astype(F32)
    share = refs[count].shape[0]
    for s, out_ref in enumerate(refs[count:]):
        out_ref[...] = total[s * share : (s + 1) * share].astype(out_ref.dtype)


def sum_in_parts(arrays, parts):
    rows, features = arrays[0].shape
    return pl.pallas_call(
        lambda *refs: sum_kernel(len(arrays), *refs),
        out_shape=[
            jax.ShapeDtypeStruct((rows // parts, features), F32 if s == 0 else BF16)
            for s in range(parts)
        ],
        compiler_params=ROOM,
    )(*arrays)


def spread_kernel(count, *refs):
    total = refs[0][...].astype(F32)
    for ref in refs[1:count]:
        total += ref[...].astype(F32)
    refs[count][...] = jnp.broadcast_to(total.astype(BF16)[None], refs[count].shape)


def sum_spread(arrays, copies):
    return pl.pallas_call(
        lambda *refs: spread_kernel(len(arrays), *refs),
        out_shape=jax.ShapeDtypeStruct((copies, *arrays[0].shape), BF16),
        compiler_params=ROOM,
    )(*arrays)


def shards(audio, video, owner, clip_feats, lengths, proj_weight):
    clips, features = audio.shape
    blocks = lax.axis_size(BLK)
    core = lax.axis_index("wide_c")
    place = lax.axis_index("blk_z").astype(jnp.int32)[None]
    audio_line = lax.all_gather(audio, "blk_z", axis=0, tiled=True)

    peers = lax.axis_size(WIDE)
    slots = clip_feats.shape[0]
    capacity = slots // peers
    length_scale = lax.rsqrt(lengths.astype(F32))[:, None]
    pooled = (clip_feats.astype(F32) * length_scale).astype(BF16)
    pooled_slots = lax.all_to_all(
        pooled.reshape(peers, capacity, features), WIDE, 0, 0, tiled=True
    ).reshape(slots, features)
    video_mate = swapped(video, "blk_x")
    slope_own = gelu_slope(dot_of(pooled, proj_weight, 1, 0))

    targets = targets_of(owner, capacity)
    placing = (targets[:, None] == jnp.arange(slots, dtype=jnp.int32)[None, :]).astype(BF16)
    clip_rows = dot_of(placing, pooled_slots, 1, 0).astype(BF16)
    row_pair = jnp.concatenate([clip_rows, swapped(clip_rows, "blk_x")])
    slope_pair = gelu_slope(dot_of(row_pair, proj_weight, 1, 0))
    picked = dot_of(picking_of(core, features), row_pair, 0, 1).astype(BF16)
    picked_mate = swapped(
        dot_of(picking_of(1 - core, features), row_pair, 0, 1).astype(BF16), "wide_c"
    )
    audio_line, video_mate, slope_pair, picked, picked_mate, slope_own, targets = (
        lax.optimization_barrier(
            (audio_line, video_mate, slope_pair, picked, picked_mate, slope_own, targets)
        )
    )

    kept, sent, pre_pair, line_grads = pair_grads(
        audio_line, video, video_mate, slope_pair, place, 4.0 / blocks, 4
    )
    audio_grad = lax.psum_scatter(line_grads, "blk_z", scatter_dimension=0, tiled=True)

    pre_mate = swapped(pre_pair, "wide_c")
    arrived = swapped(sent, "blk_x")
    parts = weight_parts(picked, picked_mate, pre_pair, pre_mate, 4)
    came = [parts[0]]
    for d in (2, 1, 3):
        pairs = [(at, at ^ d) for at in range(4)]
        came.append(lax.ppermute(parts[d], ("wide_x", "blk_x"), pairs))

    arrived, parts = lax.optimization_barrier((arrived, parts))
    packed = clip_grads(kept, arrived, targets, slots)
    packed, came = lax.optimization_barrier((packed, came))
    received = lax.all_to_all(
        packed.reshape(peers, capacity, features), WIDE, 0, 0, tiled=True
    ).reshape(slots, features)

    packed, came = lax.optimization_barrier((packed, came))
    ny = lax.axis_size("wide_y")
    parts = sum_in_parts(came, ny)
    came = [parts[0]]
    for s in range(1, ny):
        pairs = [(at, (at + s) % ny) for at in range(ny)]
        came.append(lax.ppermute(parts[s], "wide_y", pairs))
    received, came = lax.optimization_barrier((received, came))
    total = sum_spread(came, blocks)
    gathered = lax.all_to_all(total, BLK, 0, 0, tiled=True)
    pre_grad = (received.astype(F32) * slope_own).astype(BF16)
    feats_grad = (dot_of(pre_grad, proj_weight, 1, 1) * length_scale).astype(BF16)
    gathered, feats_grad = lax.optimization_barrier((gathered, feats_grad))
    gathered = gathered.reshape(lax.axis_size("blk_x"), -1, *total.shape[1:])
    weight_grad = jnp.sum(gathered.astype(F32), axis=1).reshape(-1, features)
    return (audio_grad, feats_grad, weight_grad)


def solution(mesh):
    finer = Mesh(mesh.devices.reshape(8, 2, 2, 2, 8), AXES)
    rows = P(AXES, None)
    return jax.shard_map(
        shards,
        mesh=finer,
        in_specs=(rows, rows, rows, rows, P(AXES), P()),
        out_specs=(rows, rows, P(WIDE, None)),
        check_vma=False,
    )
```

time: 158 us -> 167 us (1.057)
  starting transfers between devices: 44.9 us -> 79.4 us
  blocking collectives: 18.5 us -> 0 us
  waiting for transfers between devices: 54.2 us -> 43.2 us
  local copies, waits for them, and re-layouts: 7.96 us -> 2.82 us
  Pallas kernels: 5.65 us -> 10.5 us
  matrix products: 7.21 us -> 11.7 us
    ppermute x3 -> x10, starting transfers between devices: 9.82 us -> 40.3 us  [the longest x7 29.9 us: shards(): came.append(lax.ppermute(parts[s], 'wide_y', pairs))]
    all_to_all x1 -> x0, blocking collectives: 18.5 us -> none  [shards(): lax.all_to_all(jnp.broadcast_to(total[None], (blocks, *total.shape)), BLK...]
    all_gather x1, waiting for transfers between devices: 12.9 us -> 2.05 us  [shards(): audio_line = lax.all_gather(audio, 'blk_z', axis=0, tiled=True)]
    unnamed x24 -> x18, local copies, waits for them, and re-layouts: 7.91 us -> 2.82 us
    pallas_call x2 -> x4, Pallas kernels: 5.2 us -> 9.82 us  [the longest x1 6.75 us: pair_grads(): pl.pallas_call(lambda *refs: pair_kernel(factor, steps, *refs), in_specs=...]
    dot_general x6, matrix products: 7.21 us -> 11.7 us  [dot_of(): lax.dot_general(matrix_a, matrix_b, (((dim_a,), (dim_b,)), ((), ())), pre...]
    ppermute x3 -> x10, waiting for transfers between devices: 9.02 us -> 11.8 us  [the longest x3 9.37 us: shards(): came.append(lax.ppermute(parts[d], ('wide_x', 'blk_x'), pairs))]
    all_to_all x1, waiting for transfers between devices: 15.4 us -> 12.7 us  [shards(): lax.all_to_all(pooled.reshape(peers, capacity, features), WIDE, 0, 0, til...]
  transfers between devices with their start and end apart: 12 -> 20, of which waited for: 8 -> 7; matrix products, arithmetic and copies ran while one was open for 7% -> 9% of each run, Pallas kernels for 0% -> 2%
where the time goes in v4:
time: 167 us; the launch traced here: 166 us
  starting transfers between devices  79.4 us (48%)
  waiting for transfers between devices  43.2 us (26%)
  between operations  14.4 us (9%)
  matrix products  11.7 us (7%)
  Pallas kernels  10.5 us (6%)
  other arithmetic  3.67 us (2%)
  local copies, waits for them, and re-layouts  2.82 us (2%)
    ppermute x7, starting transfers between devices, shards(): came.append(lax.ppermute(parts[s], 'wide_y', pairs))  29.9 us
    all_to_all x1, waiting for transfers between devices, shards(): lax.all_to_all(pooled.reshape(peers, capacity, features), WIDE, 0, 0, til...  12.7 us
    ppermute x5, starting transfers between devices, swapped(): return lax.ppermute(array, axis, [(0, 1), (1, 0)])  12.2 us
    dot_general x6, matrix products, dot_of(): lax.dot_general(matrix_a, matrix_b, (((dim_a,), (dim_b,)), ((), ())), pre...  11.7 us
    ppermute x3, starting transfers between devices, shards(): came.append(lax.ppermute(parts[d], ('wide_x', 'blk_x'), pairs))  10.4 us
    all_to_all x1, starting transfers between devices, shards(): lax.all_to_all(pooled.reshape(peers, capacity, features), WIDE, 0, 0, til...  10.2 us
    ppermute x3, waiting for transfers between devices, shards(): came.append(lax.ppermute(parts[d], ('wide_x', 'blk_x'), pairs))  9.37 us
    all_to_all x1, waiting for transfers between devices, shards(): gathered = lax.all_to_all(total, BLK, 0, 0, tiled=True)  9.22 us
  transfers between devices with their start and end apart: 20, of which 7 were waited for; matrix products, arithmetic and copies ran while one was open for 9% of the time, Pallas kernels for 2%

profile of v4, /device:TPU:6, one launch (start us, length us, event | category | flops | bytes accessed | tf_op | source)
XLA Modules:
  0.0 165.7 jit_solution(5734086051037038316)
XLA Ops:
  7.2 0.0 copy-start
  7.2 0.0 all-gather.2.cloned.1.call-start
  7.3 0.7 all-gather.2.cloned.1.call-update
  7.9 0.8 convert_rsqrt_fusion
  8.7 2.0 %fusion.17 = bf16[32,8,1024]{2,1,0:T(8,128)(2,1)} fusion(f32[256]{0:T(256)S(1)} %convert_rsqrt_fusion, bf16[256,1024]{1,0:T(8,128)(2,1)} %param.9), kind=kLoop, calls=%fused_computation.27 | loop fusion | flops 786432 | bytes 1049600 | tf_op jit(solution)/shard_map/reshape | solution.py:211
  10.7 10.2 %all-to-all-start = ((bf16[32,8,1024]{2,1,0:T(8,128)(2,1)}), bf16[32,8,1024]{2,1,0:T(8,128)(2,1)S(1)}, u32[]{:S(2)}, u32[]{:S(2)}) async-start(bf16[32,8,1024]{2,1,0:T(8,128)(2,1)} %fusion.17), calls=%async_computation | async-start | bytes 1048576 | tf_op jit(solution)/shard_map/all_to_all | solution.py:210
  21.0 0.0 reduce-scatter.2.cloned.1.call-start
  21.0 2.7 %collective-permute-start = (bf16[128,1024]{1,0:T(8,128)(2,1)S(1)}, bf16[128,1024]{1,0:T(8,128)(2,1)}, u32[]{:S(2)}, u32[]{:S(2)}) collective-permute-start(bf16[128,1024]{1,0:T(8,128)(2,1)S(1)} %copy-done.7), channel_id=1, source_target_pairs={{0,8},{8,0},{1,9},{9,1},{2,10},{10,2},{3,11},{11,3},{4,12},{12,4},... | collective-permute-start | bytes 786440 | tf_op jit(solution)/shard_map/ppermute | solution.py:20
  23.8 0.1 convert_reduce_fusion.1
  23.9 2.0 %fusion.10 = f32[256,1024]{1,0:T(8,128)} fusion(bf16[1024,1024]{1,0:T(8,128)(2,1)S(1)} %copy-done, bf16[256,1024]{1,0:T(8,128)(2,1)S(1)} %copy-done.6, f32[256]{0:T(256)S(1)} %convert_rsqrt_fusion), kind=kOutput, calls=%fused_computation.18 | convolution fusion | flops 539754496 | bytes 3671040 | tf_op jit(solution)/shard_map/dot_general | solution.py:24
  26.0 12.7 %all-to-all-done = bf16[32,8,1024]{2,1,0:T(8,128)(2,1)S(1)} async-done(((bf16[32,8,1024]{2,1,0:T(8,128)(2,1)}), bf16[32,8,1024]{2,1,0:T(8,128)(2,1)S(1)}, u32[]{:S(2)}, u32[]{:S(2)}) %all-to-all-start) | async-done | bytes 524320 | tf_op jit(solution)/shard_map/all_to_all | solution.py:210
  38.7 0.3 convolution_convert_fusion.2
  38.9 2.7 %collective-permute-start.1 = (bf16[128,1024]{1,0:T(8,128)(2,1)S(1)}, bf16[128,1024]{1,0:T(8,128)(2,1)}, u32[]{:S(2)}, u32[]{:S(2)}) collective-permute-start(bf16[128,1024]{1,0:T(8,128)(2,1)S(1)} %convolution_convert_fusion.2), channel_id=1, source_target_pairs={{0,8},{8,0},{1,9},{9,1},{2,10},{10,2},{3,11},{11,3},{4,12},{12,4},... | collective-permute-start | bytes 786440 | tf_op jit(solution)/shard_map/ppermute | solution.py:20
  41.7 6.7 %collective-permute-done.1 = bf16[128,1024]{1,0:T(8,128)(2,1)} collective-permute-done((bf16[128,1024]{1,0:T(8,128)(2,1)S(1)}, bf16[128,1024]{1,0:T(8,128)(2,1)}, u32[]{:S(2)}, u32[]{:S(2)}) %collective-permute-start.1) | collective-permute-done | bytes 262176 | tf_op jit(solution)/shard_map/ppermute | solution.py:20
  48.4 1.4 convolution_convert_fusion
  49.9 1.9 %collective-permute-start.2 = (bf16[512,256]{1,0:T(8,128)(2,1)S(1)}, bf16[512,256]{1,0:T(8,128)(2,1)S(1)}, u32[]{:S(2)}, u32[]{:S(2)}) collective-permute-start(bf16[512,256]{1,0:T(8,128)(2,1)S(1)} %convolution_convert_fusion), channel_id=1, source_target_pairs={{0,16},{16,0},{1,17},{17,1},{2,18},{18,2},{3,19},{19,3},{4,20},{20... | collective-permute-start | bytes 786440 | tf_op jit(solution)/shard_map/ppermute | solution.py:20
  51.8 2.9 %fusion.6.refs_4_ = f32[256,1024]{1,0:T(8,128)} fusion(bf16[1024,1024]{1,0:T(8,128)(2,1)S(1)} %copy-done, bf16[128,1024]{1,0:T(8,128)(2,1)} %collective-permute-done.1, bf16[128,1024]{1,0:T(8,128)(2,1)S(1)} %convolution_convert_fusion.2), kind=kOutput, calls=%fused_computation.14 | convolution fusion | flops 540016640 | bytes 3670016 | tf_op jit(solution)/shard_map/dot_general | solution.py:24
  54.7 2.1 %convolution_convert_fusion.1.own_picked = bf16[512,256]{1,0:T(8,128)(2,1)} fusion(s32[512]{0:T(512)S(1)} %multiply_add_fusion.1, bf16[128,1024]{1,0:T(8,128)(2,1)} %collective-permute-done.1, bf16[128,1024]{1,0:T(8,128)(2,1)S(1)} %convolution_convert_fusion.2), kind=kOutput, calls=%fused_computation.9 | convolution fusion | flops 270663680 | bytes 788480 | tf_op jit(solution)/shard_map/dot_general | solution.py:24
  56.8 2.1 %all-gather.2.cloned.1.call-done.refs_1_ = bf16[1024,1024]{1,0:T(8,128)(2,1)} async-done(((bf16[128,1024]{1,0:T(8,128)(2,1)}), bf16[1024,1024]{1,0:T(8,128)(2,1)}) %all-gather.2.cloned.1.call-update) | async-done | bytes 2097168 | tf_op jit(solution)/shard_map/all_gather | solution.py:203
  58.9 6.7 %shard_map.85 = (f32[128,1024]{1,0:T(8,128)}, bf16[128,1024]{1,0:T(8,128)(2,1)}, bf16[256,1024]{1,0:T(8,128)(2,1)}, bf16[1024,1024]{1,0:T(8,128)(2,1)}) custom-call(s32[1]{0:T(128)} %bitcast.refs_0_, bf16[1024,1024]{1,0:T(8,128)(2,1)} %all-gather.2.cloned.1.call-done.refs_1_, bf16[128,1024]{1,0:T(8,128)(2,1)} %refs_2_.1, ...), custom_call_target="tpu_custom_call" | custom-call | flops 1610612736 | bytes 5242880 | tf_op jit(solution)/shard_map/pallas_call | solution.py:100
  65.7 2.1 %collective-permute-start.4 = (bf16[256,1024]{1,0:T(8,128)(2,1)}, bf16[256,1024]{1,0:T(8,128)(2,1)S(1)}, u32[]{:S(2)}, u32[]{:S(2)}) collective-permute-start(bf16[256,1024]{1,0:T(8,128)(2,1)} %get-tuple-element.59.own_pre), channel_id=1, source_target_pairs={{0,16},{16,0},{1,17},{17,1},{2,18},{18,2},{3,19},{19,3},{4,20},{20... | collective-permute-start | bytes 1572872 | tf_op jit(solution)/shard_map/ppermute | solution.py:20
  67.7 2.8 %collective-permute-start.3 = (bf16[128,1024]{1,0:T(8,128)(2,1)}, bf16[128,1024]{1,0:T(8,128)(2,1)}, u32[]{:S(2)}, u32[]{:S(2)}) collective-permute-start(bf16[128,1024]{1,0:T(8,128)(2,1)} %get-tuple-element.56), channel_id=1, source_target_pairs={{0,8},{8,0},{1,9},{9,1},{2,10},{10,2},{3,11},{11,3},{4,12},{12,4},... | collective-permute-start | bytes 786440 | tf_op jit(solution)/shard_map/ppermute | solution.py:20
  70.5 0.0 reduce-scatter.2.cloned.1.call-update
  70.6 0.9 copy-done.4
  71.5 0.7 shard_map.86
  72.2 0.8 copy-done.2
  73.0 3.1 %collective-permute-start.6 = (bf16[128,1024]{1,0:T(8,128)(2,1)S(1)}, bf16[128,1024]{1,0:T(8,128)(2,1)S(1)}, u32[]{:S(2)}, u32[]{:S(2)}) collective-permute-start(bf16[128,1024]{1,0:T(8,128)(2,1)S(1)} %get-tuple-element.61), channel_id=1, source_target_pairs={{0,8},{8,0},{32,40},{40,32},{1,9},{9,1},{33,41},{41,33},{2,10},{10... | collective-permute-start | bytes 786440 | tf_op jit(solution)/shard_map/ppermute | solution.py:242
  76.1 3.9 %collective-permute-start.5 = (bf16[128,1024]{1,0:T(8,128)(2,1)S(1)}, bf16[128,1024]{1,0:T(8,128)(2,1)S(1)}, u32[]{:S(2)}, u32[]{:S(2)}) collective-permute-start(bf16[128,1024]{1,0:T(8,128)(2,1)S(1)} %get-tuple-element.62), channel_id=1, source_target_pairs={{0,32},{8,40},{32,0},{40,8},{1,33},{9,41},{33,1},{41,9},{2,34},{10... | collective-permute-start | bytes 786440 | tf_op jit(solution)/shard_map/ppermute | solution.py:242
  80.1 3.4 %collective-permute-start.7 = (bf16[128,1024]{1,0:T(8,128)(2,1)S(1)}, bf16[128,1024]{1,0:T(8,128)(2,1)S(1)}, u32[]{:S(2)}, u32[]{:S(2)}) collective-permute-start(bf16[128,1024]{1,0:T(8,128)(2,1)S(1)} %get-tuple-element.63), channel_id=1, source_target_pairs={{0,40},{8,32},{32,8},{40,0},{1,41},{9,33},{33,9},{41,1},{2,42},{10... | collective-permute-start | bytes 786440 | tf_op jit(solution)/shard_map/ppermute | solution.py:242
  83.5 1.0 copy-done.5
  84.5 2.1 %shard_map.87 = bf16[256,1024]{1,0:T(8,128)(2,1)} custom-call(f32[128,1024]{1,0:T(8,128)S(1)} %copy-done.5, bf16[128,1024]{1,0:T(8,128)(2,1)} %collective-permute-done.3.arrived_ref, s32[1,128]{1,0:T(1,128)S(1)} %bitcast.24), custom_call_target="tpu_custom_call" | custom-call | flops 20000000000 | bytes 1048576 | tf_op jit(solution)/shard_map/pallas_call | solution.py:135
  86.6 3.9 %collective-permute-done.5.refs_1_ = bf16[128,1024]{1,0:T(8,128)(2,1)S(1)} collective-permute-done((bf16[128,1024]{1,0:T(8,128)(2,1)S(1)}, bf16[128,1024]{1,0:T(8,128)(2,1)S(1)}, u32[]{:S(2)}, u32[]{:S(2)}) %collective-permute-start.5) | collective-permute-done | bytes 262176 | tf_op jit(solution)/shard_map/ppermute | solution.py:242
  90.5 5.5 %collective-permute-done.7.refs_3_ = bf16[128,1024]{1,0:T(8,128)(2,1)S(1)} collective-permute-done((bf16[128,1024]{1,0:T(8,128)(2,1)S(1)}, bf16[128,1024]{1,0:T(8,128)(2,1)S(1)}, u32[]{:S(2)}, u32[]{:S(2)}) %collective-permute-start.7) | collective-permute-done | bytes 262176 | tf_op jit(solution)/shard_map/ppermute | solution.py:242
  96.0 9.1 %all-to-all-start.1 = ((bf16[32,8,1024]{2,1,0:T(8,128)(2,1)}), bf16[32,8,1024]{2,1,0:T(8,128)(2,1)}, u32[]{:S(2)}, u32[]{:S(2)}) async-start(bf16[32,8,1024]{2,1,0:T(8,128)(2,1)} %bitcast.7), calls=%async_computation.2 | async-start | bytes 1048576 | tf_op jit(solution)/shard_map/all_to_all | solution.py:247
  105.1 0.1 shard_map.88
  105.3 3.4 %collective-permute-start.8 = (bf16[16,1024]{1,0:T(8,128)(2,1)S(1)}, bf16[16,1024]{1,0:T(8,128)(2,1)S(1)}, u32[]{:S(2)}, u32[]{:S(2)}) collective-permute-start(bf16[16,1024]{1,0:T(8,128)(2,1)S(1)} %get-tuple-element.76), channel_id=1, source_target_pairs={{0,64},{64,128},{128,192},{192,256},{256,320},{320,384},{384,448},... | collective-permute-start | bytes 98312 | tf_op jit(solution)/shard_map/ppermute | solution.py:257
  108.7 4.3 %collective-permute-start.9 = (bf16[16,1024]{1,0:T(8,128)(2,1)S(1)}, bf16[16,1024]{1,0:T(8,128)(2,1)S(1)}, u32[]{:S(2)}, u32[]{:S(2)}) collective-permute-start(bf16[16,1024]{1,0:T(8,128)(2,1)S(1)} %get-tuple-element.77), channel_id=1, source_target_pairs={{0,128},{64,192},{128,256},{192,320},{256,384},{320,448},{384,0},{... | collective-permute-start | bytes 98312 | tf_op jit(solution)/shard_map/ppermute | solution.py:257
  112.9 4.6 %collective-permute-start.10 = (bf16[16,1024]{1,0:T(8,128)(2,1)S(1)}, bf16[16,1024]{1,0:T(8,128)(2,1)S(1)}, u32[]{:S(2)}, u32[]{:S(2)}) collective-permute-start(bf16[16,1024]{1,0:T(8,128)(2,1)S(1)} %get-tuple-element.78), channel_id=1, source_target_pairs={{0,192},{64,256},{128,320},{192,384},{256,448},{320,0},{384,64},{4... | collective-permute-start | bytes 98312 | tf_op jit(solution)/shard_map/ppermute | solution.py:257
  117.6 4.2 %collective-permute-start.11 = (bf16[16,1024]{1,0:T(8,128)(2,1)S(1)}, bf16[16,1024]{1,0:T(8,128)(2,1)S(1)}, u32[]{:S(2)}, u32[]{:S(2)}) collective-permute-start(bf16[16,1024]{1,0:T(8,128)(2,1)S(1)} %get-tuple-element.79), channel_id=1, source_target_pairs={{0,256},{64,320},{128,384},{192,448},{256,0},{320,64},{384,128},{4... | collective-permute-start | bytes 98312 | tf_op jit(solution)/shard_map/ppermute | solution.py:257
  121.8 4.7 %collective-permute-start.12 = (bf16[16,1024]{1,0:T(8,128)(2,1)S(1)}, bf16[16,1024]{1,0:T(8,128)(2,1)S(1)}, u32[]{:S(2)}, u32[]{:S(2)}) collective-permute-start(bf16[16,1024]{1,0:T(8,128)(2,1)S(1)} %get-tuple-element.80), channel_id=1, source_target_pairs={{0,320},{64,384},{128,448},{192,0},{256,64},{320,128},{384,192},{4... | collective-permute-start | bytes 98312 | tf_op jit(solution)/shard_map/ppermute | solution.py:257
  126.5 5.4 %collective-permute-start.13 = (bf16[16,1024]{1,0:T(8,128)(2,1)S(1)}, bf16[16,1024]{1,0:T(8,128)(2,1)S(1)}, u32[]{:S(2)}, u32[]{:S(2)}) collective-permute-start(bf16[16,1024]{1,0:T(8,128)(2,1)S(1)} %get-tuple-element.81), channel_id=1, source_target_pairs={{0,384},{64,448},{128,0},{192,64},{256,128},{320,192},{384,256},{4... | collective-permute-start | bytes 98312 | tf_op jit(solution)/shard_map/ppermute | solution.py:257
  131.9 3.3 %collective-permute-start.14 = (bf16[16,1024]{1,0:T(8,128)(2,1)S(1)}, bf16[16,1024]{1,0:T(8,128)(2,1)S(1)}, u32[]{:S(2)}, u32[]{:S(2)}) collective-permute-start(bf16[16,1024]{1,0:T(8,128)(2,1)S(1)} %get-tuple-element.82), channel_id=1, source_target_pairs={{0,448},{64,0},{128,64},{192,128},{256,192},{320,256},{384,320},{4... | collective-permute-start | bytes 98312 | tf_op jit(solution)/shard_map/ppermute | solution.py:257
  135.3 2.4 %collective-permute-done.14.refs_7_ = bf16[16,1024]{1,0:T(8,128)(2,1)S(1)} collective-permute-done((bf16[16,1024]{1,0:T(8,128)(2,1)S(1)}, bf16[16,1024]{1,0:T(8,128)(2,1)S(1)}, u32[]{:S(2)}, u32[]{:S(2)}) %collective-permute-start.14) | collective-permute-done | bytes 32800 | tf_op jit(solution)/shard_map/ppermute | solution.py:257
  137.7 0.9 shard_map.89
  138.6 7.4 %all-to-all-start.2 = ((bf16[16,16,1024]{2,1,0:T(8,128)(2,1)}), bf16[16,16,1024]{2,1,0:T(8,128)(2,1)S(1)}, u32[]{:S(2)}, u32[]{:S(2)}) async-start(bf16[16,16,1024]{2,1,0:T(8,128)(2,1)} %shard_map.89), calls=%async_computation.3 | async-start | bytes 1048576 | tf_op jit(solution)/shard_map/all_to_all | solution.py:260
  146.0 2.9 %fusion.2 = bf16[256,1024]{1,0:T(8,128)(2,1)} fusion(bf16[1024,1024]{1,0:T(8,128)(2,1)S(1)} %copy-done, f32[256,1024]{1,0:T(8,128)} %fusion.10, bf16[256,1024]{1,0:T(8,128)(2,1)} %bitcast.8, f32[256]{0:T(256)S(1)} %convert_rsqrt_fusion), kind=kOutput, calls=%fused_computation.7 | convolution fusion | flops 538181632 | bytes 4195328 | tf_op jit(solution)/shard_map/dot_general | solution.py:24
  148.9 9.2 %all-to-all-done.2 = bf16[16,16,1024]{2,1,0:T(8,128)(2,1)S(1)} async-done(((bf16[16,16,1024]{2,1,0:T(8,128)(2,1)}), bf16[16,16,1024]{2,1,0:T(8,128)(2,1)S(1)}, u32[]{:S(2)}, u32[]{:S(2)}) %all-to-all-start.2) | async-done | bytes 524320 | tf_op jit(solution)/shard_map/all_to_all | solution.py:260
  158.1 0.7 convert_reduce_fusion
  (31 shorter events, 0.1 us)
Async XLA Ops:
  7.2 16.8 %copy-start = (bf16[1024,1024]{1,0:T(8,128)(2,1)S(1)}, bf16[1024,1024]{1,0:T(8,128)(2,1)}, u32[]{:S(2)}) copy-start(bf16[1024,1024]{1,0:T(8,128)(2,1)} %param.11) | copy-start | bytes 6291460
  7.2 16.7 %copy-start.6 = (bf16[256,1024]{1,0:T(8,128)(2,1)S(1)}, bf16[256,1024]{1,0:T(8,128)(2,1)}, u32[]{:S(2)}) copy-start(bf16[256,1024]{1,0:T(8,128)(2,1)} %param.9) | copy-start | bytes 1572868
  7.2 13.8 %copy-start.7 = (bf16[128,1024]{1,0:T(8,128)(2,1)S(1)}, bf16[128,1024]{1,0:T(8,128)(2,1)}, u32[]{:S(2)}) copy-start(bf16[128,1024]{1,0:T(8,128)(2,1)} %refs_2_.1) | copy-start | bytes 786436
  7.2 16.6 %copy-start.8 = (s32[128,1]{0,1:T(1,128)S(1)}, s32[128,1]{0,1:T(1,128)}, u32[]{:S(2)}) copy-start(s32[128,1]{0,1:T(1,128)} %param.8) | copy-start | bytes 1540
  7.2 51.7 %all-gather.2.cloned.1.call-start = ((), (), s32[]{:S(2)}) async-start(), calls=%async_computation.4 | async-start | bytes 2359296 | tf_op jit(solution)/shard_map/all_gather | solution.py:203
  10.7 27.9 %all-to-all-start = ((bf16[32,8,1024]{2,1,0:T(8,128)(2,1)}), bf16[32,8,1024]{2,1,0:T(8,128)(2,1)S(1)}, u32[]{:S(2)}, u32[]{:S(2)}) async-start(bf16[32,8,1024]{2,1,0:T(8,128)(2,1)} %fusion.17), calls=%async_computation | async-start | bytes 1048576 | tf_op jit(solution)/shard_map/all_to_all | solution.py:210
  21.0 137.9 %reduce-scatter.2.cloned.1.call-start = ((), (), s32[]{:S(2)}) async-start(), calls=%async_computation.5 | async-start | bytes 2359296 | tf_op jit(solution)/shard_map/reduce_scatter | solution.py:234
  21.0 35.8 %collective-permute-start = (bf16[128,1024]{1,0:T(8,128)(2,1)S(1)}, bf16[128,1024]{1,0:T(8,128)(2,1)}, u32[]{:S(2)}, u32[]{:S(2)}) collective-permute-start(bf16[128,1024]{1,0:T(8,128)(2,1)S(1)} %copy-done.7), channel_id=1, source_target_pairs={{0,8},{8,0},{1,9},{9,1},{2,10},{10,2},{3,11},{11,3},{4,12},{12,4},... | collective-permute-start | bytes 786440 | tf_op jit(solution)/shard_map/ppermute | solution.py:20
  38.9 9.5 %collective-permute-start.1 = (bf16[128,1024]{1,0:T(8,128)(2,1)S(1)}, bf16[128,1024]{1,0:T(8,128)(2,1)}, u32[]{:S(2)}, u32[]{:S(2)}) collective-permute-start(bf16[128,1024]{1,0:T(8,128)(2,1)S(1)} %convolution_convert_fusion.2), channel_id=1, source_target_pairs={{0,8},{8,0},{1,9},{9,1},{2,10},{10,2},{3,11},{11,3},{4,12},{12,4},... | collective-permute-start | bytes 786440 | tf_op jit(solution)/shard_map/ppermute | solution.py:20
  49.9 7.0 %collective-permute-start.2 = (bf16[512,256]{1,0:T(8,128)(2,1)S(1)}, bf16[512,256]{1,0:T(8,128)(2,1)S(1)}, u32[]{:S(2)}, u32[]{:S(2)}) collective-permute-start(bf16[512,256]{1,0:T(8,128)(2,1)S(1)} %convolution_convert_fusion), channel_id=1, source_target_pairs={{0,16},{16,0},{1,17},{17,1},{2,18},{18,2},{3,19},{19,3},{4,20},{20... | collective-permute-start | bytes 786440 | tf_op jit(solution)/shard_map/ppermute | solution.py:20
  65.7 4.9 %copy-start.1 = (bf16[256,1024]{1,0:T(8,128)(2,1)S(1)}, bf16[256,1024]{1,0:T(8,128)(2,1)}, u32[]{:S(2)}) copy-start(bf16[256,1024]{1,0:T(8,128)(2,1)} %get-tuple-element.59.own_pre) | copy-start | bytes 1572868
  65.7 4.9 %collective-permute-start.4 = (bf16[256,1024]{1,0:T(8,128)(2,1)}, bf16[256,1024]{1,0:T(8,128)(2,1)S(1)}, u32[]{:S(2)}, u32[]{:S(2)}) collective-permute-start(bf16[256,1024]{1,0:T(8,128)(2,1)} %get-tuple-element.59.own_pre), channel_id=1, source_target_pairs={{0,16},{16,0},{1,17},{17,1},{2,18},{18,2},{3,19},{19,3},{4,20},{20... | collective-permute-start | bytes 1572872 | tf_op jit(solution)/shard_map/ppermute | solution.py:20
  67.7 15.7 %collective-permute-start.3 = (bf16[128,1024]{1,0:T(8,128)(2,1)}, bf16[128,1024]{1,0:T(8,128)(2,1)}, u32[]{:S(2)}, u32[]{:S(2)}) collective-permute-start(bf16[128,1024]{1,0:T(8,128)(2,1)} %get-tuple-element.56), channel_id=1, source_target_pairs={{0,8},{8,0},{1,9},{9,1},{2,10},{10,2},{3,11},{11,3},{4,12},{12,4},... | collective-permute-start | bytes 786440 | tf_op jit(solution)/shard_map/ppermute | solution.py:20
  70.5 1.0 copy-start.4
  72.2 0.8 copy-start.2
  73.0 13.6 %collective-permute-start.6 = (bf16[128,1024]{1,0:T(8,128)(2,1)S(1)}, bf16[128,1024]{1,0:T(8,128)(2,1)S(1)}, u32[]{:S(2)}, u32[]{:S(2)}) collective-permute-start(bf16[128,1024]{1,0:T(8,128)(2,1)S(1)} %get-tuple-element.61), channel_id=1, source_target_pairs={{0,8},{8,0},{32,40},{40,32},{1,9},{9,1},{33,41},{41,33},{2,10},{10... | collective-permute-start | bytes 786440 | tf_op jit(solution)/shard_map/ppermute | solution.py:242
  76.1 14.4 %collective-permute-start.5 = (bf16[128,1024]{1,0:T(8,128)(2,1)S(1)}, bf16[128,1024]{1,0:T(8,128)(2,1)S(1)}, u32[]{:S(2)}, u32[]{:S(2)}) collective-permute-start(bf16[128,1024]{1,0:T(8,128)(2,1)S(1)} %get-tuple-element.62), channel_id=1, source_target_pairs={{0,32},{8,40},{32,0},{40,8},{1,33},{9,41},{33,1},{41,9},{2,34},{10... | collective-permute-start | bytes 786440 | tf_op jit(solution)/shard_map/ppermute | solution.py:242
  80.1 15.9 %collective-permute-start.7 = (bf16[128,1024]{1,0:T(8,128)(2,1)S(1)}, bf16[128,1024]{1,0:T(8,128)(2,1)S(1)}, u32[]{:S(2)}, u32[]{:S(2)}) collective-permute-start(bf16[128,1024]{1,0:T(8,128)(2,1)S(1)} %get-tuple-element.63), channel_id=1, source_target_pairs={{0,40},{8,32},{32,8},{40,0},{1,41},{9,33},{33,9},{41,1},{2,42},{10... | collective-permute-start | bytes 786440 | tf_op jit(solution)/shard_map/ppermute | solution.py:242
  83.5 1.1 copy-start.5
  84.5 20.6 %copy-start.3 = (f32[128,1024]{1,0:T(8,128)S(1)}, f32[128,1024]{1,0:T(8,128)}, u32[]{:S(2)}) copy-start(f32[128,1024]{1,0:T(8,128)} %copy-done.2) | copy-start | bytes 1572868
  96.0 41.7 %all-to-all-start.1 = ((bf16[32,8,1024]{2,1,0:T(8,128)(2,1)}), bf16[32,8,1024]{2,1,0:T(8,128)(2,1)}, u32[]{:S(2)}, u32[]{:S(2)}) async-start(bf16[32,8,1024]{2,1,0:T(8,128)(2,1)} %bitcast.7), calls=%async_computation.2 | async-start | bytes 1048576 | tf_op jit(solution)/shard_map/all_to_all | solution.py:247
  105.3 21.2 %collective-permute-start.8 = (bf16[16,1024]{1,0:T(8,128)(2,1)S(1)}, bf16[16,1024]{1,0:T(8,128)(2,1)S(1)}, u32[]{:S(2)}, u32[]{:S(2)}) collective-permute-start(bf16[16,1024]{1,0:T(8,128)(2,1)S(1)} %get-tuple-element.76), channel_id=1, source_target_pairs={{0,64},{64,128},{128,192},{192,256},{256,320},{320,384},{384,448},... | collective-permute-start | bytes 98312 | tf_op jit(solution)/shard_map/ppermute | solution.py:257
  108.7 23.3 %collective-permute-start.9 = (bf16[16,1024]{1,0:T(8,128)(2,1)S(1)}, bf16[16,1024]{1,0:T(8,128)(2,1)S(1)}, u32[]{:S(2)}, u32[]{:S(2)}) collective-permute-start(bf16[16,1024]{1,0:T(8,128)(2,1)S(1)} %get-tuple-element.77), channel_id=1, source_target_pairs={{0,128},{64,192},{128,256},{192,320},{256,384},{320,448},{384,0},{... | collective-permute-start | bytes 98312 | tf_op jit(solution)/shard_map/ppermute | solution.py:257
  112.9 22.3 %collective-permute-start.10 = (bf16[16,1024]{1,0:T(8,128)(2,1)S(1)}, bf16[16,1024]{1,0:T(8,128)(2,1)S(1)}, u32[]{:S(2)}, u32[]{:S(2)}) collective-permute-start(bf16[16,1024]{1,0:T(8,128)(2,1)S(1)} %get-tuple-element.78), channel_id=1, source_target_pairs={{0,192},{64,256},{128,320},{192,384},{256,448},{320,0},{384,64},{4... | collective-permute-start | bytes 98312 | tf_op jit(solution)/shard_map/ppermute | solution.py:257
  117.6 17.7 %collective-permute-start.11 = (bf16[16,1024]{1,0:T(8,128)(2,1)S(1)}, bf16[16,1024]{1,0:T(8,128)(2,1)S(1)}, u32[]{:S(2)}, u32[]{:S(2)}) collective-permute-start(bf16[16,1024]{1,0:T(8,128)(2,1)S(1)} %get-tuple-element.79), channel_id=1, source_target_pairs={{0,256},{64,320},{128,384},{192,448},{256,0},{320,64},{384,128},{4... | collective-permute-start | bytes 98312 | tf_op jit(solution)/shard_map/ppermute | solution.py:257
  121.8 13.5 %collective-permute-start.12 = (bf16[16,1024]{1,0:T(8,128)(2,1)S(1)}, bf16[16,1024]{1,0:T(8,128)(2,1)S(1)}, u32[]{:S(2)}, u32[]{:S(2)}) collective-permute-start(bf16[16,1024]{1,0:T(8,128)(2,1)S(1)} %get-tuple-element.80), channel_id=1, source_target_pairs={{0,320},{64,384},{128,448},{192,0},{256,64},{320,128},{384,192},{4... | collective-permute-start | bytes 98312 | tf_op jit(solution)/shard_map/ppermute | solution.py:257
  126.5 8.8 %collective-permute-start.13 = (bf16[16,1024]{1,0:T(8,128)(2,1)S(1)}, bf16[16,1024]{1,0:T(8,128)(2,1)S(1)}, u32[]{:S(2)}, u32[]{:S(2)}) collective-permute-start(bf16[16,1024]{1,0:T(8,128)(2,1)S(1)} %get-tuple-element.81), channel_id=1, source_target_pairs={{0,384},{64,448},{128,0},{192,64},{256,128},{320,192},{384,256},{4... | collective-permute-start | bytes 98312 | tf_op jit(solution)/shard_map/ppermute | solution.py:257
  131.9 5.8 %collective-permute-start.14 = (bf16[16,1024]{1,0:T(8,128)(2,1)S(1)}, bf16[16,1024]{1,0:T(8,128)(2,1)S(1)}, u32[]{:S(2)}, u32[]{:S(2)}) collective-permute-start(bf16[16,1024]{1,0:T(8,128)(2,1)S(1)} %get-tuple-element.82), channel_id=1, source_target_pairs={{0,448},{64,0},{128,64},{192,128},{256,192},{320,256},{384,320},{4... | collective-permute-start | bytes 98312 | tf_op jit(solution)/shard_map/ppermute | solution.py:257
  138.6 19.5 %all-to-all-start.2 = ((bf16[16,16,1024]{2,1,0:T(8,128)(2,1)}), bf16[16,16,1024]{2,1,0:T(8,128)(2,1)S(1)}, u32[]{:S(2)}, u32[]{:S(2)}) async-start(bf16[16,16,1024]{2,1,0:T(8,128)(2,1)} %shard_map.89), calls=%async_computation.3 | async-start | bytes 1048576 | tf_op jit(solution)/shard_map/all_to_all | solution.py:260
Sparse Core Ops, SparseCore 0:
  10.1 48.7 all-gather.1
  70.6 44.5 reduce-scatter.1

commit v5 on v4

--- a/solution.py
+++ b/solution.py
@@ -45,7 +45,7 @@
     share = half // (ny * nx * bx)
     place = jnp.arange(half, dtype=jnp.int32)
     within, rest = place % share, place // share
-    y, apart = (rest + lax.axis_index("wide_y")) % ny, rest // ny
+    y, apart = rest % ny, rest // ny
     x_wide = (apart // bx) ^ lax.axis_index("wide_x")
     x_blk = (apart % bx) ^ lax.axis_index("blk_x")
     feature = (((y * nx + x_wide) * 2 + core) * bx + x_blk) * share + within
@@ -136,7 +136,6 @@
         clip_kernel,
         out_shape=jax.ShapeDtypeStruct((slots, kept.shape[1]), BF16),
         compiler_params=ROOM,
-        cost_estimate=pl.CostEstimate(flops=2 * 10**10, bytes_accessed=2**20, transcendentals=0),
     )(kept, arrived, targets[None, :])
 
 
@@ -159,40 +158,34 @@
     )(own_picked, mate_picked, own_pre, mate_pre)
 
 
-def sum_kernel(count, *refs):
+def sum_kernel(*refs):
     total = refs[0][...].astype(F32)
-    for ref in refs[1:count]:
+    for ref in refs[1:-1]:
         total += ref[...].astype(F32)
-    share = refs[count].shape[0]
-    for s, out_ref in enumerate(refs[count:]):
-        out_ref[...] = total[s * share : (s + 1) * share].astype(out_ref.dtype)
-
-
-def sum_in_parts(arrays, parts):
-    rows, features = arrays[0].shape
-    return pl.pallas_call(
-        lambda *refs: sum_kernel(len(arrays), *refs),
-        out_shape=[
-            jax.ShapeDtypeStruct((rows // parts, features), F32 if s == 0 else BF16)
-            for s in range(parts)
-        ],
+    refs[-1][...] = total.astype(BF16)
+
+
+def sum_of(arrays):
+    return pl.pallas_call(
+        sum_kernel,
+        out_shape=jax.ShapeDtypeStruct(arrays[0].shape, BF16),
         compiler_params=ROOM,
     )(*arrays)
 
 
-def spread_kernel(count, *refs):
-    total = refs[0][...].astype(F32)
-    for ref in refs[1:count]:
-        total += ref[...].astype(F32)
-    refs[count][...] = jnp.broadcast_to(total.astype(BF16)[None], refs[count].shape)
-
-
-def sum_spread(arrays, copies):
-    return pl.pallas_call(
-        lambda *refs: spread_kernel(len(arrays), *refs),
-        out_shape=jax.ShapeDtypeStruct((copies, *arrays[0].shape), BF16),
-        compiler_params=ROOM,
-    )(*arrays)
+def spread_kernel(pieces_ref, out_ref):
+    total = pieces_ref[0].astype(F32)
+    for s in range(1, pieces_ref.shape[0]):
+        total += pieces_ref[s].astype(F32)
+    out_ref[...] = jnp.broadcast_to(total.astype(BF16)[None], out_ref.shape)
+
+
+def sum_spread(pieces, copies):
+    return pl.pallas_call(
+        spread_kernel,
+        out_shape=jax.ShapeDtypeStruct((copies, *pieces.shape[1:]), BF16),
+        compiler_params=ROOM,
+    )(pieces)
 
 
 def shards(audio, video, owner, clip_feats, lengths, proj_weight):
@@ -243,24 +236,20 @@
 
     arrived, parts = lax.optimization_barrier((arrived, parts))
     packed = clip_grads(kept, arrived, targets, slots)
-    packed, came = lax.optimization_barrier((packed, came))
     received = lax.all_to_all(
         packed.reshape(peers, capacity, features), WIDE, 0, 0, tiled=True
     ).reshape(slots, features)
 
     packed, came = lax.optimization_barrier((packed, came))
-    ny = lax.axis_size("wide_y")
-    parts = sum_in_parts(came, ny)
-    came = [parts[0]]
-    for s in range(1, ny):
-        pairs = [(at, (at + s) % ny) for at in range(ny)]
-        came.append(lax.ppermute(parts[s], "wide_y", pairs))
-    received, came = lax.optimization_barrier((received, came))
-    total = sum_spread(came, blocks)
-    gathered = lax.all_to_all(total, BLK, 0, 0, tiled=True)
+    summed, received = lax.optimization_barrier((sum_of(came), received))
+    pieces = lax.all_to_all(
+        summed.reshape(lax.axis_size("wide_y"), -1, features), "wide_y", 0, 0, tiled=True
+    )
     pre_grad = (received.astype(F32) * slope_own).astype(BF16)
     feats_grad = (dot_of(pre_grad, proj_weight, 1, 1) * length_scale).astype(BF16)
-    gathered, feats_grad = lax.optimization_barrier((gathered, feats_grad))
+    pieces, feats_grad = lax.optimization_barrier((pieces, feats_grad))
+    total = sum_spread(pieces, blocks)
+    gathered = lax.all_to_all(total, BLK, 0, 0, tiled=True)
     gathered = gathered.reshape(lax.axis_size("blk_x"), -1, *total.shape[1:])
     weight_grad = jnp.sum(gathered.astype(F32), axis=1).reshape(-1, features)
     return (audio_grad, feats_grad, weight_grad)

time: 167 us -> 160 us (0.958)
  starting transfers between devices: 79.4 us -> 48.4 us
  blocking collectives: 0 us -> 17.9 us
  waiting for transfers between devices: 43.2 us -> 51.8 us
  matrix products: 11.7 us -> 8.73 us
    ppermute x7 -> x0, starting transfers between devices: 29.9 us -> none  [shards(): came.append(lax.ppermute(parts[s], 'wide_y', pairs))]
    all_to_all x0 -> x1, blocking collectives: none -> 17.9 us  [shards(): gathered = lax.all_to_all(total, BLK, 0, 0, tiled=True)]
    ppermute x5, waiting for transfers between devices: 6.7 us -> 11.9 us  [swapped(): return lax.ppermute(array, axis, [(0, 1), (1, 0)])]
    ppermute x3, waiting for transfers between devices: 9.37 us -> 13.3 us  [shards(): came.append(lax.ppermute(parts[d], ('wide_x', 'blk_x'), pairs))]
    all_gather x1, waiting for transfers between devices: 2.05 us -> 5.09 us  [shards(): audio_line = lax.all_gather(audio, 'blk_z', axis=0, tiled=True)]
    dot_general x6, matrix products: 11.7 us -> 8.73 us  [dot_of(): lax.dot_general(matrix_a, matrix_b, (((dim_a,), (dim_b,)), ((), ())), pre...]
    ppermute x7 -> x0, waiting for transfers between devices: 2.43 us -> none  [shards(): came.append(lax.ppermute(parts[s], 'wide_y', pairs))]
    all_to_all x1, starting transfers between devices: 7.41 us -> 5.7 us  [shards(): lax.all_to_all(summed.reshape(lax.axis_size('wide_y'), -1, features), 'wi...]
  transfers between devices with their start and end apart: 20 -> 13, of which waited for: 7 -> 8; matrix products, arithmetic and copies ran while one was open for 9% -> 8% of each run, Pallas kernels for 2% -> 2%
where the time goes in v5:
time: 160 us; the launch traced here: 157 us
  waiting for transfers between devices  51.8 us (32%)
  starting transfers between devices  48.4 us (30%)
  blocking collectives  17.9 us (11%)
  between operations  14.3 us (9%)
  Pallas kernels  9.47 us (6%)
  matrix products  8.73 us (5%)
  other arithmetic  3.61 us (2%)
  local copies, waits for them, and re-layouts  3.02 us (2%)
    all_to_all x1, blocking collectives, shards(): gathered = lax.all_to_all(total, BLK, 0, 0, tiled=True)  17.9 us
    ppermute x3, waiting for transfers between devices, shards(): came.append(lax.ppermute(parts[d], ('wide_x', 'blk_x'), pairs))  13.3 us
    all_to_all x1, waiting for transfers between devices, shards(): lax.all_to_all(pooled.reshape(peers, capacity, features), WIDE, 0, 0, til...  12.7 us
    ppermute x5, starting transfers between devices, swapped(): return lax.ppermute(array, axis, [(0, 1), (1, 0)])  12.1 us
    ppermute x5, waiting for transfers between devices, swapped(): return lax.ppermute(array, axis, [(0, 1), (1, 0)])  11.9 us
    ppermute x3, starting transfers between devices, shards(): came.append(lax.ppermute(parts[d], ('wide_x', 'blk_x'), pairs))  10.4 us
    all_to_all x1, starting transfers between devices, shards(): lax.all_to_all(pooled.reshape(peers, capacity, features), WIDE, 0, 0, til...  10.2 us
    all_to_all x1, starting transfers between devices, shards(): lax.all_to_all(packed.reshape(peers, capacity, features), WIDE, 0, 0, til...  9.86 us
  transfers between devices with their start and end apart: 13, of which 8 were waited for; matrix products, arithmetic and copies ran while one was open for 8% of the time, Pallas kernels for 2%

profile of v5, /device:TPU:6, one launch (start us, length us, event | category | flops | bytes accessed | tf_op | source)
XLA Modules:
  0.0 157.2 jit_solution(14513515107548577661)
XLA Ops:
  7.2 0.0 copy-start
  7.2 0.0 copy-start.8
  7.2 0.0 all-gather.2.cloned.1.call-start
  7.2 0.7 all-gather.2.cloned.1.call-update
  7.9 0.7 convert_rsqrt_fusion
  8.7 2.0 %fusion.17 = bf16[32,8,1024]{2,1,0:T(8,128)(2,1)} fusion(f32[256]{0:T(256)S(1)} %convert_rsqrt_fusion, bf16[256,1024]{1,0:T(8,128)(2,1)} %param.9), kind=kLoop, calls=%fused_computation.27 | loop fusion | flops 786432 | bytes 1049600 | tf_op jit(solution)/shard_map/reshape | solution.py:204
  10.6 10.2 %all-to-all-start = ((bf16[32,8,1024]{2,1,0:T(8,128)(2,1)}), bf16[32,8,1024]{2,1,0:T(8,128)(2,1)S(1)}, u32[]{:S(2)}, u32[]{:S(2)}) async-start(bf16[32,8,1024]{2,1,0:T(8,128)(2,1)} %fusion.17), calls=%async_computation | async-start | bytes 1048576 | tf_op jit(solution)/shard_map/all_to_all | solution.py:203
  20.9 0.0 reduce-scatter.2.cloned.1.call-start
  20.9 2.7 %collective-permute-start = (bf16[128,1024]{1,0:T(8,128)(2,1)}, bf16[128,1024]{1,0:T(8,128)(2,1)}, u32[]{:S(2)}, u32[]{:S(2)}) collective-permute-start(bf16[128,1024]{1,0:T(8,128)(2,1)} %refs_2_.1), channel_id=1, source_target_pairs={{0,8},{8,0},{1,9},{9,1},{2,10},{10,2},{3,11},{11,3},{4,12},{12,4},... | collective-permute-start | bytes 786440 | tf_op jit(solution)/shard_map/ppermute | solution.py:20
  23.7 0.1 convert_reduce_fusion.1
  23.8 2.0 %fusion.10 = f32[256,1024]{1,0:T(8,128)} fusion(bf16[1024,1024]{1,0:T(8,128)(2,1)S(1)} %copy-done, bf16[256,1024]{1,0:T(8,128)(2,1)S(1)} %copy-done.8, f32[256]{0:T(256)S(1)} %convert_rsqrt_fusion), kind=kOutput, calls=%fused_computation.18 | convolution fusion | flops 539754496 | bytes 3671040 | tf_op jit(solution)/shard_map/dot_general | solution.py:24
  25.9 12.7 %all-to-all-done = bf16[32,8,1024]{2,1,0:T(8,128)(2,1)S(1)} async-done(((bf16[32,8,1024]{2,1,0:T(8,128)(2,1)}), bf16[32,8,1024]{2,1,0:T(8,128)(2,1)S(1)}, u32[]{:S(2)}, u32[]{:S(2)}) %all-to-all-start) | async-done | bytes 524320 | tf_op jit(solution)/shard_map/all_to_all | solution.py:203
  38.6 0.3 convolution_convert_fusion.2
  38.9 2.7 %collective-permute-start.1 = (bf16[128,1024]{1,0:T(8,128)(2,1)S(1)}, bf16[128,1024]{1,0:T(8,128)(2,1)S(1)}, u32[]{:S(2)}, u32[]{:S(2)}) collective-permute-start(bf16[128,1024]{1,0:T(8,128)(2,1)S(1)} %convolution_convert_fusion.2), channel_id=1, source_target_pairs={{0,8},{8,0},{1,9},{9,1},{2,10},{10,2},{3,11},{11,3},{4,12},{12,4},... | collective-permute-start | bytes 786440 | tf_op jit(solution)/shard_map/ppermute | solution.py:20
  41.6 6.6 %collective-permute-done.1 = bf16[128,1024]{1,0:T(8,128)(2,1)S(1)} collective-permute-done((bf16[128,1024]{1,0:T(8,128)(2,1)S(1)}, bf16[128,1024]{1,0:T(8,128)(2,1)S(1)}, u32[]{:S(2)}, u32[]{:S(2)}) %collective-permute-start.1) | collective-permute-done | bytes 262176 | tf_op jit(solution)/shard_map/ppermute | solution.py:20
  48.2 0.5 convolution_convert_fusion
  48.7 1.9 %collective-permute-start.2 = (bf16[512,256]{1,0:T(8,128)(2,1)S(1)}, bf16[512,256]{1,0:T(8,128)(2,1)S(1)}, u32[]{:S(2)}, u32[]{:S(2)}) collective-permute-start(bf16[512,256]{1,0:T(8,128)(2,1)S(1)} %convolution_convert_fusion), channel_id=1, source_target_pairs={{0,16},{16,0},{1,17},{17,1},{2,18},{18,2},{3,19},{19,3},{4,20},{20... | collective-permute-start | bytes 786440 | tf_op jit(solution)/shard_map/ppermute | solution.py:20
  50.7 2.0 %fusion.6.refs_4_ = f32[256,1024]{1,0:T(8,128)} fusion(bf16[1024,1024]{1,0:T(8,128)(2,1)S(1)} %copy-done, bf16[128,1024]{1,0:T(8,128)(2,1)S(1)} %collective-permute-done.1, bf16[128,1024]{1,0:T(8,128)(2,1)S(1)} %convolution_convert_fusion.2), kind=kOutput, calls=%fused_computation.14 | convolution fusion | flops 540016640 | bytes 3670016 | tf_op jit(solution)/shard_map/dot_general | solution.py:24
  52.6 1.2 convolution_convert_fusion.1.own_picked
  53.8 0.0 collective-permute-done.refs_3_
  53.8 0.0 collective-permute-done.2.mate_picked
  53.8 5.1 %all-gather.2.cloned.1.call-done.refs_1_ = bf16[1024,1024]{1,0:T(8,128)(2,1)} async-done(((bf16[128,1024]{1,0:T(8,128)(2,1)}), bf16[1024,1024]{1,0:T(8,128)(2,1)}) %all-gather.2.cloned.1.call-update) | async-done | bytes 2097168 | tf_op jit(solution)/shard_map/all_gather | solution.py:196
  58.9 6.7 %shard_map.85 = (f32[128,1024]{1,0:T(8,128)}, bf16[128,1024]{1,0:T(8,128)(2,1)}, bf16[256,1024]{1,0:T(8,128)(2,1)}, bf16[1024,1024]{1,0:T(8,128)(2,1)}) custom-call(s32[1]{0:T(128)} %bitcast.refs_0_, bf16[1024,1024]{1,0:T(8,128)(2,1)} %all-gather.2.cloned.1.call-done.refs_1_, bf16[128,1024]{1,0:T(8,128)(2,1)} %refs_2_.1, ...), custom_call_target="tpu_custom_call" | custom-call | flops 1610612736 | bytes 5242880 | tf_op jit(solution)/shard_map/pallas_call | solution.py:100
  65.7 0.0 copy-start.1
  65.7 0.0 reduce-scatter.2.cloned.1.call-update
  65.7 1.0 copy-done.2
  66.7 1.9 %collective-permute-start.4 = (bf16[256,1024]{1,0:T(8,128)(2,1)S(1)}, bf16[256,1024]{1,0:T(8,128)(2,1)S(1)}, u32[]{:S(2)}, u32[]{:S(2)}) collective-permute-start(bf16[256,1024]{1,0:T(8,128)(2,1)S(1)} %copy-done.2), channel_id=1, source_target_pairs={{0,16},{16,0},{1,17},{17,1},{2,18},{18,2},{3,19},{19,3},{4,20},{20... | collective-permute-start | bytes 1572872 | tf_op jit(solution)/shard_map/ppermute | solution.py:20
  68.6 2.8 %collective-permute-start.3 = (bf16[128,1024]{1,0:T(8,128)(2,1)}, bf16[128,1024]{1,0:T(8,128)(2,1)S(1)}, u32[]{:S(2)}, u32[]{:S(2)}) collective-permute-start(bf16[128,1024]{1,0:T(8,128)(2,1)} %get-tuple-element.32), channel_id=1, source_target_pairs={{0,8},{8,0},{1,9},{9,1},{2,10},{10,2},{3,11},{11,3},{4,12},{12,4},... | collective-permute-start | bytes 786440 | tf_op jit(solution)/shard_map/ppermute | solution.py:20
  71.4 1.0 copy-done.3
  72.4 0.9 copy-done.4
  73.4 0.7 shard_map.86
  74.1 5.3 %collective-permute-done.3.arrived_ref = bf16[128,1024]{1,0:T(8,128)(2,1)S(1)} collective-permute-done((bf16[128,1024]{1,0:T(8,128)(2,1)}, bf16[128,1024]{1,0:T(8,128)(2,1)S(1)}, u32[]{:S(2)}, u32[]{:S(2)}) %collective-permute-start.3) | collective-permute-done | bytes 262176 | tf_op jit(solution)/shard_map/ppermute | solution.py:20
  79.4 1.1 shard_map.87
  80.5 9.9 %all-to-all-start.1 = ((bf16[32,8,1024]{2,1,0:T(8,128)(2,1)}), bf16[32,8,1024]{2,1,0:T(8,128)(2,1)S(1)}, u32[]{:S(2)}, u32[]{:S(2)}) async-start(bf16[32,8,1024]{2,1,0:T(8,128)(2,1)} %bitcast.7), calls=%async_computation.2 | async-start | bytes 1048576 | tf_op jit(solution)/shard_map/all_to_all | solution.py:239
  90.4 2.8 %collective-permute-start.6 = (bf16[128,1024]{1,0:T(8,128)(2,1)}, bf16[128,1024]{1,0:T(8,128)(2,1)S(1)}, u32[]{:S(2)}, u32[]{:S(2)}) collective-permute-start(bf16[128,1024]{1,0:T(8,128)(2,1)} %copy-done.7), channel_id=1, source_target_pairs={{0,8},{8,0},{32,40},{40,32},{1,9},{9,1},{33,41},{41,33},{2,10},{10... | collective-permute-start | bytes 786440 | tf_op jit(solution)/shard_map/ppermute | solution.py:235
  93.2 2.7 %collective-permute-start.5 = (bf16[128,1024]{1,0:T(8,128)(2,1)}, bf16[128,1024]{1,0:T(8,128)(2,1)S(1)}, u32[]{:S(2)}, u32[]{:S(2)}) collective-permute-start(bf16[128,1024]{1,0:T(8,128)(2,1)} %copy-done.6), channel_id=1, source_target_pairs={{0,32},{8,40},{32,0},{40,8},{1,33},{9,41},{33,1},{41,9},{2,34},{10... | collective-permute-start | bytes 786440 | tf_op jit(solution)/shard_map/ppermute | solution.py:235
  95.9 4.9 %collective-permute-start.7 = (bf16[128,1024]{1,0:T(8,128)(2,1)}, bf16[128,1024]{1,0:T(8,128)(2,1)S(1)}, u32[]{:S(2)}, u32[]{:S(2)}) collective-permute-start(bf16[128,1024]{1,0:T(8,128)(2,1)} %copy-done.5), channel_id=1, source_target_pairs={{0,40},{8,32},{32,8},{40,0},{1,41},{9,33},{33,9},{41,1},{2,42},{10... | collective-permute-start | bytes 786440 | tf_op jit(solution)/shard_map/ppermute | solution.py:235
  100.9 5.2 %collective-permute-done.6.refs_2_ = bf16[128,1024]{1,0:T(8,128)(2,1)S(1)} collective-permute-done((bf16[128,1024]{1,0:T(8,128)(2,1)}, bf16[128,1024]{1,0:T(8,128)(2,1)S(1)}, u32[]{:S(2)}, u32[]{:S(2)}) %collective-permute-start.6) | collective-permute-done | bytes 262176 | tf_op jit(solution)/shard_map/ppermute | solution.py:235
  106.0 4.9 %collective-permute-done.5.refs_1_ = bf16[128,1024]{1,0:T(8,128)(2,1)S(1)} collective-permute-done((bf16[128,1024]{1,0:T(8,128)(2,1)}, bf16[128,1024]{1,0:T(8,128)(2,1)S(1)}, u32[]{:S(2)}, u32[]{:S(2)}) %collective-permute-start.5) | collective-permute-done | bytes 262176 | tf_op jit(solution)/shard_map/ppermute | solution.py:235
  110.9 3.3 %collective-permute-done.7.refs_3_ = bf16[128,1024]{1,0:T(8,128)(2,1)S(1)} collective-permute-done((bf16[128,1024]{1,0:T(8,128)(2,1)}, bf16[128,1024]{1,0:T(8,128)(2,1)S(1)}, u32[]{:S(2)}, u32[]{:S(2)}) %collective-permute-start.7) | collective-permute-done | bytes 262176 | tf_op jit(solution)/shard_map/ppermute | solution.py:235
  114.2 0.8 shard_map.88
  115.0 0.0 all-to-all-done.1
  115.0 5.7 %all-to-all-start.2 = ((bf16[8,16,1024]{2,1,0:T(8,128)(2,1)}), bf16[8,16,1024]{2,1,0:T(8,128)(2,1)S(1)}, u32[]{:S(2)}, u32[]{:S(2)}) async-start(bf16[8,16,1024]{2,1,0:T(8,128)(2,1)} %bitcast.9), calls=%async_computation.3 | async-start | bytes 524288 | tf_op jit(solution)/shard_map/all_to_all | solution.py:245
  120.7 2.8 %fusion.2 = bf16[256,1024]{1,0:T(8,128)(2,1)} fusion(bf16[1024,1024]{1,0:T(8,128)(2,1)S(1)} %copy-done, f32[256,1024]{1,0:T(8,128)} %fusion.10, bf16[256,1024]{1,0:T(8,128)(2,1)S(1)} %bitcast.26, f32[256]{0:T(256)S(1)} %convert_rsqrt_fusion), kind=kOutput, calls=%fused_computation.7 | convolution fusion | flops 538181632 | bytes 4195328 | tf_op jit(solution)/shard_map/dot_general | solution.py:24
  123.5 8.1 %all-to-all-done.2.pieces_ref = bf16[8,16,1024]{2,1,0:T(8,128)(2,1)S(1)} async-done(((bf16[8,16,1024]{2,1,0:T(8,128)(2,1)}), bf16[8,16,1024]{2,1,0:T(8,128)(2,1)S(1)}, u32[]{:S(2)}, u32[]{:S(2)}) %all-to-all-start.2) | async-done | bytes 262176 | tf_op jit(solution)/shard_map/all_to_all | solution.py:245
  131.7 0.1 shard_map.89
  131.7 17.9 %all_to_all.20 = bf16[16,16,1024]{2,1,0:T(8,128)(2,1)S(1)} all-to-all(bf16[16,16,1024]{2,1,0:T(8,128)(2,1)S(1)} %shard_map.89), channel_id=1, replica_groups=mesh['wide_y'=8,'wide_x'=2,'wide_c'=2,'blk_x'=2,'blk_z'=8] {'blk_x','blk..., dimensions={0} | all-to-all | bytes 1048576 | tf_op jit(solution)/shard_map/all_to_all | solution.py:252
  149.7 0.7 convert_reduce_fusion
  (20 shorter events, 0.1 us)
Async XLA Ops:
  7.2 16.7 %copy-start = (bf16[1024,1024]{1,0:T(8,128)(2,1)S(1)}, bf16[1024,1024]{1,0:T(8,128)(2,1)}, u32[]{:S(2)}) copy-start(bf16[1024,1024]{1,0:T(8,128)(2,1)} %param.11) | copy-start | bytes 6291460
  7.2 16.7 %copy-start.8 = (bf16[256,1024]{1,0:T(8,128)(2,1)S(1)}, bf16[256,1024]{1,0:T(8,128)(2,1)}, u32[]{:S(2)}) copy-start(bf16[256,1024]{1,0:T(8,128)(2,1)} %param.9) | copy-start | bytes 1572868
  7.2 16.5 %copy-start.9 = (s32[128,1]{0,1:T(1,128)S(1)}, s32[128,1]{0,1:T(1,128)}, u32[]{:S(2)}) copy-start(s32[128,1]{0,1:T(1,128)} %param.8) | copy-start | bytes 1540
  7.2 51.7 %all-gather.2.cloned.1.call-start = ((), (), s32[]{:S(2)}) async-start(), calls=%async_computation.5 | async-start | bytes 2359296 | tf_op jit(solution)/shard_map/all_gather | solution.py:196
  10.6 27.9 %all-to-all-start = ((bf16[32,8,1024]{2,1,0:T(8,128)(2,1)}), bf16[32,8,1024]{2,1,0:T(8,128)(2,1)S(1)}, u32[]{:S(2)}, u32[]{:S(2)}) async-start(bf16[32,8,1024]{2,1,0:T(8,128)(2,1)} %fusion.17), calls=%async_computation | async-start | bytes 1048576 | tf_op jit(solution)/shard_map/all_to_all | solution.py:203
  20.9 129.5 %reduce-scatter.2.cloned.1.call-start = ((), (), s32[]{:S(2)}) async-start(), calls=%async_computation.6 | async-start | bytes 2359296 | tf_op jit(solution)/shard_map/reduce_scatter | solution.py:227
  20.9 32.9 %collective-permute-start = (bf16[128,1024]{1,0:T(8,128)(2,1)}, bf16[128,1024]{1,0:T(8,128)(2,1)}, u32[]{:S(2)}, u32[]{:S(2)}) collective-permute-start(bf16[128,1024]{1,0:T(8,128)(2,1)} %refs_2_.1), channel_id=1, source_target_pairs={{0,8},{8,0},{1,9},{9,1},{2,10},{10,2},{3,11},{11,3},{4,12},{12,4},... | collective-permute-start | bytes 786440 | tf_op jit(solution)/shard_map/ppermute | solution.py:20
  38.9 9.4 %collective-permute-start.1 = (bf16[128,1024]{1,0:T(8,128)(2,1)S(1)}, bf16[128,1024]{1,0:T(8,128)(2,1)S(1)}, u32[]{:S(2)}, u32[]{:S(2)}) collective-permute-start(bf16[128,1024]{1,0:T(8,128)(2,1)S(1)} %convolution_convert_fusion.2), channel_id=1, source_target_pairs={{0,8},{8,0},{1,9},{9,1},{2,10},{10,2},{3,11},{11,3},{4,12},{12,4},... | collective-permute-start | bytes 786440 | tf_op jit(solution)/shard_map/ppermute | solution.py:20
  48.7 5.1 %collective-permute-start.2 = (bf16[512,256]{1,0:T(8,128)(2,1)S(1)}, bf16[512,256]{1,0:T(8,128)(2,1)S(1)}, u32[]{:S(2)}, u32[]{:S(2)}) collective-permute-start(bf16[512,256]{1,0:T(8,128)(2,1)S(1)} %convolution_convert_fusion), channel_id=1, source_target_pairs={{0,16},{16,0},{1,17},{17,1},{2,18},{18,2},{3,19},{19,3},{4,20},{20... | collective-permute-start | bytes 786440 | tf_op jit(solution)/shard_map/ppermute | solution.py:20
  65.6 1.0 copy-start.2
  65.7 13.8 %copy-start.1 = (f32[128,1024]{1,0:T(8,128)S(1)}, f32[128,1024]{1,0:T(8,128)}, u32[]{:S(2)}) copy-start(f32[128,1024]{1,0:T(8,128)} %get-tuple-element.31.kept_ref) | copy-start | bytes 1572868
  66.7 4.7 %collective-permute-start.4 = (bf16[256,1024]{1,0:T(8,128)(2,1)S(1)}, bf16[256,1024]{1,0:T(8,128)(2,1)S(1)}, u32[]{:S(2)}, u32[]{:S(2)}) collective-permute-start(bf16[256,1024]{1,0:T(8,128)(2,1)S(1)} %copy-done.2), channel_id=1, source_target_pairs={{0,16},{16,0},{1,17},{17,1},{2,18},{18,2},{3,19},{19,3},{4,20},{20... | collective-permute-start | bytes 1572872 | tf_op jit(solution)/shard_map/ppermute | solution.py:20
  68.6 10.8 %collective-permute-start.3 = (bf16[128,1024]{1,0:T(8,128)(2,1)}, bf16[128,1024]{1,0:T(8,128)(2,1)S(1)}, u32[]{:S(2)}, u32[]{:S(2)}) collective-permute-start(bf16[128,1024]{1,0:T(8,128)(2,1)} %get-tuple-element.32), channel_id=1, source_target_pairs={{0,8},{8,0},{1,9},{9,1},{2,10},{10,2},{3,11},{11,3},{4,12},{12,4},... | collective-permute-start | bytes 786440 | tf_op jit(solution)/shard_map/ppermute | solution.py:20
  71.4 1.0 copy-start.3
  72.4 0.9 copy-start.4
  74.1 6.4 %copy-start.5 = (bf16[128,1024]{1,0:T(8,128)(2,1)}, bf16[128,1024]{1,0:T(8,128)(2,1)S(1)}, u32[]{:S(2)}) copy-start(bf16[128,1024]{1,0:T(8,128)(2,1)S(1)} %get-tuple-element.39) | copy-start | bytes 786436
  74.1 6.4 %copy-start.6 = (bf16[128,1024]{1,0:T(8,128)(2,1)}, bf16[128,1024]{1,0:T(8,128)(2,1)S(1)}, u32[]{:S(2)}) copy-start(bf16[128,1024]{1,0:T(8,128)(2,1)S(1)} %get-tuple-element.38) | copy-start | bytes 786436
  74.1 6.4 %copy-start.7 = (bf16[128,1024]{1,0:T(8,128)(2,1)}, bf16[128,1024]{1,0:T(8,128)(2,1)S(1)}, u32[]{:S(2)}) copy-start(bf16[128,1024]{1,0:T(8,128)(2,1)S(1)} %get-tuple-element.37) | copy-start | bytes 786436
  80.5 34.5 %all-to-all-start.1 = ((bf16[32,8,1024]{2,1,0:T(8,128)(2,1)}), bf16[32,8,1024]{2,1,0:T(8,128)(2,1)S(1)}, u32[]{:S(2)}, u32[]{:S(2)}) async-start(bf16[32,8,1024]{2,1,0:T(8,128)(2,1)} %bitcast.7), calls=%async_computation.2 | async-start | bytes 1048576 | tf_op jit(solution)/shard_map/all_to_all | solution.py:239
  90.4 15.6 %collective-permute-start.6 = (bf16[128,1024]{1,0:T(8,128)(2,1)}, bf16[128,1024]{1,0:T(8,128)(2,1)S(1)}, u32[]{:S(2)}, u32[]{:S(2)}) collective-permute-start(bf16[128,1024]{1,0:T(8,128)(2,1)} %copy-done.7), channel_id=1, source_target_pairs={{0,8},{8,0},{32,40},{40,32},{1,9},{9,1},{33,41},{41,33},{2,10},{10... | collective-permute-start | bytes 786440 | tf_op jit(solution)/shard_map/ppermute | solution.py:235
  93.2 17.7 %collective-permute-start.5 = (bf16[128,1024]{1,0:T(8,128)(2,1)}, bf16[128,1024]{1,0:T(8,128)(2,1)S(1)}, u32[]{:S(2)}, u32[]{:S(2)}) collective-permute-start(bf16[128,1024]{1,0:T(8,128)(2,1)} %copy-done.6), channel_id=1, source_target_pairs={{0,32},{8,40},{32,0},{40,8},{1,33},{9,41},{33,1},{41,9},{2,34},{10... | collective-permute-start | bytes 786440 | tf_op jit(solution)/shard_map/ppermute | solution.py:235
  95.9 18.2 %collective-permute-start.7 = (bf16[128,1024]{1,0:T(8,128)(2,1)}, bf16[128,1024]{1,0:T(8,128)(2,1)S(1)}, u32[]{:S(2)}, u32[]{:S(2)}) collective-permute-start(bf16[128,1024]{1,0:T(8,128)(2,1)} %copy-done.5), channel_id=1, source_target_pairs={{0,40},{8,32},{32,8},{40,0},{1,41},{9,33},{33,9},{41,1},{2,42},{10... | collective-permute-start | bytes 786440 | tf_op jit(solution)/shard_map/ppermute | solution.py:235
  115.0 16.7 %all-to-all-start.2 = ((bf16[8,16,1024]{2,1,0:T(8,128)(2,1)}), bf16[8,16,1024]{2,1,0:T(8,128)(2,1)S(1)}, u32[]{:S(2)}, u32[]{:S(2)}) async-start(bf16[8,16,1024]{2,1,0:T(8,128)(2,1)} %bitcast.9), calls=%async_computation.3 | async-start | bytes 524288 | tf_op jit(solution)/shard_map/all_to_all | solution.py:245
Sparse Core Ops, SparseCore 0:
  10.1 48.7 all-gather.1
  65.8 44.3 reduce-scatter.1

commit v6 on v5

v6 whole, which is shorter than its diff:
```python
import jax
import jax.numpy as jnp
from jax import lax
from jax.experimental import pallas as pl
from jax.experimental.pallas import tpu as pltpu
from jax.sharding import Mesh
from jax.sharding import PartitionSpec as P

AXES = ("wide_y", "wide_x", "wide_c", "blk_x", "blk_z")
WIDE = ("wide_y", "wide_x", "wide_c")
BLK = ("blk_x", "blk_z")
BF16 = jnp.bfloat16
F32 = jnp.float32
ROOM = pltpu.CompilerParams(vmem_limit_bytes=56 * 2**20)
SCALAR = pl.BlockSpec(memory_space=pltpu.SMEM)


def swapped(array, axis):
    return lax.ppermute(array, axis, [(0, 1), (1, 0)])


def dot_of(matrix_a, matrix_b, dim_a, dim_b):
    return lax.dot_general(
        matrix_a, matrix_b, (((dim_a,), (dim_b,)), ((), ())), preferred_element_type=F32
    )


def gelu_slope(v):
    cdf = 0.5 * (1.0 + lax.erf(v * 0.7071067811865476))
    return cdf + v * (0.3989422804014327 * jnp.exp(-0.5 * v * v))


def ranks_of(peer):
    ids = jnp.arange(peer.shape[0], dtype=jnp.int32)
    before = (peer[:, None] == peer[None, :]) & (ids[:, None] < ids[None, :])
    return jnp.sum(before.astype(jnp.int32), axis=0)


def order_of(slots, capacity):
    ny = lax.axis_size("wide_y")
    slot = jnp.arange(slots, dtype=jnp.int32)
    rank, source = slot % capacity, slot // capacity
    core = (source % 2) ^ lax.axis_index("wide_c")
    x = (source // 2 % 2) ^ lax.axis_index("wide_x")
    return ((source // 4 * 2 + core) * 2 + x) * capacity + rank


def picking_of(core, feature_count):
    half = feature_count // 2
    ny, nx = lax.axis_size("wide_y"), lax.axis_size("wide_x")
    bx = lax.axis_size("blk_x")
    share = half // (ny * nx * bx)
    place = jnp.arange(half, dtype=jnp.int32)
    within, rest = place % share, place // share
    y, x = rest % ny, rest // ny
    feature = (((y * nx + x // bx) * 2 + core) * bx + x % bx) * share + within
    return (jnp.arange(feature_count, dtype=jnp.int32)[:, None] == feature[None, :]).astype(BF16)


def pair_kernel(factor, steps, place_ref, line_hbm, own_hbm, mate_hbm, slope_hbm,
                kept_ref, sent_ref, pre_ref, coeffs_ref, line, video, slope, came):
    rows, clips = line.shape[0] // steps, own_hbm.shape[0]
    loads = [
        pltpu.make_async_copy(own_hbm, video.at[pl.ds(0, clips)], came.at[0]),
        pltpu.make_async_copy(mate_hbm, video.at[pl.ds(clips, clips)], came.at[1]),
    ]
    for step in range(steps):
        block = pl.ds(step * rows, rows)
        loads.append(pltpu.make_async_copy(line_hbm.at[block], line.at[block], came.at[2 + step]))
    loads.append(pltpu.make_async_copy(slope_hbm, slope, came.at[2 + steps]))
    for load in loads:
        load.start()
    loads[0].wait()
    loads[1].wait()
    for step in range(steps):
        block = pl.ds(step * rows, rows)
        loads[2 + step].wait()
        scores = dot_of(video[...], line[block], 1, 1)
        row = lax.broadcasted_iota(jnp.int32, scores.shape, 0)
        col = lax.broadcasted_iota(jnp.int32, scores.shape, 1) + step * rows
        labels = ((col == place_ref[0] * clips + row) & (row < clips)).astype(F32)
        coeffs = factor * (jax.nn.sigmoid(4.0 * scores - 2.0) - labels)
        coeffs_ref[:, block] = coeffs.astype(BF16)
    loads[-1].wait()
    total = dot_of(coeffs_ref[...], line[...], 1, 0)
    kept_ref[...] = total[:clips]
    sent_ref[...] = total[clips:].astype(BF16)
    pre_ref[...] = (total * slope[...]).astype(BF16)


def pair_grads(line, own, mate, slope, place, factor, steps):
    rows, features = line.shape
    clips = own.shape[0]
    free = pl.BlockSpec(memory_space=pl.ANY)
    return pl.pallas_call(
        lambda *refs: pair_kernel(factor, steps, *refs),
        in_specs=[SCALAR, free, free, free, free],
        out_shape=[
            jax.ShapeDtypeStruct((clips, features), F32),
            jax.ShapeDtypeStruct((clips, features), BF16),
            jax.ShapeDtypeStruct((2 * clips, features), BF16),
            jax.ShapeDtypeStruct((2 * clips, rows), BF16),
        ],
        scratch_shapes=[
            pltpu.VMEM((rows, features), BF16),
            pltpu.VMEM((2 * clips, features), BF16),
            pltpu.VMEM((2 * clips, features), F32),
            pltpu.SemaphoreType.DMA((3 + steps,)),
        ],
        compiler_params=ROOM,
        cost_estimate=pl.CostEstimate(
            flops=8 * rows * clips * features, bytes_accessed=3 * rows * features, transcendentals=0
        ),
    )(place, line, own, mate, slope)


def line_kernel(coeffs_ref, own_ref, mate_ref, out_ref):
    clips = own_ref.shape[0]
    total = dot_of(coeffs_ref[:clips], own_ref[...], 0, 0)
    total += dot_of(coeffs_ref[clips:], mate_ref[...], 0, 0)
    out_ref[...] = total.astype(BF16)


def line_grads_of(coeffs, own, mate, steps):
    pairs, rows = coeffs.shape
    clips, features = own.shape
    whole = pl.BlockSpec((clips, features), lambda i: (0, 0))
    return pl.pallas_call(
        line_kernel,
        grid=(steps,),
        in_specs=[pl.BlockSpec((pairs, rows // steps), lambda i: (0, i)), whole, whole],
        out_specs=pl.BlockSpec((rows // steps, features), lambda i: (i, 0)),
        out_shape=jax.ShapeDtypeStruct((rows, features), BF16),
        compiler_params=ROOM,
        cost_estimate=pl.CostEstimate(
            flops=4 * rows * clips * features, bytes_accessed=3 * rows * features, transcendentals=0
        ),
    )(coeffs, own, mate)


def clip_kernel(kept_ref, arrived_ref, place_ref, stay_ref, core_ref):
    grad = (kept_ref[...] + arrived_ref[...].astype(F32)).astype(BF16)
    slots, clips = stay_ref.shape[0], grad.shape[0]
    slot = lax.broadcasted_iota(jnp.int32, (slots, clips), 0)
    stay_ref[...] = dot_of((slot == place_ref[...]).astype(BF16), grad, 1, 0).astype(BF16)
    core_ref[...] = dot_of((slot + slots == place_ref[...]).astype(BF16), grad, 1, 0).astype(BF16)


def clip_grads(kept, arrived, places, slots):
    shape = jax.ShapeDtypeStruct((slots // 2, kept.shape[1]), BF16)
    return pl.pallas_call(
        clip_kernel,
        out_shape=[shape, shape],
        compiler_params=ROOM,
    )(kept, arrived, places[None, :])


def weight_kernel(own_picked, mate_picked, own_pre, mate_pre, out_ref):
    product = dot_of(own_picked[...], own_pre[...], 1, 0)
    product += dot_of(mate_picked[...], mate_pre[...], 1, 0)
    out_ref[...] = product.astype(BF16)


def weight_part(own_picked, mate_picked, own_pre, mate_pre):
    return pl.pallas_call(
        weight_kernel,
        out_shape=jax.ShapeDtypeStruct((own_picked.shape[0], own_pre.shape[1]), BF16),
        compiler_params=ROOM,
    )(own_picked, mate_picked, own_pre, mate_pre)


def load_kernel(stay_ref, core_ref, x_ref, pieces_ref, out_ref):
    count, lines, features = out_ref.shape
    part = x_ref.shape[0] // 2
    cells = part // count

    def by_y(ref, at):
        return ref[pl.ds(at, part)].astype(F32).reshape(count, cells, features)

    first = jnp.concatenate([by_y(stay_ref, 0), by_y(x_ref, 0)], axis=1)
    out_ref[:, pl.ds(0, 2 * cells)] = first.astype(BF16)
    second = jnp.concatenate([by_y(core_ref, 0), by_y(x_ref, part)], axis=1)
    out_ref[:, pl.ds(2 * cells, 2 * cells)] = second.astype(BF16)
    total = pieces_ref[0].astype(F32)
    for s in range(1, pieces_ref.shape[0]):
        total += pieces_ref[s].astype(F32)
    rows = lines - 4 * cells
    out_ref[:, pl.ds(4 * cells, rows)] = total.reshape(count, rows, features).astype(BF16)


def load_of(stay, core_in, x_in, pieces, count):
    lines = (2 * stay.shape[0] + pieces.shape[1]) // count
    return pl.pallas_call(
        load_kernel,
        out_shape=jax.ShapeDtypeStruct((count, lines, stay.shape[1]), BF16),
        compiler_params=ROOM,
    )(stay, core_in, x_in, pieces)


def spread_kernel(pieces_ref, out_ref):
    total = pieces_ref[0].astype(F32)
    for s in range(1, pieces_ref.shape[0]):
        total += pieces_ref[s].astype(F32)
    out_ref[...] = jnp.broadcast_to(total.astype(BF16)[None], out_ref.shape)


def sum_spread(pieces, rows, copies):
    count, lines, features = pieces.shape
    return pl.pallas_call(
        spread_kernel,
        grid=(1,),
        in_specs=[pl.BlockSpec((count, rows, features), lambda i: (0, lines // rows - 1, 0))],
        out_specs=pl.BlockSpec((copies, rows, features), lambda i: (0, 0, 0)),
        out_shape=jax.ShapeDtypeStruct((copies, rows, features), BF16),
        compiler_params=ROOM,
    )(pieces)


def shards(audio, video, owner, clip_feats, lengths, proj_weight):
    clips, features = audio.shape
    blocks = lax.axis_size(BLK)
    core = lax.axis_index("wide_c")
    place = lax.axis_index("blk_z").astype(jnp.int32)[None]
    audio_line = lax.all_gather(audio, "blk_z", axis=0, tiled=True)

    peers = lax.axis_size(WIDE)
    slots = clip_feats.shape[0]
    capacity = slots // peers
    length_scale = lax.rsqrt(lengths.astype(F32))[:, None]
    pooled = (clip_feats.astype(F32) * length_scale).astype(BF16)
    pooled_slots = lax.all_to_all(
        pooled.reshape(peers, capacity, features), WIDE, 0, 0, tiled=True
    ).reshape(slots, features)
    video_mate = swapped(video, "blk_x")
    slope_own = gelu_slope(dot_of(pooled, proj_weight, 1, 0))

    peer = owner[:, 0]
    ranks = ranks_of(peer)
    slot_of = peer * capacity + ranks
    placing = (slot_of[:, None] == jnp.arange(slots, dtype=jnp.int32)[None, :]).astype(BF16)
    ny = lax.axis_size("wide_y")
    core_apart = (peer % 2) ^ core
    x_apart = (peer // 2 % 2) ^ lax.axis_index("wide_x")
    places = ((core_apart * 2 + x_apart) * ny + peer // 4) * capacity + ranks
    clip_rows = dot_of(placing, pooled_slots, 1, 0).astype(BF16)
    row_pair = jnp.concatenate([clip_rows, swapped(clip_rows, "blk_x")])
    slope_pair = gelu_slope(dot_of(row_pair, proj_weight, 1, 0))
    picked = dot_of(picking_of(core, features), row_pair, 0, 1).astype(BF16)
    picked_mate = swapped(
        dot_of(picking_of(1 - core, features), row_pair, 0, 1).astype(BF16), "wide_c"
    )
    audio_line, video_mate, slope_pair, picked, picked_mate, slope_own, places = (
        lax.optimization_barrier(
            (audio_line, video_mate, slope_pair, picked, picked_mate, slope_own, places)
        )
    )

    kept, sent, pre_pair, coeffs = pair_grads(
        audio_line, video, video_mate, slope_pair, place, 4.0 / blocks, 4
    )

    pre_mate = swapped(pre_pair, "wide_c")
    arrived = swapped(sent, "blk_x")
    weight_sum = weight_part(picked, picked_mate, pre_pair, pre_mate)
    pieces = lax.all_to_all(
        weight_sum.reshape(4, -1, features), ("wide_x", "blk_x"), 0, 0, tiled=True
    )

    arrived, weight_sum = lax.optimization_barrier((arrived, weight_sum))
    stay, core_out = clip_grads(kept, arrived, places, slots)
    core_in = swapped(core_out, "wide_c")

    coeffs, core_in = lax.optimization_barrier((coeffs, core_in))
    line_grads = line_grads_of(coeffs, video, video_mate, 4)
    audio_grad = lax.psum_scatter(line_grads, "blk_z", scatter_dimension=0, tiled=True)

    part = slots // 4
    x_in = swapped(jnp.concatenate([stay[part:], core_in[part:]]), "wide_x")
    rows = pieces.shape[1] // ny
    load = load_of(stay, core_in, x_in, pieces, ny)
    load = lax.all_to_all(load, "wide_y", 0, 0, tiled=True)
    total = sum_spread(load, rows, blocks)
    gathered = lax.all_to_all(total, BLK, 0, 0, tiled=True)
    order = order_of(slots, capacity)
    sorting = (order[:, None] == jnp.arange(slots, dtype=jnp.int32)[None, :]).astype(BF16)
    received = dot_of(sorting, load[:, :-rows].reshape(slots, features), 1, 0)
    pre_grad = (received * slope_own).astype(BF16)
    feats_grad = (dot_of(pre_grad, proj_weight, 1, 1) * length_scale).astype(BF16)
    gathered, feats_grad = lax.optimization_barrier((gathered, feats_grad))
    gathered = gathered.reshape(lax.axis_size("blk_x"), -1, *total.shape[1:])
    weight_grad = jnp.sum(gathered.astype(F32), axis=1).reshape(-1, features)
    return (audio_grad, feats_grad, weight_grad)


def solution(mesh):
    finer = Mesh(mesh.devices.reshape(8, 2, 2, 2, 8), AXES)
    rows = P(AXES, None)
    return jax.shard_map(
        shards,
        mesh=finer,
        in_specs=(rows, rows, rows, rows, P(AXES), P()),
        out_specs=(rows, rows, P(WIDE, None)),
        check_vma=False,
    )
```

time: 160 us -> 174 us (1.087)
  blocking collectives: 17.9 us -> 29.1 us
  starting transfers between devices: 48.4 us -> 38.6 us
  Pallas kernels: 9.47 us -> 19 us
  waiting for transfers between devices: 51.8 us -> 54 us
    ppermute x5 -> x7, waiting for transfers between devices: 11.9 us -> 26.8 us  [swapped(): return lax.ppermute(array, axis, [(0, 1), (1, 0)])]
    ppermute x3 -> x0, waiting for transfers between devices: 13.3 us -> none  [shards(): came.append(lax.ppermute(parts[d], ('wide_x', 'blk_x'), pairs))]
    pallas_call x4 -> x5, Pallas kernels: 2.73 us -> 14.2 us  [the longest x1 4.55 us: line_grads_of(): pl.pallas_call(line_kernel, grid=(steps,), in_specs=[pl.BlockSpec((pairs,...]
    all_to_all x1, blocking collectives: 17.9 us -> 29.1 us  [shards(): load = lax.all_to_all(load, 'wide_y', 0, 0, tiled=True)]
    ppermute x3 -> x0, starting transfers between devices: 10.4 us -> none  [shards(): came.append(lax.ppermute(parts[d], ('wide_x', 'blk_x'), pairs))]
    ppermute x5 -> x7, starting transfers between devices: 12.1 us -> 17.4 us  [swapped(): return lax.ppermute(array, axis, [(0, 1), (1, 0)])]
    all_to_all x2, starting transfers between devices: 15.6 us -> 11 us  [the longest x1 6.03 us: shards(): gathered = lax.all_to_all(total, BLK, 0, 0, tiled=True)]
    pallas_call x1, Pallas kernels: 6.75 us -> 4.87 us  [pair_grads(): pl.pallas_call(lambda *refs: pair_kernel(factor, steps, *refs), in_specs=...]
  transfers between devices with their start and end apart: 13 -> 12, of which waited for: 8 -> 7; matrix products, arithmetic and copies ran while one was open for 8% -> 8% of each run, Pallas kernels for 2% -> 4%
where the time goes in v6:
time: 174 us; the launch traced here: 172 us
  waiting for transfers between devices  54 us (31%)
  starting transfers between devices  38.6 us (22%)
  blocking collectives  29.1 us (17%)
  Pallas kernels  19 us (11%)
  between operations  14.3 us (8%)
  matrix products  8.81 us (5%)
  other arithmetic  4.25 us (2%)
  local copies, waits for them, and re-layouts  4.14 us (2%)
    all_to_all x1, blocking collectives, shards(): load = lax.all_to_all(load, 'wide_y', 0, 0, tiled=True)  29.1 us
    ppermute x7, waiting for transfers between devices, swapped(): return lax.ppermute(array, axis, [(0, 1), (1, 0)])  26.8 us
    ppermute x7, starting transfers between devices, swapped(): return lax.ppermute(array, axis, [(0, 1), (1, 0)])  17.4 us
    all_to_all x1, waiting for transfers between devices, shards(): lax.all_to_all(pooled.reshape(peers, capacity, features), WIDE, 0, 0, til...  12.7 us
    all_to_all x1, starting transfers between devices, shards(): lax.all_to_all(pooled.reshape(peers, capacity, features), WIDE, 0, 0, til...  10.2 us
    dot_general x6, matrix products, dot_of(): lax.dot_general(matrix_a, matrix_b, (((dim_a,), (dim_b,)), ((), ())), pre...  8.81 us
    all_to_all x1, waiting for transfers between devices, shards(): gathered = lax.all_to_all(total, BLK, 0, 0, tiled=True)  8.73 us
    all_to_all x1, starting transfers between devices, shards(): gathered = lax.all_to_all(total, BLK, 0, 0, tiled=True)  6.03 us
  transfers between devices with their start and end apart: 12, of which 7 were waited for; matrix products, arithmetic and copies ran while one was open for 8% of the time, Pallas kernels for 4%

profile of v6, /device:TPU:6, one launch (start us, length us, event | category | flops | bytes accessed | tf_op | source)
XLA Modules:
  0.0 172.2 jit_solution(9890713646341395957)
XLA Ops:
  7.2 0.0 copy-start
  7.2 0.0 copy-start.4
  7.2 0.0 copy-start.5
  7.2 0.0 all-gather.2.cloned.1.call-start
  7.3 0.7 all-gather.2.cloned.1.call-update
  7.9 0.8 convert_rsqrt_fusion
  8.7 2.0 %fusion.18 = bf16[32,8,1024]{2,1,0:T(8,128)(2,1)} fusion(f32[256]{0:T(256)S(1)} %convert_rsqrt_fusion, bf16[256,1024]{1,0:T(8,128)(2,1)} %param.9), kind=kLoop, calls=%fused_computation.30 | loop fusion | flops 786432 | bytes 1049600 | tf_op jit(solution)/shard_map/reshape | solution.py:232
  10.7 10.2 %all-to-all-start = ((bf16[32,8,1024]{2,1,0:T(8,128)(2,1)}), bf16[32,8,1024]{2,1,0:T(8,128)(2,1)S(1)}, u32[]{:S(2)}, u32[]{:S(2)}) async-start(bf16[32,8,1024]{2,1,0:T(8,128)(2,1)} %fusion.18), calls=%async_computation | async-start | bytes 1048576 | tf_op jit(solution)/shard_map/all_to_all | solution.py:231
  21.0 0.0 reduce-scatter.2.cloned.1.call-start
  21.0 2.7 %collective-permute-start = (bf16[128,1024]{1,0:T(8,128)(2,1)S(1)}, bf16[128,1024]{1,0:T(8,128)(2,1)}, u32[]{:S(2)}, u32[]{:S(2)}) collective-permute-start(bf16[128,1024]{1,0:T(8,128)(2,1)S(1)} %copy-done.5), channel_id=1, source_target_pairs={{0,8},{8,0},{1,9},{9,1},{2,10},{10,2},{3,11},{11,3},{4,12},{12,4},... | collective-permute-start | bytes 786440 | tf_op jit(solution)/shard_map/ppermute | solution.py:19
  23.8 0.1 convert_reduce_fusion.1
  23.9 2.0 %fusion.11 = f32[256,1024]{1,0:T(8,128)} fusion(bf16[1024,1024]{1,0:T(8,128)(2,1)S(1)} %copy-done, bf16[256,1024]{1,0:T(8,128)(2,1)S(1)} %copy-done.4, f32[256]{0:T(256)S(1)} %convert_rsqrt_fusion), kind=kOutput, calls=%fused_computation.20 | convolution fusion | flops 539754496 | bytes 3671040 | tf_op jit(solution)/shard_map/dot_general | solution.py:23
  25.9 12.7 %all-to-all-done = bf16[32,8,1024]{2,1,0:T(8,128)(2,1)S(1)} async-done(((bf16[32,8,1024]{2,1,0:T(8,128)(2,1)}), bf16[32,8,1024]{2,1,0:T(8,128)(2,1)S(1)}, u32[]{:S(2)}, u32[]{:S(2)}) %all-to-all-start) | async-done | bytes 524320 | tf_op jit(solution)/shard_map/all_to_all | solution.py:231
  38.7 0.3 convolution_convert_fusion.2
  38.9 2.7 %collective-permute-start.1 = (bf16[128,1024]{1,0:T(8,128)(2,1)S(1)}, bf16[128,1024]{1,0:T(8,128)(2,1)S(1)}, u32[]{:S(2)}, u32[]{:S(2)}) collective-permute-start(bf16[128,1024]{1,0:T(8,128)(2,1)S(1)} %convolution_convert_fusion.2), channel_id=1, source_target_pairs={{0,8},{8,0},{1,9},{9,1},{2,10},{10,2},{3,11},{11,3},{4,12},{12,4},... | collective-permute-start | bytes 786440 | tf_op jit(solution)/shard_map/ppermute | solution.py:19
  41.7 0.5 multiply_add_fusion.2
  42.3 6.1 %collective-permute-done.1 = bf16[128,1024]{1,0:T(8,128)(2,1)S(1)} collective-permute-done((bf16[128,1024]{1,0:T(8,128)(2,1)S(1)}, bf16[128,1024]{1,0:T(8,128)(2,1)S(1)}, u32[]{:S(2)}, u32[]{:S(2)}) %collective-permute-start.1) | collective-permute-done | bytes 262176 | tf_op jit(solution)/shard_map/ppermute | solution.py:19
  48.3 0.5 convolution_convert_fusion
  48.8 1.9 %collective-permute-start.2 = (bf16[512,256]{1,0:T(8,128)(2,1)S(1)}, bf16[512,256]{1,0:T(8,128)(2,1)S(1)}, u32[]{:S(2)}, u32[]{:S(2)}) collective-permute-start(bf16[512,256]{1,0:T(8,128)(2,1)S(1)} %convolution_convert_fusion), channel_id=1, source_target_pairs={{0,16},{16,0},{1,17},{17,1},{2,18},{18,2},{3,19},{19,3},{4,20},{20... | collective-permute-start | bytes 786440 | tf_op jit(solution)/shard_map/ppermute | solution.py:19
  50.7 1.9 %fusion.7.refs_4_ = f32[256,1024]{1,0:T(8,128)} fusion(bf16[1024,1024]{1,0:T(8,128)(2,1)S(1)} %copy-done, bf16[128,1024]{1,0:T(8,128)(2,1)S(1)} %collective-permute-done.1, bf16[128,1024]{1,0:T(8,128)(2,1)S(1)} %convolution_convert_fusion.2), kind=kOutput, calls=%fused_computation.16 | convolution fusion | flops 540016640 | bytes 3670016 | tf_op jit(solution)/shard_map/dot_general | solution.py:23
  52.7 1.2 convolution_convert_fusion.1.own_picked
  53.9 0.0 collective-permute-done.2.mate_picked
  53.9 5.0 %all-gather.2.cloned.1.call-done.refs_1_ = bf16[1024,1024]{1,0:T(8,128)(2,1)} async-done(((bf16[128,1024]{1,0:T(8,128)(2,1)}), bf16[1024,1024]{1,0:T(8,128)(2,1)}) %all-gather.2.cloned.1.call-update) | async-done | bytes 2097168 | tf_op jit(solution)/shard_map/all_gather | solution.py:224
  58.9 4.9 %shard_map.85 = (f32[128,1024]{1,0:T(8,128)}, bf16[128,1024]{1,0:T(8,128)(2,1)}, bf16[256,1024]{1,0:T(8,128)(2,1)}, bf16[256,1024]{1,0:T(8,128)(2,1)}) custom-call(s32[1]{0:T(128)} %bitcast.refs_0_, bf16[1024,1024]{1,0:T(8,128)(2,1)} %all-gather.2.cloned.1.call-done.refs_1_, bf16[128,1024]{1,0:T(8,128)(2,1)} %own_ref.1, ...), custom_call_target="tpu_custom_call" | custom-call | flops 1073741824 | bytes 3145728 | tf_op jit(solution)/shard_map/pallas_call | solution.py:95
  63.8 1.9 %collective-permute-start.4 = (bf16[256,1024]{1,0:T(8,128)(2,1)}, bf16[256,1024]{1,0:T(8,128)(2,1)S(1)}, u32[]{:S(2)}, u32[]{:S(2)}) collective-permute-start(bf16[256,1024]{1,0:T(8,128)(2,1)} %get-tuple-element.29.own_pre), channel_id=1, source_target_pairs={{0,16},{16,0},{1,17},{17,1},{2,18},{18,2},{3,19},{19,3},{4,20},{20... | collective-permute-start | bytes 1572872 | tf_op jit(solution)/shard_map/ppermute | solution.py:19
  65.7 2.8 %collective-permute-start.3 = (bf16[128,1024]{1,0:T(8,128)(2,1)}, bf16[128,1024]{1,0:T(8,128)(2,1)S(1)}, u32[]{:S(2)}, u32[]{:S(2)}) collective-permute-start(bf16[128,1024]{1,0:T(8,128)(2,1)} %get-tuple-element.26), channel_id=1, source_target_pairs={{0,8},{8,0},{1,9},{9,1},{2,10},{10,2},{3,11},{11,3},{4,12},{12,4},... | collective-permute-start | bytes 786440 | tf_op jit(solution)/shard_map/ppermute | solution.py:19
  68.5 0.8 copy-done.3
  69.3 3.0 %shard_map.86 = bf16[512,1024]{1,0:T(8,128)(2,1)} custom-call(bf16[512,256]{1,0:T(8,128)(2,1)} %convolution_convert_fusion.1.own_picked, bf16[512,256]{1,0:T(8,128)(2,1)} %copy-done.6, bf16[256,1024]{1,0:T(8,128)(2,1)} %get-tuple-element.29.own_pre, bf16[256,1024]{1,0:T(8,128)(2,1)} %copy-done.3), custom_call_target="tpu_custom_call" | custom-call | tf_op jit(solution)/shard_map/pallas_call | solution.py:165
  72.3 4.2 %collective-permute-done.3.arrived_ref = bf16[128,1024]{1,0:T(8,128)(2,1)S(1)} collective-permute-done((bf16[128,1024]{1,0:T(8,128)(2,1)}, bf16[128,1024]{1,0:T(8,128)(2,1)S(1)}, u32[]{:S(2)}, u32[]{:S(2)}) %collective-permute-start.3) | collective-permute-done | bytes 262176 | tf_op jit(solution)/shard_map/ppermute | solution.py:19
  76.5 0.7 copy-done.8
  77.2 2.2 %shard_map.87 = (bf16[128,1024]{1,0:T(8,128)(2,1)}, bf16[128,1024]{1,0:T(8,128)(2,1)}) custom-call(f32[128,1024]{1,0:T(8,128)} %get-tuple-element.25.kept_ref, bf16[128,1024]{1,0:T(8,128)(2,1)} %copy-done.8, s32[1,128]{1,0:T(1,128)} %bitcast.27), custom_call_target="tpu_custom_call" | custom-call | tf_op jit(solution)/shard_map/pallas_call | solution.py:151
  79.4 1.9 %collective-permute-start.5 = (bf16[128,1024]{1,0:T(8,128)(2,1)}, bf16[128,1024]{1,0:T(8,128)(2,1)}, u32[]{:S(2)}, u32[]{:S(2)}) collective-permute-start(bf16[128,1024]{1,0:T(8,128)(2,1)} %get-tuple-element.32), channel_id=1, source_target_pairs={{0,16},{16,0},{1,17},{17,1},{2,18},{18,2},{3,19},{19,3},{4,20},{20... | collective-permute-start | bytes 786440 | tf_op jit(solution)/shard_map/ppermute | solution.py:19
  81.3 1.8 %collective-permute-done.5.core_ref = bf16[128,1024]{1,0:T(8,128)(2,1)} collective-permute-done((bf16[128,1024]{1,0:T(8,128)(2,1)}, bf16[128,1024]{1,0:T(8,128)(2,1)}, u32[]{:S(2)}, u32[]{:S(2)}) %collective-permute-start.5) | collective-permute-done | bytes 262176 | tf_op jit(solution)/shard_map/ppermute | solution.py:19
  83.2 4.5 %shard_map.88 = bf16[1024,1024]{1,0:T(8,128)(2,1)} custom-call(bf16[256,1024]{1,0:T(8,128)(2,1)} %get-tuple-element.33.coeffs_ref, bf16[128,1024]{1,0:T(8,128)(2,1)} %own_ref.1, bf16[128,1024]{1,0:T(8,128)(2,1)} %collective-permute-done.refs_3_.mate_ref), custom_call_target="tpu_custom_call" | custom-call | flops 536870912 | bytes 3145728 | tf_op jit(solution)/shard_map/pallas_call | solution.py:128
  87.7 0.0 reduce-scatter.2.cloned.1.call-update
  87.7 4.9 %all-to-all-start.1 = ((bf16[4,128,1024]{2,1,0:T(8,128)(2,1)}), bf16[4,128,1024]{2,1,0:T(8,128)(2,1)S(1)}, u32[]{:S(2)}, u32[]{:S(2)}) async-start(bf16[4,128,1024]{2,1,0:T(8,128)(2,1)} %bitcast.7), calls=%async_computation.2 | async-start | bytes 2097152 | tf_op jit(solution)/shard_map/all_to_all | solution.py:265
  92.7 0.9 slice.10
  93.6 3.4 %collective-permute-start.6 = (bf16[128,1024]{1,0:T(8,128)(2,1)S(1)}, bf16[128,1024]{1,0:T(8,128)(2,1)S(1)}, u32[]{:S(2)}, u32[]{:S(2)}) collective-permute-start(bf16[128,1024]{1,0:T(8,128)(2,1)S(1)} %pad_maximum_fusion.1), channel_id=1, source_target_pairs={{0,32},{32,0},{1,33},{33,1},{2,34},{34,2},{3,35},{35,3},{4,36},{36... | collective-permute-start | bytes 786440 | tf_op jit(solution)/shard_map/ppermute | solution.py:19
  97.0 14.7 %collective-permute-done.6.x_ref = bf16[128,1024]{1,0:T(8,128)(2,1)S(1)} collective-permute-done((bf16[128,1024]{1,0:T(8,128)(2,1)S(1)}, bf16[128,1024]{1,0:T(8,128)(2,1)S(1)}, u32[]{:S(2)}, u32[]{:S(2)}) %collective-permute-start.6) | collective-permute-done | bytes 262176 | tf_op jit(solution)/shard_map/ppermute | solution.py:19
  111.7 0.7 copy-done.7
  112.4 1.0 copy-done.1
  113.4 2.5 %shard_map.89 = bf16[8,48,1024]{2,1,0:T(8,128)(2,1)} custom-call(bf16[128,1024]{1,0:T(8,128)(2,1)} %get-tuple-element.34.stay_ref, bf16[128,1024]{1,0:T(8,128)(2,1)} %collective-permute-done.5.core_ref, bf16[128,1024]{1,0:T(8,128)(2,1)} %copy-done.7, bf16[4,128,1024]{2,1,0:T(8,128)(2,1)} %copy-done.1), custom_call_target="tpu_custom_call" | custom-call | tf_op jit(solution)/shard_map/pallas_call | solution.py:193
  115.9 29.1 %all_to_all.20.pieces_ref = bf16[8,48,1024]{2,1,0:T(8,128)(2,1)} all-to-all(bf16[8,48,1024]{2,1,0:T(8,128)(2,1)} %shard_map.89), channel_id=1, replica_groups=mesh['wide_y'=8,'wide_x'=2,'wide_c'=2,'blk_x'=2,'blk_z'=8] {'wide_y'}, dimensions={0} | all-to-all | bytes 1572864 | tf_op jit(solution)/shard_map/all_to_all | solution.py:281
  145.0 1.9 %shard_map.90 = bf16[16,16,1024]{2,1,0:T(8,128)(2,1)} custom-call(bf16[8,48,1024]{2,1,0:T(8,128)(2,1)} %all_to_all.20.pieces_ref), custom_call_target="tpu_custom_call" | custom-call | tf_op jit(solution)/shard_map/pallas_call | solution.py:209
  146.9 6.0 %all-to-all-start.3 = ((bf16[16,16,1024]{2,1,0:T(8,128)(2,1)}), bf16[16,16,1024]{2,1,0:T(8,128)(2,1)S(1)}, u32[]{:S(2)}, u32[]{:S(2)}) async-start(bf16[16,16,1024]{2,1,0:T(8,128)(2,1)} %shard_map.90), calls=%async_computation.4 | async-start | bytes 1048576 | tf_op jit(solution)/shard_map/all_to_all | solution.py:283
  153.0 2.9 %fusion.3 = bf16[256,1024]{1,0:T(8,128)(2,1)} fusion(bf16[1024,1024]{1,0:T(8,128)(2,1)S(1)} %copy-done, f32[256,1024]{1,0:T(8,128)} %fusion.11, bf16[256,1024]{1,0:T(8,128)(2,1)S(1)} %bitcast.25, f32[256]{0:T(256)S(1)} %convert_rsqrt_fusion, s32[256]{0:T(256)S(1)} %fusion.41), kind=kOutput, calls=%fused_computation.9 | convolution fusion | flops 672202752 | bytes 4196352 | tf_op jit(solution)/shard_map/dot_general | solution.py:23
  155.9 8.7 %all-to-all-done.3 = bf16[16,16,1024]{2,1,0:T(8,128)(2,1)S(1)} async-done(((bf16[16,16,1024]{2,1,0:T(8,128)(2,1)}), bf16[16,16,1024]{2,1,0:T(8,128)(2,1)S(1)}, u32[]{:S(2)}, u32[]{:S(2)}) %all-to-all-start.3) | async-done | bytes 524320 | tf_op jit(solution)/shard_map/all_to_all | solution.py:283
  164.6 0.7 convert_reduce_fusion
  (25 shorter events, 0.1 us)
Async XLA Ops:
  7.2 16.7 %copy-start = (bf16[1024,1024]{1,0:T(8,128)(2,1)S(1)}, bf16[1024,1024]{1,0:T(8,128)(2,1)}, u32[]{:S(2)}) copy-start(bf16[1024,1024]{1,0:T(8,128)(2,1)} %param.11) | copy-start | bytes 6291460
  7.2 16.7 %copy-start.4 = (bf16[256,1024]{1,0:T(8,128)(2,1)S(1)}, bf16[256,1024]{1,0:T(8,128)(2,1)}, u32[]{:S(2)}) copy-start(bf16[256,1024]{1,0:T(8,128)(2,1)} %param.9) | copy-start | bytes 1572868
  7.2 13.8 %copy-start.5 = (bf16[128,1024]{1,0:T(8,128)(2,1)S(1)}, bf16[128,1024]{1,0:T(8,128)(2,1)}, u32[]{:S(2)}) copy-start(bf16[128,1024]{1,0:T(8,128)(2,1)} %own_ref.1) | copy-start | bytes 786436
  7.2 16.6 %copy-start.9 = (s32[128,1]{0,1:T(1,128)S(1)}, s32[128,1]{0,1:T(1,128)}, u32[]{:S(2)}) copy-start(s32[128,1]{0,1:T(1,128)} %param.8) | copy-start | bytes 1540
  7.2 51.7 %all-gather.2.cloned.1.call-start = ((), (), s32[]{:S(2)}) async-start(), calls=%async_computation.5 | async-start | bytes 2359296 | tf_op jit(solution)/shard_map/all_gather | solution.py:224
  10.7 27.9 %all-to-all-start = ((bf16[32,8,1024]{2,1,0:T(8,128)(2,1)}), bf16[32,8,1024]{2,1,0:T(8,128)(2,1)S(1)}, u32[]{:S(2)}, u32[]{:S(2)}) async-start(bf16[32,8,1024]{2,1,0:T(8,128)(2,1)} %fusion.18), calls=%async_computation | async-start | bytes 1048576 | tf_op jit(solution)/shard_map/all_to_all | solution.py:231
  21.0 144.4 %reduce-scatter.2.cloned.1.call-start = ((), (), s32[]{:S(2)}) async-start(), calls=%async_computation.6 | async-start | bytes 2359296 | tf_op jit(solution)/shard_map/reduce_scatter | solution.py:275
  21.0 32.9 %collective-permute-start = (bf16[128,1024]{1,0:T(8,128)(2,1)S(1)}, bf16[128,1024]{1,0:T(8,128)(2,1)}, u32[]{:S(2)}, u32[]{:S(2)}) collective-permute-start(bf16[128,1024]{1,0:T(8,128)(2,1)S(1)} %copy-done.5), channel_id=1, source_target_pairs={{0,8},{8,0},{1,9},{9,1},{2,10},{10,2},{3,11},{11,3},{4,12},{12,4},... | collective-permute-start | bytes 786440 | tf_op jit(solution)/shard_map/ppermute | solution.py:19
  38.9 9.4 %collective-permute-start.1 = (bf16[128,1024]{1,0:T(8,128)(2,1)S(1)}, bf16[128,1024]{1,0:T(8,128)(2,1)S(1)}, u32[]{:S(2)}, u32[]{:S(2)}) collective-permute-start(bf16[128,1024]{1,0:T(8,128)(2,1)S(1)} %convolution_convert_fusion.2), channel_id=1, source_target_pairs={{0,8},{8,0},{1,9},{9,1},{2,10},{10,2},{3,11},{11,3},{4,12},{12,4},... | collective-permute-start | bytes 786440 | tf_op jit(solution)/shard_map/ppermute | solution.py:19
  48.8 5.1 %collective-permute-start.2 = (bf16[512,256]{1,0:T(8,128)(2,1)S(1)}, bf16[512,256]{1,0:T(8,128)(2,1)S(1)}, u32[]{:S(2)}, u32[]{:S(2)}) collective-permute-start(bf16[512,256]{1,0:T(8,128)(2,1)S(1)} %convolution_convert_fusion), channel_id=1, source_target_pairs={{0,16},{16,0},{1,17},{17,1},{2,18},{18,2},{3,19},{19,3},{4,20},{20... | collective-permute-start | bytes 786440 | tf_op jit(solution)/shard_map/ppermute | solution.py:19
  53.9 14.6 %copy-start.6 = (bf16[512,256]{1,0:T(8,128)(2,1)}, bf16[512,256]{1,0:T(8,128)(2,1)S(1)}, u32[]{:S(2)}) copy-start(bf16[512,256]{1,0:T(8,128)(2,1)S(1)} %collective-permute-done.2.mate_picked) | copy-start | bytes 786436
  63.8 4.7 %collective-permute-start.4 = (bf16[256,1024]{1,0:T(8,128)(2,1)}, bf16[256,1024]{1,0:T(8,128)(2,1)S(1)}, u32[]{:S(2)}, u32[]{:S(2)}) collective-permute-start(bf16[256,1024]{1,0:T(8,128)(2,1)} %get-tuple-element.29.own_pre), channel_id=1, source_target_pairs={{0,16},{16,0},{1,17},{17,1},{2,18},{18,2},{3,19},{19,3},{4,20},{20... | collective-permute-start | bytes 1572872 | tf_op jit(solution)/shard_map/ppermute | solution.py:19
  65.7 10.8 %collective-permute-start.3 = (bf16[128,1024]{1,0:T(8,128)(2,1)}, bf16[128,1024]{1,0:T(8,128)(2,1)S(1)}, u32[]{:S(2)}, u32[]{:S(2)}) collective-permute-start(bf16[128,1024]{1,0:T(8,128)(2,1)} %get-tuple-element.26), channel_id=1, source_target_pairs={{0,8},{8,0},{1,9},{9,1},{2,10},{10,2},{3,11},{11,3},{4,12},{12,4},... | collective-permute-start | bytes 786440 | tf_op jit(solution)/shard_map/ppermute | solution.py:19
  68.5 0.8 copy-start.3
  76.5 0.7 copy-start.8
  79.4 3.8 %collective-permute-start.5 = (bf16[128,1024]{1,0:T(8,128)(2,1)}, bf16[128,1024]{1,0:T(8,128)(2,1)}, u32[]{:S(2)}, u32[]{:S(2)}) collective-permute-start(bf16[128,1024]{1,0:T(8,128)(2,1)} %get-tuple-element.32), channel_id=1, source_target_pairs={{0,16},{16,0},{1,17},{17,1},{2,18},{18,2},{3,19},{19,3},{4,20},{20... | collective-permute-start | bytes 786440 | tf_op jit(solution)/shard_map/ppermute | solution.py:19
  87.7 5.0 %copy-start.2 = (bf16[128,1024]{1,0:T(8,128)(2,1)S(1)}, bf16[128,1024]{1,0:T(8,128)(2,1)}, u32[]{:S(2)}) copy-start(bf16[128,1024]{1,0:T(8,128)(2,1)} %get-tuple-element.34.stay_ref) | copy-start | bytes 786436
  87.7 24.0 %all-to-all-start.1 = ((bf16[4,128,1024]{2,1,0:T(8,128)(2,1)}), bf16[4,128,1024]{2,1,0:T(8,128)(2,1)S(1)}, u32[]{:S(2)}, u32[]{:S(2)}) async-start(bf16[4,128,1024]{2,1,0:T(8,128)(2,1)} %bitcast.7), calls=%async_computation.2 | async-start | bytes 2097152 | tf_op jit(solution)/shard_map/all_to_all | solution.py:265
  93.6 18.1 %collective-permute-start.6 = (bf16[128,1024]{1,0:T(8,128)(2,1)S(1)}, bf16[128,1024]{1,0:T(8,128)(2,1)S(1)}, u32[]{:S(2)}, u32[]{:S(2)}) collective-permute-start(bf16[128,1024]{1,0:T(8,128)(2,1)S(1)} %pad_maximum_fusion.1), channel_id=1, source_target_pairs={{0,32},{32,0},{1,33},{33,1},{2,34},{34,2},{3,35},{35,3},{4,36},{36... | collective-permute-start | bytes 786440 | tf_op jit(solution)/shard_map/ppermute | solution.py:19
  111.7 0.7 copy-start.7
  112.4 1.0 copy-start.1
  145.0 7.9 %slice-start = ((bf16[8,48,1024]{2,1,0:T(8,128)(2,1)}), bf16[8,32,1024]{2,1,0:T(8,128)(2,1)S(1)}, s32[]{:S(2)}) async-start(bf16[8,48,1024]{2,1,0:T(8,128)(2,1)} %all_to_all.20.pieces_ref), calls=%async_computation.7 | async-start | bytes 1048576 | tf_op jit(solution)/shard_map/slice | solution.py:286
  146.9 17.7 %all-to-all-start.3 = ((bf16[16,16,1024]{2,1,0:T(8,128)(2,1)}), bf16[16,16,1024]{2,1,0:T(8,128)(2,1)S(1)}, u32[]{:S(2)}, u32[]{:S(2)}) async-start(bf16[16,16,1024]{2,1,0:T(8,128)(2,1)} %shard_map.90), calls=%async_computation.4 | async-start | bytes 1048576 | tf_op jit(solution)/shard_map/all_to_all | solution.py:283
Sparse Core Ops, SparseCore 0:
  10.1 48.7 all-gather.1
  87.8 44.3 reduce-scatter.1

commit v7 on v5

--- a/solution.py
+++ b/solution.py
@@ -45,10 +45,8 @@
     share = half // (ny * nx * bx)
     place = jnp.arange(half, dtype=jnp.int32)
     within, rest = place % share, place // share
-    y, apart = rest % ny, rest // ny
-    x_wide = (apart // bx) ^ lax.axis_index("wide_x")
-    x_blk = (apart % bx) ^ lax.axis_index("blk_x")
-    feature = (((y * nx + x_wide) * 2 + core) * bx + x_blk) * share + within
+    y, x = rest % ny, rest // ny
+    feature = (((y * nx + x // bx) * 2 + core) * bx + x % bx) * share + within
     return (jnp.arange(feature_count, dtype=jnp.int32)[:, None] == feature[None, :]).astype(BF16)
 
 
@@ -67,21 +65,29 @@
         load.start()
     loads[0].wait()
     loads[1].wait()
-    stores = []
-    for step in range(steps):
+
+    def coeffs_of(step):
         block = pl.ds(step * rows, rows)
         loads[2 + step].wait()
         scores = dot_of(video[...], line[block], 1, 1)
         row = lax.broadcasted_iota(jnp.int32, scores.shape, 0)
         col = lax.broadcasted_iota(jnp.int32, scores.shape, 1) + step * rows
         labels = ((col == place_ref[0] * clips + row) & (row < clips)).astype(F32)
-        coeffs = (factor * (jax.nn.sigmoid(4.0 * scores - 2.0) - labels)).astype(BF16)
-        part = dot_of(coeffs, line[block], 1, 0)
+        return (factor * (jax.nn.sigmoid(4.0 * scores - 2.0) - labels)).astype(BF16)
+
+    stores = []
+    coeffs = coeffs_of(0)
+    for step in range(steps):
+        block = pl.ds(step * rows, rows)
+        ready = coeffs
+        if step + 1 < steps:
+            coeffs = coeffs_of(step + 1)
+        part = dot_of(ready, line[block], 1, 0)
         if step == 0:
             total[...] = part
         else:
             total[...] += part
-        grads[block] = dot_of(coeffs, video[...], 0, 0).astype(BF16)
+        grads[block] = dot_of(ready, video[...], 0, 0).astype(BF16)
         stores.append(pltpu.make_async_copy(grads.at[block], grads_hbm.at[block], gone.at[step]))
         stores[-1].start()
     loads[-1].wait()
@@ -139,38 +145,33 @@
     )(kept, arrived, targets[None, :])
 
 
-def weight_kernel(own_picked, mate_picked, own_pre, mate_pre, *out_refs):
-    share = out_refs[0].shape[0]
-    for d, out_ref in enumerate(out_refs):
-        block = pl.ds(d * share, share)
-        product = dot_of(own_picked[block], own_pre[...], 1, 0)
-        product += dot_of(mate_picked[block], mate_pre[...], 1, 0)
-        out_ref[...] = product.astype(out_ref.dtype)
-
-
-def weight_parts(own_picked, mate_picked, own_pre, mate_pre, count):
-    half, features = own_picked.shape[0], own_pre.shape[1]
-    shape = (half // count, features)
+def weight_kernel(own_picked, mate_picked, own_pre, mate_pre, out_ref):
+    product = dot_of(own_picked[...], own_pre[...], 1, 0)
+    product += dot_of(mate_picked[...], mate_pre[...], 1, 0)
+    out_ref[...] = product.astype(BF16)
+
+
+def weight_part(own_picked, mate_picked, own_pre, mate_pre):
     return pl.pallas_call(
         weight_kernel,
-        out_shape=[jax.ShapeDtypeStruct(shape, F32 if d == 0 else BF16) for d in range(count)],
+        out_shape=jax.ShapeDtypeStruct((own_picked.shape[0], own_pre.shape[1]), BF16),
         compiler_params=ROOM,
     )(own_picked, mate_picked, own_pre, mate_pre)
 
 
-def sum_kernel(*refs):
-    total = refs[0][...].astype(F32)
-    for ref in refs[1:-1]:
-        total += ref[...].astype(F32)
-    refs[-1][...] = total.astype(BF16)
-
-
-def sum_of(arrays):
+def sum_kernel(pieces_ref, out_ref):
+    total = pieces_ref[0].astype(F32)
+    for s in range(1, pieces_ref.shape[0]):
+        total += pieces_ref[s].astype(F32)
+    out_ref[...] = total.astype(BF16)
+
+
+def sum_of(pieces):
     return pl.pallas_call(
         sum_kernel,
-        out_shape=jax.ShapeDtypeStruct(arrays[0].shape, BF16),
-        compiler_params=ROOM,
-    )(*arrays)
+        out_shape=jax.ShapeDtypeStruct(pieces.shape[1:], BF16),
+        compiler_params=ROOM,
+    )(pieces)
 
 
 def spread_kernel(pieces_ref, out_ref):
@@ -228,20 +229,19 @@
 
     pre_mate = swapped(pre_pair, "wide_c")
     arrived = swapped(sent, "blk_x")
-    parts = weight_parts(picked, picked_mate, pre_pair, pre_mate, 4)
-    came = [parts[0]]
-    for d in (2, 1, 3):
-        pairs = [(at, at ^ d) for at in range(4)]
-        came.append(lax.ppermute(parts[d], ("wide_x", "blk_x"), pairs))
-
-    arrived, parts = lax.optimization_barrier((arrived, parts))
+    weight_sum = weight_part(picked, picked_mate, pre_pair, pre_mate)
+    pieces = lax.all_to_all(
+        weight_sum.reshape(4, -1, features), ("wide_x", "blk_x"), 0, 0, tiled=True
+    )
+
+    arrived, pieces = lax.optimization_barrier((arrived, pieces))
     packed = clip_grads(kept, arrived, targets, slots)
     received = lax.all_to_all(
         packed.reshape(peers, capacity, features), WIDE, 0, 0, tiled=True
     ).reshape(slots, features)
 
-    packed, came = lax.optimization_barrier((packed, came))
-    summed, received = lax.optimization_barrier((sum_of(came), received))
+    pieces, packed = lax.optimization_barrier((pieces, packed))
+    summed, received = lax.optimization_barrier((sum_of(pieces), received))
     pieces = lax.all_to_all(
         summed.reshape(lax.axis_size("wide_y"), -1, features), "wide_y", 0, 0, tiled=True
     )

time: 160 us -> 168 us (1.050)
  waiting for transfers between devices: 51.8 us -> 68.7 us
  starting transfers between devices: 48.4 us -> 40.9 us
  Pallas kernels: 9.47 us -> 7.71 us
    all_to_all x1, waiting for transfers between devices: 0.01 us -> 16.9 us  [shards(): lax.all_to_all(packed.reshape(peers, capacity, features), WIDE, 0, 0, til...]
    ppermute x3 -> x0, waiting for transfers between devices: 13.3 us -> none  [shards(): came.append(lax.ppermute(parts[d], ('wide_x', 'blk_x'), pairs))]
    ppermute x5, waiting for transfers between devices: 11.9 us -> 24.1 us  [swapped(): return lax.ppermute(array, axis, [(0, 1), (1, 0)])]
    ppermute x3 -> x0, starting transfers between devices: 10.4 us -> none  [shards(): came.append(lax.ppermute(parts[d], ('wide_x', 'blk_x'), pairs))]
    all_to_all x0 -> x1, starting transfers between devices: none -> 4.8 us  [shards(): lax.all_to_all(weight_sum.reshape(4, -1, features), ('wide_x', 'blk_x'),...]
    all_to_all x1, starting transfers between devices: 5.7 us -> 3.41 us  [shards(): lax.all_to_all(summed.reshape(lax.axis_size('wide_y'), -1, features), 'wi...]
    unnamed x20 -> x14, local copies, waits for them, and re-layouts: 3.02 us -> 3.83 us
  transfers between devices with their start and end apart: 13 -> 11, of which waited for: 8 -> 7; matrix products, arithmetic and copies ran while one was open for 8% -> 7% of each run, Pallas kernels for 2% -> 1%
where the time goes in v7:
time: 168 us; the launch traced here: 165 us
  waiting for transfers between devices  68.7 us (41%)
  starting transfers between devices  40.9 us (24%)
  blocking collectives  18.1 us (11%)
  between operations  14.3 us (9%)
  matrix products  8.16 us (5%)
  Pallas kernels  7.71 us (5%)
  local copies, waits for them, and re-layouts  3.83 us (2%)
  other arithmetic  3.61 us (2%)
    ppermute x5, waiting for transfers between devices, swapped(): return lax.ppermute(array, axis, [(0, 1), (1, 0)])  24.1 us
    all_to_all x1, blocking collectives, shards(): gathered = lax.all_to_all(total, BLK, 0, 0, tiled=True)  18.1 us
    all_to_all x1, waiting for transfers between devices, shards(): lax.all_to_all(packed.reshape(peers, capacity, features), WIDE, 0, 0, til...  16.9 us
    all_to_all x1, waiting for transfers between devices, shards(): lax.all_to_all(pooled.reshape(peers, capacity, features), WIDE, 0, 0, til...  12.7 us
    ppermute x5, starting transfers between devices, swapped(): return lax.ppermute(array, axis, [(0, 1), (1, 0)])  12.1 us
    all_to_all x1, starting transfers between devices, shards(): lax.all_to_all(packed.reshape(peers, capacity, features), WIDE, 0, 0, til...  10.3 us
    all_to_all x1, starting transfers between devices, shards(): lax.all_to_all(pooled.reshape(peers, capacity, features), WIDE, 0, 0, til...  10.2 us
    all_to_all x1, waiting for transfers between devices, shards(): lax.all_to_all(summed.reshape(lax.axis_size('wide_y'), -1, features), 'wi...  8.61 us
  transfers between devices with their start and end apart: 11, of which 7 were waited for; matrix products, arithmetic and copies ran while one was open for 7% of the time, Pallas kernels for 1%

profile of v7, /device:TPU:6, one launch (start us, length us, event | category | flops | bytes accessed | tf_op | source)
XLA Modules:
  0.0 165.2 jit_solution(580578341588915653)
XLA Ops:
  7.2 0.0 copy-start
  7.2 0.0 copy-start.5
  7.2 0.0 copy-start.6
  7.2 0.0 all-gather.2.cloned.1.call-start
  7.2 0.7 all-gather.2.cloned.1.call-update
  7.9 0.7 convert_rsqrt_fusion
  8.7 2.0 %fusion.17 = bf16[32,8,1024]{2,1,0:T(8,128)(2,1)} fusion(f32[256]{0:T(256)S(1)} %convert_rsqrt_fusion, bf16[256,1024]{1,0:T(8,128)(2,1)} %param.9), kind=kLoop, calls=%fused_computation.27 | loop fusion | flops 786432 | bytes 1049600 | tf_op jit(solution)/shard_map/reshape | solution.py:205
  10.6 10.2 %all-to-all-start = ((bf16[32,8,1024]{2,1,0:T(8,128)(2,1)}), bf16[32,8,1024]{2,1,0:T(8,128)(2,1)S(1)}, u32[]{:S(2)}, u32[]{:S(2)}) async-start(bf16[32,8,1024]{2,1,0:T(8,128)(2,1)} %fusion.17), calls=%async_computation | async-start | bytes 1048576 | tf_op jit(solution)/shard_map/all_to_all | solution.py:204
  20.9 0.0 reduce-scatter.2.cloned.1.call-start
  20.9 2.7 %collective-permute-start = (bf16[128,1024]{1,0:T(8,128)(2,1)}, bf16[128,1024]{1,0:T(8,128)(2,1)}, u32[]{:S(2)}, u32[]{:S(2)}) collective-permute-start(bf16[128,1024]{1,0:T(8,128)(2,1)} %refs_2_.1), channel_id=1, source_target_pairs={{0,8},{8,0},{1,9},{9,1},{2,10},{10,2},{3,11},{11,3},{4,12},{12,4},... | collective-permute-start | bytes 786440 | tf_op jit(solution)/shard_map/ppermute | solution.py:20
  23.7 0.0 copy-done.6
  23.7 0.1 convert_reduce_fusion.1
  23.8 2.0 %fusion.10 = f32[256,1024]{1,0:T(8,128)} fusion(bf16[1024,1024]{1,0:T(8,128)(2,1)S(1)} %copy-done, bf16[256,1024]{1,0:T(8,128)(2,1)S(1)} %copy-done.5, f32[256]{0:T(256)S(1)} %convert_rsqrt_fusion), kind=kOutput, calls=%fused_computation.18 | convolution fusion | flops 539754496 | bytes 3671040 | tf_op jit(solution)/shard_map/dot_general | solution.py:24
  25.9 12.7 %all-to-all-done = bf16[32,8,1024]{2,1,0:T(8,128)(2,1)S(1)} async-done(((bf16[32,8,1024]{2,1,0:T(8,128)(2,1)}), bf16[32,8,1024]{2,1,0:T(8,128)(2,1)S(1)}, u32[]{:S(2)}, u32[]{:S(2)}) %all-to-all-start) | async-done | bytes 524320 | tf_op jit(solution)/shard_map/all_to_all | solution.py:204
  38.6 0.3 convolution_convert_fusion.2
  38.9 2.7 %collective-permute-start.1 = (bf16[128,1024]{1,0:T(8,128)(2,1)S(1)}, bf16[128,1024]{1,0:T(8,128)(2,1)S(1)}, u32[]{:S(2)}, u32[]{:S(2)}) collective-permute-start(bf16[128,1024]{1,0:T(8,128)(2,1)S(1)} %convolution_convert_fusion.2), channel_id=1, source_target_pairs={{0,8},{8,0},{1,9},{9,1},{2,10},{10,2},{3,11},{11,3},{4,12},{12,4},... | collective-permute-start | bytes 786440 | tf_op jit(solution)/shard_map/ppermute | solution.py:20
  41.6 6.6 %collective-permute-done.1 = bf16[128,1024]{1,0:T(8,128)(2,1)S(1)} collective-permute-done((bf16[128,1024]{1,0:T(8,128)(2,1)S(1)}, bf16[128,1024]{1,0:T(8,128)(2,1)S(1)}, u32[]{:S(2)}, u32[]{:S(2)}) %collective-permute-start.1) | collective-permute-done | bytes 262176 | tf_op jit(solution)/shard_map/ppermute | solution.py:20
  48.2 0.5 convolution_convert_fusion
  48.7 1.9 %collective-permute-start.2 = (bf16[512,256]{1,0:T(8,128)(2,1)S(1)}, bf16[512,256]{1,0:T(8,128)(2,1)S(1)}, u32[]{:S(2)}, u32[]{:S(2)}) collective-permute-start(bf16[512,256]{1,0:T(8,128)(2,1)S(1)} %convolution_convert_fusion), channel_id=1, source_target_pairs={{0,16},{16,0},{1,17},{17,1},{2,18},{18,2},{3,19},{19,3},{4,20},{20... | collective-permute-start | bytes 786440 | tf_op jit(solution)/shard_map/ppermute | solution.py:20
  50.7 2.0 %fusion.6.refs_4_ = f32[256,1024]{1,0:T(8,128)} fusion(bf16[1024,1024]{1,0:T(8,128)(2,1)S(1)} %copy-done, bf16[128,1024]{1,0:T(8,128)(2,1)S(1)} %collective-permute-done.1, bf16[128,1024]{1,0:T(8,128)(2,1)S(1)} %convolution_convert_fusion.2), kind=kOutput, calls=%fused_computation.14 | convolution fusion | flops 540016640 | bytes 3670016 | tf_op jit(solution)/shard_map/dot_general | solution.py:24
  52.7 0.5 convolution_convert_fusion.1.own_picked
  53.2 0.0 collective-permute-done.refs_3_
  53.2 0.0 collective-permute-done.2.mate_picked
  53.2 5.7 %all-gather.2.cloned.1.call-done.refs_1_ = bf16[1024,1024]{1,0:T(8,128)(2,1)} async-done(((bf16[128,1024]{1,0:T(8,128)(2,1)}), bf16[1024,1024]{1,0:T(8,128)(2,1)}) %all-gather.2.cloned.1.call-update) | async-done | bytes 2097168 | tf_op jit(solution)/shard_map/all_gather | solution.py:197
  58.9 5.8 %shard_map.85 = (f32[128,1024]{1,0:T(8,128)}, bf16[128,1024]{1,0:T(8,128)(2,1)}, bf16[256,1024]{1,0:T(8,128)(2,1)}, bf16[1024,1024]{1,0:T(8,128)(2,1)}) custom-call(s32[1]{0:T(128)} %bitcast.refs_0_, bf16[1024,1024]{1,0:T(8,128)(2,1)} %all-gather.2.cloned.1.call-done.refs_1_, bf16[128,1024]{1,0:T(8,128)(2,1)} %refs_2_.1, ...), custom_call_target="tpu_custom_call" | custom-call | flops 1610612736 | bytes 5242880 | tf_op jit(solution)/shard_map/pallas_call | solution.py:106
  64.7 0.0 reduce-scatter.2.cloned.1.call-update
  64.7 1.0 copy-done.4
  65.7 1.9 %collective-permute-start.4 = (bf16[256,1024]{1,0:T(8,128)(2,1)S(1)}, bf16[256,1024]{1,0:T(8,128)(2,1)S(1)}, u32[]{:S(2)}, u32[]{:S(2)}) collective-permute-start(bf16[256,1024]{1,0:T(8,128)(2,1)S(1)} %copy-done.4), channel_id=1, source_target_pairs={{0,16},{16,0},{1,17},{17,1},{2,18},{18,2},{3,19},{19,3},{4,20},{20... | collective-permute-start | bytes 1572872 | tf_op jit(solution)/shard_map/ppermute | solution.py:20
  67.7 1.9 %collective-permute-done.4.mate_pre = bf16[256,1024]{1,0:T(8,128)(2,1)S(1)} collective-permute-done((bf16[256,1024]{1,0:T(8,128)(2,1)S(1)}, bf16[256,1024]{1,0:T(8,128)(2,1)S(1)}, u32[]{:S(2)}, u32[]{:S(2)}) %collective-permute-start.4) | collective-permute-done | bytes 524320 | tf_op jit(solution)/shard_map/ppermute | solution.py:20
  69.5 0.7 shard_map.86
  70.3 1.0 copy-done.1
  71.2 4.8 %all-to-all-start.1 = ((bf16[4,128,1024]{2,1,0:T(8,128)(2,1)}), bf16[4,128,1024]{2,1,0:T(8,128)(2,1)S(1)}, u32[]{:S(2)}, u32[]{:S(2)}) async-start(bf16[4,128,1024]{2,1,0:T(8,128)(2,1)} %bitcast.26), calls=%async_computation.2 | async-start | bytes 2097152 | tf_op jit(solution)/shard_map/all_to_all | solution.py:233
  76.0 2.8 %collective-permute-start.3 = (bf16[128,1024]{1,0:T(8,128)(2,1)}, bf16[128,1024]{1,0:T(8,128)(2,1)S(1)}, u32[]{:S(2)}, u32[]{:S(2)}) collective-permute-start(bf16[128,1024]{1,0:T(8,128)(2,1)} %get-tuple-element.25), channel_id=1, source_target_pairs={{0,8},{8,0},{1,9},{9,1},{2,10},{10,2},{3,11},{11,3},{4,12},{12,4},... | collective-permute-start | bytes 786440 | tf_op jit(solution)/shard_map/ppermute | solution.py:20
  78.8 15.6 %collective-permute-done.3.arrived_ref = bf16[128,1024]{1,0:T(8,128)(2,1)S(1)} collective-permute-done((bf16[128,1024]{1,0:T(8,128)(2,1)}, bf16[128,1024]{1,0:T(8,128)(2,1)S(1)}, u32[]{:S(2)}, u32[]{:S(2)}) %collective-permute-start.3) | collective-permute-done | bytes 262176 | tf_op jit(solution)/shard_map/ppermute | solution.py:20
  94.4 0.0 all-to-all-done.1.pieces_ref
  94.4 1.0 copy-done.3
  95.4 0.3 shard_map.87
  95.7 0.0 copy-start.2
  95.7 0.8 copy-done.2
  96.5 10.3 %all-to-all-start.2 = ((bf16[32,8,1024]{2,1,0:T(8,128)(2,1)}), bf16[32,8,1024]{2,1,0:T(8,128)(2,1)}, u32[]{:S(2)}, u32[]{:S(2)}) async-start(bf16[32,8,1024]{2,1,0:T(8,128)(2,1)} %bitcast.27), calls=%async_computation.3 | async-start | bytes 1048576 | tf_op jit(solution)/shard_map/all_to_all | solution.py:239
  106.8 0.9 shard_map.88
  107.7 16.9 %all-to-all-done.2 = bf16[32,8,1024]{2,1,0:T(8,128)(2,1)} async-done(((bf16[32,8,1024]{2,1,0:T(8,128)(2,1)}), bf16[32,8,1024]{2,1,0:T(8,128)(2,1)}, u32[]{:S(2)}, u32[]{:S(2)}) %all-to-all-start.2) | async-done | bytes 524320 | tf_op jit(solution)/shard_map/all_to_all | solution.py:239
  124.6 3.4 %all-to-all-start.3 = ((bf16[8,16,1024]{2,1,0:T(8,128)(2,1)}), bf16[8,16,1024]{2,1,0:T(8,128)(2,1)S(1)}, u32[]{:S(2)}, u32[]{:S(2)}) async-start(bf16[8,16,1024]{2,1,0:T(8,128)(2,1)} %bitcast.10), calls=%async_computation.4 | async-start | bytes 524288 | tf_op jit(solution)/shard_map/all_to_all | solution.py:245
  128.0 2.9 %fusion.2 = bf16[256,1024]{1,0:T(8,128)(2,1)} fusion(bf16[1024,1024]{1,0:T(8,128)(2,1)S(1)} %copy-done, f32[256,1024]{1,0:T(8,128)} %fusion.10, bf16[256,1024]{1,0:T(8,128)(2,1)} %bitcast.9, f32[256]{0:T(256)S(1)} %convert_rsqrt_fusion), kind=kOutput, calls=%fused_computation.7 | convolution fusion | flops 538181632 | bytes 4195328 | tf_op jit(solution)/shard_map/dot_general | solution.py:24
  130.9 8.6 %all-to-all-done.3.pieces_ref = bf16[8,16,1024]{2,1,0:T(8,128)(2,1)S(1)} async-done(((bf16[8,16,1024]{2,1,0:T(8,128)(2,1)}), bf16[8,16,1024]{2,1,0:T(8,128)(2,1)S(1)}, u32[]{:S(2)}, u32[]{:S(2)}) %all-to-all-start.3) | async-done | bytes 262176 | tf_op jit(solution)/shard_map/all_to_all | solution.py:245
  139.5 0.1 shard_map.89
  139.6 18.1 %all_to_all.25 = bf16[16,16,1024]{2,1,0:T(8,128)(2,1)S(1)} all-to-all(bf16[16,16,1024]{2,1,0:T(8,128)(2,1)S(1)} %shard_map.89), channel_id=1, replica_groups=mesh['wide_y'=8,'wide_x'=2,'wide_c'=2,'blk_x'=2,'blk_z'=8] {'blk_x','blk..., dimensions={0} | all-to-all | bytes 1048576 | tf_op jit(solution)/shard_map/all_to_all | solution.py:252
  157.7 0.7 convert_reduce_fusion
  (10 shorter events, 0.1 us)
Async XLA Ops:
  7.2 16.7 %copy-start = (bf16[1024,1024]{1,0:T(8,128)(2,1)S(1)}, bf16[1024,1024]{1,0:T(8,128)(2,1)}, u32[]{:S(2)}) copy-start(bf16[1024,1024]{1,0:T(8,128)(2,1)} %param.11) | copy-start | bytes 6291460
  7.2 16.7 %copy-start.5 = (bf16[256,1024]{1,0:T(8,128)(2,1)S(1)}, bf16[256,1024]{1,0:T(8,128)(2,1)}, u32[]{:S(2)}) copy-start(bf16[256,1024]{1,0:T(8,128)(2,1)} %param.9) | copy-start | bytes 1572868
  7.2 16.5 %copy-start.6 = (s32[128,1]{0,1:T(1,128)S(1)}, s32[128,1]{0,1:T(1,128)}, u32[]{:S(2)}) copy-start(s32[128,1]{0,1:T(1,128)} %param.8) | copy-start | bytes 1540
  7.2 51.7 %all-gather.2.cloned.1.call-start = ((), (), s32[]{:S(2)}) async-start(), calls=%async_computation.6 | async-start | bytes 2359296 | tf_op jit(solution)/shard_map/all_gather | solution.py:197
  10.6 27.9 %all-to-all-start = ((bf16[32,8,1024]{2,1,0:T(8,128)(2,1)}), bf16[32,8,1024]{2,1,0:T(8,128)(2,1)S(1)}, u32[]{:S(2)}, u32[]{:S(2)}) async-start(bf16[32,8,1024]{2,1,0:T(8,128)(2,1)} %fusion.17), calls=%async_computation | async-start | bytes 1048576 | tf_op jit(solution)/shard_map/all_to_all | solution.py:204
  20.9 137.5 %reduce-scatter.2.cloned.1.call-start = ((), (), s32[]{:S(2)}) async-start(), calls=%async_computation.7 | async-start | bytes 2359296 | tf_op jit(solution)/shard_map/reduce_scatter | solution.py:228
  20.9 32.2 %collective-permute-start = (bf16[128,1024]{1,0:T(8,128)(2,1)}, bf16[128,1024]{1,0:T(8,128)(2,1)}, u32[]{:S(2)}, u32[]{:S(2)}) collective-permute-start(bf16[128,1024]{1,0:T(8,128)(2,1)} %refs_2_.1), channel_id=1, source_target_pairs={{0,8},{8,0},{1,9},{9,1},{2,10},{10,2},{3,11},{11,3},{4,12},{12,4},... | collective-permute-start | bytes 786440 | tf_op jit(solution)/shard_map/ppermute | solution.py:20
  38.9 9.4 %collective-permute-start.1 = (bf16[128,1024]{1,0:T(8,128)(2,1)S(1)}, bf16[128,1024]{1,0:T(8,128)(2,1)S(1)}, u32[]{:S(2)}, u32[]{:S(2)}) collective-permute-start(bf16[128,1024]{1,0:T(8,128)(2,1)S(1)} %convolution_convert_fusion.2), channel_id=1, source_target_pairs={{0,8},{8,0},{1,9},{9,1},{2,10},{10,2},{3,11},{11,3},{4,12},{12,4},... | collective-permute-start | bytes 786440 | tf_op jit(solution)/shard_map/ppermute | solution.py:20
  48.7 4.4 %collective-permute-start.2 = (bf16[512,256]{1,0:T(8,128)(2,1)S(1)}, bf16[512,256]{1,0:T(8,128)(2,1)S(1)}, u32[]{:S(2)}, u32[]{:S(2)}) collective-permute-start(bf16[512,256]{1,0:T(8,128)(2,1)S(1)} %convolution_convert_fusion), channel_id=1, source_target_pairs={{0,16},{16,0},{1,17},{17,1},{2,18},{18,2},{3,19},{19,3},{4,20},{20... | collective-permute-start | bytes 786440 | tf_op jit(solution)/shard_map/ppermute | solution.py:20
  64.7 1.0 copy-start.4
  65.7 3.8 %collective-permute-start.4 = (bf16[256,1024]{1,0:T(8,128)(2,1)S(1)}, bf16[256,1024]{1,0:T(8,128)(2,1)S(1)}, u32[]{:S(2)}, u32[]{:S(2)}) collective-permute-start(bf16[256,1024]{1,0:T(8,128)(2,1)S(1)} %copy-done.4), channel_id=1, source_target_pairs={{0,16},{16,0},{1,17},{17,1},{2,18},{18,2},{3,19},{19,3},{4,20},{20... | collective-permute-start | bytes 1572872 | tf_op jit(solution)/shard_map/ppermute | solution.py:20
  70.2 1.0 copy-start.1
  71.2 23.1 %all-to-all-start.1 = ((bf16[4,128,1024]{2,1,0:T(8,128)(2,1)}), bf16[4,128,1024]{2,1,0:T(8,128)(2,1)S(1)}, u32[]{:S(2)}, u32[]{:S(2)}) async-start(bf16[4,128,1024]{2,1,0:T(8,128)(2,1)} %bitcast.26), calls=%async_computation.2 | async-start | bytes 2097152 | tf_op jit(solution)/shard_map/all_to_all | solution.py:233
  76.0 18.3 %collective-permute-start.3 = (bf16[128,1024]{1,0:T(8,128)(2,1)}, bf16[128,1024]{1,0:T(8,128)(2,1)S(1)}, u32[]{:S(2)}, u32[]{:S(2)}) collective-permute-start(bf16[128,1024]{1,0:T(8,128)(2,1)} %get-tuple-element.25), channel_id=1, source_target_pairs={{0,8},{8,0},{1,9},{9,1},{2,10},{10,2},{3,11},{11,3},{4,12},{12,4},... | collective-permute-start | bytes 786440 | tf_op jit(solution)/shard_map/ppermute | solution.py:20
  94.4 1.0 copy-start.3
  95.7 0.8 copy-start.2
  96.5 28.1 %all-to-all-start.2 = ((bf16[32,8,1024]{2,1,0:T(8,128)(2,1)}), bf16[32,8,1024]{2,1,0:T(8,128)(2,1)}, u32[]{:S(2)}, u32[]{:S(2)}) async-start(bf16[32,8,1024]{2,1,0:T(8,128)(2,1)} %bitcast.27), calls=%async_computation.3 | async-start | bytes 1048576 | tf_op jit(solution)/shard_map/all_to_all | solution.py:239
  124.6 14.9 %all-to-all-start.3 = ((bf16[8,16,1024]{2,1,0:T(8,128)(2,1)}), bf16[8,16,1024]{2,1,0:T(8,128)(2,1)S(1)}, u32[]{:S(2)}, u32[]{:S(2)}) async-start(bf16[8,16,1024]{2,1,0:T(8,128)(2,1)} %bitcast.10), calls=%async_computation.4 | async-start | bytes 524288 | tf_op jit(solution)/shard_map/all_to_all | solution.py:245
Sparse Core Ops, SparseCore 0:
  10.1 48.7 all-gather.1
  64.9 44.2 reduce-scatter.1

commit v8 on v3

--- a/solution.py
+++ b/solution.py
@@ -11,7 +11,8 @@
 BLK = ("blk_x", "blk_z")
 BF16 = jnp.bfloat16
 F32 = jnp.float32
-ROOM = pltpu.CompilerParams(vmem_limit_bytes=40 * 2**20)
+ROOM = pltpu.CompilerParams(vmem_limit_bytes=24 * 2**20)
+ALL_ROOM = pltpu.CompilerParams(vmem_limit_bytes=56 * 2**20)
 SCALAR = pl.BlockSpec(memory_space=pltpu.SMEM)
 
 
@@ -51,51 +52,74 @@
     return (jnp.arange(feature_count, dtype=jnp.int32)[:, None] == feature[None, :]).astype(BF16)
 
 
-def pair_kernel(factor, place_ref, line_ref, own_ref, mate_ref, kept_ref, sent_ref, line_grad_ref, total):
-    step = pl.program_id(0)
-    rows, clips = line_ref.shape[0], own_ref.shape[0]
-    line = line_ref[...]
-    video = jnp.concatenate([own_ref[...], mate_ref[...]], axis=0)
-    scores = dot_of(video, line, 1, 1)
-    row = lax.broadcasted_iota(jnp.int32, scores.shape, 0)
-    col = lax.broadcasted_iota(jnp.int32, scores.shape, 1) + step * rows
-    labels = ((col == place_ref[0] * clips + row) & (row < clips)).astype(F32)
-    coeffs = (factor * (jax.nn.sigmoid(4.0 * scores - 2.0) - labels)).astype(BF16)
-    part = dot_of(coeffs, line, 1, 0)
-
-    @pl.when(step == 0)
-    def _():
-        total[...] = part
-
-    @pl.when(step > 0)
-    def _():
-        total[...] += part
-
-    line_grad_ref[...] = dot_of(coeffs, video, 0, 0).astype(BF16)
-
-    @pl.when(step == pl.num_programs(0) - 1)
-    def _():
-        kept_ref[...] = total[:clips]
-        sent_ref[...] = total[clips:].astype(BF16)
+def pair_kernel(factor, steps, place_ref, line_hbm, own_hbm, mate_hbm,
+                kept_ref, sent_ref, grads_hbm, line, video, grads, total, came, gone):
+    rows, clips = line.shape[0] // steps, own_hbm.shape[0]
+    loads = [
+        pltpu.make_async_copy(own_hbm, video.at[pl.ds(0, clips)], came.at[0]),
+        pltpu.make_async_copy(mate_hbm, video.at[pl.ds(clips, clips)], came.at[1]),
+    ]
+    for step in range(steps):
+        block = pl.ds(step * rows, rows)
+        loads.append(pltpu.make_async_copy(line_hbm.at[block], line.at[block], came.at[2 + step]))
+    for load in loads:
+        load.start()
+    loads[0].wait()
+    loads[1].wait()
+
+    def coeffs_of(step):
+        block = pl.ds(step * rows, rows)
+        loads[2 + step].wait()
+        scores = dot_of(video[...], line[block], 1, 1)
+        row = lax.broadcasted_iota(jnp.int32, scores.shape, 0)
+        col = lax.broadcasted_iota(jnp.int32, scores.shape, 1) + step * rows
+        labels = ((col == place_ref[0] * clips + row) & (row < clips)).astype(F32)
+        return (factor * (jax.nn.sigmoid(4.0 * scores - 2.0) - labels)).astype(BF16)
+
+    stores = []
+    coeffs = coeffs_of(0)
+    for step in range(steps):
+        block = pl.ds(step * rows, rows)
+        ready = coeffs
+        if step + 1 < steps:
+            coeffs = coeffs_of(step + 1)
+        part = dot_of(ready, line[block], 1, 0)
+        if step == 0:
+            total[...] = part
+        else:
+            total[...] += part
+        grads[block] = dot_of(ready, video[...], 0, 0).astype(BF16)
+        stores.append(pltpu.make_async_copy(grads.at[block], grads_hbm.at[block], gone.at[step]))
+        stores[-1].start()
+    kept_ref[...] = total[:clips]
+    sent_ref[...] = total[clips:].astype(BF16)
+    for store in stores:
+        store.wait()
 
 
 def pair_grads(line, own, mate, place, factor, steps):
     rows, features = line.shape
     clips = own.shape[0]
-    whole = pl.BlockSpec((clips, features), lambda i: (0, 0))
-    part = pl.BlockSpec((rows // steps, features), lambda i: (i, 0))
+    free = pl.BlockSpec(memory_space=pl.ANY)
+    held = pl.BlockSpec(memory_space=pltpu.VMEM)
     return pl.pallas_call(
-        lambda *refs: pair_kernel(factor, *refs),
-        grid=(steps,),
-        in_specs=[SCALAR, part, whole, whole],
-        out_specs=[whole, whole, part],
+        lambda *refs: pair_kernel(factor, steps, *refs),
+        in_specs=[SCALAR, free, free, free],
+        out_specs=[held, held, free],
         out_shape=[
             jax.ShapeDtypeStruct((clips, features), F32),
             jax.ShapeDtypeStruct((clips, features), BF16),
             jax.ShapeDtypeStruct((rows, features), BF16),
         ],
-        scratch_shapes=[pltpu.VMEM((2 * clips, features), F32)],
-        compiler_params=ROOM,
+        scratch_shapes=[
+            pltpu.VMEM((rows, features), BF16),
+            pltpu.VMEM((2 * clips, features), BF16),
+            pltpu.VMEM((rows, features), BF16),
+            pltpu.VMEM((2 * clips, features), F32),
+            pltpu.SemaphoreType.DMA((2 + steps,)),
+            pltpu.SemaphoreType.DMA((steps,)),
+        ],
+        compiler_params=ALL_ROOM,
         cost_estimate=pl.CostEstimate(
             flops=12 * rows * clips * features, bytes_accessed=5 * rows * features, transcendentals=0
         ),

time: 158 us -> 154 us (0.975)
  local copies, waits for them, and re-layouts: 7.96 us -> 2.68 us
    unnamed x24 -> x14, local copies, waits for them, and re-layouts: 7.91 us -> 2.63 us
  transfers between devices with their start and end apart: 12 -> 12, of which waited for: 8 -> 9; matrix products, arithmetic and copies ran while one was open for 7% -> 8% of each run, Pallas kernels for 0% -> 1%
where the time goes in v8:
time: 154 us
  waiting for transfers between devices  54.7 us (36%)
  starting transfers between devices  45 us (29%)
  blocking collectives  18.7 us (12%)
  between operations  14.3 us (9%)
  matrix products  7.22 us (5%)
  Pallas kernels  6.44 us (4%)
  other arithmetic  4.46 us (3%)
  local copies, waits for them, and re-layouts  2.68 us (2%)
    all_to_all x1, blocking collectives, shards(): lax.all_to_all(jnp.broadcast_to(total[None], (blocks, *total.shape)), BLK...  18.7 us
    all_to_all x1, waiting for transfers between devices, shards(): lax.all_to_all(pooled.reshape(peers, capacity, features), WIDE, 0, 0, til...  15.4 us
    all_gather x1, waiting for transfers between devices, shards(): audio_line = lax.all_gather(audio, 'blk_z', axis=0, tiled=True)  13.4 us
    all_to_all x1, starting transfers between devices, shards(): lax.all_to_all(pooled.reshape(peers, capacity, features), WIDE, 0, 0, til...  10.2 us
    ppermute x3, starting transfers between devices, shards(): lax.ppermute(parts[d], ('wide_x', 'blk_x'), pairs).astype(F32)  9.82 us
    all_to_all x1, starting transfers between devices, shards(): lax.all_to_all(packed.reshape(peers, capacity, features), WIDE, 0, 0, til...  9.75 us
    ppermute x4, starting transfers between devices, swapped(): return lax.ppermute(array, axis, [(0, 1), (1, 0)])  9.58 us
    all_to_all x1, waiting for transfers between devices, shards(): lax.all_to_all(summed.reshape(ny, -1, features), 'wide_y', 0, 0, tiled=True)  9.1 us
  transfers between devices with their start and end apart: 12, of which 9 were waited for; matrix products, arithmetic and copies ran while one was open for 8% of the time, Pallas kernels for 1%

profile of v8, /device:TPU:6, one launch (start us, length us, event | category | flops | bytes accessed | tf_op | source)
XLA Modules:
  0.0 153.5 jit_solution(15658309080541282642)
XLA Ops:
  7.2 0.0 copy-start
  7.2 0.0 copy-start.4
  7.2 0.0 all-gather.2.cloned.1.call-start
  7.2 0.7 all-gather.2.cloned.1.call-update
  7.9 2.9 %collective-permute-start = (bf16[128,1024]{1,0:T(8,128)(2,1)}, bf16[128,1024]{1,0:T(8,128)(2,1)}, u32[]{:S(2)}, u32[]{:S(2)}) collective-permute-start(bf16[128,1024]{1,0:T(8,128)(2,1)} %refs_2_.1), channel_id=1, source_target_pairs={{0,8},{8,0},{1,9},{9,1},{2,10},{10,2},{3,11},{11,3},{4,12},{12,4},... | collective-permute-start | bytes 786440 | tf_op jit(solution)/shard_map/ppermute | solution.py:20
  10.8 0.7 convert_rsqrt_fusion
  11.5 2.0 %fusion.17 = bf16[32,8,1024]{2,1,0:T(8,128)(2,1)} fusion(f32[256]{0:T(256)S(1)} %convert_rsqrt_fusion, bf16[256,1024]{1,0:T(8,128)(2,1)} %param.9), kind=kLoop, calls=%fused_computation.27 | loop fusion | flops 786432 | bytes 1049600 | tf_op jit(solution)/shard_map/reshape | solution.py:182
  13.5 10.2 %all-to-all-start = ((bf16[32,8,1024]{2,1,0:T(8,128)(2,1)}), bf16[32,8,1024]{2,1,0:T(8,128)(2,1)S(1)}, u32[]{:S(2)}, u32[]{:S(2)}) async-start(bf16[32,8,1024]{2,1,0:T(8,128)(2,1)} %fusion.17), calls=%async_computation | async-start | bytes 1048576 | tf_op jit(solution)/shard_map/all_to_all | solution.py:181
  23.7 0.0 reduce-scatter.2.cloned.1.call-start
  23.8 0.1 convert_reduce_fusion.1
  24.0 2.0 %fusion.8 = f32[256,1024]{1,0:T(8,128)} fusion(bf16[1024,1024]{1,0:T(8,128)(2,1)S(1)} %copy-done, bf16[256,1024]{1,0:T(8,128)(2,1)S(1)} %copy-done.4, f32[256]{0:T(256)S(1)} %convert_rsqrt_fusion), kind=kOutput, calls=%fused_computation.13 | convolution fusion | flops 539754496 | bytes 3671040 | tf_op jit(solution)/shard_map/dot_general | solution.py:24
  26.0 15.4 %all-to-all-done = bf16[32,8,1024]{2,1,0:T(8,128)(2,1)S(1)} async-done(((bf16[32,8,1024]{2,1,0:T(8,128)(2,1)}), bf16[32,8,1024]{2,1,0:T(8,128)(2,1)S(1)}, u32[]{:S(2)}, u32[]{:S(2)}) %all-to-all-start) | async-done | bytes 524320 | tf_op jit(solution)/shard_map/all_to_all | solution.py:181
  41.4 0.3 convolution_convert_fusion
  41.7 0.5 fusion.14.slope_ref
  42.2 0.5 fusion.3
  42.7 1.9 %collective-permute-start.1 = (bf16[128,512]{1,0:T(8,128)(2,1)S(1)}, bf16[128,512]{1,0:T(8,128)(2,1)S(1)}, u32[]{:S(2)}, u32[]{:S(2)}) collective-permute-start(bf16[128,512]{1,0:T(8,128)(2,1)S(1)} %fusion.3), channel_id=1, source_target_pairs={{0,16},{16,0},{1,17},{17,1},{2,18},{18,2},{3,19},{19,3},{4,20},{20... | collective-permute-start | bytes 393224 | tf_op jit(solution)/shard_map/ppermute | solution.py:20
  44.7 1.1 fusion.4.own_picked
  45.8 0.0 collective-permute-done.refs_3_
  45.8 0.2 collective-permute-done.1.mate_picked
  46.0 13.4 %all-gather.2.cloned.1.call-done.refs_1_ = bf16[1024,1024]{1,0:T(8,128)(2,1)} async-done(((bf16[128,1024]{1,0:T(8,128)(2,1)}), bf16[1024,1024]{1,0:T(8,128)(2,1)}) %all-gather.2.cloned.1.call-update) | async-done | bytes 2097168 | tf_op jit(solution)/shard_map/all_gather | solution.py:174
  59.4 5.6 %shard_map.85 = (f32[128,1024]{1,0:T(8,128)}, bf16[128,1024]{1,0:T(8,128)(2,1)}, bf16[1024,1024]{1,0:T(8,128)(2,1)}) custom-call(s32[1]{0:T(128)} %bitcast.refs_0_, bf16[1024,1024]{1,0:T(8,128)(2,1)} %all-gather.2.cloned.1.call-done.refs_1_, bf16[128,1024]{1,0:T(8,128)(2,1)} %refs_2_.1, bf16[128,1024]{1,0:T(8,128)(2,1)} %collective-permute-done.refs_3_), custom_call_target="tpu_custom_call" | custom-call | flops 1610612736 | bytes 5242880 | tf_op jit(solution)/shard_map/pallas_call | solution.py:105
  65.1 0.0 copy-start.1
  65.1 0.0 reduce-scatter.2.cloned.1.call-update
  65.1 0.9 copy-done.5
  66.0 2.7 %collective-permute-start.2 = (bf16[128,1024]{1,0:T(8,128)(2,1)S(1)}, bf16[128,1024]{1,0:T(8,128)(2,1)S(1)}, u32[]{:S(2)}, u32[]{:S(2)}) collective-permute-start(bf16[128,1024]{1,0:T(8,128)(2,1)S(1)} %copy-done.5), channel_id=1, source_target_pairs={{0,8},{8,0},{1,9},{9,1},{2,10},{10,2},{3,11},{11,3},{4,12},{12,4},... | collective-permute-start | bytes 786440 | tf_op jit(solution)/shard_map/ppermute | solution.py:20
  68.7 5.5 %collective-permute-done.2.arrived_ref = bf16[128,1024]{1,0:T(8,128)(2,1)S(1)} collective-permute-done((bf16[128,1024]{1,0:T(8,128)(2,1)S(1)}, bf16[128,1024]{1,0:T(8,128)(2,1)S(1)}, u32[]{:S(2)}, u32[]{:S(2)}) %collective-permute-start.2) | collective-permute-done | bytes 262176 | tf_op jit(solution)/shard_map/ppermute | solution.py:20
  74.3 0.3 shard_map.86
  74.6 0.0 copy-start.2
  74.6 0.8 copy-done.2
  75.4 9.8 %all-to-all-start.1 = ((bf16[32,8,1024]{2,1,0:T(8,128)(2,1)}), bf16[32,8,1024]{2,1,0:T(8,128)(2,1)S(1)}, u32[]{:S(2)}, u32[]{:S(2)}) async-start(bf16[32,8,1024]{2,1,0:T(8,128)(2,1)} %bitcast.28), calls=%async_computation.2 | async-start | bytes 1048576 | tf_op jit(solution)/shard_map/all_to_all | solution.py:205
  85.2 2.1 %collective-permute-start.3 = (bf16[128,1024]{1,0:T(8,128)(2,1)S(1)}, bf16[128,1024]{1,0:T(8,128)(2,1)S(1)}, u32[]{:S(2)}, u32[]{:S(2)}) collective-permute-start(bf16[128,1024]{1,0:T(8,128)(2,1)S(1)} %get-tuple-element.32.own_pre), channel_id=1, source_target_pairs={{0,16},{16,0},{1,17},{17,1},{2,18},{18,2},{3,19},{19,3},{4,20},{20... | collective-permute-start | bytes 786440 | tf_op jit(solution)/shard_map/ppermute | solution.py:20
  87.2 1.4 collective-permute-done.3.mate_pre
  88.6 0.9 copy-done.3
  89.5 0.5 shard_map.87
  90.0 2.1 %collective-permute-start.4 = (bf16[128,1024]{1,0:T(8,128)(2,1)S(1)}, bf16[128,1024]{1,0:T(8,128)(2,1)S(1)}, u32[]{:S(2)}, u32[]{:S(2)}) collective-permute-start(bf16[128,1024]{1,0:T(8,128)(2,1)S(1)} %get-tuple-element.34), channel_id=1, source_target_pairs={{0,32},{8,40},{32,0},{40,8},{1,33},{9,41},{33,1},{41,9},{2,34},{10... | collective-permute-start | bytes 786440 | tf_op jit(solution)/shard_map/ppermute | solution.py:214
  92.1 2.9 %collective-permute-start.5 = (bf16[128,1024]{1,0:T(8,128)(2,1)S(1)}, bf16[128,1024]{1,0:T(8,128)(2,1)S(1)}, u32[]{:S(2)}, u32[]{:S(2)}) collective-permute-start(bf16[128,1024]{1,0:T(8,128)(2,1)S(1)} %get-tuple-element.35), channel_id=1, source_target_pairs={{0,8},{8,0},{32,40},{40,32},{1,9},{9,1},{33,41},{41,33},{2,10},{10... | collective-permute-start | bytes 786440 | tf_op jit(solution)/shard_map/ppermute | solution.py:214
  95.1 4.7 %collective-permute-start.6 = (bf16[128,1024]{1,0:T(8,128)(2,1)S(1)}, bf16[128,1024]{1,0:T(8,128)(2,1)S(1)}, u32[]{:S(2)}, u32[]{:S(2)}) collective-permute-start(bf16[128,1024]{1,0:T(8,128)(2,1)S(1)} %get-tuple-element.36), channel_id=1, source_target_pairs={{0,40},{8,32},{32,8},{40,0},{1,41},{9,33},{33,9},{41,1},{2,42},{10... | collective-permute-start | bytes 786440 | tf_op jit(solution)/shard_map/ppermute | solution.py:214
  99.8 3.8 %collective-permute-done.4 = bf16[128,1024]{1,0:T(8,128)(2,1)S(1)} collective-permute-done((bf16[128,1024]{1,0:T(8,128)(2,1)S(1)}, bf16[128,1024]{1,0:T(8,128)(2,1)S(1)}, u32[]{:S(2)}, u32[]{:S(2)}) %collective-permute-start.4) | collective-permute-done | bytes 262176 | tf_op jit(solution)/shard_map/ppermute | solution.py:214
  103.7 4.4 %collective-permute-done.5 = bf16[128,1024]{1,0:T(8,128)(2,1)S(1)} collective-permute-done((bf16[128,1024]{1,0:T(8,128)(2,1)S(1)}, bf16[128,1024]{1,0:T(8,128)(2,1)S(1)}, u32[]{:S(2)}, u32[]{:S(2)}) %collective-permute-start.5) | collective-permute-done | bytes 262176 | tf_op jit(solution)/shard_map/ppermute | solution.py:214
  108.1 0.7 collective-permute-done.6
  108.8 0.9 add_convert_fusion
  109.7 0.0 all-to-all-done.1
  109.7 5.5 %all-to-all-start.2 = ((bf16[8,16,1024]{2,1,0:T(8,128)(2,1)}), bf16[8,16,1024]{2,1,0:T(8,128)(2,1)S(1)}, u32[]{:S(2)}, u32[]{:S(2)}) async-start(bf16[8,16,1024]{2,1,0:T(8,128)(2,1)} %bitcast.9), calls=%async_computation.3 | async-start | bytes 524288 | tf_op jit(solution)/shard_map/all_to_all | solution.py:218
  115.2 2.8 %fusion.2 = bf16[256,1024]{1,0:T(8,128)(2,1)} fusion(bf16[1024,1024]{1,0:T(8,128)(2,1)S(1)} %copy-done, f32[256,1024]{1,0:T(8,128)} %fusion.8, bf16[256,1024]{1,0:T(8,128)(2,1)S(1)} %bitcast.30, f32[256]{0:T(256)S(1)} %convert_rsqrt_fusion), kind=kOutput, calls=%fused_computation.6 | convolution fusion | flops 538181632 | bytes 4195328 | tf_op jit(solution)/shard_map/dot_general | solution.py:24
  118.0 9.1 %all-to-all-done.2 = bf16[8,16,1024]{2,1,0:T(8,128)(2,1)S(1)} async-done(((bf16[8,16,1024]{2,1,0:T(8,128)(2,1)}), bf16[8,16,1024]{2,1,0:T(8,128)(2,1)S(1)}, u32[]{:S(2)}, u32[]{:S(2)}) %all-to-all-start.2) | async-done | bytes 262176 | tf_op jit(solution)/shard_map/all_to_all | solution.py:218
  127.1 0.1 broadcast_in_dim.8
  127.2 18.7 %all_to_all.20 = bf16[16,16,1024]{2,1,0:T(8,128)(2,1)S(1)} all-to-all(bf16[16,16,1024]{2,1,0:T(8,128)(2,1)S(1)} %broadcast_in_dim.8), channel_id=1, replica_groups=mesh['wide_y'=8,'wide_x'=2,'wide_c'=2,'blk_x'=2,'blk_z'=8] {'blk_x','blk..., dimensions={0} | all-to-all | bytes 1048576 | tf_op jit(solution)/shard_map/all_to_all | solution.py:223
  146.0 0.7 convert_reduce_fusion
  (13 shorter events, 0.1 us)
Async XLA Ops:
  7.2 16.8 %copy-start = (bf16[1024,1024]{1,0:T(8,128)(2,1)S(1)}, bf16[1024,1024]{1,0:T(8,128)(2,1)}, u32[]{:S(2)}) copy-start(bf16[1024,1024]{1,0:T(8,128)(2,1)} %param.11) | copy-start | bytes 6291460
  7.2 16.8 %copy-start.4 = (bf16[256,1024]{1,0:T(8,128)(2,1)S(1)}, bf16[256,1024]{1,0:T(8,128)(2,1)}, u32[]{:S(2)}) copy-start(bf16[256,1024]{1,0:T(8,128)(2,1)} %param.9) | copy-start | bytes 1572868
  7.2 16.6 %copy-start.6 = (s32[128,1]{0,1:T(1,128)S(1)}, s32[128,1]{0,1:T(1,128)}, u32[]{:S(2)}) copy-start(s32[128,1]{0,1:T(1,128)} %param.8) | copy-start | bytes 1540
  7.2 52.2 %all-gather.2.cloned.1.call-start = ((), (), s32[]{:S(2)}) async-start(), calls=%async_computation.5 | async-start | bytes 2359296 | tf_op jit(solution)/shard_map/all_gather | solution.py:174
  7.9 37.9 %collective-permute-start = (bf16[128,1024]{1,0:T(8,128)(2,1)}, bf16[128,1024]{1,0:T(8,128)(2,1)}, u32[]{:S(2)}, u32[]{:S(2)}) collective-permute-start(bf16[128,1024]{1,0:T(8,128)(2,1)} %refs_2_.1), channel_id=1, source_target_pairs={{0,8},{8,0},{1,9},{9,1},{2,10},{10,2},{3,11},{11,3},{4,12},{12,4},... | collective-permute-start | bytes 786440 | tf_op jit(solution)/shard_map/ppermute | solution.py:20
  13.5 27.9 %all-to-all-start = ((bf16[32,8,1024]{2,1,0:T(8,128)(2,1)}), bf16[32,8,1024]{2,1,0:T(8,128)(2,1)S(1)}, u32[]{:S(2)}, u32[]{:S(2)}) async-start(bf16[32,8,1024]{2,1,0:T(8,128)(2,1)} %fusion.17), calls=%async_computation | async-start | bytes 1048576 | tf_op jit(solution)/shard_map/all_to_all | solution.py:181
  23.7 123.0 %reduce-scatter.2.cloned.1.call-start = ((), (), s32[]{:S(2)}) async-start(), calls=%async_computation.6 | async-start | bytes 2359296 | tf_op jit(solution)/shard_map/reduce_scatter | solution.py:202
  42.7 3.2 %collective-permute-start.1 = (bf16[128,512]{1,0:T(8,128)(2,1)S(1)}, bf16[128,512]{1,0:T(8,128)(2,1)S(1)}, u32[]{:S(2)}, u32[]{:S(2)}) collective-permute-start(bf16[128,512]{1,0:T(8,128)(2,1)S(1)} %fusion.3), channel_id=1, source_target_pairs={{0,16},{16,0},{1,17},{17,1},{2,18},{18,2},{3,19},{19,3},{4,20},{20... | collective-permute-start | bytes 393224 | tf_op jit(solution)/shard_map/ppermute | solution.py:20
  65.1 1.0 copy-start.5
  65.1 9.2 %copy-start.1 = (f32[128,1024]{1,0:T(8,128)S(1)}, f32[128,1024]{1,0:T(8,128)}, u32[]{:S(2)}) copy-start(f32[128,1024]{1,0:T(8,128)} %get-tuple-element.28.kept_ref) | copy-start | bytes 1572868
  66.0 8.3 %collective-permute-start.2 = (bf16[128,1024]{1,0:T(8,128)(2,1)S(1)}, bf16[128,1024]{1,0:T(8,128)(2,1)S(1)}, u32[]{:S(2)}, u32[]{:S(2)}) collective-permute-start(bf16[128,1024]{1,0:T(8,128)(2,1)S(1)} %copy-done.5), channel_id=1, source_target_pairs={{0,8},{8,0},{1,9},{9,1},{2,10},{10,2},{3,11},{11,3},{4,12},{12,4},... | collective-permute-start | bytes 786440 | tf_op jit(solution)/shard_map/ppermute | solution.py:20
  74.6 0.8 copy-start.2
  75.4 34.3 %all-to-all-start.1 = ((bf16[32,8,1024]{2,1,0:T(8,128)(2,1)}), bf16[32,8,1024]{2,1,0:T(8,128)(2,1)S(1)}, u32[]{:S(2)}, u32[]{:S(2)}) async-start(bf16[32,8,1024]{2,1,0:T(8,128)(2,1)} %bitcast.28), calls=%async_computation.2 | async-start | bytes 1048576 | tf_op jit(solution)/shard_map/all_to_all | solution.py:205
  85.2 3.4 %collective-permute-start.3 = (bf16[128,1024]{1,0:T(8,128)(2,1)S(1)}, bf16[128,1024]{1,0:T(8,128)(2,1)S(1)}, u32[]{:S(2)}, u32[]{:S(2)}) collective-permute-start(bf16[128,1024]{1,0:T(8,128)(2,1)S(1)} %get-tuple-element.32.own_pre), channel_id=1, source_target_pairs={{0,16},{16,0},{1,17},{17,1},{2,18},{18,2},{3,19},{19,3},{4,20},{20... | collective-permute-start | bytes 786440 | tf_op jit(solution)/shard_map/ppermute | solution.py:20
  88.6 0.9 copy-start.3
  90.0 13.7 %collective-permute-start.4 = (bf16[128,1024]{1,0:T(8,128)(2,1)S(1)}, bf16[128,1024]{1,0:T(8,128)(2,1)S(1)}, u32[]{:S(2)}, u32[]{:S(2)}) collective-permute-start(bf16[128,1024]{1,0:T(8,128)(2,1)S(1)} %get-tuple-element.34), channel_id=1, source_target_pairs={{0,32},{8,40},{32,0},{40,8},{1,33},{9,41},{33,1},{41,9},{2,34},{10... | collective-permute-start | bytes 786440 | tf_op jit(solution)/shard_map/ppermute | solution.py:214
  92.1 16.0 %collective-permute-start.5 = (bf16[128,1024]{1,0:T(8,128)(2,1)S(1)}, bf16[128,1024]{1,0:T(8,128)(2,1)S(1)}, u32[]{:S(2)}, u32[]{:S(2)}) collective-permute-start(bf16[128,1024]{1,0:T(8,128)(2,1)S(1)} %get-tuple-element.35), channel_id=1, source_target_pairs={{0,8},{8,0},{32,40},{40,32},{1,9},{9,1},{33,41},{41,33},{2,10},{10... | collective-permute-start | bytes 786440 | tf_op jit(solution)/shard_map/ppermute | solution.py:214
  95.1 13.8 %collective-permute-start.6 = (bf16[128,1024]{1,0:T(8,128)(2,1)S(1)}, bf16[128,1024]{1,0:T(8,128)(2,1)S(1)}, u32[]{:S(2)}, u32[]{:S(2)}) collective-permute-start(bf16[128,1024]{1,0:T(8,128)(2,1)S(1)} %get-tuple-element.36), channel_id=1, source_target_pairs={{0,40},{8,32},{32,8},{40,0},{1,41},{9,33},{33,9},{41,1},{2,42},{10... | collective-permute-start | bytes 786440 | tf_op jit(solution)/shard_map/ppermute | solution.py:214
  109.7 17.4 %all-to-all-start.2 = ((bf16[8,16,1024]{2,1,0:T(8,128)(2,1)}), bf16[8,16,1024]{2,1,0:T(8,128)(2,1)S(1)}, u32[]{:S(2)}, u32[]{:S(2)}) async-start(bf16[8,16,1024]{2,1,0:T(8,128)(2,1)} %bitcast.9), calls=%async_computation.3 | async-start | bytes 524288 | tf_op jit(solution)/shard_map/all_to_all | solution.py:218
Sparse Core Ops, SparseCore 0:
  10.1 49.2 all-gather.1
  65.2 43.3 reduce-scatter.1

commit v9 on v8

--- a/solution.py
+++ b/solution.py
@@ -31,11 +31,10 @@
     return cdf + v * (0.3989422804014327 * jnp.exp(-0.5 * v * v))
 
 
-def targets_of(owner, capacity):
-    ids = jnp.arange(owner.shape[0], dtype=jnp.int32)
-    peer = owner[:, 0]
+def ranks_of(peer):
+    ids = jnp.arange(peer.shape[0], dtype=jnp.int32)
     before = (peer[:, None] == peer[None, :]) & (ids[:, None] < ids[None, :])
-    return peer * capacity + jnp.sum(before.astype(jnp.int32), axis=0)
+    return jnp.sum(before.astype(jnp.int32), axis=0)
 
 
 def picking_of(core, feature_count):
@@ -126,44 +125,69 @@
     )(place, line, own, mate)
 
 
-def clip_kernel(kept_ref, arrived_ref, slope_ref, target_ref, packed_ref, pre_ref):
+def clip_kernel(kept_ref, arrived_ref, slope_ref, place_ref, stay_ref, give_ref):
     grad = (kept_ref[...] + arrived_ref[...].astype(F32)).astype(BF16)
-    pre_ref[...] = (grad.astype(F32) * slope_ref[...]).astype(BF16)
-    slots, clips = packed_ref.shape[0], grad.shape[0]
+    slots, clips = stay_ref.shape[0], grad.shape[0]
     slot = lax.broadcasted_iota(jnp.int32, (slots, clips), 0)
-    placing = (slot == target_ref[...]).astype(BF16)
-    packed_ref[...] = dot_of(placing, grad, 1, 0).astype(BF16)
-
-
-def clip_grads(kept, arrived, slope, targets, slots):
+    stay_ref[...] = dot_of((slot == place_ref[...]).astype(BF16), grad, 1, 0).astype(BF16)
+    other = dot_of((slot + slots == place_ref[...]).astype(BF16), grad, 1, 0)
+    give_ref[pl.ds(0, slots)] = other.astype(BF16)
+    give_ref[pl.ds(slots, clips)] = (grad.astype(F32) * slope_ref[...]).astype(BF16)
+
+
+def clip_grads(kept, arrived, slope, places, slots):
     clips, features = kept.shape
     return pl.pallas_call(
         clip_kernel,
         out_shape=[
-            jax.ShapeDtypeStruct((slots, features), BF16),
-            jax.ShapeDtypeStruct((clips, features), BF16),
+            jax.ShapeDtypeStruct((slots // 2, features), BF16),
+            jax.ShapeDtypeStruct((slots // 2 + clips, features), BF16),
         ],
         compiler_params=ROOM,
-    )(kept, arrived, slope, targets[None, :])
-
-
-def weight_kernel(own_picked, mate_picked, own_pre, mate_pre, *out_refs):
+    )(kept, arrived, slope, places[None, :])
+
+
+def merge_kernel(core_ref, stay_ref, got_ref, out_ref):
+    count, lines, features = out_ref.shape
+    shape = (count, lines // 2, features)
+    stay = stay_ref[...].astype(F32).reshape(shape)
+    got = got_ref[pl.ds(0, stay_ref.shape[0])].astype(F32).reshape(shape)
+    first = core_ref[0] == 0
+    pair = [jnp.where(first, stay, got), jnp.where(first, got, stay)]
+    out_ref[...] = jnp.concatenate(pair, axis=1).astype(BF16)
+
+
+def merged(stay, got, core, count):
+    rows, features = stay.shape
+    held = pl.BlockSpec(memory_space=pltpu.VMEM)
+    return pl.pallas_call(
+        merge_kernel,
+        in_specs=[SCALAR, held, held],
+        out_specs=held,
+        out_shape=jax.ShapeDtypeStruct((count, 2 * rows // count, features), BF16),
+        compiler_params=ROOM,
+    )(core, stay, got)
+
+
+def weight_kernel(own_picked, mate_picked, own_ref, mate_ref, *out_refs):
     share = out_refs[0].shape[0]
+    clips = own_picked.shape[0]
+    rows = pl.ds(own_ref.shape[0] - clips, clips)
     picked = jnp.concatenate([own_picked[...], mate_picked[...]], axis=0)
-    pre = jnp.concatenate([own_pre[...], mate_pre[...]], axis=0)
+    pre = jnp.concatenate([own_ref[rows], mate_ref[rows]], axis=0)
     product = dot_of(picked, pre, 0, 0)
     for d, out_ref in enumerate(out_refs):
         out_ref[...] = product[d * share : (d + 1) * share].astype(out_ref.dtype)
 
 
-def weight_parts(own_picked, mate_picked, own_pre, mate_pre, count):
-    half, features = own_picked.shape[1], own_pre.shape[1]
+def weight_parts(own_picked, mate_picked, own, mate, count):
+    half, features = own_picked.shape[1], own.shape[1]
     shape = (half // count, features)
     return pl.pallas_call(
         weight_kernel,
         out_shape=[jax.ShapeDtypeStruct(shape, F32 if d == 0 else BF16) for d in range(count)],
         compiler_params=ROOM,
-    )(own_picked, mate_picked, own_pre, mate_pre)
+    )(own_picked, mate_picked, own, mate)
 
 
 def shards(audio, video, owner, clip_feats, lengths, proj_weight):
@@ -184,30 +208,33 @@
     video_mate = swapped(video, "blk_x")
     slope_own = gelu_slope(dot_of(pooled, proj_weight, 1, 0))
 
-    targets = targets_of(owner, capacity)
-    placing = (targets[:, None] == jnp.arange(slots, dtype=jnp.int32)[None, :]).astype(BF16)
+    peer = owner[:, 0]
+    ranks = ranks_of(peer)
+    slot_of = peer * capacity + ranks
+    placing = (slot_of[:, None] == jnp.arange(slots, dtype=jnp.int32)[None, :]).astype(BF16)
+    places = (((peer % 2) ^ core) * (peers // 2) + peer // 2) * capacity + ranks
     clip_rows = dot_of(placing, pooled_slots, 1, 0).astype(BF16)
     slope_rows = gelu_slope(dot_of(clip_rows, proj_weight, 1, 0))
     picked = dot_of(clip_rows, picking_of(core, features), 1, 0).astype(BF16)
     picked_mate = swapped(
         dot_of(clip_rows, picking_of(1 - core, features), 1, 0).astype(BF16), "wide_c"
     )
-    audio_line, video_mate, slope_rows, picked, picked_mate, slope_own, targets = (
+    audio_line, video_mate, slope_rows, picked, picked_mate, slope_own, places = (
         lax.optimization_barrier(
-            (audio_line, video_mate, slope_rows, picked, picked_mate, slope_own, targets)
+            (audio_line, video_mate, slope_rows, picked, picked_mate, slope_own, places)
         )
     )
 
     kept, sent, line_grads = pair_grads(audio_line, video, video_mate, place, 4.0 / blocks, 4)
     audio_grad = lax.psum_scatter(line_grads, "blk_z", scatter_dimension=0, tiled=True)
     arrived = swapped(sent, "blk_x")
-    packed, pre_rows = clip_grads(kept, arrived, slope_rows, targets, slots)
-    received = lax.all_to_all(
-        packed.reshape(peers, capacity, features), WIDE, 0, 0, tiled=True
-    ).reshape(slots, features)
-
-    pre_mate = swapped(pre_rows, "wide_c")
-    parts = weight_parts(picked, picked_mate, pre_rows, pre_mate, 4)
+    stay, give = clip_grads(kept, arrived, slope_rows, places, slots)
+    got = swapped(give, "wide_c")
+    packed = merged(stay, got, core.astype(jnp.int32)[None], peers // 2)
+    received = lax.all_to_all(packed, ("wide_y", "wide_x"), 0, 0, tiled=True)
+    received = received.reshape(slots, features)
+
+    parts = weight_parts(picked, picked_mate, give, got, 4)
     summed = parts[0]
     for d in (2, 1, 3):
         pairs = [(at, at ^ d) for at in range(4)]

time: 154 us -> 157 us (1.019)
  waiting for transfers between devices: 54.7 us -> 58.1 us
  local copies, waits for them, and re-layouts: 2.68 us -> 0.88 us
    ppermute x3, waiting for transfers between devices: 9.01 us -> 11.5 us  [shards(): lax.ppermute(parts[d], ('wide_x', 'blk_x'), pairs).astype(F32)]
    unnamed x14, local copies, waits for them, and re-layouts: 2.63 us -> 0.83 us
  transfers between devices with their start and end apart: 12 -> 12, of which waited for: 9 -> 9; matrix products, arithmetic and copies ran while one was open for 8% -> 7% of each run, Pallas kernels for 1% -> 1%
where the time goes in v9:
time: 157 us; the launch traced here: 156 us
  waiting for transfers between devices  58.1 us (37%)
  starting transfers between devices  46 us (29%)
  blocking collectives  18.6 us (12%)
  between operations  14.3 us (9%)
  Pallas kernels  7.31 us (5%)
  matrix products  6.38 us (4%)
  other arithmetic  4.49 us (3%)
    all_to_all x1, blocking collectives, shards(): lax.all_to_all(jnp.broadcast_to(total[None], (blocks, *total.shape)), BLK...  18.6 us
    all_to_all x1, waiting for transfers between devices, shards(): lax.all_to_all(pooled.reshape(peers, capacity, features), WIDE, 0, 0, til...  15.4 us
    all_gather x1, waiting for transfers between devices, shards(): audio_line = lax.all_gather(audio, 'blk_z', axis=0, tiled=True)  13.4 us
    ppermute x3, waiting for transfers between devices, shards(): lax.ppermute(parts[d], ('wide_x', 'blk_x'), pairs).astype(F32)  11.5 us
    all_to_all x1, starting transfers between devices, shards(): lax.all_to_all(pooled.reshape(peers, capacity, features), WIDE, 0, 0, til...  10.2 us
    ppermute x3, starting transfers between devices, shards(): lax.ppermute(parts[d], ('wide_x', 'blk_x'), pairs).astype(F32)  9.95 us
    all_to_all x1, starting transfers between devices, shards(): received = lax.all_to_all(packed, ('wide_y', 'wide_x'), 0, 0, tiled=True)  9.61 us
    ppermute x4, starting transfers between devices, swapped(): return lax.ppermute(array, axis, [(0, 1), (1, 0)])  9.58 us
  transfers between devices with their start and end apart: 12, of which 9 were waited for; matrix products, arithmetic and copies ran while one was open for 7% of the time, Pallas kernels for 1%

profile of v9, /device:TPU:6, one launch (start us, length us, event | category | flops | bytes accessed | tf_op | source)
XLA Modules:
  0.0 156.1 jit_solution(11521371374770822064)
XLA Ops:
  7.2 0.0 copy-start
  7.2 0.0 copy-start.5
  7.2 0.0 all-gather.2.cloned.1.call-start
  7.2 0.7 all-gather.2.cloned.1.call-update
  7.9 2.9 %collective-permute-start = (bf16[128,1024]{1,0:T(8,128)(2,1)}, bf16[128,1024]{1,0:T(8,128)(2,1)}, u32[]{:S(2)}, u32[]{:S(2)}) collective-permute-start(bf16[128,1024]{1,0:T(8,128)(2,1)} %refs_2_.1), channel_id=1, source_target_pairs={{0,8},{8,0},{1,9},{9,1},{2,10},{10,2},{3,11},{11,3},{4,12},{12,4},... | collective-permute-start | bytes 786440 | tf_op jit(solution)/shard_map/ppermute | solution.py:20
  10.8 0.7 convert_rsqrt_fusion
  11.5 2.0 %fusion.17 = bf16[32,8,1024]{2,1,0:T(8,128)(2,1)} fusion(f32[256]{0:T(256)S(1)} %convert_rsqrt_fusion, bf16[256,1024]{1,0:T(8,128)(2,1)} %param.9), kind=kLoop, calls=%fused_computation.27 | loop fusion | flops 786432 | bytes 1049600 | tf_op jit(solution)/shard_map/reshape | solution.py:206
  13.5 10.2 %all-to-all-start = ((bf16[32,8,1024]{2,1,0:T(8,128)(2,1)}), bf16[32,8,1024]{2,1,0:T(8,128)(2,1)S(1)}, u32[]{:S(2)}, u32[]{:S(2)}) async-start(bf16[32,8,1024]{2,1,0:T(8,128)(2,1)} %fusion.17), calls=%async_computation | async-start | bytes 1048576 | tf_op jit(solution)/shard_map/all_to_all | solution.py:205
  23.7 0.0 reduce-scatter.2.cloned.1.call-start
  23.8 0.0 copy-done.6
  23.8 0.1 convert_reduce_fusion.1
  24.0 2.0 %fusion.8 = f32[256,1024]{1,0:T(8,128)} fusion(bf16[1024,1024]{1,0:T(8,128)(2,1)S(1)} %copy-done, bf16[256,1024]{1,0:T(8,128)(2,1)S(1)} %copy-done.5, f32[256]{0:T(256)S(1)} %convert_rsqrt_fusion), kind=kOutput, calls=%fused_computation.13 | convolution fusion | flops 539754496 | bytes 3671040 | tf_op jit(solution)/shard_map/dot_general | solution.py:24
  26.0 15.4 %all-to-all-done = bf16[32,8,1024]{2,1,0:T(8,128)(2,1)S(1)} async-done(((bf16[32,8,1024]{2,1,0:T(8,128)(2,1)}), bf16[32,8,1024]{2,1,0:T(8,128)(2,1)S(1)}, u32[]{:S(2)}, u32[]{:S(2)}) %all-to-all-start) | async-done | bytes 524320 | tf_op jit(solution)/shard_map/all_to_all | solution.py:205
  41.4 0.3 convolution_convert_fusion
  41.7 0.5 fusion.14.slope_ref
  42.2 0.5 fusion.3
  42.7 1.9 %collective-permute-start.1 = (bf16[128,512]{1,0:T(8,128)(2,1)S(1)}, bf16[128,512]{1,0:T(8,128)(2,1)S(1)}, u32[]{:S(2)}, u32[]{:S(2)}) collective-permute-start(bf16[128,512]{1,0:T(8,128)(2,1)S(1)} %fusion.3), channel_id=1, source_target_pairs={{0,16},{16,0},{1,17},{17,1},{2,18},{18,2},{3,19},{19,3},{4,20},{20... | collective-permute-start | bytes 393224 | tf_op jit(solution)/shard_map/ppermute | solution.py:20
  44.7 0.5 fusion.4.own_picked
  45.2 0.0 collective-permute-done.refs_3_
  45.2 0.8 collective-permute-done.1.mate_picked
  46.0 13.4 %all-gather.2.cloned.1.call-done.refs_1_ = bf16[1024,1024]{1,0:T(8,128)(2,1)} async-done(((bf16[128,1024]{1,0:T(8,128)(2,1)}), bf16[1024,1024]{1,0:T(8,128)(2,1)}) %all-gather.2.cloned.1.call-update) | async-done | bytes 2097168 | tf_op jit(solution)/shard_map/all_gather | solution.py:198
  59.4 5.6 %shard_map.85 = (f32[128,1024]{1,0:T(8,128)}, bf16[128,1024]{1,0:T(8,128)(2,1)}, bf16[1024,1024]{1,0:T(8,128)(2,1)}) custom-call(s32[1]{0:T(128)} %bitcast.refs_0_, bf16[1024,1024]{1,0:T(8,128)(2,1)} %all-gather.2.cloned.1.call-done.refs_1_, bf16[128,1024]{1,0:T(8,128)(2,1)} %refs_2_.1, bf16[128,1024]{1,0:T(8,128)(2,1)} %collective-permute-done.refs_3_), custom_call_target="tpu_custom_call" | custom-call | flops 1610612736 | bytes 5242880 | tf_op jit(solution)/shard_map/pallas_call | solution.py:104
  65.0 0.0 copy-start.1
  65.1 0.0 reduce-scatter.2.cloned.1.call-update
  65.1 2.9 %collective-permute-start.2 = (bf16[128,1024]{1,0:T(8,128)(2,1)}, bf16[128,1024]{1,0:T(8,128)(2,1)S(1)}, u32[]{:S(2)}, u32[]{:S(2)}) collective-permute-start(bf16[128,1024]{1,0:T(8,128)(2,1)} %get-tuple-element.29), channel_id=1, source_target_pairs={{0,8},{8,0},{1,9},{9,1},{2,10},{10,2},{3,11},{11,3},{4,12},{12,4},... | collective-permute-start | bytes 786440 | tf_op jit(solution)/shard_map/ppermute | solution.py:20
  68.0 5.7 %collective-permute-done.2.arrived_ref = bf16[128,1024]{1,0:T(8,128)(2,1)S(1)} collective-permute-done((bf16[128,1024]{1,0:T(8,128)(2,1)}, bf16[128,1024]{1,0:T(8,128)(2,1)S(1)}, u32[]{:S(2)}, u32[]{:S(2)}) %collective-permute-start.2) | collective-permute-done | bytes 262176 | tf_op jit(solution)/shard_map/ppermute | solution.py:20
  73.7 0.3 shard_map.86
  74.0 1.9 %collective-permute-start.3 = (bf16[256,1024]{1,0:T(8,128)(2,1)S(1)}, bf16[256,1024]{1,0:T(8,128)(2,1)S(1)}, u32[]{:S(2)}, u32[]{:S(2)}) collective-permute-start(bf16[256,1024]{1,0:T(8,128)(2,1)S(1)} %get-tuple-element.32.own_ref), channel_id=1, source_target_pairs={{0,16},{16,0},{1,17},{17,1},{2,18},{18,2},{3,19},{19,3},{4,20},{20... | collective-permute-start | bytes 1572872 | tf_op jit(solution)/shard_map/ppermute | solution.py:20
  76.0 0.0 copy-start.2
  76.0 0.8 copy-done.2
  76.8 1.1 collective-permute-done.3.mate_ref.got_ref
  77.9 0.9 shard_map.88
  78.7 9.6 %all-to-all-start.1 = ((bf16[16,16,1024]{2,1,0:T(8,128)(2,1)}), bf16[16,16,1024]{2,1,0:T(8,128)(2,1)}, u32[]{:S(2)}, u32[]{:S(2)}) async-start(bf16[16,16,1024]{2,1,0:T(8,128)(2,1)} %shard_map.88), calls=%async_computation.2 | async-start | bytes 1048576 | tf_op jit(solution)/shard_map/all_to_all | solution.py:234
  88.3 0.5 shard_map.87
  88.8 2.2 %collective-permute-start.4 = (bf16[128,1024]{1,0:T(8,128)(2,1)S(1)}, bf16[128,1024]{1,0:T(8,128)(2,1)S(1)}, u32[]{:S(2)}, u32[]{:S(2)}) collective-permute-start(bf16[128,1024]{1,0:T(8,128)(2,1)S(1)} %get-tuple-element.34), channel_id=1, source_target_pairs={{0,32},{8,40},{32,0},{40,8},{1,33},{9,41},{33,1},{41,9},{2,34},{10... | collective-permute-start | bytes 786440 | tf_op jit(solution)/shard_map/ppermute | solution.py:241
  91.0 2.9 %collective-permute-start.5 = (bf16[128,1024]{1,0:T(8,128)(2,1)S(1)}, bf16[128,1024]{1,0:T(8,128)(2,1)S(1)}, u32[]{:S(2)}, u32[]{:S(2)}) collective-permute-start(bf16[128,1024]{1,0:T(8,128)(2,1)S(1)} %get-tuple-element.35), channel_id=1, source_target_pairs={{0,8},{8,0},{32,40},{40,32},{1,9},{9,1},{33,41},{41,33},{2,10},{10... | collective-permute-start | bytes 786440 | tf_op jit(solution)/shard_map/ppermute | solution.py:241
  94.0 4.8 %collective-permute-start.6 = (bf16[128,1024]{1,0:T(8,128)(2,1)S(1)}, bf16[128,1024]{1,0:T(8,128)(2,1)S(1)}, u32[]{:S(2)}, u32[]{:S(2)}) collective-permute-start(bf16[128,1024]{1,0:T(8,128)(2,1)S(1)} %get-tuple-element.36), channel_id=1, source_target_pairs={{0,40},{8,32},{32,8},{40,0},{1,41},{9,33},{33,9},{41,1},{2,42},{10... | collective-permute-start | bytes 786440 | tf_op jit(solution)/shard_map/ppermute | solution.py:241
  98.8 7.2 %collective-permute-done.4 = bf16[128,1024]{1,0:T(8,128)(2,1)S(1)} collective-permute-done((bf16[128,1024]{1,0:T(8,128)(2,1)S(1)}, bf16[128,1024]{1,0:T(8,128)(2,1)S(1)}, u32[]{:S(2)}, u32[]{:S(2)}) %collective-permute-start.4) | collective-permute-done | bytes 262176 | tf_op jit(solution)/shard_map/ppermute | solution.py:241
  106.0 2.6 %collective-permute-done.5 = bf16[128,1024]{1,0:T(8,128)(2,1)S(1)} collective-permute-done((bf16[128,1024]{1,0:T(8,128)(2,1)S(1)}, bf16[128,1024]{1,0:T(8,128)(2,1)S(1)}, u32[]{:S(2)}, u32[]{:S(2)}) %collective-permute-start.5) | collective-permute-done | bytes 262176 | tf_op jit(solution)/shard_map/ppermute | solution.py:241
  108.6 1.7 %collective-permute-done.6 = bf16[128,1024]{1,0:T(8,128)(2,1)S(1)} collective-permute-done((bf16[128,1024]{1,0:T(8,128)(2,1)S(1)}, bf16[128,1024]{1,0:T(8,128)(2,1)S(1)}, u32[]{:S(2)}, u32[]{:S(2)}) %collective-permute-start.6) | collective-permute-done | bytes 262176 | tf_op jit(solution)/shard_map/ppermute | solution.py:241
  110.3 0.9 add_convert_fusion
  111.2 0.0 all-to-all-done.1
  111.2 6.6 %all-to-all-start.2 = ((bf16[8,16,1024]{2,1,0:T(8,128)(2,1)}), bf16[8,16,1024]{2,1,0:T(8,128)(2,1)S(1)}, u32[]{:S(2)}, u32[]{:S(2)}) async-start(bf16[8,16,1024]{2,1,0:T(8,128)(2,1)} %bitcast.29), calls=%async_computation.3 | async-start | bytes 524288 | tf_op jit(solution)/shard_map/all_to_all | solution.py:245
  117.8 2.6 %fusion.2 = bf16[256,1024]{1,0:T(8,128)(2,1)} fusion(bf16[1024,1024]{1,0:T(8,128)(2,1)S(1)} %copy-done, f32[256,1024]{1,0:T(8,128)S(1)} %copy-done.4, bf16[256,1024]{1,0:T(8,128)(2,1)} %bitcast.8, f32[256]{0:T(256)S(1)} %convert_rsqrt_fusion), kind=kOutput, calls=%fused_computation.6 | convolution fusion | flops 538181632 | bytes 4195328 | tf_op jit(solution)/shard_map/dot_general | solution.py:24
  120.4 9.5 %all-to-all-done.2 = bf16[8,16,1024]{2,1,0:T(8,128)(2,1)S(1)} async-done(((bf16[8,16,1024]{2,1,0:T(8,128)(2,1)}), bf16[8,16,1024]{2,1,0:T(8,128)(2,1)S(1)}, u32[]{:S(2)}, u32[]{:S(2)}) %all-to-all-start.2) | async-done | bytes 262176 | tf_op jit(solution)/shard_map/all_to_all | solution.py:245
  129.9 0.1 broadcast_in_dim.11
  129.9 18.6 %all_to_all.20 = bf16[16,16,1024]{2,1,0:T(8,128)(2,1)S(1)} all-to-all(bf16[16,16,1024]{2,1,0:T(8,128)(2,1)S(1)} %broadcast_in_dim.11), channel_id=1, replica_groups=mesh['wide_y'=8,'wide_x'=2,'wide_c'=2,'blk_x'=2,'blk_z'=8] {'blk_x','blk..., dimensions={0} | all-to-all | bytes 1048576 | tf_op jit(solution)/shard_map/all_to_all | solution.py:250
  148.5 0.7 convert_reduce_fusion
  (14 shorter events, 0.1 us)
Async XLA Ops:
  7.2 16.8 %copy-start = (bf16[1024,1024]{1,0:T(8,128)(2,1)S(1)}, bf16[1024,1024]{1,0:T(8,128)(2,1)}, u32[]{:S(2)}) copy-start(bf16[1024,1024]{1,0:T(8,128)(2,1)} %param.11) | copy-start | bytes 6291460
  7.2 16.8 %copy-start.5 = (bf16[256,1024]{1,0:T(8,128)(2,1)S(1)}, bf16[256,1024]{1,0:T(8,128)(2,1)}, u32[]{:S(2)}) copy-start(bf16[256,1024]{1,0:T(8,128)(2,1)} %param.9) | copy-start | bytes 1572868
  7.2 16.6 %copy-start.6 = (s32[128,1]{0,1:T(1,128)S(1)}, s32[128,1]{0,1:T(1,128)}, u32[]{:S(2)}) copy-start(s32[128,1]{0,1:T(1,128)} %param.8) | copy-start | bytes 1540
  7.2 52.2 %all-gather.2.cloned.1.call-start = ((), (), s32[]{:S(2)}) async-start(), calls=%async_computation.5 | async-start | bytes 2359296 | tf_op jit(solution)/shard_map/all_gather | solution.py:198
  7.9 37.2 %collective-permute-start = (bf16[128,1024]{1,0:T(8,128)(2,1)}, bf16[128,1024]{1,0:T(8,128)(2,1)}, u32[]{:S(2)}, u32[]{:S(2)}) collective-permute-start(bf16[128,1024]{1,0:T(8,128)(2,1)} %refs_2_.1), channel_id=1, source_target_pairs={{0,8},{8,0},{1,9},{9,1},{2,10},{10,2},{3,11},{11,3},{4,12},{12,4},... | collective-permute-start | bytes 786440 | tf_op jit(solution)/shard_map/ppermute | solution.py:20
  13.5 27.9 %all-to-all-start = ((bf16[32,8,1024]{2,1,0:T(8,128)(2,1)}), bf16[32,8,1024]{2,1,0:T(8,128)(2,1)S(1)}, u32[]{:S(2)}, u32[]{:S(2)}) async-start(bf16[32,8,1024]{2,1,0:T(8,128)(2,1)} %fusion.17), calls=%async_computation | async-start | bytes 1048576 | tf_op jit(solution)/shard_map/all_to_all | solution.py:205
  23.7 125.5 %reduce-scatter.2.cloned.1.call-start = ((), (), s32[]{:S(2)}) async-start(), calls=%async_computation.6 | async-start | bytes 2359296 | tf_op jit(solution)/shard_map/reduce_scatter | solution.py:229
  42.7 3.2 %collective-permute-start.1 = (bf16[128,512]{1,0:T(8,128)(2,1)S(1)}, bf16[128,512]{1,0:T(8,128)(2,1)S(1)}, u32[]{:S(2)}, u32[]{:S(2)}) collective-permute-start(bf16[128,512]{1,0:T(8,128)(2,1)S(1)} %fusion.3), channel_id=1, source_target_pairs={{0,16},{16,0},{1,17},{17,1},{2,18},{18,2},{3,19},{19,3},{4,20},{20... | collective-permute-start | bytes 393224 | tf_op jit(solution)/shard_map/ppermute | solution.py:20
  65.0 8.6 %copy-start.1 = (f32[128,1024]{1,0:T(8,128)S(1)}, f32[128,1024]{1,0:T(8,128)}, u32[]{:S(2)}) copy-start(f32[128,1024]{1,0:T(8,128)} %get-tuple-element.28.kept_ref) | copy-start | bytes 1572868
  65.1 8.6 %collective-permute-start.2 = (bf16[128,1024]{1,0:T(8,128)(2,1)}, bf16[128,1024]{1,0:T(8,128)(2,1)S(1)}, u32[]{:S(2)}, u32[]{:S(2)}) collective-permute-start(bf16[128,1024]{1,0:T(8,128)(2,1)} %get-tuple-element.29), channel_id=1, source_target_pairs={{0,8},{8,0},{1,9},{9,1},{2,10},{10,2},{3,11},{11,3},{4,12},{12,4},... | collective-permute-start | bytes 786440 | tf_op jit(solution)/shard_map/ppermute | solution.py:20
  74.0 3.8 %collective-permute-start.3 = (bf16[256,1024]{1,0:T(8,128)(2,1)S(1)}, bf16[256,1024]{1,0:T(8,128)(2,1)S(1)}, u32[]{:S(2)}, u32[]{:S(2)}) collective-permute-start(bf16[256,1024]{1,0:T(8,128)(2,1)S(1)} %get-tuple-element.32.own_ref), channel_id=1, source_target_pairs={{0,16},{16,0},{1,17},{17,1},{2,18},{18,2},{3,19},{19,3},{4,20},{20... | collective-permute-start | bytes 1572872 | tf_op jit(solution)/shard_map/ppermute | solution.py:20
  76.0 0.8 copy-start.2
  77.9 10.5 %copy-start.3 = (bf16[256,1024]{1,0:T(8,128)(2,1)S(1)}, bf16[256,1024]{1,0:T(8,128)(2,1)}, u32[]{:S(2)}) copy-start(bf16[256,1024]{1,0:T(8,128)(2,1)} %copy-done.2) | copy-start | bytes 1572868
  78.7 32.5 %all-to-all-start.1 = ((bf16[16,16,1024]{2,1,0:T(8,128)(2,1)}), bf16[16,16,1024]{2,1,0:T(8,128)(2,1)}, u32[]{:S(2)}, u32[]{:S(2)}) async-start(bf16[16,16,1024]{2,1,0:T(8,128)(2,1)} %shard_map.88), calls=%async_computation.2 | async-start | bytes 1048576 | tf_op jit(solution)/shard_map/all_to_all | solution.py:234
  88.8 29.0 %copy-start.4 = (f32[256,1024]{1,0:T(8,128)S(1)}, f32[256,1024]{1,0:T(8,128)}, u32[]{:S(2)}) copy-start(f32[256,1024]{1,0:T(8,128)} %fusion.8) | copy-start | bytes 3145732
  88.8 17.2 %collective-permute-start.4 = (bf16[128,1024]{1,0:T(8,128)(2,1)S(1)}, bf16[128,1024]{1,0:T(8,128)(2,1)S(1)}, u32[]{:S(2)}, u32[]{:S(2)}) collective-permute-start(bf16[128,1024]{1,0:T(8,128)(2,1)S(1)} %get-tuple-element.34), channel_id=1, source_target_pairs={{0,32},{8,40},{32,0},{40,8},{1,33},{9,41},{33,1},{41,9},{2,34},{10... | collective-permute-start | bytes 786440 | tf_op jit(solution)/shard_map/ppermute | solution.py:241
  91.0 17.6 %collective-permute-start.5 = (bf16[128,1024]{1,0:T(8,128)(2,1)S(1)}, bf16[128,1024]{1,0:T(8,128)(2,1)S(1)}, u32[]{:S(2)}, u32[]{:S(2)}) collective-permute-start(bf16[128,1024]{1,0:T(8,128)(2,1)S(1)} %get-tuple-element.35), channel_id=1, source_target_pairs={{0,8},{8,0},{32,40},{40,32},{1,9},{9,1},{33,41},{41,33},{2,10},{10... | collective-permute-start | bytes 786440 | tf_op jit(solution)/shard_map/ppermute | solution.py:241
  94.0 16.4 %collective-permute-start.6 = (bf16[128,1024]{1,0:T(8,128)(2,1)S(1)}, bf16[128,1024]{1,0:T(8,128)(2,1)S(1)}, u32[]{:S(2)}, u32[]{:S(2)}) collective-permute-start(bf16[128,1024]{1,0:T(8,128)(2,1)S(1)} %get-tuple-element.36), channel_id=1, source_target_pairs={{0,40},{8,32},{32,8},{40,0},{1,41},{9,33},{33,9},{41,1},{2,42},{10... | collective-permute-start | bytes 786440 | tf_op jit(solution)/shard_map/ppermute | solution.py:241
  111.2 18.6 %all-to-all-start.2 = ((bf16[8,16,1024]{2,1,0:T(8,128)(2,1)}), bf16[8,16,1024]{2,1,0:T(8,128)(2,1)S(1)}, u32[]{:S(2)}, u32[]{:S(2)}) async-start(bf16[8,16,1024]{2,1,0:T(8,128)(2,1)} %bitcast.29), calls=%async_computation.3 | async-start | bytes 524288 | tf_op jit(solution)/shard_map/all_to_all | solution.py:245
Sparse Core Ops, SparseCore 0:
  10.1 49.2 all-gather.1
  65.2 43.6 reduce-scatter.1

commit v10 on v7

--- a/solution.py
+++ b/solution.py
@@ -31,11 +31,10 @@
     return cdf + v * (0.3989422804014327 * jnp.exp(-0.5 * v * v))
 
 
-def targets_of(owner, capacity):
-    ids = jnp.arange(owner.shape[0], dtype=jnp.int32)
-    peer = owner[:, 0]
+def ranks_of(peer):
+    ids = jnp.arange(peer.shape[0], dtype=jnp.int32)
     before = (peer[:, None] == peer[None, :]) & (ids[:, None] < ids[None, :])
-    return peer * capacity + jnp.sum(before.astype(jnp.int32), axis=0)
+    return jnp.sum(before.astype(jnp.int32), axis=0)
 
 
 def picking_of(core, feature_count):
@@ -45,8 +44,8 @@
     share = half // (ny * nx * bx)
     place = jnp.arange(half, dtype=jnp.int32)
     within, rest = place % share, place // share
-    y, x = rest % ny, rest // ny
-    feature = (((y * nx + x // bx) * 2 + core) * bx + x % bx) * share + within
+    owner, line = rest % (ny * nx), (rest // (ny * nx)) ^ lax.axis_index("blk_x")
+    feature = ((owner * 2 + core) * bx + line) * share + within
     return (jnp.arange(feature_count, dtype=jnp.int32)[:, None] == feature[None, :]).astype(BF16)
 
 
@@ -129,49 +128,64 @@
     )(place, line, own, mate, slope)
 
 
-def clip_kernel(kept_ref, arrived_ref, target_ref, packed_ref):
+def clip_kernel(kept_ref, arrived_ref, place_ref, stay_ref, give_ref):
     grad = (kept_ref[...] + arrived_ref[...].astype(F32)).astype(BF16)
-    slots, clips = packed_ref.shape[0], grad.shape[0]
+    slots, clips = stay_ref.shape[0], grad.shape[0]
     slot = lax.broadcasted_iota(jnp.int32, (slots, clips), 0)
-    placing = (slot == target_ref[...]).astype(BF16)
-    packed_ref[...] = dot_of(placing, grad, 1, 0).astype(BF16)
-
-
-def clip_grads(kept, arrived, targets, slots):
+    stay_ref[...] = dot_of((slot == place_ref[...]).astype(BF16), grad, 1, 0).astype(BF16)
+    give_ref[...] = dot_of((slot + slots == place_ref[...]).astype(BF16), grad, 1, 0).astype(BF16)
+
+
+def clip_grads(kept, arrived, places, slots):
+    shape = jax.ShapeDtypeStruct((slots // 2, kept.shape[1]), BF16)
     return pl.pallas_call(
         clip_kernel,
-        out_shape=jax.ShapeDtypeStruct((slots, kept.shape[1]), BF16),
-        compiler_params=ROOM,
-    )(kept, arrived, targets[None, :])
-
-
-def weight_kernel(own_picked, mate_picked, own_pre, mate_pre, out_ref):
-    product = dot_of(own_picked[...], own_pre[...], 1, 0)
-    product += dot_of(mate_picked[...], mate_pre[...], 1, 0)
-    out_ref[...] = product.astype(BF16)
-
-
-def weight_part(own_picked, mate_picked, own_pre, mate_pre):
+        out_shape=[shape, shape],
+        compiler_params=ROOM,
+    )(kept, arrived, places[None, :])
+
+
+def weight_kernel(own_picked, mate_picked, own_pre, mate_pre, keep_ref, give_ref):
+    half = keep_ref.shape[0]
+    for at, out_ref in ((half, give_ref), (0, keep_ref)):
+        block = pl.ds(at, half)
+        product = dot_of(own_picked[block], own_pre[...], 1, 0)
+        product += dot_of(mate_picked[block], mate_pre[...], 1, 0)
+        out_ref[...] = product.astype(out_ref.dtype)
+
+
+def weight_parts(own_picked, mate_picked, own_pre, mate_pre):
+    shape = (own_picked.shape[0] // 2, own_pre.shape[1])
     return pl.pallas_call(
         weight_kernel,
-        out_shape=jax.ShapeDtypeStruct((own_picked.shape[0], own_pre.shape[1]), BF16),
+        out_shape=[jax.ShapeDtypeStruct(shape, F32), jax.ShapeDtypeStruct(shape, BF16)],
         compiler_params=ROOM,
     )(own_picked, mate_picked, own_pre, mate_pre)
 
 
-def sum_kernel(pieces_ref, out_ref):
-    total = pieces_ref[0].astype(F32)
-    for s in range(1, pieces_ref.shape[0]):
-        total += pieces_ref[s].astype(F32)
-    out_ref[...] = total.astype(BF16)
-
-
-def sum_of(pieces):
-    return pl.pallas_call(
-        sum_kernel,
-        out_shape=jax.ShapeDtypeStruct(pieces.shape[1:], BF16),
-        compiler_params=ROOM,
-    )(pieces)
+def load_kernel(core_ref, stay_ref, got_ref, keep_ref, came_ref, out_ref):
+    count, lines, features = out_ref.shape
+    cells = stay_ref.shape[0] // count
+    stay = stay_ref[...].astype(F32).reshape(count, cells, features)
+    got = got_ref[...].astype(F32).reshape(count, cells, features)
+    first = core_ref[0] == 0
+    pair = [jnp.where(first, stay, got), jnp.where(first, got, stay)]
+    out_ref[:, pl.ds(0, 2 * cells)] = jnp.concatenate(pair, axis=1).astype(BF16)
+    rows = lines - 2 * cells
+    total = (keep_ref[...] + came_ref[...].astype(F32)).reshape(count, rows, features)
+    out_ref[:, pl.ds(2 * cells, rows)] = total.astype(BF16)
+
+
+def load_of(core, stay, got, keep, came, count):
+    lines = (2 * stay.shape[0] + keep.shape[0]) // count
+    held = pl.BlockSpec(memory_space=pltpu.VMEM)
+    return pl.pallas_call(
+        load_kernel,
+        in_specs=[SCALAR, held, held, held, held],
+        out_specs=held,
+        out_shape=jax.ShapeDtypeStruct((count, lines, stay.shape[1]), BF16),
+        compiler_params=ROOM,
+    )(core, stay, got, keep, came)
 
 
 def spread_kernel(pieces_ref, out_ref):
@@ -181,10 +195,14 @@
     out_ref[...] = jnp.broadcast_to(total.astype(BF16)[None], out_ref.shape)
 
 
-def sum_spread(pieces, copies):
+def sum_spread(pieces, rows, copies):
+    count, lines, features = pieces.shape
     return pl.pallas_call(
         spread_kernel,
-        out_shape=jax.ShapeDtypeStruct((copies, *pieces.shape[1:]), BF16),
+        grid=(1,),
+        in_specs=[pl.BlockSpec((count, rows, features), lambda i: (0, lines // rows - 1, 0))],
+        out_specs=pl.BlockSpec((copies, rows, features), lambda i: (0, 0, 0)),
+        out_shape=jax.ShapeDtypeStruct((copies, rows, features), BF16),
         compiler_params=ROOM,
     )(pieces)
 
@@ -207,8 +225,11 @@
     video_mate = swapped(video, "blk_x")
     slope_own = gelu_slope(dot_of(pooled, proj_weight, 1, 0))
 
-    targets = targets_of(owner, capacity)
-    placing = (targets[:, None] == jnp.arange(slots, dtype=jnp.int32)[None, :]).astype(BF16)
+    peer = owner[:, 0]
+    ranks = ranks_of(peer)
+    slot_of = peer * capacity + ranks
+    placing = (slot_of[:, None] == jnp.arange(slots, dtype=jnp.int32)[None, :]).astype(BF16)
+    places = (((peer % 2) ^ core) * (peers // 2) + peer // 2) * capacity + ranks
     clip_rows = dot_of(placing, pooled_slots, 1, 0).astype(BF16)
     row_pair = jnp.concatenate([clip_rows, swapped(clip_rows, "blk_x")])
     slope_pair = gelu_slope(dot_of(row_pair, proj_weight, 1, 0))
@@ -216,9 +237,9 @@
     picked_mate = swapped(
         dot_of(picking_of(1 - core, features), row_pair, 0, 1).astype(BF16), "wide_c"
     )
-    audio_line, video_mate, slope_pair, picked, picked_mate, slope_own, targets = (
+    audio_line, video_mate, slope_pair, picked, picked_mate, slope_own, places = (
         lax.optimization_barrier(
-            (audio_line, video_mate, slope_pair, picked, picked_mate, slope_own, targets)
+            (audio_line, video_mate, slope_pair, picked, picked_mate, slope_own, places)
         )
     )
 
@@ -229,27 +250,22 @@
 
     pre_mate = swapped(pre_pair, "wide_c")
     arrived = swapped(sent, "blk_x")
-    weight_sum = weight_part(picked, picked_mate, pre_pair, pre_mate)
-    pieces = lax.all_to_all(
-        weight_sum.reshape(4, -1, features), ("wide_x", "blk_x"), 0, 0, tiled=True
-    )
-
-    arrived, pieces = lax.optimization_barrier((arrived, pieces))
-    packed = clip_grads(kept, arrived, targets, slots)
-    received = lax.all_to_all(
-        packed.reshape(peers, capacity, features), WIDE, 0, 0, tiled=True
-    ).reshape(slots, features)
-
-    pieces, packed = lax.optimization_barrier((pieces, packed))
-    summed, received = lax.optimization_barrier((sum_of(pieces), received))
-    pieces = lax.all_to_all(
-        summed.reshape(lax.axis_size("wide_y"), -1, features), "wide_y", 0, 0, tiled=True
-    )
+    keep, other_line = weight_parts(picked, picked_mate, pre_pair, pre_mate)
+    came = swapped(other_line, "blk_x")
+
+    arrived, other_line = lax.optimization_barrier((arrived, other_line))
+    stay, give = clip_grads(kept, arrived, places, slots)
+    got = swapped(give, "wide_c")
+    load = load_of(core.astype(jnp.int32)[None], stay, got, keep, came, peers // 2)
+    rows = keep.shape[0] // (peers // 2)
+    load = lax.all_to_all(load, ("wide_y", "wide_x"), 0, 0, tiled=True)
+
+    total = sum_spread(load, rows, blocks)
+    gathered = lax.all_to_all(total, BLK, 0, 0, tiled=True)
+    received = load[:, :-rows].reshape(slots, features)
     pre_grad = (received.astype(F32) * slope_own).astype(BF16)
     feats_grad = (dot_of(pre_grad, proj_weight, 1, 1) * length_scale).astype(BF16)
-    pieces, feats_grad = lax.optimization_barrier((pieces, feats_grad))
-    total = sum_spread(pieces, blocks)
-    gathered = lax.all_to_all(total, BLK, 0, 0, tiled=True)
+    gathered, feats_grad = lax.optimization_barrier((gathered, feats_grad))
     gathered = gathered.reshape(lax.axis_size("blk_x"), -1, *total.shape[1:])
     weight_grad = jnp.sum(gathered.astype(F32), axis=1).reshape(-1, features)
     return (audio_grad, feats_grad, weight_grad)

time: 168 us -> 158 us (0.940)
  waiting for transfers between devices: 68.7 us -> 47.5 us
  blocking collectives: 18.1 us -> 36.8 us
  starting transfers between devices: 40.9 us -> 33 us
    all_to_all x1, blocking collectives: 18.1 us -> 36.8 us  [shards(): load = lax.all_to_all(load, ('wide_y', 'wide_x'), 0, 0, tiled=True)]
    all_to_all x3 -> x1, waiting for transfers between devices: 25.5 us -> 10.2 us  [shards(): gathered = lax.all_to_all(total, BLK, 0, 0, tiled=True)]
    all_to_all x3 -> x1, starting transfers between devices: 18.5 us -> 5.66 us  [shards(): gathered = lax.all_to_all(total, BLK, 0, 0, tiled=True)]
    ppermute x5 -> x7, waiting for transfers between devices: 24.1 us -> 18.9 us  [swapped(): return lax.ppermute(array, axis, [(0, 1), (1, 0)])]
    ppermute x5 -> x7, starting transfers between devices: 12.1 us -> 17.1 us  [swapped(): return lax.ppermute(array, axis, [(0, 1), (1, 0)])]
  transfers between devices with their start and end apart: 11 -> 11, of which waited for: 7 -> 7; matrix products, arithmetic and copies ran while one was open for 7% -> 9% of each run, Pallas kernels for 1% -> 1%
where the time goes in v10:
time: 158 us; the launch traced here: 155 us
  waiting for transfers between devices  47.5 us (30%)
  blocking collectives  36.8 us (23%)
  starting transfers between devices  33 us (21%)
  between operations  14.3 us (9%)
  matrix products  8.74 us (6%)
  Pallas kernels  7.07 us (4%)
  other arithmetic  4.64 us (3%)
  local copies, waits for them, and re-layouts  2.8 us (2%)
    all_to_all x1, blocking collectives, shards(): load = lax.all_to_all(load, ('wide_y', 'wide_x'), 0, 0, tiled=True)  36.8 us
    ppermute x7, waiting for transfers between devices, swapped(): return lax.ppermute(array, axis, [(0, 1), (1, 0)])  18.9 us
    ppermute x7, starting transfers between devices, swapped(): return lax.ppermute(array, axis, [(0, 1), (1, 0)])  17.1 us
    all_to_all x1, waiting for transfers between devices, shards(): lax.all_to_all(pooled.reshape(peers, capacity, features), WIDE, 0, 0, til...  12.7 us
    all_to_all x1, starting transfers between devices, shards(): lax.all_to_all(pooled.reshape(peers, capacity, features), WIDE, 0, 0, til...  10.2 us
    all_to_all x1, waiting for transfers between devices, shards(): gathered = lax.all_to_all(total, BLK, 0, 0, tiled=True)  10.2 us
    dot_general x6, matrix products, dot_of(): lax.dot_general(matrix_a, matrix_b, (((dim_a,), (dim_b,)), ((), ())), pre...  8.74 us
    pallas_call x1, Pallas kernels, pair_grads(): pl.pallas_call(lambda *refs: pair_kernel(factor, steps, *refs), in_specs=...  5.8 us
  transfers between devices with their start and end apart: 11, of which 7 were waited for; matrix products, arithmetic and copies ran while one was open for 9% of the time, Pallas kernels for 1%

profile of v10, /device:TPU:6, one launch (start us, length us, event | category | flops | bytes accessed | tf_op | source)
XLA Modules:
  0.0 154.9 jit_solution(42857355163594341)
XLA Ops:
  7.2 0.0 copy-start
  7.2 0.0 copy-start.5
  7.2 0.0 copy-start.6
  7.2 0.0 all-gather.2.cloned.1.call-start
  7.2 0.7 all-gather.2.cloned.1.call-update
  7.9 0.7 convert_rsqrt_fusion
  8.7 2.0 %fusion.19 = bf16[32,8,1024]{2,1,0:T(8,128)(2,1)} fusion(f32[256]{0:T(256)S(1)} %convert_rsqrt_fusion, bf16[256,1024]{1,0:T(8,128)(2,1)} %param.9), kind=kLoop, calls=%fused_computation.28 | loop fusion | flops 786432 | bytes 1049600 | tf_op jit(solution)/shard_map/reshape | solution.py:223
  10.6 10.2 %all-to-all-start = ((bf16[32,8,1024]{2,1,0:T(8,128)(2,1)}), bf16[32,8,1024]{2,1,0:T(8,128)(2,1)S(1)}, u32[]{:S(2)}, u32[]{:S(2)}) async-start(bf16[32,8,1024]{2,1,0:T(8,128)(2,1)} %fusion.19), calls=%async_computation | async-start | bytes 1048576 | tf_op jit(solution)/shard_map/all_to_all | solution.py:222
  20.9 0.0 reduce-scatter.2.cloned.1.call-start
  20.9 2.7 %collective-permute-start = (bf16[128,1024]{1,0:T(8,128)(2,1)}, bf16[128,1024]{1,0:T(8,128)(2,1)}, u32[]{:S(2)}, u32[]{:S(2)}) collective-permute-start(bf16[128,1024]{1,0:T(8,128)(2,1)} %refs_2_.1), channel_id=1, source_target_pairs={{0,8},{8,0},{1,9},{9,1},{2,10},{10,2},{3,11},{11,3},{4,12},{12,4},... | collective-permute-start | bytes 786440 | tf_op jit(solution)/shard_map/ppermute | solution.py:20
  23.7 0.0 copy-done.6
  23.7 0.1 convert_reduce_fusion.1
  23.8 0.0 copy-done
  23.8 2.0 %fusion.10 = f32[256,1024]{1,0:T(8,128)} fusion(bf16[1024,1024]{1,0:T(8,128)(2,1)S(1)} %copy-done, bf16[256,1024]{1,0:T(8,128)(2,1)S(1)} %copy-done.5, f32[256]{0:T(256)S(1)} %convert_rsqrt_fusion), kind=kOutput, calls=%fused_computation.18 | convolution fusion | flops 539754496 | bytes 3671040 | tf_op jit(solution)/shard_map/dot_general | solution.py:24
  25.8 12.7 %all-to-all-done = bf16[32,8,1024]{2,1,0:T(8,128)(2,1)S(1)} async-done(((bf16[32,8,1024]{2,1,0:T(8,128)(2,1)}), bf16[32,8,1024]{2,1,0:T(8,128)(2,1)S(1)}, u32[]{:S(2)}, u32[]{:S(2)}) %all-to-all-start) | async-done | bytes 524320 | tf_op jit(solution)/shard_map/all_to_all | solution.py:222
  38.6 0.3 convolution_convert_fusion.2
  38.9 2.7 %collective-permute-start.1 = (bf16[128,1024]{1,0:T(8,128)(2,1)S(1)}, bf16[128,1024]{1,0:T(8,128)(2,1)S(1)}, u32[]{:S(2)}, u32[]{:S(2)}) collective-permute-start(bf16[128,1024]{1,0:T(8,128)(2,1)S(1)} %convolution_convert_fusion.2), channel_id=1, source_target_pairs={{0,8},{8,0},{1,9},{9,1},{2,10},{10,2},{3,11},{11,3},{4,12},{12,4},... | collective-permute-start | bytes 786440 | tf_op jit(solution)/shard_map/ppermute | solution.py:20
  41.6 6.6 %collective-permute-done.1 = bf16[128,1024]{1,0:T(8,128)(2,1)S(1)} collective-permute-done((bf16[128,1024]{1,0:T(8,128)(2,1)S(1)}, bf16[128,1024]{1,0:T(8,128)(2,1)S(1)}, u32[]{:S(2)}, u32[]{:S(2)}) %collective-permute-start.1) | collective-permute-done | bytes 262176 | tf_op jit(solution)/shard_map/ppermute | solution.py:20
  48.2 0.5 convolution_convert_fusion
  48.7 1.9 %collective-permute-start.2 = (bf16[512,256]{1,0:T(8,128)(2,1)S(1)}, bf16[512,256]{1,0:T(8,128)(2,1)S(1)}, u32[]{:S(2)}, u32[]{:S(2)}) collective-permute-start(bf16[512,256]{1,0:T(8,128)(2,1)S(1)} %convolution_convert_fusion), channel_id=1, source_target_pairs={{0,16},{16,0},{1,17},{17,1},{2,18},{18,2},{3,19},{19,3},{4,20},{20... | collective-permute-start | bytes 786440 | tf_op jit(solution)/shard_map/ppermute | solution.py:20
  50.7 2.0 %fusion.6.refs_4_ = f32[256,1024]{1,0:T(8,128)} fusion(bf16[1024,1024]{1,0:T(8,128)(2,1)S(1)} %copy-done, bf16[128,1024]{1,0:T(8,128)(2,1)S(1)} %collective-permute-done.1, bf16[128,1024]{1,0:T(8,128)(2,1)S(1)} %convolution_convert_fusion.2), kind=kOutput, calls=%fused_computation.14 | convolution fusion | flops 540016640 | bytes 3670016 | tf_op jit(solution)/shard_map/dot_general | solution.py:24
  52.7 1.2 convolution_convert_fusion.1.own_picked
  53.9 0.0 collective-permute-done.refs_3_
  53.9 0.0 collective-permute-done.2.mate_picked
  53.9 5.0 %all-gather.2.cloned.1.call-done.refs_1_ = bf16[1024,1024]{1,0:T(8,128)(2,1)} async-done(((bf16[128,1024]{1,0:T(8,128)(2,1)}), bf16[1024,1024]{1,0:T(8,128)(2,1)}) %all-gather.2.cloned.1.call-update) | async-done | bytes 2097168 | tf_op jit(solution)/shard_map/all_gather | solution.py:215
  58.9 5.8 %shard_map.85 = (f32[128,1024]{1,0:T(8,128)}, bf16[128,1024]{1,0:T(8,128)(2,1)}, bf16[256,1024]{1,0:T(8,128)(2,1)}, bf16[1024,1024]{1,0:T(8,128)(2,1)}) custom-call(s32[1]{0:T(128)} %bitcast.refs_0_, bf16[1024,1024]{1,0:T(8,128)(2,1)} %all-gather.2.cloned.1.call-done.refs_1_, bf16[128,1024]{1,0:T(8,128)(2,1)} %refs_2_.1, ...), custom_call_target="tpu_custom_call" | custom-call | flops 1610612736 | bytes 5242880 | tf_op jit(solution)/shard_map/pallas_call | solution.py:105
  64.7 0.0 copy-start.3
  64.7 0.0 reduce-scatter.2.cloned.1.call-update
  64.7 1.0 copy-done.2
  65.7 1.9 %collective-permute-start.4 = (bf16[256,1024]{1,0:T(8,128)(2,1)S(1)}, bf16[256,1024]{1,0:T(8,128)(2,1)S(1)}, u32[]{:S(2)}, u32[]{:S(2)}) collective-permute-start(bf16[256,1024]{1,0:T(8,128)(2,1)S(1)} %copy-done.2), channel_id=1, source_target_pairs={{0,16},{16,0},{1,17},{17,1},{2,18},{18,2},{3,19},{19,3},{4,20},{20... | collective-permute-start | bytes 1572872 | tf_op jit(solution)/shard_map/ppermute | solution.py:20
  67.7 2.8 %collective-permute-start.3 = (bf16[128,1024]{1,0:T(8,128)(2,1)}, bf16[128,1024]{1,0:T(8,128)(2,1)S(1)}, u32[]{:S(2)}, u32[]{:S(2)}) collective-permute-start(bf16[128,1024]{1,0:T(8,128)(2,1)} %get-tuple-element.26), channel_id=1, source_target_pairs={{0,8},{8,0},{1,9},{9,1},{2,10},{10,2},{3,11},{11,3},{4,12},{12,4},... | collective-permute-start | bytes 786440 | tf_op jit(solution)/shard_map/ppermute | solution.py:20
  70.4 0.0 collective-permute-done.4.mate_pre
  70.5 0.9 copy-done.4
  71.4 0.7 shard_map.86
  72.1 3.1 %collective-permute-start.6 = (bf16[256,1024]{1,0:T(8,128)(2,1)S(1)}, bf16[256,1024]{1,0:T(8,128)(2,1)S(1)}, u32[]{:S(2)}, u32[]{:S(2)}) collective-permute-start(bf16[256,1024]{1,0:T(8,128)(2,1)S(1)} %get-tuple-element.30), channel_id=1, source_target_pairs={{0,8},{8,0},{1,9},{9,1},{2,10},{10,2},{3,11},{11,3},{4,12},{12,4},... | collective-permute-start | bytes 1572872 | tf_op jit(solution)/shard_map/ppermute | solution.py:20
  75.2 3.7 %collective-permute-done.3.arrived_ref = bf16[128,1024]{1,0:T(8,128)(2,1)S(1)} collective-permute-done((bf16[128,1024]{1,0:T(8,128)(2,1)}, bf16[128,1024]{1,0:T(8,128)(2,1)S(1)}, u32[]{:S(2)}, u32[]{:S(2)}) %collective-permute-start.3) | collective-permute-done | bytes 262176 | tf_op jit(solution)/shard_map/ppermute | solution.py:20
  78.9 0.3 shard_map.87
  79.2 1.9 %collective-permute-start.5 = (bf16[128,1024]{1,0:T(8,128)(2,1)S(1)}, bf16[128,1024]{1,0:T(8,128)(2,1)S(1)}, u32[]{:S(2)}, u32[]{:S(2)}) collective-permute-start(bf16[128,1024]{1,0:T(8,128)(2,1)S(1)} %get-tuple-element.34), channel_id=1, source_target_pairs={{0,16},{16,0},{1,17},{17,1},{2,18},{18,2},{3,19},{19,3},{4,20},{20... | collective-permute-start | bytes 786440 | tf_op jit(solution)/shard_map/ppermute | solution.py:20
  81.1 1.5 collective-permute-done.5.got_ref
  82.6 7.1 %collective-permute-done.6.came_ref = bf16[256,1024]{1,0:T(8,128)(2,1)S(1)} collective-permute-done((bf16[256,1024]{1,0:T(8,128)(2,1)S(1)}, bf16[256,1024]{1,0:T(8,128)(2,1)S(1)}, u32[]{:S(2)}, u32[]{:S(2)}) %collective-permute-start.6) | collective-permute-done | bytes 524320 | tf_op jit(solution)/shard_map/ppermute | solution.py:20
  89.7 0.2 shard_map.88
  89.9 36.8 %all_to_all.15.pieces_ref = bf16[16,32,1024]{2,1,0:T(8,128)(2,1)S(1)} all-to-all(bf16[16,32,1024]{2,1,0:T(8,128)(2,1)S(1)} %shard_map.88), channel_id=1, replica_groups=mesh['wide_y'=8,'wide_x'=2,'wide_c'=2,'blk_x'=2,'blk_z'=8] {'wide_y','wi..., dimensions={0} | all-to-all | bytes 2097152 | tf_op jit(solution)/shard_map/all_to_all | solution.py:261
  126.7 0.1 shard_map.89
  126.8 0.8 copy-done.1
  127.5 5.7 %all-to-all-start.2 = ((bf16[16,16,1024]{2,1,0:T(8,128)(2,1)}), bf16[16,16,1024]{2,1,0:T(8,128)(2,1)}, u32[]{:S(2)}, u32[]{:S(2)}) async-start(bf16[16,16,1024]{2,1,0:T(8,128)(2,1)} %copy-done.1), calls=%async_computation.3 | async-start | bytes 1048576 | tf_op jit(solution)/shard_map/all_to_all | solution.py:264
  133.2 2.8 %fusion.2 = bf16[256,1024]{1,0:T(8,128)(2,1)} fusion(bf16[1024,1024]{1,0:T(8,128)(2,1)S(1)} %copy-done, f32[256,1024]{1,0:T(8,128)} %fusion.10, bf16[256,1024]{1,0:T(8,128)(2,1)S(1)} %bitcast.26, f32[256]{0:T(256)S(1)} %convert_rsqrt_fusion), kind=kOutput, calls=%fused_computation.7 | convolution fusion | flops 538181632 | bytes 4195328 | tf_op jit(solution)/shard_map/dot_general | solution.py:24
  136.0 10.2 %all-to-all-done.2 = bf16[16,16,1024]{2,1,0:T(8,128)(2,1)} async-done(((bf16[16,16,1024]{2,1,0:T(8,128)(2,1)}), bf16[16,16,1024]{2,1,0:T(8,128)(2,1)}, u32[]{:S(2)}, u32[]{:S(2)}) %all-to-all-start.2) | async-done | bytes 524320 | tf_op jit(solution)/shard_map/all_to_all | solution.py:264
  146.2 1.8 %convert_reduce_fusion = f32[2,16,1024]{2,1,0:T(8,128)} fusion(bf16[16,16,1024]{2,1,0:T(8,128)(2,1)} %all-to-all-done.2), kind=kLoop, calls=%fused_computation.19 | loop fusion | flops 491520 | bytes 655360 | tf_op jit(solution)/shard_map/reduce_sum | solution.py:270
  (11 shorter events, 0.1 us)
Async XLA Ops:
  7.2 16.7 %copy-start = (bf16[1024,1024]{1,0:T(8,128)(2,1)S(1)}, bf16[1024,1024]{1,0:T(8,128)(2,1)}, u32[]{:S(2)}) copy-start(bf16[1024,1024]{1,0:T(8,128)(2,1)} %param.11) | copy-start | bytes 6291460
  7.2 16.7 %copy-start.5 = (bf16[256,1024]{1,0:T(8,128)(2,1)S(1)}, bf16[256,1024]{1,0:T(8,128)(2,1)}, u32[]{:S(2)}) copy-start(bf16[256,1024]{1,0:T(8,128)(2,1)} %param.9) | copy-start | bytes 1572868
  7.2 16.5 %copy-start.6 = (s32[128,1]{0,1:T(1,128)S(1)}, s32[128,1]{0,1:T(1,128)}, u32[]{:S(2)}) copy-start(s32[128,1]{0,1:T(1,128)} %param.8) | copy-start | bytes 1540
  7.2 51.7 %all-gather.2.cloned.1.call-start = ((), (), s32[]{:S(2)}) async-start(), calls=%async_computation.4 | async-start | bytes 2359296 | tf_op jit(solution)/shard_map/all_gather | solution.py:215
  10.6 27.9 %all-to-all-start = ((bf16[32,8,1024]{2,1,0:T(8,128)(2,1)}), bf16[32,8,1024]{2,1,0:T(8,128)(2,1)S(1)}, u32[]{:S(2)}, u32[]{:S(2)}) async-start(bf16[32,8,1024]{2,1,0:T(8,128)(2,1)} %fusion.19), calls=%async_computation | async-start | bytes 1048576 | tf_op jit(solution)/shard_map/all_to_all | solution.py:222
  20.9 127.1 %reduce-scatter.2.cloned.1.call-start = ((), (), s32[]{:S(2)}) async-start(), calls=%async_computation.5 | async-start | bytes 2359296 | tf_op jit(solution)/shard_map/reduce_scatter | solution.py:249
  20.9 32.9 %collective-permute-start = (bf16[128,1024]{1,0:T(8,128)(2,1)}, bf16[128,1024]{1,0:T(8,128)(2,1)}, u32[]{:S(2)}, u32[]{:S(2)}) collective-permute-start(bf16[128,1024]{1,0:T(8,128)(2,1)} %refs_2_.1), channel_id=1, source_target_pairs={{0,8},{8,0},{1,9},{9,1},{2,10},{10,2},{3,11},{11,3},{4,12},{12,4},... | collective-permute-start | bytes 786440 | tf_op jit(solution)/shard_map/ppermute | solution.py:20
  38.9 9.4 %collective-permute-start.1 = (bf16[128,1024]{1,0:T(8,128)(2,1)S(1)}, bf16[128,1024]{1,0:T(8,128)(2,1)S(1)}, u32[]{:S(2)}, u32[]{:S(2)}) collective-permute-start(bf16[128,1024]{1,0:T(8,128)(2,1)S(1)} %convolution_convert_fusion.2), channel_id=1, source_target_pairs={{0,8},{8,0},{1,9},{9,1},{2,10},{10,2},{3,11},{11,3},{4,12},{12,4},... | collective-permute-start | bytes 786440 | tf_op jit(solution)/shard_map/ppermute | solution.py:20
  48.7 5.1 %collective-permute-start.2 = (bf16[512,256]{1,0:T(8,128)(2,1)S(1)}, bf16[512,256]{1,0:T(8,128)(2,1)S(1)}, u32[]{:S(2)}, u32[]{:S(2)}) collective-permute-start(bf16[512,256]{1,0:T(8,128)(2,1)S(1)} %convolution_convert_fusion), channel_id=1, source_target_pairs={{0,16},{16,0},{1,17},{17,1},{2,18},{18,2},{3,19},{19,3},{4,20},{20... | collective-permute-start | bytes 786440 | tf_op jit(solution)/shard_map/ppermute | solution.py:20
  64.7 1.0 copy-start.2
  64.7 14.2 %copy-start.3 = (f32[128,1024]{1,0:T(8,128)S(1)}, f32[128,1024]{1,0:T(8,128)}, u32[]{:S(2)}) copy-start(f32[128,1024]{1,0:T(8,128)} %get-tuple-element.25.kept_ref) | copy-start | bytes 1572868
  65.7 4.7 %collective-permute-start.4 = (bf16[256,1024]{1,0:T(8,128)(2,1)S(1)}, bf16[256,1024]{1,0:T(8,128)(2,1)S(1)}, u32[]{:S(2)}, u32[]{:S(2)}) collective-permute-start(bf16[256,1024]{1,0:T(8,128)(2,1)S(1)} %copy-done.2), channel_id=1, source_target_pairs={{0,16},{16,0},{1,17},{17,1},{2,18},{18,2},{3,19},{19,3},{4,20},{20... | collective-permute-start | bytes 1572872 | tf_op jit(solution)/shard_map/ppermute | solution.py:20
  67.7 11.2 %collective-permute-start.3 = (bf16[128,1024]{1,0:T(8,128)(2,1)}, bf16[128,1024]{1,0:T(8,128)(2,1)S(1)}, u32[]{:S(2)}, u32[]{:S(2)}) collective-permute-start(bf16[128,1024]{1,0:T(8,128)(2,1)} %get-tuple-element.26), channel_id=1, source_target_pairs={{0,8},{8,0},{1,9},{9,1},{2,10},{10,2},{3,11},{11,3},{4,12},{12,4},... | collective-permute-start | bytes 786440 | tf_op jit(solution)/shard_map/ppermute | solution.py:20
  70.4 1.0 copy-start.4
  72.1 17.6 %collective-permute-start.6 = (bf16[256,1024]{1,0:T(8,128)(2,1)S(1)}, bf16[256,1024]{1,0:T(8,128)(2,1)S(1)}, u32[]{:S(2)}, u32[]{:S(2)}) collective-permute-start(bf16[256,1024]{1,0:T(8,128)(2,1)S(1)} %get-tuple-element.30), channel_id=1, source_target_pairs={{0,8},{8,0},{1,9},{9,1},{2,10},{10,2},{3,11},{11,3},{4,12},{12,4},... | collective-permute-start | bytes 1572872 | tf_op jit(solution)/shard_map/ppermute | solution.py:20
  79.2 3.4 %collective-permute-start.5 = (bf16[128,1024]{1,0:T(8,128)(2,1)S(1)}, bf16[128,1024]{1,0:T(8,128)(2,1)S(1)}, u32[]{:S(2)}, u32[]{:S(2)}) collective-permute-start(bf16[128,1024]{1,0:T(8,128)(2,1)S(1)} %get-tuple-element.34), channel_id=1, source_target_pairs={{0,16},{16,0},{1,17},{17,1},{2,18},{18,2},{3,19},{19,3},{4,20},{20... | collective-permute-start | bytes 786440 | tf_op jit(solution)/shard_map/ppermute | solution.py:20
  126.7 0.8 copy-start.1
  127.5 18.7 %all-to-all-start.2 = ((bf16[16,16,1024]{2,1,0:T(8,128)(2,1)}), bf16[16,16,1024]{2,1,0:T(8,128)(2,1)}, u32[]{:S(2)}, u32[]{:S(2)}) async-start(bf16[16,16,1024]{2,1,0:T(8,128)(2,1)} %copy-done.1), calls=%async_computation.3 | async-start | bytes 1048576 | tf_op jit(solution)/shard_map/all_to_all | solution.py:264
Sparse Core Ops, SparseCore 0:
  10.1 48.7 all-gather.1
  64.9 44.0 reduce-scatter.1

commit v11 on v8

--- a/solution.py
+++ b/solution.py
@@ -126,25 +126,33 @@
     )(place, line, own, mate)
 
 
-def clip_kernel(kept_ref, arrived_ref, slope_ref, target_ref, packed_ref, pre_ref):
+def clip_kernel(kept_ref, arrived_ref, target_ref, packed_ref):
     grad = (kept_ref[...] + arrived_ref[...].astype(F32)).astype(BF16)
-    pre_ref[...] = (grad.astype(F32) * slope_ref[...]).astype(BF16)
     slots, clips = packed_ref.shape[0], grad.shape[0]
     slot = lax.broadcasted_iota(jnp.int32, (slots, clips), 0)
     placing = (slot == target_ref[...]).astype(BF16)
     packed_ref[...] = dot_of(placing, grad, 1, 0).astype(BF16)
 
 
-def clip_grads(kept, arrived, slope, targets, slots):
-    clips, features = kept.shape
+def clip_grads(kept, arrived, targets, slots):
     return pl.pallas_call(
         clip_kernel,
-        out_shape=[
-            jax.ShapeDtypeStruct((slots, features), BF16),
-            jax.ShapeDtypeStruct((clips, features), BF16),
-        ],
+        out_shape=jax.ShapeDtypeStruct((slots, kept.shape[1]), BF16),
         compiler_params=ROOM,
-    )(kept, arrived, slope, targets[None, :])
+    )(kept, arrived, targets[None, :])
+
+
+def product_kernel(kept_ref, arrived_ref, slope_ref, pre_ref):
+    grad = (kept_ref[...] + arrived_ref[...].astype(F32)).astype(BF16)
+    pre_ref[...] = (grad.astype(F32) * slope_ref[...]).astype(BF16)
+
+
+def product_rows(kept, arrived, slope):
+    return pl.pallas_call(
+        product_kernel,
+        out_shape=jax.ShapeDtypeStruct(kept.shape, BF16),
+        compiler_params=ROOM,
+    )(kept, arrived, slope)
 
 
 def weight_kernel(own_picked, mate_picked, own_pre, mate_pre, *out_refs):
@@ -201,7 +209,8 @@
     kept, sent, line_grads = pair_grads(audio_line, video, video_mate, place, 4.0 / blocks, 4)
     audio_grad = lax.psum_scatter(line_grads, "blk_z", scatter_dimension=0, tiled=True)
     arrived = swapped(sent, "blk_x")
-    packed, pre_rows = clip_grads(kept, arrived, slope_rows, targets, slots)
+    packed = clip_grads(kept, arrived, targets, slots)
+    pre_rows = product_rows(kept, arrived, slope_rows)
     received = lax.all_to_all(
         packed.reshape(peers, capacity, features), WIDE, 0, 0, tiled=True
     ).reshape(slots, features)

time: 154 us -> 154 us (level)
  local copies, waits for them, and re-layouts: 2.68 us -> 0.99 us
    unnamed x14 -> x12, local copies, waits for them, and re-layouts: 2.63 us -> 0.94 us
where the time goes in v11:
time: 154 us; the launch traced here: 153 us
  waiting for transfers between devices  55 us (36%)
  starting transfers between devices  45.2 us (29%)
  blocking collectives  18.8 us (12%)
  between operations  14.3 us (9%)
  Pallas kernels  7.25 us (5%)
  matrix products  7.04 us (5%)
  other arithmetic  4.48 us (3%)
    all_to_all x1, blocking collectives, shards(): lax.all_to_all(jnp.broadcast_to(total[None], (blocks, *total.shape)), BLK...  18.8 us
    all_to_all x1, waiting for transfers between devices, shards(): lax.all_to_all(pooled.reshape(peers, capacity, features), WIDE, 0, 0, til...  15.4 us
    all_gather x1, waiting for transfers between devices, shards(): audio_line = lax.all_gather(audio, 'blk_z', axis=0, tiled=True)  13.4 us
    all_to_all x1, starting transfers between devices, shards(): lax.all_to_all(pooled.reshape(peers, capacity, features), WIDE, 0, 0, til...  10.2 us
    ppermute x3, starting transfers between devices, shards(): lax.ppermute(parts[d], ('wide_x', 'blk_x'), pairs).astype(F32)  9.82 us
    all_to_all x1, starting transfers between devices, shards(): lax.all_to_all(packed.reshape(peers, capacity, features), WIDE, 0, 0, til...  9.8 us
    ppermute x4, starting transfers between devices, swapped(): return lax.ppermute(array, axis, [(0, 1), (1, 0)])  9.72 us
    all_to_all x1, waiting for transfers between devices, shards(): lax.all_to_all(summed.reshape(ny, -1, features), 'wide_y', 0, 0, tiled=True)  9.26 us
  transfers between devices with their start and end apart: 12, of which 9 were waited for; matrix products, arithmetic and copies ran while one was open for 8% of the time, Pallas kernels for 1%

profile of v11, /device:TPU:6, one launch (start us, length us, event | category | flops | bytes accessed | tf_op | source)
XLA Modules:
  0.0 153.0 jit_solution(5548292581382289160)
XLA Ops:
  7.2 0.0 copy-start
  7.2 0.0 copy-start.4
  7.2 0.0 copy-start.5
  7.2 0.0 all-gather.2.cloned.1.call-start
  7.2 0.7 all-gather.2.cloned.1.call-update
  7.9 2.9 %collective-permute-start = (bf16[128,1024]{1,0:T(8,128)(2,1)}, bf16[128,1024]{1,0:T(8,128)(2,1)}, u32[]{:S(2)}, u32[]{:S(2)}) collective-permute-start(bf16[128,1024]{1,0:T(8,128)(2,1)} %refs_2_.1), channel_id=1, source_target_pairs={{0,8},{8,0},{1,9},{9,1},{2,10},{10,2},{3,11},{11,3},{4,12},{12,4},... | collective-permute-start | bytes 786440 | tf_op jit(solution)/shard_map/ppermute | solution.py:20
  10.8 0.7 convert_rsqrt_fusion
  11.5 2.0 %fusion.17 = bf16[32,8,1024]{2,1,0:T(8,128)(2,1)} fusion(f32[256]{0:T(256)S(1)} %convert_rsqrt_fusion, bf16[256,1024]{1,0:T(8,128)(2,1)} %param.9), kind=kLoop, calls=%fused_computation.27 | loop fusion | flops 786432 | bytes 1049600 | tf_op jit(solution)/shard_map/reshape | solution.py:190
  13.5 10.2 %all-to-all-start = ((bf16[32,8,1024]{2,1,0:T(8,128)(2,1)}), bf16[32,8,1024]{2,1,0:T(8,128)(2,1)S(1)}, u32[]{:S(2)}, u32[]{:S(2)}) async-start(bf16[32,8,1024]{2,1,0:T(8,128)(2,1)} %fusion.17), calls=%async_computation | async-start | bytes 1048576 | tf_op jit(solution)/shard_map/all_to_all | solution.py:189
  23.7 0.0 reduce-scatter.2.cloned.1.call-start
  23.8 0.0 copy-done.5
  23.8 0.1 convert_reduce_fusion.1
  24.0 2.0 %fusion.8 = f32[256,1024]{1,0:T(8,128)} fusion(bf16[1024,1024]{1,0:T(8,128)(2,1)S(1)} %copy-done, bf16[256,1024]{1,0:T(8,128)(2,1)S(1)} %copy-done.4, f32[256]{0:T(256)S(1)} %convert_rsqrt_fusion), kind=kOutput, calls=%fused_computation.13 | convolution fusion | flops 539754496 | bytes 3671040 | tf_op jit(solution)/shard_map/dot_general | solution.py:24
  26.0 15.4 %all-to-all-done = bf16[32,8,1024]{2,1,0:T(8,128)(2,1)S(1)} async-done(((bf16[32,8,1024]{2,1,0:T(8,128)(2,1)}), bf16[32,8,1024]{2,1,0:T(8,128)(2,1)S(1)}, u32[]{:S(2)}, u32[]{:S(2)}) %all-to-all-start) | async-done | bytes 524320 | tf_op jit(solution)/shard_map/all_to_all | solution.py:189
  41.4 0.3 convolution_convert_fusion
  41.7 0.5 fusion.14.slope_ref
  42.2 0.5 fusion.3
  42.7 1.9 %collective-permute-start.1 = (bf16[128,512]{1,0:T(8,128)(2,1)S(1)}, bf16[128,512]{1,0:T(8,128)(2,1)S(1)}, u32[]{:S(2)}, u32[]{:S(2)}) collective-permute-start(bf16[128,512]{1,0:T(8,128)(2,1)S(1)} %fusion.3), channel_id=1, source_target_pairs={{0,16},{16,0},{1,17},{17,1},{2,18},{18,2},{3,19},{19,3},{4,20},{20... | collective-permute-start | bytes 393224 | tf_op jit(solution)/shard_map/ppermute | solution.py:20
  44.7 1.1 fusion.4.own_picked
  45.8 0.0 collective-permute-done.refs_3_
  45.8 0.2 collective-permute-done.1.mate_picked
  46.0 13.4 %all-gather.2.cloned.1.call-done.refs_1_ = bf16[1024,1024]{1,0:T(8,128)(2,1)} async-done(((bf16[128,1024]{1,0:T(8,128)(2,1)}), bf16[1024,1024]{1,0:T(8,128)(2,1)}) %all-gather.2.cloned.1.call-update) | async-done | bytes 2097168 | tf_op jit(solution)/shard_map/all_gather | solution.py:182
  59.4 5.6 %shard_map.85 = (f32[128,1024]{1,0:T(8,128)}, bf16[128,1024]{1,0:T(8,128)(2,1)}, bf16[1024,1024]{1,0:T(8,128)(2,1)}) custom-call(s32[1]{0:T(128)} %bitcast.refs_0_, bf16[1024,1024]{1,0:T(8,128)(2,1)} %all-gather.2.cloned.1.call-done.refs_1_, bf16[128,1024]{1,0:T(8,128)(2,1)} %refs_2_.1, bf16[128,1024]{1,0:T(8,128)(2,1)} %collective-permute-done.refs_3_), custom_call_target="tpu_custom_call" | custom-call | flops 1610612736 | bytes 5242880 | tf_op jit(solution)/shard_map/pallas_call | solution.py:105
  65.0 0.0 copy-start.1
  65.0 0.0 reduce-scatter.2.cloned.1.call-update
  65.1 2.9 %collective-permute-start.2 = (bf16[128,1024]{1,0:T(8,128)(2,1)}, bf16[128,1024]{1,0:T(8,128)(2,1)S(1)}, u32[]{:S(2)}, u32[]{:S(2)}) collective-permute-start(bf16[128,1024]{1,0:T(8,128)(2,1)} %get-tuple-element.27), channel_id=1, source_target_pairs={{0,8},{8,0},{1,9},{9,1},{2,10},{10,2},{3,11},{11,3},{4,12},{12,4},... | collective-permute-start | bytes 786440 | tf_op jit(solution)/shard_map/ppermute | solution.py:20
  68.0 5.7 %collective-permute-done.2.arrived_ref = bf16[128,1024]{1,0:T(8,128)(2,1)S(1)} collective-permute-done((bf16[128,1024]{1,0:T(8,128)(2,1)}, bf16[128,1024]{1,0:T(8,128)(2,1)S(1)}, u32[]{:S(2)}, u32[]{:S(2)}) %collective-permute-start.2) | collective-permute-done | bytes 262176 | tf_op jit(solution)/shard_map/ppermute | solution.py:20
  73.7 1.1 shard_map.88
  74.8 9.8 %all-to-all-start.1 = ((bf16[32,8,1024]{2,1,0:T(8,128)(2,1)}), bf16[32,8,1024]{2,1,0:T(8,128)(2,1)}, u32[]{:S(2)}, u32[]{:S(2)}) async-start(bf16[32,8,1024]{2,1,0:T(8,128)(2,1)} %bitcast.7), calls=%async_computation.2 | async-start | bytes 1048576 | tf_op jit(solution)/shard_map/all_to_all | solution.py:214
  84.6 0.1 shard_map.86.own_pre
  84.7 2.1 %collective-permute-start.3 = (bf16[128,1024]{1,0:T(8,128)(2,1)S(1)}, bf16[128,1024]{1,0:T(8,128)(2,1)S(1)}, u32[]{:S(2)}, u32[]{:S(2)}) collective-permute-start(bf16[128,1024]{1,0:T(8,128)(2,1)S(1)} %shard_map.86.own_pre), channel_id=1, source_target_pairs={{0,16},{16,0},{1,17},{17,1},{2,18},{18,2},{3,19},{19,3},{4,20},{20... | collective-permute-start | bytes 786440 | tf_op jit(solution)/shard_map/ppermute | solution.py:20
  86.7 1.4 collective-permute-done.3.mate_pre
  88.1 0.9 copy-done.2
  89.0 0.5 shard_map.87
  89.5 2.2 %collective-permute-start.4 = (bf16[128,1024]{1,0:T(8,128)(2,1)S(1)}, bf16[128,1024]{1,0:T(8,128)(2,1)S(1)}, u32[]{:S(2)}, u32[]{:S(2)}) collective-permute-start(bf16[128,1024]{1,0:T(8,128)(2,1)S(1)} %get-tuple-element.30), channel_id=1, source_target_pairs={{0,32},{8,40},{32,0},{40,8},{1,33},{9,41},{33,1},{41,9},{2,34},{10... | collective-permute-start | bytes 786440 | tf_op jit(solution)/shard_map/ppermute | solution.py:223
  91.7 2.9 %collective-permute-start.5 = (bf16[128,1024]{1,0:T(8,128)(2,1)S(1)}, bf16[128,1024]{1,0:T(8,128)(2,1)S(1)}, u32[]{:S(2)}, u32[]{:S(2)}) collective-permute-start(bf16[128,1024]{1,0:T(8,128)(2,1)S(1)} %get-tuple-element.31), channel_id=1, source_target_pairs={{0,8},{8,0},{32,40},{40,32},{1,9},{9,1},{33,41},{41,33},{2,10},{10... | collective-permute-start | bytes 786440 | tf_op jit(solution)/shard_map/ppermute | solution.py:223
  94.7 4.7 %collective-permute-start.6 = (bf16[128,1024]{1,0:T(8,128)(2,1)S(1)}, bf16[128,1024]{1,0:T(8,128)(2,1)S(1)}, u32[]{:S(2)}, u32[]{:S(2)}) collective-permute-start(bf16[128,1024]{1,0:T(8,128)(2,1)S(1)} %get-tuple-element.32), channel_id=1, source_target_pairs={{0,40},{8,32},{32,8},{40,0},{1,41},{9,33},{33,9},{41,1},{2,42},{10... | collective-permute-start | bytes 786440 | tf_op jit(solution)/shard_map/ppermute | solution.py:223
  99.3 3.8 %collective-permute-done.4 = bf16[128,1024]{1,0:T(8,128)(2,1)S(1)} collective-permute-done((bf16[128,1024]{1,0:T(8,128)(2,1)S(1)}, bf16[128,1024]{1,0:T(8,128)(2,1)S(1)}, u32[]{:S(2)}, u32[]{:S(2)}) %collective-permute-start.4) | collective-permute-done | bytes 262176 | tf_op jit(solution)/shard_map/ppermute | solution.py:223
  103.2 4.3 %collective-permute-done.5 = bf16[128,1024]{1,0:T(8,128)(2,1)S(1)} collective-permute-done((bf16[128,1024]{1,0:T(8,128)(2,1)S(1)}, bf16[128,1024]{1,0:T(8,128)(2,1)S(1)}, u32[]{:S(2)}, u32[]{:S(2)}) %collective-permute-start.5) | collective-permute-done | bytes 262176 | tf_op jit(solution)/shard_map/ppermute | solution.py:223
  107.5 0.8 collective-permute-done.6
  108.3 0.9 add_convert_fusion
  109.1 0.0 all-to-all-done.1
  109.1 5.6 %all-to-all-start.2 = ((bf16[8,16,1024]{2,1,0:T(8,128)(2,1)}), bf16[8,16,1024]{2,1,0:T(8,128)(2,1)S(1)}, u32[]{:S(2)}, u32[]{:S(2)}) async-start(bf16[8,16,1024]{2,1,0:T(8,128)(2,1)} %bitcast.29), calls=%async_computation.3 | async-start | bytes 524288 | tf_op jit(solution)/shard_map/all_to_all | solution.py:227
  114.7 2.6 %fusion.2 = bf16[256,1024]{1,0:T(8,128)(2,1)} fusion(bf16[1024,1024]{1,0:T(8,128)(2,1)S(1)} %copy-done, f32[256,1024]{1,0:T(8,128)S(1)} %copy-done.3, bf16[256,1024]{1,0:T(8,128)(2,1)} %bitcast.8, f32[256]{0:T(256)S(1)} %convert_rsqrt_fusion), kind=kOutput, calls=%fused_computation.6 | convolution fusion | flops 538181632 | bytes 4195328 | tf_op jit(solution)/shard_map/dot_general | solution.py:24
  117.3 9.3 %all-to-all-done.2 = bf16[8,16,1024]{2,1,0:T(8,128)(2,1)S(1)} async-done(((bf16[8,16,1024]{2,1,0:T(8,128)(2,1)}), bf16[8,16,1024]{2,1,0:T(8,128)(2,1)S(1)}, u32[]{:S(2)}, u32[]{:S(2)}) %all-to-all-start.2) | async-done | bytes 262176 | tf_op jit(solution)/shard_map/all_to_all | solution.py:227
  126.6 0.1 broadcast_in_dim.8
  126.7 18.8 %all_to_all.20 = bf16[16,16,1024]{2,1,0:T(8,128)(2,1)S(1)} all-to-all(bf16[16,16,1024]{2,1,0:T(8,128)(2,1)S(1)} %broadcast_in_dim.8), channel_id=1, replica_groups=mesh['wide_y'=8,'wide_x'=2,'wide_c'=2,'blk_x'=2,'blk_z'=8] {'blk_x','blk..., dimensions={0} | all-to-all | bytes 1048576 | tf_op jit(solution)/shard_map/all_to_all | solution.py:232
  145.5 0.7 convert_reduce_fusion
  (12 shorter events, 0.1 us)
Async XLA Ops:
  7.2 16.8 %copy-start = (bf16[1024,1024]{1,0:T(8,128)(2,1)S(1)}, bf16[1024,1024]{1,0:T(8,128)(2,1)}, u32[]{:S(2)}) copy-start(bf16[1024,1024]{1,0:T(8,128)(2,1)} %param.11) | copy-start | bytes 6291460
  7.2 16.8 %copy-start.4 = (bf16[256,1024]{1,0:T(8,128)(2,1)S(1)}, bf16[256,1024]{1,0:T(8,128)(2,1)}, u32[]{:S(2)}) copy-start(bf16[256,1024]{1,0:T(8,128)(2,1)} %param.9) | copy-start | bytes 1572868
  7.2 16.6 %copy-start.5 = (s32[128,1]{0,1:T(1,128)S(1)}, s32[128,1]{0,1:T(1,128)}, u32[]{:S(2)}) copy-start(s32[128,1]{0,1:T(1,128)} %param.8) | copy-start | bytes 1540
  7.2 52.2 %all-gather.2.cloned.1.call-start = ((), (), s32[]{:S(2)}) async-start(), calls=%async_computation.5 | async-start | bytes 2359296 | tf_op jit(solution)/shard_map/all_gather | solution.py:182
  7.9 37.9 %collective-permute-start = (bf16[128,1024]{1,0:T(8,128)(2,1)}, bf16[128,1024]{1,0:T(8,128)(2,1)}, u32[]{:S(2)}, u32[]{:S(2)}) collective-permute-start(bf16[128,1024]{1,0:T(8,128)(2,1)} %refs_2_.1), channel_id=1, source_target_pairs={{0,8},{8,0},{1,9},{9,1},{2,10},{10,2},{3,11},{11,3},{4,12},{12,4},... | collective-permute-start | bytes 786440 | tf_op jit(solution)/shard_map/ppermute | solution.py:20
  13.5 27.9 %all-to-all-start = ((bf16[32,8,1024]{2,1,0:T(8,128)(2,1)}), bf16[32,8,1024]{2,1,0:T(8,128)(2,1)S(1)}, u32[]{:S(2)}, u32[]{:S(2)}) async-start(bf16[32,8,1024]{2,1,0:T(8,128)(2,1)} %fusion.17), calls=%async_computation | async-start | bytes 1048576 | tf_op jit(solution)/shard_map/all_to_all | solution.py:189
  23.7 122.5 %reduce-scatter.2.cloned.1.call-start = ((), (), s32[]{:S(2)}) async-start(), calls=%async_computation.6 | async-start | bytes 2359296 | tf_op jit(solution)/shard_map/reduce_scatter | solution.py:210
  42.7 3.2 %collective-permute-start.1 = (bf16[128,512]{1,0:T(8,128)(2,1)S(1)}, bf16[128,512]{1,0:T(8,128)(2,1)S(1)}, u32[]{:S(2)}, u32[]{:S(2)}) collective-permute-start(bf16[128,512]{1,0:T(8,128)(2,1)S(1)} %fusion.3), channel_id=1, source_target_pairs={{0,16},{16,0},{1,17},{17,1},{2,18},{18,2},{3,19},{19,3},{4,20},{20... | collective-permute-start | bytes 393224 | tf_op jit(solution)/shard_map/ppermute | solution.py:20
  65.0 8.6 %copy-start.1 = (f32[128,1024]{1,0:T(8,128)S(1)}, f32[128,1024]{1,0:T(8,128)}, u32[]{:S(2)}) copy-start(f32[128,1024]{1,0:T(8,128)} %get-tuple-element.26.kept_ref) | copy-start | bytes 1572868
  65.1 8.6 %collective-permute-start.2 = (bf16[128,1024]{1,0:T(8,128)(2,1)}, bf16[128,1024]{1,0:T(8,128)(2,1)S(1)}, u32[]{:S(2)}, u32[]{:S(2)}) collective-permute-start(bf16[128,1024]{1,0:T(8,128)(2,1)} %get-tuple-element.27), channel_id=1, source_target_pairs={{0,8},{8,0},{1,9},{9,1},{2,10},{10,2},{3,11},{11,3},{4,12},{12,4},... | collective-permute-start | bytes 786440 | tf_op jit(solution)/shard_map/ppermute | solution.py:20
  74.8 34.4 %all-to-all-start.1 = ((bf16[32,8,1024]{2,1,0:T(8,128)(2,1)}), bf16[32,8,1024]{2,1,0:T(8,128)(2,1)}, u32[]{:S(2)}, u32[]{:S(2)}) async-start(bf16[32,8,1024]{2,1,0:T(8,128)(2,1)} %bitcast.7), calls=%async_computation.2 | async-start | bytes 1048576 | tf_op jit(solution)/shard_map/all_to_all | solution.py:214
  84.7 3.4 %collective-permute-start.3 = (bf16[128,1024]{1,0:T(8,128)(2,1)S(1)}, bf16[128,1024]{1,0:T(8,128)(2,1)S(1)}, u32[]{:S(2)}, u32[]{:S(2)}) collective-permute-start(bf16[128,1024]{1,0:T(8,128)(2,1)S(1)} %shard_map.86.own_pre), channel_id=1, source_target_pairs={{0,16},{16,0},{1,17},{17,1},{2,18},{18,2},{3,19},{19,3},{4,20},{20... | collective-permute-start | bytes 786440 | tf_op jit(solution)/shard_map/ppermute | solution.py:20
  88.1 0.9 copy-start.2
  89.0 25.7 %copy-start.3 = (f32[256,1024]{1,0:T(8,128)S(1)}, f32[256,1024]{1,0:T(8,128)}, u32[]{:S(2)}) copy-start(f32[256,1024]{1,0:T(8,128)} %fusion.8) | copy-start | bytes 3145732
  89.5 13.7 %collective-permute-start.4 = (bf16[128,1024]{1,0:T(8,128)(2,1)S(1)}, bf16[128,1024]{1,0:T(8,128)(2,1)S(1)}, u32[]{:S(2)}, u32[]{:S(2)}) collective-permute-start(bf16[128,1024]{1,0:T(8,128)(2,1)S(1)} %get-tuple-element.30), channel_id=1, source_target_pairs={{0,32},{8,40},{32,0},{40,8},{1,33},{9,41},{33,1},{41,9},{2,34},{10... | collective-permute-start | bytes 786440 | tf_op jit(solution)/shard_map/ppermute | solution.py:223
  91.7 15.8 %collective-permute-start.5 = (bf16[128,1024]{1,0:T(8,128)(2,1)S(1)}, bf16[128,1024]{1,0:T(8,128)(2,1)S(1)}, u32[]{:S(2)}, u32[]{:S(2)}) collective-permute-start(bf16[128,1024]{1,0:T(8,128)(2,1)S(1)} %get-tuple-element.31), channel_id=1, source_target_pairs={{0,8},{8,0},{32,40},{40,32},{1,9},{9,1},{33,41},{41,33},{2,10},{10... | collective-permute-start | bytes 786440 | tf_op jit(solution)/shard_map/ppermute | solution.py:223
  94.7 13.6 %collective-permute-start.6 = (bf16[128,1024]{1,0:T(8,128)(2,1)S(1)}, bf16[128,1024]{1,0:T(8,128)(2,1)S(1)}, u32[]{:S(2)}, u32[]{:S(2)}) collective-permute-start(bf16[128,1024]{1,0:T(8,128)(2,1)S(1)} %get-tuple-element.32), channel_id=1, source_target_pairs={{0,40},{8,32},{32,8},{40,0},{1,41},{9,33},{33,9},{41,1},{2,42},{10... | collective-permute-start | bytes 786440 | tf_op jit(solution)/shard_map/ppermute | solution.py:223
  109.1 17.5 %all-to-all-start.2 = ((bf16[8,16,1024]{2,1,0:T(8,128)(2,1)}), bf16[8,16,1024]{2,1,0:T(8,128)(2,1)S(1)}, u32[]{:S(2)}, u32[]{:S(2)}) async-start(bf16[8,16,1024]{2,1,0:T(8,128)(2,1)} %bitcast.29), calls=%async_computation.3 | async-start | bytes 524288 | tf_op jit(solution)/shard_map/all_to_all | solution.py:227
Sparse Core Ops, SparseCore 0:
  10.1 49.2 all-gather.1
  65.2 43.4 reduce-scatter.1

commit v12 on v11

--- a/solution.py
+++ b/solution.py
@@ -45,10 +45,8 @@
     share = half // (ny * nx * bx)
     place = jnp.arange(half, dtype=jnp.int32)
     within, rest = place % share, place // share
-    y, apart = rest % ny, rest // ny
-    x_wide = (apart // bx) ^ lax.axis_index("wide_x")
-    x_blk = (apart % bx) ^ lax.axis_index("blk_x")
-    feature = (((y * nx + x_wide) * 2 + core) * bx + x_blk) * share + within
+    owner, line = rest % (ny * nx), (rest // (ny * nx)) ^ lax.axis_index("blk_x")
+    feature = ((owner * 2 + core) * bx + line) * share + within
     return (jnp.arange(feature_count, dtype=jnp.int32)[:, None] == feature[None, :]).astype(BF16)
 
 
@@ -216,15 +214,13 @@
     ).reshape(slots, features)
 
     pre_mate = swapped(pre_rows, "wide_c")
-    parts = weight_parts(picked, picked_mate, pre_rows, pre_mate, 4)
-    summed = parts[0]
-    for d in (2, 1, 3):
-        pairs = [(at, at ^ d) for at in range(4)]
-        summed = summed + lax.ppermute(parts[d], ("wide_x", "blk_x"), pairs).astype(F32)
-    summed = summed.astype(BF16)
+    keep, give = weight_parts(picked, picked_mate, pre_rows, pre_mate, 2)
+    summed = (keep + swapped(give, "blk_x").astype(F32)).astype(BF16)
     summed, received = lax.optimization_barrier((summed, received))
-    ny = lax.axis_size("wide_y")
-    pieces = lax.all_to_all(summed.reshape(ny, -1, features), "wide_y", 0, 0, tiled=True)
+    chips = peers // 2
+    pieces = lax.all_to_all(
+        summed.reshape(chips, -1, features), ("wide_y", "wide_x"), 0, 0, tiled=True
+    )
     pre_grad = (received.astype(F32) * slope_own).astype(BF16)
     feats_grad = (dot_of(pre_grad, proj_weight, 1, 1) * length_scale).astype(BF16)
     pieces, feats_grad = lax.optimization_barrier((pieces, feats_grad))

time: 154 us -> 163 us (1.058)
  the two profiles are of different devices: /device:TPU:6 before, /device:TPU:24 now
where the time goes in v12:
time: 163 us; the launch traced here: 162 us
  waiting for transfers between devices  64.9 us (40%)
  starting transfers between devices  41.9 us (26%)
  blocking collectives  19.9 us (12%)
  between operations  14.3 us (9%)
  matrix products  7.33 us (4%)
  Pallas kernels  7.28 us (4%)
  other arithmetic  4.57 us (3%)
  local copies, waits for them, and re-layouts  1.89 us (1%)
    ppermute x5, waiting for transfers between devices, swapped(): return lax.ppermute(array, axis, [(0, 1), (1, 0)])  22 us
    all_to_all x1, blocking collectives, shards(): lax.all_to_all(jnp.broadcast_to(total[None], (blocks, *total.shape)), BLK...  19.9 us
    all_gather x1, waiting for transfers between devices, shards(): audio_line = lax.all_gather(audio, 'blk_z', axis=0, tiled=True)  14.4 us
    all_to_all x1, waiting for transfers between devices, shards(): lax.all_to_all(pooled.reshape(peers, capacity, features), WIDE, 0, 0, til...  14.2 us
    all_to_all x1, waiting for transfers between devices, shards(): lax.all_to_all(summed.reshape(chips, -1, features), ('wide_y', 'wide_x'),...  13.6 us
    ppermute x5, starting transfers between devices, swapped(): return lax.ppermute(array, axis, [(0, 1), (1, 0)])  13 us
    all_to_all x1, starting transfers between devices, shards(): lax.all_to_all(packed.reshape(peers, capacity, features), WIDE, 0, 0, til...  10.1 us
    all_to_all x1, starting transfers between devices, shards(): lax.all_to_all(pooled.reshape(peers, capacity, features), WIDE, 0, 0, til...  9.65 us
  transfers between devices with their start and end apart: 10, of which 6 were waited for; matrix products, arithmetic and copies ran while one was open for 7% of the time, Pallas kernels for 1%

profile of v12, /device:TPU:24, one launch (start us, length us, event | category | flops | bytes accessed | tf_op | source)
XLA Modules:
  0.0 162.0 jit_solution(9454967966579022881)
XLA Ops:
  7.2 0.0 copy-start
  7.2 0.0 copy-start.3
  7.2 0.0 copy-start.6
  7.2 0.0 all-gather.2.cloned.1.call-start
  7.2 0.7 all-gather.2.cloned.1.call-update
  7.9 3.5 %collective-permute-start = (bf16[128,1024]{1,0:T(8,128)(2,1)}, bf16[128,1024]{1,0:T(8,128)(2,1)S(1)}, u32[]{:S(2)}, u32[]{:S(2)}) collective-permute-start(bf16[128,1024]{1,0:T(8,128)(2,1)} %refs_2_.1), channel_id=1, source_target_pairs={{0,8},{8,0},{1,9},{9,1},{2,10},{10,2},{3,11},{11,3},{4,12},{12,4},... | collective-permute-start | bytes 786440 | tf_op jit(solution)/shard_map/ppermute | solution.py:20
  11.5 0.7 convert_rsqrt_fusion
  12.2 2.0 %fusion.17 = bf16[32,8,1024]{2,1,0:T(8,128)(2,1)} fusion(f32[256]{0:T(256)S(1)} %convert_rsqrt_fusion, bf16[256,1024]{1,0:T(8,128)(2,1)} %param.9), kind=kLoop, calls=%fused_computation.27 | loop fusion | flops 786432 | bytes 1049600 | tf_op jit(solution)/shard_map/reshape | solution.py:188
  14.2 9.7 %all-to-all-start = ((bf16[32,8,1024]{2,1,0:T(8,128)(2,1)}), bf16[32,8,1024]{2,1,0:T(8,128)(2,1)S(1)}, u32[]{:S(2)}, u32[]{:S(2)}) async-start(bf16[32,8,1024]{2,1,0:T(8,128)(2,1)} %fusion.17), calls=%async_computation | async-start | bytes 1048576 | tf_op jit(solution)/shard_map/all_to_all | solution.py:187
  23.8 0.0 reduce-scatter.2.cloned.1.call-start
  23.9 0.0 copy-done.6
  23.9 0.1 convert_reduce_fusion.1
  24.1 2.0 %fusion.8 = f32[256,1024]{1,0:T(8,128)} fusion(bf16[1024,1024]{1,0:T(8,128)(2,1)S(1)} %copy-done, bf16[256,1024]{1,0:T(8,128)(2,1)S(1)} %copy-done.3, f32[256]{0:T(256)S(1)} %convert_rsqrt_fusion), kind=kOutput, calls=%fused_computation.13 | convolution fusion | flops 539754496 | bytes 3671040 | tf_op jit(solution)/shard_map/dot_general | solution.py:24
  26.1 14.2 %all-to-all-done = bf16[32,8,1024]{2,1,0:T(8,128)(2,1)S(1)} async-done(((bf16[32,8,1024]{2,1,0:T(8,128)(2,1)}), bf16[32,8,1024]{2,1,0:T(8,128)(2,1)S(1)}, u32[]{:S(2)}, u32[]{:S(2)}) %all-to-all-start) | async-done | bytes 524320 | tf_op jit(solution)/shard_map/all_to_all | solution.py:187
  40.2 0.3 convolution_convert_fusion
  40.5 0.5 fusion.14.slope_ref
  41.1 0.5 fusion.3
  41.5 1.9 %collective-permute-start.1 = (bf16[128,512]{1,0:T(8,128)(2,1)S(1)}, bf16[128,512]{1,0:T(8,128)(2,1)S(1)}, u32[]{:S(2)}, u32[]{:S(2)}) collective-permute-start(bf16[128,512]{1,0:T(8,128)(2,1)S(1)} %fusion.3), channel_id=1, source_target_pairs={{0,16},{16,0},{1,17},{17,1},{2,18},{18,2},{3,19},{19,3},{4,20},{20... | collective-permute-start | bytes 393224 | tf_op jit(solution)/shard_map/ppermute | solution.py:20
  43.5 1.1 fusion.4.own_picked
  44.6 0.0 collective-permute-done.refs_3_
  44.6 0.2 collective-permute-done.1.mate_picked
  44.8 14.4 %all-gather.2.cloned.1.call-done.refs_1_ = bf16[1024,1024]{1,0:T(8,128)(2,1)} async-done(((bf16[128,1024]{1,0:T(8,128)(2,1)}), bf16[1024,1024]{1,0:T(8,128)(2,1)}) %all-gather.2.cloned.1.call-update) | async-done | bytes 2097168 | tf_op jit(solution)/shard_map/all_gather | solution.py:180
  59.2 5.6 %shard_map.85 = (f32[128,1024]{1,0:T(8,128)}, bf16[128,1024]{1,0:T(8,128)(2,1)}, bf16[1024,1024]{1,0:T(8,128)(2,1)}) custom-call(s32[1]{0:T(128)} %bitcast.refs_0_, bf16[1024,1024]{1,0:T(8,128)(2,1)} %all-gather.2.cloned.1.call-done.refs_1_, bf16[128,1024]{1,0:T(8,128)(2,1)} %refs_2_.1, bf16[128,1024]{1,0:T(8,128)(2,1)} %copy-done.4), custom_call_target="tpu_custom_call" | custom-call | flops 1610612736 | bytes 5242880 | tf_op jit(solution)/shard_map/pallas_call | solution.py:103
  64.8 0.0 copy-start.5
  64.8 0.0 copy-start.1
  64.9 0.0 reduce-scatter.2.cloned.1.call-update
  64.9 0.9 copy-done.5
  65.8 3.3 %collective-permute-start.2 = (bf16[128,1024]{1,0:T(8,128)(2,1)S(1)}, bf16[128,1024]{1,0:T(8,128)(2,1)S(1)}, u32[]{:S(2)}, u32[]{:S(2)}) collective-permute-start(bf16[128,1024]{1,0:T(8,128)(2,1)S(1)} %copy-done.5), channel_id=1, source_target_pairs={{0,8},{8,0},{1,9},{9,1},{2,10},{10,2},{3,11},{11,3},{4,12},{12,4},... | collective-permute-start | bytes 786440 | tf_op jit(solution)/shard_map/ppermute | solution.py:20
  69.1 4.9 %collective-permute-done.2.arrived_ref = bf16[128,1024]{1,0:T(8,128)(2,1)S(1)} collective-permute-done((bf16[128,1024]{1,0:T(8,128)(2,1)S(1)}, bf16[128,1024]{1,0:T(8,128)(2,1)S(1)}, u32[]{:S(2)}, u32[]{:S(2)}) %collective-permute-start.2) | collective-permute-done | bytes 262176 | tf_op jit(solution)/shard_map/ppermute | solution.py:20
  74.0 0.1 shard_map.86.own_pre
  74.1 1.9 %collective-permute-start.3 = (bf16[128,1024]{1,0:T(8,128)(2,1)S(1)}, bf16[128,1024]{1,0:T(8,128)(2,1)S(1)}, u32[]{:S(2)}, u32[]{:S(2)}) collective-permute-start(bf16[128,1024]{1,0:T(8,128)(2,1)S(1)} %shard_map.86.own_pre), channel_id=1, source_target_pairs={{0,16},{16,0},{1,17},{17,1},{2,18},{18,2},{3,19},{19,3},{4,20},{20... | collective-permute-start | bytes 786440 | tf_op jit(solution)/shard_map/ppermute | solution.py:20
  76.1 1.1 shard_map.88
  77.2 10.1 %all-to-all-start.1 = ((bf16[32,8,1024]{2,1,0:T(8,128)(2,1)}), bf16[32,8,1024]{2,1,0:T(8,128)(2,1)}, u32[]{:S(2)}, u32[]{:S(2)}) async-start(bf16[32,8,1024]{2,1,0:T(8,128)(2,1)} %bitcast.7), calls=%async_computation.2 | async-start | bytes 1048576 | tf_op jit(solution)/shard_map/all_to_all | solution.py:212
  87.2 0.0 collective-permute-done.3.mate_pre
  87.2 0.0 copy-start.2
  87.3 0.9 copy-done.2
  88.2 0.5 shard_map.87
  88.6 2.3 %collective-permute-start.4 = (bf16[256,1024]{1,0:T(8,128)(2,1)S(1)}, bf16[256,1024]{1,0:T(8,128)(2,1)S(1)}, u32[]{:S(2)}, u32[]{:S(2)}) collective-permute-start(bf16[256,1024]{1,0:T(8,128)(2,1)S(1)} %get-tuple-element.28), channel_id=1, source_target_pairs={{0,8},{8,0},{1,9},{9,1},{2,10},{10,2},{3,11},{11,3},{4,12},{12,4},... | collective-permute-start | bytes 1572872 | tf_op jit(solution)/shard_map/ppermute | solution.py:20
  90.9 17.0 %collective-permute-done.4 = bf16[256,1024]{1,0:T(8,128)(2,1)S(1)} collective-permute-done((bf16[256,1024]{1,0:T(8,128)(2,1)S(1)}, bf16[256,1024]{1,0:T(8,128)(2,1)S(1)}, u32[]{:S(2)}, u32[]{:S(2)}) %collective-permute-start.4) | collective-permute-done | bytes 524320 | tf_op jit(solution)/shard_map/ppermute | solution.py:20
  107.9 0.9 add_convert_fusion
  108.8 0.0 all-to-all-done.1
  108.8 9.1 %all-to-all-start.2 = ((bf16[16,16,1024]{2,1,0:T(8,128)(2,1)}), bf16[16,16,1024]{2,1,0:T(8,128)(2,1)S(1)}, u32[]{:S(2)}, u32[]{:S(2)}) async-start(bf16[16,16,1024]{2,1,0:T(8,128)(2,1)} %bitcast.9), calls=%async_computation.3 | async-start | bytes 1048576 | tf_op jit(solution)/shard_map/all_to_all | solution.py:221
  118.0 2.9 %fusion.2 = bf16[256,1024]{1,0:T(8,128)(2,1)} fusion(bf16[1024,1024]{1,0:T(8,128)(2,1)S(1)} %copy-done, f32[256,1024]{1,0:T(8,128)} %fusion.8, bf16[256,1024]{1,0:T(8,128)(2,1)} %bitcast.8, f32[256]{0:T(256)S(1)} %convert_rsqrt_fusion), kind=kOutput, calls=%fused_computation.6 | convolution fusion | flops 538181632 | bytes 4195328 | tf_op jit(solution)/shard_map/dot_general | solution.py:24
  120.9 13.6 %all-to-all-done.2 = bf16[16,16,1024]{2,1,0:T(8,128)(2,1)S(1)} async-done(((bf16[16,16,1024]{2,1,0:T(8,128)(2,1)}), bf16[16,16,1024]{2,1,0:T(8,128)(2,1)S(1)}, u32[]{:S(2)}, u32[]{:S(2)}) %all-to-all-start.2) | async-done | bytes 524320 | tf_op jit(solution)/shard_map/all_to_all | solution.py:221
  134.4 0.1 reduce_sum.34
  134.5 0.1 broadcast_in_dim.8
  134.6 19.9 %all_to_all.20 = bf16[16,16,1024]{2,1,0:T(8,128)(2,1)S(1)} all-to-all(bf16[16,16,1024]{2,1,0:T(8,128)(2,1)S(1)} %broadcast_in_dim.8), channel_id=1, replica_groups=mesh['wide_y'=8,'wide_x'=2,'wide_c'=2,'blk_x'=2,'blk_z'=8] {'blk_x','blk..., dimensions={0} | all-to-all | bytes 1048576 | tf_op jit(solution)/shard_map/all_to_all | solution.py:228
  154.4 0.7 convert_reduce_fusion
  (10 shorter events, 0.0 us)
Async XLA Ops:
  7.2 16.9 %copy-start = (bf16[1024,1024]{1,0:T(8,128)(2,1)S(1)}, bf16[1024,1024]{1,0:T(8,128)(2,1)}, u32[]{:S(2)}) copy-start(bf16[1024,1024]{1,0:T(8,128)(2,1)} %param.11) | copy-start | bytes 6291460
  7.2 16.9 %copy-start.3 = (bf16[256,1024]{1,0:T(8,128)(2,1)S(1)}, bf16[256,1024]{1,0:T(8,128)(2,1)}, u32[]{:S(2)}) copy-start(bf16[256,1024]{1,0:T(8,128)(2,1)} %param.9) | copy-start | bytes 1572868
  7.2 16.7 %copy-start.6 = (s32[128,1]{0,1:T(1,128)S(1)}, s32[128,1]{0,1:T(1,128)}, u32[]{:S(2)}) copy-start(s32[128,1]{0,1:T(1,128)} %param.8) | copy-start | bytes 1540
  7.2 52.0 %all-gather.2.cloned.1.call-start = ((), (), s32[]{:S(2)}) async-start(), calls=%async_computation.5 | async-start | bytes 2359296 | tf_op jit(solution)/shard_map/all_gather | solution.py:180
  7.9 36.7 %collective-permute-start = (bf16[128,1024]{1,0:T(8,128)(2,1)}, bf16[128,1024]{1,0:T(8,128)(2,1)S(1)}, u32[]{:S(2)}, u32[]{:S(2)}) collective-permute-start(bf16[128,1024]{1,0:T(8,128)(2,1)} %refs_2_.1), channel_id=1, source_target_pairs={{0,8},{8,0},{1,9},{9,1},{2,10},{10,2},{3,11},{11,3},{4,12},{12,4},... | collective-permute-start | bytes 786440 | tf_op jit(solution)/shard_map/ppermute | solution.py:20
  14.2 26.1 %all-to-all-start = ((bf16[32,8,1024]{2,1,0:T(8,128)(2,1)}), bf16[32,8,1024]{2,1,0:T(8,128)(2,1)S(1)}, u32[]{:S(2)}, u32[]{:S(2)}) async-start(bf16[32,8,1024]{2,1,0:T(8,128)(2,1)} %fusion.17), calls=%async_computation | async-start | bytes 1048576 | tf_op jit(solution)/shard_map/all_to_all | solution.py:187
  23.8 131.4 %reduce-scatter.2.cloned.1.call-start = ((), (), s32[]{:S(2)}) async-start(), calls=%async_computation.6 | async-start | bytes 2359296 | tf_op jit(solution)/shard_map/reduce_scatter | solution.py:208
  41.5 3.2 %collective-permute-start.1 = (bf16[128,512]{1,0:T(8,128)(2,1)S(1)}, bf16[128,512]{1,0:T(8,128)(2,1)S(1)}, u32[]{:S(2)}, u32[]{:S(2)}) collective-permute-start(bf16[128,512]{1,0:T(8,128)(2,1)S(1)} %fusion.3), channel_id=1, source_target_pairs={{0,16},{16,0},{1,17},{17,1},{2,18},{18,2},{3,19},{19,3},{4,20},{20... | collective-permute-start | bytes 393224 | tf_op jit(solution)/shard_map/ppermute | solution.py:20
  44.6 14.6 %copy-start.4 = (bf16[128,1024]{1,0:T(8,128)(2,1)}, bf16[128,1024]{1,0:T(8,128)(2,1)S(1)}, u32[]{:S(2)}) copy-start(bf16[128,1024]{1,0:T(8,128)(2,1)S(1)} %collective-permute-done.refs_3_) | copy-start | bytes 786436
  64.8 1.0 copy-start.5
  64.8 9.2 %copy-start.1 = (f32[128,1024]{1,0:T(8,128)S(1)}, f32[128,1024]{1,0:T(8,128)}, u32[]{:S(2)}) copy-start(f32[128,1024]{1,0:T(8,128)} %get-tuple-element.24.kept_ref) | copy-start | bytes 1572868
  65.8 8.3 %collective-permute-start.2 = (bf16[128,1024]{1,0:T(8,128)(2,1)S(1)}, bf16[128,1024]{1,0:T(8,128)(2,1)S(1)}, u32[]{:S(2)}, u32[]{:S(2)}) collective-permute-start(bf16[128,1024]{1,0:T(8,128)(2,1)S(1)} %copy-done.5), channel_id=1, source_target_pairs={{0,8},{8,0},{1,9},{9,1},{2,10},{10,2},{3,11},{11,3},{4,12},{12,4},... | collective-permute-start | bytes 786440 | tf_op jit(solution)/shard_map/ppermute | solution.py:20
  74.1 13.1 %collective-permute-start.3 = (bf16[128,1024]{1,0:T(8,128)(2,1)S(1)}, bf16[128,1024]{1,0:T(8,128)(2,1)S(1)}, u32[]{:S(2)}, u32[]{:S(2)}) collective-permute-start(bf16[128,1024]{1,0:T(8,128)(2,1)S(1)} %shard_map.86.own_pre), channel_id=1, source_target_pairs={{0,16},{16,0},{1,17},{17,1},{2,18},{18,2},{3,19},{19,3},{4,20},{20... | collective-permute-start | bytes 786440 | tf_op jit(solution)/shard_map/ppermute | solution.py:20
  77.2 31.6 %all-to-all-start.1 = ((bf16[32,8,1024]{2,1,0:T(8,128)(2,1)}), bf16[32,8,1024]{2,1,0:T(8,128)(2,1)}, u32[]{:S(2)}, u32[]{:S(2)}) async-start(bf16[32,8,1024]{2,1,0:T(8,128)(2,1)} %bitcast.7), calls=%async_computation.2 | async-start | bytes 1048576 | tf_op jit(solution)/shard_map/all_to_all | solution.py:212
  87.2 0.9 copy-start.2
  88.6 19.3 %collective-permute-start.4 = (bf16[256,1024]{1,0:T(8,128)(2,1)S(1)}, bf16[256,1024]{1,0:T(8,128)(2,1)S(1)}, u32[]{:S(2)}, u32[]{:S(2)}) collective-permute-start(bf16[256,1024]{1,0:T(8,128)(2,1)S(1)} %get-tuple-element.28), channel_id=1, source_target_pairs={{0,8},{8,0},{1,9},{9,1},{2,10},{10,2},{3,11},{11,3},{4,12},{12,4},... | collective-permute-start | bytes 1572872 | tf_op jit(solution)/shard_map/ppermute | solution.py:20
  108.8 25.6 %all-to-all-start.2 = ((bf16[16,16,1024]{2,1,0:T(8,128)(2,1)}), bf16[16,16,1024]{2,1,0:T(8,128)(2,1)S(1)}, u32[]{:S(2)}, u32[]{:S(2)}) async-start(bf16[16,16,1024]{2,1,0:T(8,128)(2,1)} %bitcast.9), calls=%async_computation.3 | async-start | bytes 1048576 | tf_op jit(solution)/shard_map/all_to_all | solution.py:221
Sparse Core Ops, SparseCore 0:
  10.1 49.0 all-gather.1
  65.0 43.3 reduce-scatter.1

commit v13 on v11

--- a/solution.py
+++ b/solution.py
@@ -218,7 +218,7 @@
     pre_mate = swapped(pre_rows, "wide_c")
     parts = weight_parts(picked, picked_mate, pre_rows, pre_mate, 4)
     summed = parts[0]
-    for d in (2, 1, 3):
+    for d in (1, 3, 2):
         pairs = [(at, at ^ d) for at in range(4)]
         summed = summed + lax.ppermute(parts[d], ("wide_x", "blk_x"), pairs).astype(F32)
     summed = summed.astype(BF16)

time: 154 us -> 155 us (level)
  blocking collectives: 18.8 us -> 17.2 us
    all_to_all x1, blocking collectives: 18.8 us -> 17.2 us  [shards(): lax.all_to_all(jnp.broadcast_to(total[None], (blocks, *total.shape)), BLK...]
  transfers between devices with their start and end apart: 12 -> 12, of which waited for: 9 -> 8; matrix products, arithmetic and copies ran while one was open for 8% -> 8% of each run, Pallas kernels for 1% -> 1%
where the time goes in v13:
time: 155 us; the launch traced here: 153 us
  waiting for transfers between devices  55.5 us (36%)
  starting transfers between devices  45.9 us (30%)
  blocking collectives  17.2 us (11%)
  between operations  14.3 us (9%)
  Pallas kernels  7.25 us (5%)
  matrix products  7.04 us (5%)
  other arithmetic  4.48 us (3%)
    all_to_all x1, blocking collectives, shards(): lax.all_to_all(jnp.broadcast_to(total[None], (blocks, *total.shape)), BLK...  17.2 us
    all_to_all x1, waiting for transfers between devices, shards(): lax.all_to_all(pooled.reshape(peers, capacity, features), WIDE, 0, 0, til...  15.4 us
    all_gather x1, waiting for transfers between devices, shards(): audio_line = lax.all_gather(audio, 'blk_z', axis=0, tiled=True)  13.4 us
    ppermute x3, waiting for transfers between devices, shards(): lax.ppermute(parts[d], ('wide_x', 'blk_x'), pairs).astype(F32)  10.3 us
    all_to_all x1, starting transfers between devices, shards(): lax.all_to_all(pooled.reshape(peers, capacity, features), WIDE, 0, 0, til...  10.2 us
    ppermute x3, starting transfers between devices, shards(): lax.ppermute(parts[d], ('wide_x', 'blk_x'), pairs).astype(F32)  9.82 us
    all_to_all x1, starting transfers between devices, shards(): lax.all_to_all(packed.reshape(peers, capacity, features), WIDE, 0, 0, til...  9.8 us
    ppermute x4, starting transfers between devices, swapped(): return lax.ppermute(array, axis, [(0, 1), (1, 0)])  9.72 us
  transfers between devices with their start and end apart: 12, of which 8 were waited for; matrix products, arithmetic and copies ran while one was open for 8% of the time, Pallas kernels for 1%

profile of v13, /device:TPU:6, one launch (start us, length us, event | category | flops | bytes accessed | tf_op | source)
XLA Modules:
  0.0 152.6 jit_solution(15323657335688562735)
XLA Ops:
  7.2 0.0 copy-start
  7.2 0.0 copy-start.4
  7.2 0.0 copy-start.5
  7.2 0.0 all-gather.2.cloned.1.call-start
  7.2 0.7 all-gather.2.cloned.1.call-update
  7.9 2.9 %collective-permute-start = (bf16[128,1024]{1,0:T(8,128)(2,1)}, bf16[128,1024]{1,0:T(8,128)(2,1)}, u32[]{:S(2)}, u32[]{:S(2)}) collective-permute-start(bf16[128,1024]{1,0:T(8,128)(2,1)} %refs_2_.1), channel_id=1, source_target_pairs={{0,8},{8,0},{1,9},{9,1},{2,10},{10,2},{3,11},{11,3},{4,12},{12,4},... | collective-permute-start | bytes 786440 | tf_op jit(solution)/shard_map/ppermute | solution.py:20
  10.8 0.7 convert_rsqrt_fusion
  11.5 2.0 %fusion.17 = bf16[32,8,1024]{2,1,0:T(8,128)(2,1)} fusion(f32[256]{0:T(256)S(1)} %convert_rsqrt_fusion, bf16[256,1024]{1,0:T(8,128)(2,1)} %param.9), kind=kLoop, calls=%fused_computation.27 | loop fusion | flops 786432 | bytes 1049600 | tf_op jit(solution)/shard_map/reshape | solution.py:190
  13.5 10.2 %all-to-all-start = ((bf16[32,8,1024]{2,1,0:T(8,128)(2,1)}), bf16[32,8,1024]{2,1,0:T(8,128)(2,1)S(1)}, u32[]{:S(2)}, u32[]{:S(2)}) async-start(bf16[32,8,1024]{2,1,0:T(8,128)(2,1)} %fusion.17), calls=%async_computation | async-start | bytes 1048576 | tf_op jit(solution)/shard_map/all_to_all | solution.py:189
  23.7 0.0 reduce-scatter.2.cloned.1.call-start
  23.8 0.0 copy-done.5
  23.8 0.1 convert_reduce_fusion.1
  24.0 2.0 %fusion.8 = f32[256,1024]{1,0:T(8,128)} fusion(bf16[1024,1024]{1,0:T(8,128)(2,1)S(1)} %copy-done, bf16[256,1024]{1,0:T(8,128)(2,1)S(1)} %copy-done.4, f32[256]{0:T(256)S(1)} %convert_rsqrt_fusion), kind=kOutput, calls=%fused_computation.13 | convolution fusion | flops 539754496 | bytes 3671040 | tf_op jit(solution)/shard_map/dot_general | solution.py:24
  26.0 15.4 %all-to-all-done = bf16[32,8,1024]{2,1,0:T(8,128)(2,1)S(1)} async-done(((bf16[32,8,1024]{2,1,0:T(8,128)(2,1)}), bf16[32,8,1024]{2,1,0:T(8,128)(2,1)S(1)}, u32[]{:S(2)}, u32[]{:S(2)}) %all-to-all-start) | async-done | bytes 524320 | tf_op jit(solution)/shard_map/all_to_all | solution.py:189
  41.4 0.3 convolution_convert_fusion
  41.7 0.5 fusion.14.slope_ref
  42.2 0.5 fusion.3
  42.7 1.9 %collective-permute-start.1 = (bf16[128,512]{1,0:T(8,128)(2,1)S(1)}, bf16[128,512]{1,0:T(8,128)(2,1)S(1)}, u32[]{:S(2)}, u32[]{:S(2)}) collective-permute-start(bf16[128,512]{1,0:T(8,128)(2,1)S(1)} %fusion.3), channel_id=1, source_target_pairs={{0,16},{16,0},{1,17},{17,1},{2,18},{18,2},{3,19},{19,3},{4,20},{20... | collective-permute-start | bytes 393224 | tf_op jit(solution)/shard_map/ppermute | solution.py:20
  44.7 1.1 fusion.4.own_picked
  45.8 0.0 collective-permute-done.refs_3_
  45.8 0.2 collective-permute-done.1.mate_picked
  46.0 13.4 %all-gather.2.cloned.1.call-done.refs_1_ = bf16[1024,1024]{1,0:T(8,128)(2,1)} async-done(((bf16[128,1024]{1,0:T(8,128)(2,1)}), bf16[1024,1024]{1,0:T(8,128)(2,1)}) %all-gather.2.cloned.1.call-update) | async-done | bytes 2097168 | tf_op jit(solution)/shard_map/all_gather | solution.py:182
  59.4 5.6 %shard_map.85 = (f32[128,1024]{1,0:T(8,128)}, bf16[128,1024]{1,0:T(8,128)(2,1)}, bf16[1024,1024]{1,0:T(8,128)(2,1)}) custom-call(s32[1]{0:T(128)} %bitcast.refs_0_, bf16[1024,1024]{1,0:T(8,128)(2,1)} %all-gather.2.cloned.1.call-done.refs_1_, bf16[128,1024]{1,0:T(8,128)(2,1)} %refs_2_.1, bf16[128,1024]{1,0:T(8,128)(2,1)} %collective-permute-done.refs_3_), custom_call_target="tpu_custom_call" | custom-call | flops 1610612736 | bytes 5242880 | tf_op jit(solution)/shard_map/pallas_call | solution.py:105
  65.0 0.0 copy-start.1
  65.0 0.0 reduce-scatter.2.cloned.1.call-update
  65.1 2.9 %collective-permute-start.2 = (bf16[128,1024]{1,0:T(8,128)(2,1)}, bf16[128,1024]{1,0:T(8,128)(2,1)S(1)}, u32[]{:S(2)}, u32[]{:S(2)}) collective-permute-start(bf16[128,1024]{1,0:T(8,128)(2,1)} %get-tuple-element.27), channel_id=1, source_target_pairs={{0,8},{8,0},{1,9},{9,1},{2,10},{10,2},{3,11},{11,3},{4,12},{12,4},... | collective-permute-start | bytes 786440 | tf_op jit(solution)/shard_map/ppermute | solution.py:20
  68.0 5.7 %collective-permute-done.2.arrived_ref = bf16[128,1024]{1,0:T(8,128)(2,1)S(1)} collective-permute-done((bf16[128,1024]{1,0:T(8,128)(2,1)}, bf16[128,1024]{1,0:T(8,128)(2,1)S(1)}, u32[]{:S(2)}, u32[]{:S(2)}) %collective-permute-start.2) | collective-permute-done | bytes 262176 | tf_op jit(solution)/shard_map/ppermute | solution.py:20
  73.7 1.1 shard_map.88
  74.8 9.8 %all-to-all-start.1 = ((bf16[32,8,1024]{2,1,0:T(8,128)(2,1)}), bf16[32,8,1024]{2,1,0:T(8,128)(2,1)}, u32[]{:S(2)}, u32[]{:S(2)}) async-start(bf16[32,8,1024]{2,1,0:T(8,128)(2,1)} %bitcast.7), calls=%async_computation.2 | async-start | bytes 1048576 | tf_op jit(solution)/shard_map/all_to_all | solution.py:214
  84.6 0.1 shard_map.86.own_pre
  84.7 2.1 %collective-permute-start.3 = (bf16[128,1024]{1,0:T(8,128)(2,1)S(1)}, bf16[128,1024]{1,0:T(8,128)(2,1)S(1)}, u32[]{:S(2)}, u32[]{:S(2)}) collective-permute-start(bf16[128,1024]{1,0:T(8,128)(2,1)S(1)} %shard_map.86.own_pre), channel_id=1, source_target_pairs={{0,16},{16,0},{1,17},{17,1},{2,18},{18,2},{3,19},{19,3},{4,20},{20... | collective-permute-start | bytes 786440 | tf_op jit(solution)/shard_map/ppermute | solution.py:20
  86.7 1.4 collective-permute-done.3.mate_pre
  88.1 0.9 copy-done.2
  89.0 0.5 shard_map.87
  89.5 2.9 %collective-permute-start.4 = (bf16[128,1024]{1,0:T(8,128)(2,1)S(1)}, bf16[128,1024]{1,0:T(8,128)(2,1)S(1)}, u32[]{:S(2)}, u32[]{:S(2)}) collective-permute-start(bf16[128,1024]{1,0:T(8,128)(2,1)S(1)} %get-tuple-element.30), channel_id=1, source_target_pairs={{0,8},{8,0},{32,40},{40,32},{1,9},{9,1},{33,41},{41,33},{2,10},{10... | collective-permute-start | bytes 786440 | tf_op jit(solution)/shard_map/ppermute | solution.py:223
  92.4 1.9 %collective-permute-start.5 = (bf16[128,1024]{1,0:T(8,128)(2,1)S(1)}, bf16[128,1024]{1,0:T(8,128)(2,1)S(1)}, u32[]{:S(2)}, u32[]{:S(2)}) collective-permute-start(bf16[128,1024]{1,0:T(8,128)(2,1)S(1)} %get-tuple-element.31), channel_id=1, source_target_pairs={{0,40},{8,32},{32,8},{40,0},{1,41},{9,33},{33,9},{41,1},{2,42},{10... | collective-permute-start | bytes 786440 | tf_op jit(solution)/shard_map/ppermute | solution.py:223
  94.4 5.0 %collective-permute-start.6 = (bf16[128,1024]{1,0:T(8,128)(2,1)S(1)}, bf16[128,1024]{1,0:T(8,128)(2,1)S(1)}, u32[]{:S(2)}, u32[]{:S(2)}) collective-permute-start(bf16[128,1024]{1,0:T(8,128)(2,1)S(1)} %get-tuple-element.32), channel_id=1, source_target_pairs={{0,32},{8,40},{32,0},{40,8},{1,33},{9,41},{33,1},{41,9},{2,34},{10... | collective-permute-start | bytes 786440 | tf_op jit(solution)/shard_map/ppermute | solution.py:223
  99.3 3.4 %collective-permute-done.4 = bf16[128,1024]{1,0:T(8,128)(2,1)S(1)} collective-permute-done((bf16[128,1024]{1,0:T(8,128)(2,1)S(1)}, bf16[128,1024]{1,0:T(8,128)(2,1)S(1)}, u32[]{:S(2)}, u32[]{:S(2)}) %collective-permute-start.4) | collective-permute-done | bytes 262176 | tf_op jit(solution)/shard_map/ppermute | solution.py:223
  102.7 6.9 %collective-permute-done.5 = bf16[128,1024]{1,0:T(8,128)(2,1)S(1)} collective-permute-done((bf16[128,1024]{1,0:T(8,128)(2,1)S(1)}, bf16[128,1024]{1,0:T(8,128)(2,1)S(1)}, u32[]{:S(2)}, u32[]{:S(2)}) %collective-permute-start.5) | collective-permute-done | bytes 262176 | tf_op jit(solution)/shard_map/ppermute | solution.py:223
  109.6 0.0 collective-permute-done.6
  109.6 0.9 add_convert_fusion
  110.5 0.0 all-to-all-done.1
  110.5 6.3 %all-to-all-start.2 = ((bf16[8,16,1024]{2,1,0:T(8,128)(2,1)}), bf16[8,16,1024]{2,1,0:T(8,128)(2,1)S(1)}, u32[]{:S(2)}, u32[]{:S(2)}) async-start(bf16[8,16,1024]{2,1,0:T(8,128)(2,1)} %bitcast.29), calls=%async_computation.3 | async-start | bytes 524288 | tf_op jit(solution)/shard_map/all_to_all | solution.py:227
  116.8 2.6 %fusion.2 = bf16[256,1024]{1,0:T(8,128)(2,1)} fusion(bf16[1024,1024]{1,0:T(8,128)(2,1)S(1)} %copy-done, f32[256,1024]{1,0:T(8,128)S(1)} %copy-done.3, bf16[256,1024]{1,0:T(8,128)(2,1)} %bitcast.8, f32[256]{0:T(256)S(1)} %convert_rsqrt_fusion), kind=kOutput, calls=%fused_computation.6 | convolution fusion | flops 538181632 | bytes 4195328 | tf_op jit(solution)/shard_map/dot_general | solution.py:24
  119.4 8.4 %all-to-all-done.2 = bf16[8,16,1024]{2,1,0:T(8,128)(2,1)S(1)} async-done(((bf16[8,16,1024]{2,1,0:T(8,128)(2,1)}), bf16[8,16,1024]{2,1,0:T(8,128)(2,1)S(1)}, u32[]{:S(2)}, u32[]{:S(2)}) %all-to-all-start.2) | async-done | bytes 262176 | tf_op jit(solution)/shard_map/all_to_all | solution.py:227
  127.8 0.1 broadcast_in_dim.8
  127.9 17.2 %all_to_all.20 = bf16[16,16,1024]{2,1,0:T(8,128)(2,1)S(1)} all-to-all(bf16[16,16,1024]{2,1,0:T(8,128)(2,1)S(1)} %broadcast_in_dim.8), channel_id=1, replica_groups=mesh['wide_y'=8,'wide_x'=2,'wide_c'=2,'blk_x'=2,'blk_z'=8] {'blk_x','blk..., dimensions={0} | all-to-all | bytes 1048576 | tf_op jit(solution)/shard_map/all_to_all | solution.py:232
  145.1 0.7 convert_reduce_fusion
  (12 shorter events, 0.1 us)
Async XLA Ops:
  7.2 16.8 %copy-start = (bf16[1024,1024]{1,0:T(8,128)(2,1)S(1)}, bf16[1024,1024]{1,0:T(8,128)(2,1)}, u32[]{:S(2)}) copy-start(bf16[1024,1024]{1,0:T(8,128)(2,1)} %param.11) | copy-start | bytes 6291460
  7.2 16.8 %copy-start.4 = (bf16[256,1024]{1,0:T(8,128)(2,1)S(1)}, bf16[256,1024]{1,0:T(8,128)(2,1)}, u32[]{:S(2)}) copy-start(bf16[256,1024]{1,0:T(8,128)(2,1)} %param.9) | copy-start | bytes 1572868
  7.2 16.6 %copy-start.5 = (s32[128,1]{0,1:T(1,128)S(1)}, s32[128,1]{0,1:T(1,128)}, u32[]{:S(2)}) copy-start(s32[128,1]{0,1:T(1,128)} %param.8) | copy-start | bytes 1540
  7.2 52.2 %all-gather.2.cloned.1.call-start = ((), (), s32[]{:S(2)}) async-start(), calls=%async_computation.5 | async-start | bytes 2359296 | tf_op jit(solution)/shard_map/all_gather | solution.py:182
  7.9 37.9 %collective-permute-start = (bf16[128,1024]{1,0:T(8,128)(2,1)}, bf16[128,1024]{1,0:T(8,128)(2,1)}, u32[]{:S(2)}, u32[]{:S(2)}) collective-permute-start(bf16[128,1024]{1,0:T(8,128)(2,1)} %refs_2_.1), channel_id=1, source_target_pairs={{0,8},{8,0},{1,9},{9,1},{2,10},{10,2},{3,11},{11,3},{4,12},{12,4},... | collective-permute-start | bytes 786440 | tf_op jit(solution)/shard_map/ppermute | solution.py:20
  13.5 27.9 %all-to-all-start = ((bf16[32,8,1024]{2,1,0:T(8,128)(2,1)}), bf16[32,8,1024]{2,1,0:T(8,128)(2,1)S(1)}, u32[]{:S(2)}, u32[]{:S(2)}) async-start(bf16[32,8,1024]{2,1,0:T(8,128)(2,1)} %fusion.17), calls=%async_computation | async-start | bytes 1048576 | tf_op jit(solution)/shard_map/all_to_all | solution.py:189
  23.7 122.1 %reduce-scatter.2.cloned.1.call-start = ((), (), s32[]{:S(2)}) async-start(), calls=%async_computation.6 | async-start | bytes 2359296 | tf_op jit(solution)/shard_map/reduce_scatter | solution.py:210
  42.7 3.2 %collective-permute-start.1 = (bf16[128,512]{1,0:T(8,128)(2,1)S(1)}, bf16[128,512]{1,0:T(8,128)(2,1)S(1)}, u32[]{:S(2)}, u32[]{:S(2)}) collective-permute-start(bf16[128,512]{1,0:T(8,128)(2,1)S(1)} %fusion.3), channel_id=1, source_target_pairs={{0,16},{16,0},{1,17},{17,1},{2,18},{18,2},{3,19},{19,3},{4,20},{20... | collective-permute-start | bytes 393224 | tf_op jit(solution)/shard_map/ppermute | solution.py:20
  65.0 8.6 %copy-start.1 = (f32[128,1024]{1,0:T(8,128)S(1)}, f32[128,1024]{1,0:T(8,128)}, u32[]{:S(2)}) copy-start(f32[128,1024]{1,0:T(8,128)} %get-tuple-element.26.kept_ref) | copy-start | bytes 1572868
  65.1 8.6 %collective-permute-start.2 = (bf16[128,1024]{1,0:T(8,128)(2,1)}, bf16[128,1024]{1,0:T(8,128)(2,1)S(1)}, u32[]{:S(2)}, u32[]{:S(2)}) collective-permute-start(bf16[128,1024]{1,0:T(8,128)(2,1)} %get-tuple-element.27), channel_id=1, source_target_pairs={{0,8},{8,0},{1,9},{9,1},{2,10},{10,2},{3,11},{11,3},{4,12},{12,4},... | collective-permute-start | bytes 786440 | tf_op jit(solution)/shard_map/ppermute | solution.py:20
  74.8 35.7 %all-to-all-start.1 = ((bf16[32,8,1024]{2,1,0:T(8,128)(2,1)}), bf16[32,8,1024]{2,1,0:T(8,128)(2,1)}, u32[]{:S(2)}, u32[]{:S(2)}) async-start(bf16[32,8,1024]{2,1,0:T(8,128)(2,1)} %bitcast.7), calls=%async_computation.2 | async-start | bytes 1048576 | tf_op jit(solution)/shard_map/all_to_all | solution.py:214
  84.7 3.4 %collective-permute-start.3 = (bf16[128,1024]{1,0:T(8,128)(2,1)S(1)}, bf16[128,1024]{1,0:T(8,128)(2,1)S(1)}, u32[]{:S(2)}, u32[]{:S(2)}) collective-permute-start(bf16[128,1024]{1,0:T(8,128)(2,1)S(1)} %shard_map.86.own_pre), channel_id=1, source_target_pairs={{0,16},{16,0},{1,17},{17,1},{2,18},{18,2},{3,19},{19,3},{4,20},{20... | collective-permute-start | bytes 786440 | tf_op jit(solution)/shard_map/ppermute | solution.py:20
  88.1 0.9 copy-start.2
  89.0 27.7 %copy-start.3 = (f32[256,1024]{1,0:T(8,128)S(1)}, f32[256,1024]{1,0:T(8,128)}, u32[]{:S(2)}) copy-start(f32[256,1024]{1,0:T(8,128)} %fusion.8) | copy-start | bytes 3145732
  89.5 13.2 %collective-permute-start.4 = (bf16[128,1024]{1,0:T(8,128)(2,1)S(1)}, bf16[128,1024]{1,0:T(8,128)(2,1)S(1)}, u32[]{:S(2)}, u32[]{:S(2)}) collective-permute-start(bf16[128,1024]{1,0:T(8,128)(2,1)S(1)} %get-tuple-element.30), channel_id=1, source_target_pairs={{0,8},{8,0},{32,40},{40,32},{1,9},{9,1},{33,41},{41,33},{2,10},{10... | collective-permute-start | bytes 786440 | tf_op jit(solution)/shard_map/ppermute | solution.py:223
  92.4 17.2 %collective-permute-start.5 = (bf16[128,1024]{1,0:T(8,128)(2,1)S(1)}, bf16[128,1024]{1,0:T(8,128)(2,1)S(1)}, u32[]{:S(2)}, u32[]{:S(2)}) collective-permute-start(bf16[128,1024]{1,0:T(8,128)(2,1)S(1)} %get-tuple-element.31), channel_id=1, source_target_pairs={{0,40},{8,32},{32,8},{40,0},{1,41},{9,33},{33,9},{41,1},{2,42},{10... | collective-permute-start | bytes 786440 | tf_op jit(solution)/shard_map/ppermute | solution.py:223
  94.4 15.2 %collective-permute-start.6 = (bf16[128,1024]{1,0:T(8,128)(2,1)S(1)}, bf16[128,1024]{1,0:T(8,128)(2,1)S(1)}, u32[]{:S(2)}, u32[]{:S(2)}) collective-permute-start(bf16[128,1024]{1,0:T(8,128)(2,1)S(1)} %get-tuple-element.32), channel_id=1, source_target_pairs={{0,32},{8,40},{32,0},{40,8},{1,33},{9,41},{33,1},{41,9},{2,34},{10... | collective-permute-start | bytes 786440 | tf_op jit(solution)/shard_map/ppermute | solution.py:223
  110.5 17.3 %all-to-all-start.2 = ((bf16[8,16,1024]{2,1,0:T(8,128)(2,1)}), bf16[8,16,1024]{2,1,0:T(8,128)(2,1)S(1)}, u32[]{:S(2)}, u32[]{:S(2)}) async-start(bf16[8,16,1024]{2,1,0:T(8,128)(2,1)} %bitcast.29), calls=%async_computation.3 | async-start | bytes 524288 | tf_op jit(solution)/shard_map/all_to_all | solution.py:227
Sparse Core Ops, SparseCore 0:
  10.1 49.2 all-gather.1
  65.2 43.4 reduce-scatter.1
